TPU v7x, 32 devices: a whole 2x2x4 slice. The times are simulated.
32 devices in a mesh: replica: 16 (over z, y, core), fsdp: 2 (over x).
Axes of the slice: x: 2, y: 2, z: 4, core: 2. Of those that a mesh axis runs over, the one named last changes fastest.
Arguments:
- hidden: bfloat16 [2, 8192, 2048], P(None, ('replica', 'fsdp')), may hold values from -6 to 6
- targets: int32 [2, 8192], P(None, ('replica', 'fsdp')), may hold values from 0 to 511
- valid: int32 [2, 8192], P(None, ('replica', 'fsdp')), may hold values 0 or 1
- plan: int32 [2], replicated, may hold values from 0 to 1, each once
- outer_head: float32 [2048, 512], P('fsdp'), may hold values from -6 to 6
- drift: bfloat16 [16, 2048, 512], P('replica', 'fsdp'), may hold values from -4 to 4
- ref_head: bfloat16 [2048, 512], P(('replica', 'fsdp')), may hold values from -6 to 6
Outputs:
- new_outer: float32 [2048, 512], P('fsdp')
- new_inner: float32 [16, 2048, 512], P('replica', 'fsdp')
Inputs may be any that keep to these rules, and one draw needn't show every extreme that they name: `plan`: each column block appears exactly once.
All inputs are finite; a program needn't handle non-finite values. No bound on the sum of `valid` on one device may be relied on, other than what follows from the above.
Results may differ from a plain program's by a relative error of at most 0.0003.
Values may be sent and summed in bfloat16 or wider, within the bound.
No kernel may reach another device: no remote copies, remote signals or barrier semaphores. Data moves between devices by JAX's collectives and lax.ppermute only.
A program may use at most 64 MiB of HBM per device.

v0:
```python
import math

import jax
import jax.numpy as jnp
from jax import lax
from jax.sharding import PartitionSpec as P

D = 2048
FRAGS = 2
STEPS = 2


soft_cap = 30.0
kl_weight = 0.5
inner_rate = 0.5
outer_rate = 0.7
mix_weight = 0.5
norm_eps = 1e-05


def normalize(hidden_rows):
    values = hidden_rows.astype(jnp.float32)
    factor = lax.rsqrt(jnp.mean(values * values, axis=-1, keepdims=True) + norm_eps)
    return (values * factor).astype(jnp.bfloat16)


def capped(raw):
    return soft_cap * jnp.tanh(raw * (4.0 / math.sqrt(D)) / soft_cap)


def logit_grads(policy, refer, target_ids, valid_rows):
    policy_log = policy - jnp.log(jnp.sum(jnp.exp(policy), axis=-1, keepdims=True))
    refer_log = refer - jnp.log(jnp.sum(jnp.exp(refer), axis=-1, keepdims=True))
    policy_prob = jnp.exp(policy_log)
    diverge = policy_log - refer_log
    kl_value = jnp.sum(policy_prob * diverge, axis=-1, keepdims=True)
    entries = jnp.arange(policy.shape[-1], dtype=jnp.int32)
    onehot = (target_ids[:, None] == entries[None, :]).astype(jnp.float32)
    upstream = valid_rows[:, None].astype(jnp.float32) * (
        policy_prob - onehot + kl_weight * policy_prob * (diverge - kl_value)
    )
    ratio = policy / soft_cap
    return (upstream * (1.0 - ratio * ratio) * (4.0 / math.sqrt(D))).astype(jnp.bfloat16)


def settle(outer_head, inner, pending, width_part, replicas):
    start, carried = pending
    fresh = lax.dynamic_slice_in_dim(outer_head, start, width_part, 1) - outer_rate * (
        carried / replicas
    )
    outer_head = lax.dynamic_update_slice_in_dim(outer_head, fresh, start, 1)
    inner_cols = lax.dynamic_slice_in_dim(inner, start, width_part, 1)
    mixed = mix_weight * inner_cols + (1.0 - mix_weight) * fresh
    inner = lax.dynamic_update_slice_in_dim(inner, mixed, start, 1)
    return (outer_head, inner)


def shards(hidden, targets, valid, plan, outer_head, drift, ref_head):
    replicas = lax.axis_size("replica")
    rows_local, width = outer_head.shape
    width_part = width // FRAGS
    inner = outer_head + drift[0].astype(jnp.float32)
    pending = None
    for index_step in range(STEPS):
        normed = normalize(hidden[index_step])

        def add_rows(piece):
            return jnp.dot(normed, piece, preferred_element_type=jnp.float32)

        policy_raw = add_rows(
            lax.all_gather(inner.astype(jnp.bfloat16), "fsdp", axis=0, tiled=True)
        )
        refer_raw = add_rows(lax.all_gather(ref_head, ("replica", "fsdp"), axis=0, tiled=True))
        grads = logit_grads(
            capped(policy_raw), capped(refer_raw), targets[index_step], valid[index_step]
        )
        columns_all = lax.all_to_all(normed, "fsdp", split_axis=1, concat_axis=0, tiled=True)
        gradient = lax.dot_general(
            columns_all,
            lax.all_gather(grads, "fsdp", axis=0, tiled=True),
            (((0,), (0,)), ((), ())),
            preferred_element_type=jnp.float32,
        )
        inner = inner - inner_rate * gradient
        if pending is not None:
            outer_head, inner = settle(outer_head, inner, pending, width_part, replicas)
        start = plan[index_step] * width_part
        outer_cols = lax.dynamic_slice_in_dim(outer_head, start, width_part, 1)
        delta = outer_cols - lax.dynamic_slice_in_dim(inner, start, width_part, 1)
        summed = lax.psum(delta, "replica")
        pending = (start, summed)
    outer_head, inner = settle(outer_head, inner, pending, width_part, replicas)
    return (outer_head, inner[None])


def solution(mesh):
    in_specs = (
        P(None, ("replica", "fsdp"), None),
        P(None, ("replica", "fsdp")),
        P(None, ("replica", "fsdp")),
        P(),
        P("fsdp", None),
        P("replica", "fsdp", None),
        P(("replica", "fsdp"), None),
    )
    out_specs = (P("fsdp", None), P("replica", "fsdp", None))
    return jax.shard_map(shards, mesh=mesh, in_specs=in_specs, out_specs=out_specs, check_vma=False)
```

profile of v0, /device:TPU:0, one launch (start us, length us, event | category | flops | bytes accessed | tf_op | source)
XLA Modules:
  0.0 380.3 jit_solution(4469024983411709812)
XLA Ops:
  7.2 0.0 all-gather.4.cloned.1.call-start
  7.2 1.7 copy.22
  8.9 0.2 copy-done.5
  9.1 1.3 fusion.4
  10.4 0.0 all-gather.6.cloned.1.call-start
  10.5 0.7 all-gather.6.cloned.1.call-update
  11.2 3.1 fusion.17
  14.3 1.5 copy.13
  15.7 0.3 fusion.2
  16.1 1.2 multiply_convert_fusion.1
  17.2 4.5 %all-to-all-start = ((bf16[256,2,1024]{0,2,1:T(8,128)(2,1)}), bf16[256,2,1024]{0,2,1:T(8,128)(2,1)}, u32[]{:S(2)}, u32[]{:S(2)}) async-start(bf16[256,2,1024]{0,2,1:T(8,128)(2,1)} %multiply_convert_fusion.1), calls=%async_computation | async-start | bytes 2097152 | tf_op jit(solution)/shard_map/all_to_all | solution.py:77
  21.8 0.0 all-gather.8.cloned.1.call-start
  21.9 26.8 %all-to-all-done = bf16[256,2,1024]{0,2,1:T(8,128)(2,1)} async-done(((bf16[256,2,1024]{0,2,1:T(8,128)(2,1)}), bf16[256,2,1024]{0,2,1:T(8,128)(2,1)}, u32[]{:S(2)}, u32[]{:S(2)}) %all-to-all-start) | async-done | bytes 1048608 | tf_op jit(solution)/shard_map/all_to_all | solution.py:77
  48.7 2.3 copy.10
  50.9 6.7 %all-gather.4.cloned.1.call-done = bf16[2048,512]{1,0:T(8,128)(2,1)} async-done(((bf16[1024,512]{1,0:T(8,128)(2,1)}), bf16[2048,512]{1,0:T(8,128)(2,1)}) %all-gather.4.cloned.1.call-update) | async-done | bytes 2097168 | tf_op jit(solution)/shard_map/all_gather | solution.py:71
  57.6 3.2 exponential_reduce_fusion.3
  60.8 56.3 %all-gather.6.cloned.1.call-done = bf16[2048,512]{1,0:T(8,128)(2,1)} async-done(((bf16[64,512]{1,0:T(8,128)(2,1)}), bf16[2048,512]{1,0:T(8,128)(2,1)}) %all-gather.6.cloned.1.call-update) | async-done | bytes 2097168 | tf_op jit(solution)/shard_map/all_gather | solution.py:73
  117.1 2.5 exponential_reduce_fusion.2
  119.7 0.3 multiply_reduce_fusion.1
  120.0 0.4 multiply_convert_fusion.3
  120.4 9.2 %all_gather.18 = bf16[512,512]{1,0:T(8,128)(2,1)S(1)} all-gather(bf16[256,512]{1,0:T(8,128)(2,1)S(1)} %multiply_convert_fusion.3), channel_id=1, replica_groups=mesh['replica'=16,'fsdp'=2] {'fsdp'}, dimensions={0}, use_global_device_ids=true | all-gather | bytes 786432 | tf_op jit(solution)/shard_map/all_gather | solution.py:80
  129.6 2.4 fusion.20
  132.1 1.5 copy.14
  133.6 0.3 fusion
  133.9 1.2 multiply_convert_fusion
  135.0 4.5 %all-to-all-start.1 = ((bf16[256,2,1024]{0,2,1:T(8,128)(2,1)}), bf16[256,2,1024]{0,2,1:T(8,128)(2,1)}, u32[]{:S(2)}, u32[]{:S(2)}) async-start(bf16[256,2,1024]{0,2,1:T(8,128)(2,1)} %multiply_convert_fusion), calls=%async_computation.1 | async-start | bytes 2097152 | tf_op jit(solution)/shard_map/all_to_all | solution.py:77
  139.6 0.0 all-reduce.3.cloned.1.call-start
  139.6 0.7 fusion.19
  141.5 23.8 %all-to-all-done.1 = bf16[256,2,1024]{0,2,1:T(8,128)(2,1)} async-done(((bf16[256,2,1024]{0,2,1:T(8,128)(2,1)}), bf16[256,2,1024]{0,2,1:T(8,128)(2,1)}, u32[]{:S(2)}, u32[]{:S(2)}) %all-to-all-start.1) | async-done | bytes 1048608 | tf_op jit(solution)/shard_map/all_to_all | solution.py:77
  165.2 2.3 copy.12
  167.5 3.4 exponential_reduce_fusion
  170.9 1.3 dynamic-slice_subtract_fusion
  172.2 0.0 all-reduce.3.cloned.1.call-update
  172.2 0.0 all-reduce.5.cloned.1.call-start
  172.2 3.2 all-gather.8.cloned.1.call-done
  175.4 2.5 exponential_reduce_fusion.1
  178.0 0.3 multiply_reduce_fusion
  178.3 0.4 multiply_convert_fusion.2
  178.7 8.9 %all_gather.20 = bf16[512,512]{1,0:T(8,128)(2,1)S(1)} all-gather(bf16[256,512]{1,0:T(8,128)(2,1)S(1)} %multiply_convert_fusion.2), channel_id=1, replica_groups=mesh['replica'=16,'fsdp'=2] {'fsdp'}, dimensions={0}, use_global_device_ids=true | all-gather | bytes 786432 | tf_op jit(solution)/shard_map/all_gather | solution.py:80
  187.7 2.1 multiply_subtract_fusion
  189.7 81.4 %all-reduce.3.cloned.1.call-done = f32[1024,256]{1,0:T(8,128)} async-done(((f32[1024,256]{1,0:T(8,128)}), f32[1024,256]{1,0:T(8,128)}) %all-reduce.3.cloned.1.call-update) | async-done | bytes 1048592 | tf_op jit(solution)/shard_map/psum | solution.py:90
  271.2 3.0 multiply_dynamic-update-slice_fusion
  274.1 2.4 dynamic-slice_subtract_fusion.1
  276.6 3.1 copy.20
  279.7 89.7 %all-reduce.5.cloned.1.call-done = f32[1024,256]{1,0:T(8,128)} async-done(((f32[1024,256]{1,0:T(8,128)}), f32[1024,256]{1,0:T(8,128)}) %all-reduce.5.cloned.1.call-update) | async-done | bytes 1048592 | tf_op jit(solution)/shard_map/psum | solution.py:90
  369.3 2.9 bitcast_dynamic-update-slice_fusion
  372.2 0.3 fusion.16
  372.5 1.3 copy-done
  (35 shorter events, 0.2 us)
Async XLA Ops:
  7.2 50.4 %all-gather.4.cloned.1.call-start = ((), (), s32[]{:S(2)}) async-start(), calls=%async_computation.2 | async-start | bytes 3145728 | tf_op jit(solution)/shard_map/all_gather | solution.py:71
  7.2 1.9 copy-start.5
  10.4 106.7 %all-gather.6.cloned.1.call-start = ((), (), s32[]{:S(2)}) async-start(), calls=%async_computation.3 | async-start | bytes 2162688 | tf_op jit(solution)/shard_map/all_gather | solution.py:73
  16.1 5.7 %copy-start.10 = (s32[2,256]{1,0:T(2,128)S(1)}, s32[2,256]{1,0:T(2,128)}, u32[]{:S(2)}) copy-start(s32[2,256]{1,0:T(2,128)} %param.8) | copy-start | bytes 6148
  16.1 5.8 %copy-start.11 = (s32[2,256]{1,0:T(2,128)S(1)}, s32[2,256]{1,0:T(2,128)}, u32[]{:S(2)}) copy-start(s32[2,256]{1,0:T(2,128)} %param.9) | copy-start | bytes 6148
  17.2 31.4 %all-to-all-start = ((bf16[256,2,1024]{0,2,1:T(8,128)(2,1)}), bf16[256,2,1024]{0,2,1:T(8,128)(2,1)}, u32[]{:S(2)}, u32[]{:S(2)}) async-start(bf16[256,2,1024]{0,2,1:T(8,128)(2,1)} %multiply_convert_fusion.1), calls=%async_computation | async-start | bytes 2097152 | tf_op jit(solution)/shard_map/all_to_all | solution.py:77
  21.8 153.7 %all-gather.8.cloned.1.call-start = ((), (), s32[]{:S(2)}) async-start(), calls=%async_computation.5 | async-start | bytes 3145728 | tf_op jit(solution)/shard_map/all_gather | solution.py:71
  117.1 2.6 copy-start.9
  119.7 9.9 %copy-start.3 = (bf16[2,256,1024]{2,1,0:T(8,128)(2,1)S(1)}, bf16[2,256,1024]{2,1,0:T(8,128)(2,1)}, u32[]{:S(2)}) copy-start(bf16[2,256,1024]{2,1,0:T(8,128)(2,1)} %copy.10) | copy-start | bytes 3145732
  119.7 9.9 %copy-start.6 = (bf16[1,1024,512]{2,1,0:T(8,128)(2,1)S(1)}, bf16[1,1024,512]{2,1,0:T(8,128)(2,1)}, u32[]{:S(2)}) copy-start(bf16[1,1024,512]{2,1,0:T(8,128)(2,1)} %param.12) | copy-start | bytes 3145732
  133.9 5.7 %copy-start.12 = (s32[2]{0:T(128)S(1)}, s32[2]{0:T(128)}, u32[]{:S(2)}) copy-start(s32[2]{0:T(128)} %param.10) | copy-start | bytes 28
  135.0 30.2 %all-to-all-start.1 = ((bf16[256,2,1024]{0,2,1:T(8,128)(2,1)}), bf16[256,2,1024]{0,2,1:T(8,128)(2,1)}, u32[]{:S(2)}, u32[]{:S(2)}) async-start(bf16[256,2,1024]{0,2,1:T(8,128)(2,1)} %multiply_convert_fusion), calls=%async_computation.1 | async-start | bytes 2097152 | tf_op jit(solution)/shard_map/all_to_all | solution.py:77
  139.6 131.6 %all-reduce.3.cloned.1.call-start = ((), (), s32[]{:S(2)}) async-start(), calls=%async_computation.4 | async-start | bytes 2097152 | tf_op jit(solution)/shard_map/psum | solution.py:90
  167.5 3.4 copy-start.1
  172.2 197.2 %all-reduce.5.cloned.1.call-start = ((), (), s32[]{:S(2)}) async-start(), calls=%async_computation.6 | async-start | bytes 2097152 | tf_op jit(solution)/shard_map/psum | solution.py:90
  175.4 2.6 copy-start.8
  178.0 9.7 %copy-start.2 = (f32[1024,512]{1,0:T(8,128)S(1)}, f32[1024,512]{1,0:T(8,128)}, u32[]{:S(2)}) copy-start(f32[1024,512]{1,0:T(8,128)} %get-tuple-element.17) | copy-start | bytes 6291460
  178.0 9.7 %copy-start.7 = (bf16[2,256,1024]{2,1,0:T(8,128)(2,1)S(1)}, bf16[2,256,1024]{2,1,0:T(8,128)(2,1)}, u32[]{:S(2)}) copy-start(bf16[2,256,1024]{2,1,0:T(8,128)(2,1)} %copy.12) | copy-start | bytes 3145732
  369.3 2.9 copy-start.4
  372.5 1.3 copy-start
Sparse Core Ops, SparseCore 0:
  10.5 47.0 all-gather.3
  60.6 56.4 all-gather.5
  132.2 43.1 all-gather.7
  178.7 92.3 all-reduce.2
  276.7 92.6 all-reduce.4
where the time goes:
time: 381 us; the launch traced here: 380 us
  waiting for transfers between devices  289 us (76%)
  blocking collectives  18.1 us (5%)
  local copies, waits for them, and re-layouts  17.6 us (5%)
  matrix products  16.2 us (4%)
  other arithmetic  15.5 us (4%)
  between operations  15.2 us (4%)
  starting transfers between devices  9.22 us (2%)
    psum x2, waiting for transfers between devices, shards(): summed = lax.psum(delta, 'replica')  171 us
    all_gather x1, waiting for transfers between devices, shards(): lax.all_gather(ref_head, ('replica', 'fsdp'), axis=0, tiled=True)  56.3 us
    all_to_all x2, waiting for transfers between devices, shards(): lax.all_to_all(normed, 'fsdp', split_axis=1, concat_axis=0, tiled=True)  50.5 us
    all_gather x2, blocking collectives, shards(): lax.all_gather(grads, 'fsdp', axis=0, tiled=True)  18.1 us
    dot_general x4, matrix products, add_rows(): return jnp.dot(normed, piece, preferred_element_type=jnp.float32)  11.7 us
    all_gather x2, waiting for transfers between devices, shards(): lax.all_gather(inner.astype(jnp.bfloat16), 'fsdp', axis=0, tiled=True)  9.88 us
    unnamed x30, local copies, waits for them, and re-layouts  9.25 us
    all_to_all x2, starting transfers between devices, shards(): lax.all_to_all(normed, 'fsdp', split_axis=1, concat_axis=0, tiled=True)  9.01 us
  transfers between devices with their start and end apart: 7, of which 7 were waited for; matrix products, arithmetic and copies ran while one was open for 8% of the time, Pallas kernels for 0%

commit v1 on v0

v1 whole, which is shorter than its diff:
```python
import math

import jax
import jax.numpy as jnp
from jax import lax
from jax.sharding import PartitionSpec as P

D = 2048
FRAGS = 2
STEPS = 2
CORES = 2
MAJOR = 4

soft_cap = 30.0
kl_weight = 0.5
inner_rate = 0.5
outer_rate = 0.7
mix_weight = 0.5
norm_eps = 1e-05

f32 = jnp.float32
bf16 = jnp.bfloat16
f16 = jnp.float16
logit_type = jnp.float32


def swap(value, axis, mask):
    size = lax.axis_size(axis)
    return lax.ppermute(value, axis, [(i, i ^ mask) for i in range(size)])


def rows_at(value, block, count):
    return lax.dynamic_slice_in_dim(value, block * count, count, 0)


def columns_at(value, block, count):
    return lax.dynamic_slice_in_dim(value, block * count, count, 1)


def place(pieces, spots):
    count = pieces[0].shape[0]
    whole = jnp.zeros((count * len(pieces),) + pieces[0].shape[1:], pieces[0].dtype)
    for piece, spot in zip(pieces, spots):
        whole = lax.dynamic_update_slice_in_dim(whole, piece, spot * count, 0)
    return whole


def in_pair(first, own, other):
    return jnp.where(
        first, jnp.concatenate([own, other], 0), jnp.concatenate([other, own], 0)
    )


def grid_of_replicas():
    chips = lax.axis_size("replica") // CORES
    minor = chips // MAJOR
    me = lax.axis_index("replica")
    return minor, me % CORES, me // (CORES * minor)


def gather_reference(rows):
    minor, core, major = grid_of_replicas()
    fsdp = lax.axis_size("fsdp")
    me = lax.axis_index("fsdp")
    masks = range(fsdp)
    block = place([rows] + [swap(rows, "fsdp", m) for m in masks[1:]], [me ^ m for m in masks])
    spots = lax.axis_index("replica")
    blocks = [(block, spots)]
    step = CORES * minor
    blocks = [(swap(b, "replica", m * step) if m else b, s ^ (m * step)) for b, s in blocks for m in range(MAJOR)]
    mask = CORES
    while mask < step:
        stacked = jnp.concatenate([b for b, _ in blocks], 0)
        other = swap(stacked, "replica", mask)
        blocks = blocks + [
            (p, s ^ mask) for p, (_, s) in zip(jnp.split(other, len(blocks), 0), blocks)
        ]
        mask *= 2
    stacked = jnp.concatenate([b for b, _ in blocks], 0)
    other = swap(stacked, "replica", 1)
    blocks = blocks + [(p, s ^ 1) for p, (_, s) in zip(jnp.split(other, len(blocks), 0), blocks)]
    return place([b for b, _ in blocks], [s for _, s in blocks])


def mean_over_replicas(delta):
    minor, core, major = grid_of_replicas()
    replicas = lax.axis_size("replica")
    delta = delta * (1.0 / replicas)
    half = delta.shape[0] // CORES
    part = rows_at(delta, core, half) + swap(rows_at(delta, 1 - core, half), "replica", 1)
    step = CORES * minor
    quarter = half // MAJOR
    sent = part.astype(f16)
    own = rows_at(part, major, quarter)
    for m in (2, 1, 3):
        own = own + swap(rows_at(sent, major ^ m, quarter), "replica", m * step).astype(f32)
    mask = CORES
    while mask < step:
        own = own + swap(own, "replica", mask)
        mask *= 2
    own = own.astype(f16)
    pieces = [own] + [swap(own, "replica", m * step) for m in (2, 1, 3)]
    gathered = place(pieces, [major ^ m for m in (0, 2, 1, 3)])
    return in_pair(core == 0, gathered, swap(gathered, "replica", 1)).astype(f32)


def normalize(hidden_rows):
    values = hidden_rows.astype(f32)
    factor = lax.rsqrt(jnp.mean(values * values, axis=-1, keepdims=True) + norm_eps)
    return (values * factor).astype(bf16)


def capped(raw):
    return soft_cap * jnp.tanh(raw * (4.0 / math.sqrt(D)) / soft_cap)


def log_softmax(logits):
    return logits - jnp.log(jnp.sum(jnp.exp(logits), axis=-1, keepdims=True))


def logit_grads(policy, refer_log, target_ids, valid_rows):
    policy_log = log_softmax(policy)
    policy_prob = jnp.exp(policy_log)
    diverge = policy_log - refer_log
    kl_value = jnp.sum(policy_prob * diverge, axis=-1, keepdims=True)
    entries = jnp.arange(policy.shape[-1], dtype=jnp.int32)
    onehot = (target_ids[:, None] == entries[None, :]).astype(f32)
    upstream = valid_rows[:, None].astype(f32) * (
        policy_prob - onehot + kl_weight * policy_prob * (diverge - kl_value)
    )
    ratio = policy / soft_cap
    return (upstream * (1.0 - ratio * ratio) * (4.0 / math.sqrt(D))).astype(bf16)


def dot(a, b):
    return jnp.dot(a, b, preferred_element_type=f32)


def dot_rows(a, b):
    return lax.dot_general(a, b, (((0,), (0,)), ((), ())), preferred_element_type=f32)


def shards(hidden, targets, valid, plan, outer_head, drift, ref_head):
    rows_local, width = outer_head.shape
    part = width // FRAGS
    fsdp = lax.axis_size("fsdp")
    me = lax.axis_index("fsdp")
    masks = range(fsdp)

    normed = [normalize(hidden[s]) for s in range(STEPS)]
    features = [
        [columns_at(n, me, rows_local)]
        + [swap(columns_at(n, me ^ m, rows_local), "fsdp", m) for m in masks[1:]]
        for n in normed
    ]
    reference = gather_reference(ref_head)
    refer_log = [log_softmax(capped(dot(n, reference))) for n in normed]

    inner = outer_head + drift[0].astype(f32)
    means = []
    for s in range(STEPS):
        weights = inner.astype(bf16)
        raw = dot(features[s][0], weights)
        for m in masks[1:]:
            raw = raw + swap(dot(features[s][m], weights).astype(logit_type), "fsdp", m).astype(f32)
        grads = logit_grads(capped(raw), refer_log[s], targets[s], valid[s])
        total = dot_rows(features[s][0], grads)
        for m in masks[1:]:
            total = total + dot_rows(features[s][m], swap(grads, "fsdp", m))
        inner = inner - inner_rate * total
        start = plan[s] * part
        delta = lax.dynamic_slice_in_dim(outer_head - inner, start, part, 1)
        means.append(mean_over_replicas(delta))
    first, second = means
    mean = jnp.where(
        plan[0] == 0,
        jnp.concatenate([first, second], 1),
        jnp.concatenate([second, first], 1),
    )
    new_outer = outer_head - outer_rate * mean
    new_inner = mix_weight * inner + (1.0 - mix_weight) * new_outer
    return (new_outer, new_inner[None])


def solution(mesh):
    in_specs = (
        P(None, ("replica", "fsdp"), None),
        P(None, ("replica", "fsdp")),
        P(None, ("replica", "fsdp")),
        P(),
        P("fsdp", None),
        P("replica", "fsdp", None),
        P(("replica", "fsdp"), None),
    )
    out_specs = (P("fsdp", None), P("replica", "fsdp", None))
    return jax.shard_map(shards, mesh=mesh, in_specs=in_specs, out_specs=out_specs, check_vma=False)
```

time: 381 us -> 127 us (0.33)
  waiting for transfers between devices: 289 us -> 48.9 us
  starting transfers between devices: 9.22 us -> 36.4 us
  blocking collectives: 18.1 us -> 0 us
  between operations: 15.2 us -> 3.21 us
  local copies, waits for them, and re-layouts: 17.6 us -> 10.2 us
    psum x2 -> x0, waiting for transfers between devices: 171 us -> none  [shards(): summed = lax.psum(delta, 'replica')]
    all_gather x3 -> x0, waiting for transfers between devices: 66.2 us -> none  [the longest x1 56.3 us: shards(): lax.all_gather(ref_head, ('replica', 'fsdp'), axis=0, tiled=True)]
    all_to_all x2 -> x0, waiting for transfers between devices: 50.5 us -> none  [shards(): lax.all_to_all(normed, 'fsdp', split_axis=1, concat_axis=0, tiled=True)]
    ppermute x0 -> x30, waiting for transfers between devices: none -> 48.9 us  [swap(): return lax.ppermute(value, axis, [(i, i ^ mask) for i in range(size)])]
    ppermute x0 -> x30, starting transfers between devices: none -> 36.4 us  [swap(): return lax.ppermute(value, axis, [(i, i ^ mask) for i in range(size)])]
    all_gather x2 -> x0, blocking collectives: 18.1 us -> none  [shards(): lax.all_gather(grads, 'fsdp', axis=0, tiled=True)]
    all_to_all x2 -> x0, starting transfers between devices: 9.01 us -> none  [shards(): lax.all_to_all(normed, 'fsdp', split_axis=1, concat_axis=0, tiled=True)]
    dynamic_update_slice x3 -> x2, other arithmetic: 6.1 us -> 0.04 us  [place(): whole = lax.dynamic_update_slice_in_dim(whole, piece, spot * count, 0)]
  transfers between devices with their start and end apart: 7 -> 30, of which waited for: 7 -> 15; matrix products, arithmetic and copies ran while one was open for 8% -> 17% of each run, Pallas kernels for 0% -> 0%
where the time goes in v1:
time: 127 us
  waiting for transfers between devices  48.9 us (39%)
  starting transfers between devices  36.4 us (29%)
  other arithmetic  14.1 us (11%)
  matrix products  13.9 us (11%)
  local copies, waits for them, and re-layouts  10.2 us (8%)
  between operations  3.21 us (3%)
    ppermute x30, waiting for transfers between devices, swap(): return lax.ppermute(value, axis, [(i, i ^ mask) for i in range(size)])  48.9 us
    ppermute x30, starting transfers between devices, swap(): return lax.ppermute(value, axis, [(i, i ^ mask) for i in range(size)])  36.4 us
    dot_general x6, matrix products, dot(): return jnp.dot(a, b, preferred_element_type=f32)  9.68 us
    unnamed x32, local copies, waits for them, and re-layouts  4.52 us
    dot_general x4, matrix products, dot_rows(): lax.dot_general(a, b, (((0,), (0,)), ((), ())), preferred_element_type=f32)  4.19 us
    broadcast_in_dim x1, other arithmetic, shards(): return (new_outer, new_inner[None])  2.87 us
    dynamic_slice x2, local copies, waits for them, and re-layouts, columns_at(): return lax.dynamic_slice_in_dim(value, block * count, count, 1)  2.74 us
  transfers between devices with their start and end apart: 30, of which 15 were waited for; matrix products, arithmetic and copies ran while one was open for 17% of the time, Pallas kernels for 0%

profile of v1, /device:TPU:0, one launch (start us, length us, event | category | flops | bytes accessed | tf_op | source)
XLA Modules:
  0.0 126.8 jit_solution(1631711514598274796)
XLA Ops:
  0.6 3.0 %collective-permute-start.2 = (bf16[64,512]{1,0:T(8,128)(2,1)}, bf16[64,512]{1,0:T(8,128)(2,1)S(1)}, u32[]{:S(2)}, u32[]{:S(2)}) collective-permute-start(bf16[64,512]{1,0:T(8,128)(2,1)} %param.13), channel_id=1, source_target_pairs={{0,1},{1,0},{2,3},{3,2},{4,5},{5,4},{6,7},{7,6},{8,9},{9,8},{10,11... | collective-permute-start | bytes 196616 | tf_op jit(solution)/shard_map/ppermute | solution.py:29
  3.6 2.0 %fusion.2 = (f32[256]{0:T(256)S(1)}, f32[256]{0:T(256)S(1)}) fusion(bf16[2,256,2048]{2,1,0:T(8,128)(2,1)} %param.7), kind=kLoop, calls=%fused_computation.6 | loop fusion | flops 3145216 | bytes 2099200 | tf_op jit(solution)/shard_map/reduce_sum | solution.py:109
  5.7 1.3 %fusion.3 = (bf16[256,2048]{1,0:T(8,128)(2,1)S(1)}, bf16[256,2048]{1,0:T(8,128)(2,1)}) fusion(f32[256]{0:T(256)S(1)} %get-tuple-element.46, bf16[2,256,2048]{2,1,0:T(8,128)(2,1)S(1)} %copy-done.6, f32[256]{0:T(256)S(1)} %get-tuple-element.47), kind=kLoop, calls=%fused_computation.7 | loop fusion | flops 3145728 | bytes 4196352 | tf_op jit(solution)/shard_map/convert_element_type | solution.py:110
  7.0 1.9 %constant_dynamic-slice_fusion.9 = bf16[256,1024]{1,0:T(8,128)(2,1)} fusion(bf16[256,2048]{1,0:T(8,128)(2,1)} %get-tuple-element.17, s32[]{:T(128)S(6)} %select_n.138), kind=kLoop, calls=%fused_computation.107 | loop fusion | bytes 1048580 | tf_op jit(solution)/shard_map/dynamic_slice | solution.py:37
  9.1 0.8 constant_dynamic-slice_fusion.4
  9.9 1.9 %collective-permute-start.18 = (bf16[256,1024]{1,0:T(8,128)(2,1)}, bf16[256,1024]{1,0:T(8,128)(2,1)}, u32[]{:S(2)}, u32[]{:S(2)}) collective-permute-start(bf16[256,1024]{1,0:T(8,128)(2,1)} %constant_dynamic-slice_fusion.4), channel_id=1, source_target_pairs={{0,1},{1,0},{2,3},{3,2},{4,5},{5,4},{6,7},{7,6},{8,9},{9,8},{10,11... | collective-permute-start | bytes 1572872 | tf_op jit(solution)/shard_map/ppermute | solution.py:29
  11.9 1.6 %collective-permute-start.3 = (bf16[128,512]{1,0:T(8,128)(2,1)S(1)}, bf16[128,512]{1,0:T(8,128)(2,1)}, u32[]{:S(2)}, u32[]{:S(2)}) collective-permute-start(bf16[128,512]{1,0:T(8,128)(2,1)S(1)} %constant_dynamic-update-slice_fusion.17), channel_id=1, source_target_pairs={{0,8},{2,10},{4,12},{6,14},{8,0},{10,2},{12,4},{14,6},{16,24},{18,... | collective-permute-start | bytes 393224 | tf_op jit(solution)/shard_map/ppermute | solution.py:29
  13.5 2.6 %collective-permute-start.4 = (bf16[128,512]{1,0:T(8,128)(2,1)S(1)}, bf16[128,512]{1,0:T(8,128)(2,1)S(1)}, u32[]{:S(2)}, u32[]{:S(2)}) collective-permute-start(bf16[128,512]{1,0:T(8,128)(2,1)S(1)} %constant_dynamic-update-slice_fusion.17), channel_id=1, source_target_pairs={{0,16},{2,18},{4,20},{6,22},{8,24},{10,26},{12,28},{14,30},{16,0},... | collective-permute-start | bytes 393224 | tf_op jit(solution)/shard_map/ppermute | solution.py:29
  16.5 2.0 %collective-permute-done.3 = bf16[128,512]{1,0:T(8,128)(2,1)} collective-permute-done((bf16[128,512]{1,0:T(8,128)(2,1)S(1)}, bf16[128,512]{1,0:T(8,128)(2,1)}, u32[]{:S(2)}, u32[]{:S(2)}) %collective-permute-start.3) | collective-permute-done | bytes 131104 | tf_op jit(solution)/shard_map/ppermute | solution.py:29
  18.5 7.1 %collective-permute-done.4 = bf16[128,512]{1,0:T(8,128)(2,1)S(1)} collective-permute-done((bf16[128,512]{1,0:T(8,128)(2,1)S(1)}, bf16[128,512]{1,0:T(8,128)(2,1)S(1)}, u32[]{:S(2)}, u32[]{:S(2)}) %collective-permute-start.4) | collective-permute-done | bytes 131104 | tf_op jit(solution)/shard_map/ppermute | solution.py:29
  25.6 0.9 pad_maximum_fusion
  26.5 1.6 %collective-permute-start.6 = (bf16[512,512]{1,0:T(8,128)(2,1)S(1)}, bf16[512,512]{1,0:T(8,128)(2,1)S(1)}, u32[]{:S(2)}, u32[]{:S(2)}) collective-permute-start(bf16[512,512]{1,0:T(8,128)(2,1)S(1)} %pad_maximum_fusion), channel_id=1, source_target_pairs={{0,4},{2,6},{4,0},{6,2},{8,12},{10,14},{12,8},{14,10},{16,20},{18,... | collective-permute-start | bytes 1572872 | tf_op jit(solution)/shard_map/ppermute | solution.py:29
  28.1 0.9 constant_dynamic-update-slice_fusion.3
  29.1 1.5 %fusion.30 = f32[256,512]{1,0:T(8,128)S(1)} fusion(bf16[256,1024]{1,0:T(8,128)(2,1)} %collective-permute-done, f32[1024,512]{1,0:T(8,128)S(1)} %copy-done, bf16[1,1024,512]{2,1,0:T(8,128)(2,1)S(1)} %copy-done.5), kind=kOutput, calls=%fused_computation.113 | convolution fusion | flops 270008320 | bytes 4194304 | tf_op jit(solution)/shard_map/dot_general | solution.py:136
  31.5 5.1 %collective-permute-done.6 = bf16[512,512]{1,0:T(8,128)(2,1)S(1)} collective-permute-done((bf16[512,512]{1,0:T(8,128)(2,1)S(1)}, bf16[512,512]{1,0:T(8,128)(2,1)S(1)}, u32[]{:S(2)}, u32[]{:S(2)}) %collective-permute-start.6) | collective-permute-done | bytes 524320 | tf_op jit(solution)/shard_map/ppermute | solution.py:29
  36.8 8.2 %collective-permute-done.1 = f32[256,512]{1,0:T(8,128)S(1)} collective-permute-done((f32[256,512]{1,0:T(8,128)S(1)}, f32[256,512]{1,0:T(8,128)S(1)}, u32[]{:S(2)}, u32[]{:S(2)}) %collective-permute-start.1) | collective-permute-done | bytes 524320 | tf_op jit(solution)/shard_map/ppermute | solution.py:29
  45.9 0.9 exponential_reduce_fusion.2
  49.0 5.9 %collective-permute-done.8 = bf16[256,512]{1,0:T(8,128)(2,1)S(1)} collective-permute-done((bf16[256,512]{1,0:T(8,128)(2,1)S(1)}, bf16[256,512]{1,0:T(8,128)(2,1)S(1)}, u32[]{:S(2)}, u32[]{:S(2)}) %collective-permute-start.8) | collective-permute-done | bytes 262176 | tf_op jit(solution)/shard_map/ppermute | solution.py:29
  54.9 1.7 %multiply_subtract_fusion.1 = f32[1024,512]{1,0:T(8,128)S(1)} fusion(f32[1024,512]{1,0:T(8,128)S(1)} %fusion.22, bf16[256,1024]{1,0:T(8,128)(2,1)} %collective-permute-done, bf16[256,512]{1,0:T(8,128)(2,1)S(1)} %collective-permute-done.8, f32[1024,512]{1,0:T(8,128)S(1)} %copy-done, bf16[1,1024,512]{2,1,0:T(8,128)(2,1)S(1)} %copy-done.5), kind=kOutput, calls=%fused_computation.14 | convolution fusion | flops 271056896 | bytes 8126464 | tf_op jit(solution)/shard_map/dot_general | solution.py:140
  56.6 1.3 %copy-done.1 = f32[1024,512]{1,0:T(8,128)} copy-done((f32[1024,512]{1,0:T(8,128)}, f32[1024,512]{1,0:T(8,128)S(1)}, u32[]{:S(2)}) %copy-start.1) | copy-done | bytes 2097176
  57.9 2.3 %fusion.15 = f32[256,512]{1,0:T(8,128)} fusion(bf16[256,1024]{1,0:T(8,128)(2,1)} %collective-permute-done.18, f32[1024,512]{1,0:T(8,128)S(1)} %multiply_subtract_fusion.1), kind=kOutput, calls=%fused_computation.39 | convolution fusion | flops 268959744 | bytes 3145728 | tf_op jit(solution)/shard_map/dot_general | solution.py:136
  62.9 2.6 %exponential_reduce_fusion = (f32[256]{0:T(256)S(1)}, f32[256,512]{1,0:T(8,128)S(1)}) fusion(bf16[256,2048]{1,0:T(8,128)(2,1)S(1)} %get-tuple-element.16, bf16[2048,512]{1,0:T(8,128)(2,1)} %copy-done.9), kind=kOutput, calls=%fused_computation.35 | convolution fusion | flops 537263872 | bytes 3671040 | tf_op jit(solution)/shard_map/dot_general | solution.py:136
  65.5 6.6 %collective-permute-done.19 = f32[256,512]{1,0:T(8,128)} collective-permute-done((f32[256,512]{1,0:T(8,128)}, f32[256,512]{1,0:T(8,128)}, u32[]{:S(2)}, u32[]{:S(2)}) %collective-permute-start.19) | collective-permute-done | bytes 524320 | tf_op jit(solution)/shard_map/ppermute | solution.py:29
  72.1 1.7 %exponential_reduce_fusion.1 = (f32[256]{0:T(256)S(1)}, f32[256,512]{1,0:T(8,128)S(1)}) fusion(f32[256,512]{1,0:T(8,128)} %collective-permute-done.19, f32[1024,512]{1,0:T(8,128)S(1)} %copy-done.2, bf16[256,2048]{1,0:T(8,128)(2,1)S(1)} %get-tuple-element.16, s32[]{:T(128)S(6)} %select_n.137), kind=kOutput, calls=%fused_computation.37 | convolution fusion | flops 269483776 | bytes 3671044 | tf_op jit(solution)/shard_map/dot_general | solution.py:136
  73.8 1.4 %multiply_reduce_fusion = f32[256]{0:T(256)S(1)} fusion(f32[256,512]{1,0:T(8,128)S(1)} %get-tuple-element.43, f32[256]{0:T(256)S(1)} %log.35, f32[256]{0:T(256)S(1)} %log.34, f32[256,512]{1,0:T(8,128)S(1)} %get-tuple-element.45, f32[256,512]{1,0:T(8,128)} %collective-permute-done.19), kind=kLoop, calls=%fused_computation.33 | loop fusion | flops 1048320 | bytes 1575936 | tf_op jit(solution)/shard_map/reduce_sum | solution.py:125
  75.1 1.5 %multiply_convert_fusion = bf16[256,512]{1,0:T(8,128)(2,1)S(1)} fusion(f32[256,512]{1,0:T(8,128)S(1)} %get-tuple-element.43, f32[256]{0:T(256)S(1)} %multiply_reduce_fusion, f32[256]{0:T(256)S(1)} %log.35, s32[256]{0:T(256)S(1)} %bitcast.38, f32[256]{0:T(256)S(1)} %log.34, f32[256]{0:T(256)S(1)} %bitcast.37, f32[256,512]{1,0:T(8,128)S(1)} %get-tuple-element.45, ...), kind=kLoop, calls=%fused_computation.32 | loop fusion | flops 2490368 | bytes 1840128 | tf_op jit(solution)/shard_map/convert_element_type | solution.py:132
  76.6 1.1 collective-permute-start.20
  78.2 4.8 %collective-permute-done.20 = bf16[256,512]{1,0:T(8,128)(2,1)S(1)} collective-permute-done((bf16[256,512]{1,0:T(8,128)(2,1)S(1)}, bf16[256,512]{1,0:T(8,128)(2,1)S(1)}, u32[]{:S(2)}, u32[]{:S(2)}) %collective-permute-start.20) | collective-permute-done | bytes 262176 | tf_op jit(solution)/shard_map/ppermute | solution.py:29
  83.1 1.6 %multiply_subtract_fusion = f32[1024,512]{1,0:T(8,128)S(1)} fusion(f32[1024,512]{1,0:T(8,128)S(1)} %copy-done.2, f32[1024,512]{1,0:T(8,128)S(1)} %fusion.19, bf16[256,1024]{1,0:T(8,128)(2,1)} %collective-permute-done.18, bf16[256,512]{1,0:T(8,128)(2,1)S(1)} %collective-permute-done.20), kind=kOutput, calls=%fused_computation.13 | convolution fusion | flops 270008320 | bytes 7077888 | tf_op jit(solution)/shard_map/dot_general | solution.py:140
  86.0 1.0 copy-done.8
  89.1 0.9 collective-permute-done.21
  90.0 1.3 %fusion.35 = (f16[512,256]{1,0:T(8,128)(2,1)S(1)}, f32[512,256]{1,0:T(8,128)S(1)}) fusion(f32[512,256]{1,0:T(8,128)} %collective-permute-done.21, f32[1024,256]{1,0:T(8,128)} %copy-done.8, s32[]{:T(128)S(6)} %select_n.158), kind=kLoop, calls=%fused_computation.115 | loop fusion | flops 262144 | bytes 1835012 | tf_op jit(solution)/shard_map/convert_element_type | solution.py:93
  91.4 2.7 %collective-permute-start.22 = (f16[128,256]{1,0:T(8,128)(2,1)S(1)}, f16[128,256]{1,0:T(8,128)(2,1)S(1)}, u32[]{:S(2)}, u32[]{:S(2)}) collective-permute-start(f16[128,256]{1,0:T(8,128)(2,1)S(1)} %get-tuple-element.18), channel_id=1, source_target_pairs={{0,16},{2,18},{4,20},{6,22},{8,24},{10,26},{12,28},{14,30},{16,0},... | collective-permute-start | bytes 196616 | tf_op jit(solution)/shard_map/ppermute | solution.py:29
  94.0 1.6 %collective-permute-start.23 = (f16[128,256]{1,0:T(8,128)(2,1)S(1)}, f16[128,256]{1,0:T(8,128)(2,1)S(1)}, u32[]{:S(2)}, u32[]{:S(2)}) collective-permute-start(f16[128,256]{1,0:T(8,128)(2,1)S(1)} %get-tuple-element.20), channel_id=1, source_target_pairs={{0,8},{2,10},{4,12},{6,14},{8,0},{10,2},{12,4},{14,6},{16,24},{18,... | collective-permute-start | bytes 196616 | tf_op jit(solution)/shard_map/ppermute | solution.py:29
  95.8 1.1 fusion.34
  97.0 1.8 %collective-permute-start.10 = (f16[128,256]{1,0:T(8,128)(2,1)S(1)}, f16[128,256]{1,0:T(8,128)(2,1)S(1)}, u32[]{:S(2)}, u32[]{:S(2)}) collective-permute-start(f16[128,256]{1,0:T(8,128)(2,1)S(1)} %get-tuple-element.21), channel_id=1, source_target_pairs={{0,16},{2,18},{4,20},{6,22},{8,24},{10,26},{12,28},{14,30},{16,0},... | collective-permute-start | bytes 196616 | tf_op jit(solution)/shard_map/ppermute | solution.py:29
  98.7 2.5 %collective-permute-start.11 = (f16[128,256]{1,0:T(8,128)(2,1)S(1)}, f16[128,256]{1,0:T(8,128)(2,1)S(1)}, u32[]{:S(2)}, u32[]{:S(2)}) collective-permute-start(f16[128,256]{1,0:T(8,128)(2,1)S(1)} %get-tuple-element.23), channel_id=1, source_target_pairs={{0,8},{2,10},{4,12},{6,14},{8,0},{10,2},{12,4},{14,6},{16,24},{18,... | collective-permute-start | bytes 196616 | tf_op jit(solution)/shard_map/ppermute | solution.py:29
  101.2 1.0 collective-permute-start.12
  102.5 1.6 %collective-permute-start.25 = (f32[128,256]{1,0:T(8,128)S(1)}, f32[128,256]{1,0:T(8,128)S(1)}, u32[]{:S(2)}, u32[]{:S(2)}) collective-permute-start(f32[128,256]{1,0:T(8,128)S(1)} %convert_add_fusion.1), channel_id=1, source_target_pairs={{0,4},{2,6},{4,0},{6,2},{8,12},{10,14},{12,8},{14,10},{16,20},{18,... | collective-permute-start | bytes 393224 | tf_op jit(solution)/shard_map/ppermute | solution.py:29
  104.3 3.0 %collective-permute-done.12 = f16[128,256]{1,0:T(8,128)(2,1)S(1)} collective-permute-done((f16[128,256]{1,0:T(8,128)(2,1)S(1)}, f16[128,256]{1,0:T(8,128)(2,1)S(1)}, u32[]{:S(2)}, u32[]{:S(2)}) %collective-permute-start.12) | collective-permute-done | bytes 65568 | tf_op jit(solution)/shard_map/ppermute | solution.py:29
  107.3 1.6 %collective-permute-start.13 = (f32[128,256]{1,0:T(8,128)S(1)}, f32[128,256]{1,0:T(8,128)S(1)}, u32[]{:S(2)}, u32[]{:S(2)}) collective-permute-start(f32[128,256]{1,0:T(8,128)S(1)} %convert_add_fusion.2), channel_id=1, source_target_pairs={{0,4},{2,6},{4,0},{6,2},{8,12},{10,14},{12,8},{14,10},{16,20},{18,... | collective-permute-start | bytes 393224 | tf_op jit(solution)/shard_map/ppermute | solution.py:29
  109.0 1.7 %collective-permute-start.26 = (f16[128,256]{1,0:T(8,128)(2,1)S(1)}, f16[128,256]{1,0:T(8,128)(2,1)S(1)}, u32[]{:S(2)}, u32[]{:S(2)}) collective-permute-start(f16[128,256]{1,0:T(8,128)(2,1)S(1)} %get-tuple-element.11), channel_id=1, source_target_pairs={{0,16},{2,18},{4,20},{6,22},{8,24},{10,26},{12,28},{14,30},{16,0},... | collective-permute-start | bytes 196616 | tf_op jit(solution)/shard_map/ppermute | solution.py:29
  110.8 2.6 %collective-permute-start.28 = (f16[128,256]{1,0:T(8,128)(2,1)S(1)}, f16[128,256]{1,0:T(8,128)(2,1)S(1)}, u32[]{:S(2)}, u32[]{:S(2)}) collective-permute-start(f16[128,256]{1,0:T(8,128)(2,1)S(1)} %get-tuple-element.11), channel_id=1, source_target_pairs={{0,24},{2,26},{4,28},{6,30},{8,16},{10,18},{12,20},{14,22},{16,8},... | collective-permute-start | bytes 196616 | tf_op jit(solution)/shard_map/ppermute | solution.py:29
  113.5 1.0 collective-permute-start.14
  114.5 0.9 collective-permute-start.15
  115.9 2.3 %collective-permute-start.16 = (f16[128,256]{1,0:T(8,128)(2,1)S(1)}, f16[128,256]{1,0:T(8,128)(2,1)S(1)}, u32[]{:S(2)}, u32[]{:S(2)}) collective-permute-start(f16[128,256]{1,0:T(8,128)(2,1)S(1)} %get-tuple-element.7), channel_id=1, source_target_pairs={{0,24},{2,26},{4,28},{6,30},{8,16},{10,18},{12,20},{14,22},{16,8},... | collective-permute-start | bytes 196616 | tf_op jit(solution)/shard_map/ppermute | solution.py:29
  118.4 2.9 %collective-permute-done.14 = f16[128,256]{1,0:T(8,128)(2,1)S(1)} collective-permute-done((f16[128,256]{1,0:T(8,128)(2,1)S(1)}, f16[128,256]{1,0:T(8,128)(2,1)S(1)}, u32[]{:S(2)}, u32[]{:S(2)}) %collective-permute-start.14) | collective-permute-done | bytes 65568 | tf_op jit(solution)/shard_map/ppermute | solution.py:29
  123.9 2.9 %multiply_bitcast_fusion = (f32[1,1024,512]{2,1,0:T(8,128)}, f32[1024,512]{1,0:T(8,128)}) fusion(f32[1024,512]{1,0:T(8,128)S(1)} %copy-done.4, f32[1024,512]{1,0:T(8,128)S(1)} %copy-done, f32[1024,256]{1,0:T(8,128)S(1)} %fusion.13, f32[1024,256]{1,0:T(8,128)S(1)} %fusion.14, pred[]{:T(512)} %bitcast), kind=kLoop, calls=%fused_computation.12 | loop fusion | flops 3670016 | bytes 10485761 | tf_op jit(solution)/shard_map/broadcast_in_dim | solution.py:182
  (110 shorter events, 13.7 us)
Async XLA Ops:
  0.6 5.1 %copy-start.6 = (bf16[2,256,2048]{2,1,0:T(8,128)(2,1)S(1)}, bf16[2,256,2048]{2,1,0:T(8,128)(2,1)}, u32[]{:S(2)}) copy-start(bf16[2,256,2048]{2,1,0:T(8,128)(2,1)} %param.7) | copy-start | bytes 6291460
  0.6 11.2 %collective-permute-start.2 = (bf16[64,512]{1,0:T(8,128)(2,1)}, bf16[64,512]{1,0:T(8,128)(2,1)S(1)}, u32[]{:S(2)}, u32[]{:S(2)}) collective-permute-start(bf16[64,512]{1,0:T(8,128)(2,1)} %param.13), channel_id=1, source_target_pairs={{0,1},{1,0},{2,3},{3,2},{4,5},{5,4},{6,7},{7,6},{8,9},{9,8},{10,11... | collective-permute-start | bytes 196616 | tf_op jit(solution)/shard_map/ppermute | solution.py:29
  7.0 4.8 %copy-start.11 = (s32[2,256]{1,0:T(2,128)S(1)}, s32[2,256]{1,0:T(2,128)}, u32[]{:S(2)}) copy-start(s32[2,256]{1,0:T(2,128)} %param.9) | copy-start | bytes 6148
  7.0 4.8 %copy-start.10 = (bf16[64,512]{1,0:T(8,128)(2,1)S(1)}, bf16[64,512]{1,0:T(8,128)(2,1)}, u32[]{:S(2)}) copy-start(bf16[64,512]{1,0:T(8,128)(2,1)} %param.13) | copy-start | bytes 196612
  7.0 9.3 %copy-start.12 = (s32[2,256]{1,0:T(2,128)S(1)}, s32[2,256]{1,0:T(2,128)}, u32[]{:S(2)}) copy-start(s32[2,256]{1,0:T(2,128)} %param.8) | copy-start | bytes 6148
  8.9 20.2 %collective-permute-start = (bf16[256,1024]{1,0:T(8,128)(2,1)}, bf16[256,1024]{1,0:T(8,128)(2,1)}, u32[]{:S(2)}, u32[]{:S(2)}) collective-permute-start(bf16[256,1024]{1,0:T(8,128)(2,1)} %constant_dynamic-slice_fusion.9), channel_id=1, source_target_pairs={{0,1},{1,0},{2,3},{3,2},{4,5},{5,4},{6,7},{7,6},{8,9},{9,8},{10,11... | collective-permute-start | bytes 1572872 | tf_op jit(solution)/shard_map/ppermute | solution.py:29
  9.9 46.7 %collective-permute-start.18 = (bf16[256,1024]{1,0:T(8,128)(2,1)}, bf16[256,1024]{1,0:T(8,128)(2,1)}, u32[]{:S(2)}, u32[]{:S(2)}) collective-permute-start(bf16[256,1024]{1,0:T(8,128)(2,1)} %constant_dynamic-slice_fusion.4), channel_id=1, source_target_pairs={{0,1},{1,0},{2,3},{3,2},{4,5},{5,4},{6,7},{7,6},{8,9},{9,8},{10,11... | collective-permute-start | bytes 1572872 | tf_op jit(solution)/shard_map/ppermute | solution.py:29
  11.9 6.6 %collective-permute-start.3 = (bf16[128,512]{1,0:T(8,128)(2,1)S(1)}, bf16[128,512]{1,0:T(8,128)(2,1)}, u32[]{:S(2)}, u32[]{:S(2)}) collective-permute-start(bf16[128,512]{1,0:T(8,128)(2,1)S(1)} %constant_dynamic-update-slice_fusion.17), channel_id=1, source_target_pairs={{0,8},{2,10},{4,12},{6,14},{8,0},{10,2},{12,4},{14,6},{16,24},{18,... | collective-permute-start | bytes 393224 | tf_op jit(solution)/shard_map/ppermute | solution.py:29
  13.5 12.1 %collective-permute-start.4 = (bf16[128,512]{1,0:T(8,128)(2,1)S(1)}, bf16[128,512]{1,0:T(8,128)(2,1)S(1)}, u32[]{:S(2)}, u32[]{:S(2)}) collective-permute-start(bf16[128,512]{1,0:T(8,128)(2,1)S(1)} %constant_dynamic-update-slice_fusion.17), channel_id=1, source_target_pairs={{0,16},{2,18},{4,20},{6,22},{8,24},{10,26},{12,28},{14,30},{16,0},... | collective-permute-start | bytes 393224 | tf_op jit(solution)/shard_map/ppermute | solution.py:29
  16.1 9.5 %collective-permute-start.5 = (bf16[128,512]{1,0:T(8,128)(2,1)S(1)}, bf16[128,512]{1,0:T(8,128)(2,1)S(1)}, u32[]{:S(2)}, u32[]{:S(2)}) collective-permute-start(bf16[128,512]{1,0:T(8,128)(2,1)S(1)} %constant_dynamic-update-slice_fusion.17), channel_id=1, source_target_pairs={{0,24},{2,26},{4,28},{6,30},{8,16},{10,18},{12,20},{14,22},{16,8},... | collective-permute-start | bytes 393224 | tf_op jit(solution)/shard_map/ppermute | solution.py:29
  16.3 12.8 %copy-start = (f32[1024,512]{1,0:T(8,128)S(1)}, f32[1024,512]{1,0:T(8,128)}, u32[]{:S(2)}) copy-start(f32[1024,512]{1,0:T(8,128)} %param.11) | copy-start | bytes 6291460
  16.3 12.8 %copy-start.5 = (bf16[1,1024,512]{2,1,0:T(8,128)(2,1)S(1)}, bf16[1,1024,512]{2,1,0:T(8,128)(2,1)}, u32[]{:S(2)}) copy-start(bf16[1,1024,512]{2,1,0:T(8,128)(2,1)} %param.12) | copy-start | bytes 3145732
  26.5 10.0 %collective-permute-start.6 = (bf16[512,512]{1,0:T(8,128)(2,1)S(1)}, bf16[512,512]{1,0:T(8,128)(2,1)S(1)}, u32[]{:S(2)}, u32[]{:S(2)}) collective-permute-start(bf16[512,512]{1,0:T(8,128)(2,1)S(1)} %pad_maximum_fusion), channel_id=1, source_target_pairs={{0,4},{2,6},{4,0},{6,2},{8,12},{10,14},{12,8},{14,10},{16,20},{18,... | collective-permute-start | bytes 1572872 | tf_op jit(solution)/shard_map/ppermute | solution.py:29
  30.7 14.3 %copy-start.7 = (bf16[256,2048]{1,0:T(8,128)(2,1)S(1)}, bf16[256,2048]{1,0:T(8,128)(2,1)}, u32[]{:S(2)}) copy-start(bf16[256,2048]{1,0:T(8,128)(2,1)} %get-tuple-element.17) | copy-start | bytes 3145732
  30.7 14.3 %collective-permute-start.1 = (f32[256,512]{1,0:T(8,128)S(1)}, f32[256,512]{1,0:T(8,128)S(1)}, u32[]{:S(2)}, u32[]{:S(2)}) collective-permute-start(f32[256,512]{1,0:T(8,128)S(1)} %fusion.30), channel_id=1, source_target_pairs={{0,1},{1,0},{2,3},{3,2},{4,5},{5,4},{6,7},{7,6},{8,9},{9,8},{10,11... | collective-permute-start | bytes 1572872 | tf_op jit(solution)/shard_map/ppermute | solution.py:29
  36.6 9.0 %collective-permute-start.7 = (bf16[1024,512]{1,0:T(8,128)(2,1)S(1)}, bf16[1024,512]{1,0:T(8,128)(2,1)S(1)}, u32[]{:S(2)}, u32[]{:S(2)}) collective-permute-start(bf16[1024,512]{1,0:T(8,128)(2,1)S(1)} %constant_dynamic-update-slice_fusion), channel_id=1, source_target_pairs={{0,2},{2,0},{4,6},{6,4},{8,10},{10,8},{12,14},{14,12},{16,18},{18,... | collective-permute-start | bytes 3145736 | tf_op jit(solution)/shard_map/ppermute | solution.py:29
  45.8 1.3 %copy-start.9 = (bf16[2048,512]{1,0:T(8,128)(2,1)}, bf16[2048,512]{1,0:T(8,128)(2,1)S(1)}, u32[]{:S(2)}) copy-start(bf16[2048,512]{1,0:T(8,128)(2,1)S(1)} %slice_dynamic-update-slice_fusion) | copy-start | bytes 6291460
  48.0 6.9 %collective-permute-start.8 = (bf16[256,512]{1,0:T(8,128)(2,1)S(1)}, bf16[256,512]{1,0:T(8,128)(2,1)S(1)}, u32[]{:S(2)}, u32[]{:S(2)}) collective-permute-start(bf16[256,512]{1,0:T(8,128)(2,1)S(1)} %multiply_convert_fusion.1), channel_id=1, source_target_pairs={{0,1},{1,0},{2,3},{3,2},{4,5},{5,4},{6,7},{7,6},{8,9},{9,8},{10,11... | collective-permute-start | bytes 786440 | tf_op jit(solution)/shard_map/ppermute | solution.py:29
  56.6 1.3 %copy-start.1 = (f32[1024,512]{1,0:T(8,128)}, f32[1024,512]{1,0:T(8,128)S(1)}, u32[]{:S(2)}) copy-start(f32[1024,512]{1,0:T(8,128)S(1)} %multiply_subtract_fusion.1) | copy-start | bytes 6291460
  56.6 4.4 %copy-start.13 = (s32[2]{0:T(128)S(1)}, s32[2]{0:T(128)}, u32[]{:S(2)}) copy-start(s32[2]{0:T(128)} %param.10) | copy-start | bytes 28
  60.2 11.9 %collective-permute-start.19 = (f32[256,512]{1,0:T(8,128)}, f32[256,512]{1,0:T(8,128)}, u32[]{:S(2)}, u32[]{:S(2)}) collective-permute-start(f32[256,512]{1,0:T(8,128)} %fusion.15), channel_id=1, source_target_pairs={{0,1},{1,0},{2,3},{3,2},{4,5},{5,4},{6,7},{7,6},{8,9},{9,8},{10,11... | collective-permute-start | bytes 1572872 | tf_op jit(solution)/shard_map/ppermute | solution.py:29
  62.9 9.2 %copy-start.2 = (f32[1024,512]{1,0:T(8,128)S(1)}, f32[1024,512]{1,0:T(8,128)}, u32[]{:S(2)}) copy-start(f32[1024,512]{1,0:T(8,128)} %copy-done.1) | copy-start | bytes 6291460
  76.6 6.4 %collective-permute-start.20 = (bf16[256,512]{1,0:T(8,128)(2,1)S(1)}, bf16[256,512]{1,0:T(8,128)(2,1)S(1)}, u32[]{:S(2)}, u32[]{:S(2)}) collective-permute-start(bf16[256,512]{1,0:T(8,128)(2,1)S(1)} %multiply_convert_fusion), channel_id=1, source_target_pairs={{0,1},{1,0},{2,3},{3,2},{4,5},{5,4},{6,7},{7,6},{8,9},{9,8},{10,11... | collective-permute-start | bytes 786440 | tf_op jit(solution)/shard_map/ppermute | solution.py:29
  84.6 1.3 %copy-start.3 = (f32[1024,512]{1,0:T(8,128)}, f32[1024,512]{1,0:T(8,128)S(1)}, u32[]{:S(2)}) copy-start(f32[1024,512]{1,0:T(8,128)S(1)} %multiply_subtract_fusion) | copy-start | bytes 6291460
  86.0 1.0 copy-start.8
  87.8 2.3 %collective-permute-start.21 = (f32[512,256]{1,0:T(8,128)}, f32[512,256]{1,0:T(8,128)}, u32[]{:S(2)}, u32[]{:S(2)}) collective-permute-start(f32[512,256]{1,0:T(8,128)} %constant_dynamic-slice_fusion.3), channel_id=1, source_target_pairs={{0,2},{2,0},{4,6},{6,4},{8,10},{10,8},{12,14},{14,12},{16,18},{18,... | collective-permute-start | bytes 1572872 | tf_op jit(solution)/shard_map/ppermute | solution.py:29
  88.6 7.2 %collective-permute-start.9 = (f32[512,256]{1,0:T(8,128)}, f32[512,256]{1,0:T(8,128)}, u32[]{:S(2)}, u32[]{:S(2)}) collective-permute-start(f32[512,256]{1,0:T(8,128)} %constant_dynamic-slice_fusion.8), channel_id=1, source_target_pairs={{0,2},{2,0},{4,6},{6,4},{8,10},{10,8},{12,14},{14,12},{16,18},{18,... | collective-permute-start | bytes 1572872 | tf_op jit(solution)/shard_map/ppermute | solution.py:29
  91.4 9.8 %collective-permute-start.22 = (f16[128,256]{1,0:T(8,128)(2,1)S(1)}, f16[128,256]{1,0:T(8,128)(2,1)S(1)}, u32[]{:S(2)}, u32[]{:S(2)}) collective-permute-start(f16[128,256]{1,0:T(8,128)(2,1)S(1)} %get-tuple-element.18), channel_id=1, source_target_pairs={{0,16},{2,18},{4,20},{6,22},{8,24},{10,26},{12,28},{14,30},{16,0},... | collective-permute-start | bytes 196616 | tf_op jit(solution)/shard_map/ppermute | solution.py:29
  94.0 8.2 %collective-permute-start.23 = (f16[128,256]{1,0:T(8,128)(2,1)S(1)}, f16[128,256]{1,0:T(8,128)(2,1)S(1)}, u32[]{:S(2)}, u32[]{:S(2)}) collective-permute-start(f16[128,256]{1,0:T(8,128)(2,1)S(1)} %get-tuple-element.20), channel_id=1, source_target_pairs={{0,8},{2,10},{4,12},{6,14},{8,0},{10,2},{12,4},{14,6},{16,24},{18,... | collective-permute-start | bytes 196616 | tf_op jit(solution)/shard_map/ppermute | solution.py:29
  95.6 6.9 %collective-permute-start.24 = (f16[128,256]{1,0:T(8,128)(2,1)S(1)}, f16[128,256]{1,0:T(8,128)(2,1)S(1)}, u32[]{:S(2)}, u32[]{:S(2)}) collective-permute-start(f16[128,256]{1,0:T(8,128)(2,1)S(1)} %get-tuple-element.19), channel_id=1, source_target_pairs={{0,24},{2,26},{4,28},{6,30},{8,16},{10,18},{12,20},{14,22},{16,8},... | collective-permute-start | bytes 196616 | tf_op jit(solution)/shard_map/ppermute | solution.py:29
  97.0 7.3 %collective-permute-start.10 = (f16[128,256]{1,0:T(8,128)(2,1)S(1)}, f16[128,256]{1,0:T(8,128)(2,1)S(1)}, u32[]{:S(2)}, u32[]{:S(2)}) collective-permute-start(f16[128,256]{1,0:T(8,128)(2,1)S(1)} %get-tuple-element.21), channel_id=1, source_target_pairs={{0,16},{2,18},{4,20},{6,22},{8,24},{10,26},{12,28},{14,30},{16,0},... | collective-permute-start | bytes 196616 | tf_op jit(solution)/shard_map/ppermute | solution.py:29
  98.7 5.6 %collective-permute-start.11 = (f16[128,256]{1,0:T(8,128)(2,1)S(1)}, f16[128,256]{1,0:T(8,128)(2,1)S(1)}, u32[]{:S(2)}, u32[]{:S(2)}) collective-permute-start(f16[128,256]{1,0:T(8,128)(2,1)S(1)} %get-tuple-element.23), channel_id=1, source_target_pairs={{0,8},{2,10},{4,12},{6,14},{8,0},{10,2},{12,4},{14,6},{16,24},{18,... | collective-permute-start | bytes 196616 | tf_op jit(solution)/shard_map/ppermute | solution.py:29
  101.2 6.1 %collective-permute-start.12 = (f16[128,256]{1,0:T(8,128)(2,1)S(1)}, f16[128,256]{1,0:T(8,128)(2,1)S(1)}, u32[]{:S(2)}, u32[]{:S(2)}) collective-permute-start(f16[128,256]{1,0:T(8,128)(2,1)S(1)} %get-tuple-element.22), channel_id=1, source_target_pairs={{0,24},{2,26},{4,28},{6,30},{8,16},{10,18},{12,20},{14,22},{16,8},... | collective-permute-start | bytes 196616 | tf_op jit(solution)/shard_map/ppermute | solution.py:29
  102.5 6.4 %collective-permute-start.25 = (f32[128,256]{1,0:T(8,128)S(1)}, f32[128,256]{1,0:T(8,128)S(1)}, u32[]{:S(2)}, u32[]{:S(2)}) collective-permute-start(f32[128,256]{1,0:T(8,128)S(1)} %convert_add_fusion.1), channel_id=1, source_target_pairs={{0,4},{2,6},{4,0},{6,2},{8,12},{10,14},{12,8},{14,10},{16,20},{18,... | collective-permute-start | bytes 393224 | tf_op jit(solution)/shard_map/ppermute | solution.py:29
  107.3 6.1 %collective-permute-start.13 = (f32[128,256]{1,0:T(8,128)S(1)}, f32[128,256]{1,0:T(8,128)S(1)}, u32[]{:S(2)}, u32[]{:S(2)}) collective-permute-start(f32[128,256]{1,0:T(8,128)S(1)} %convert_add_fusion.2), channel_id=1, source_target_pairs={{0,4},{2,6},{4,0},{6,2},{8,12},{10,14},{12,8},{14,10},{16,20},{18,... | collective-permute-start | bytes 393224 | tf_op jit(solution)/shard_map/ppermute | solution.py:29
  109.0 7.0 %collective-permute-start.26 = (f16[128,256]{1,0:T(8,128)(2,1)S(1)}, f16[128,256]{1,0:T(8,128)(2,1)S(1)}, u32[]{:S(2)}, u32[]{:S(2)}) collective-permute-start(f16[128,256]{1,0:T(8,128)(2,1)S(1)} %get-tuple-element.11), channel_id=1, source_target_pairs={{0,16},{2,18},{4,20},{6,22},{8,24},{10,26},{12,28},{14,30},{16,0},... | collective-permute-start | bytes 196616 | tf_op jit(solution)/shard_map/ppermute | solution.py:29
  110.6 7.6 %collective-permute-start.27 = (f16[128,256]{1,0:T(8,128)(2,1)S(1)}, f16[128,256]{1,0:T(8,128)(2,1)S(1)}, u32[]{:S(2)}, u32[]{:S(2)}) collective-permute-start(f16[128,256]{1,0:T(8,128)(2,1)S(1)} %get-tuple-element.11), channel_id=1, source_target_pairs={{0,8},{2,10},{4,12},{6,14},{8,0},{10,2},{12,4},{14,6},{16,24},{18,... | collective-permute-start | bytes 196616 | tf_op jit(solution)/shard_map/ppermute | solution.py:29
  110.8 7.4 %collective-permute-start.28 = (f16[128,256]{1,0:T(8,128)(2,1)S(1)}, f16[128,256]{1,0:T(8,128)(2,1)S(1)}, u32[]{:S(2)}, u32[]{:S(2)}) collective-permute-start(f16[128,256]{1,0:T(8,128)(2,1)S(1)} %get-tuple-element.11), channel_id=1, source_target_pairs={{0,24},{2,26},{4,28},{6,30},{8,16},{10,18},{12,20},{14,22},{16,8},... | collective-permute-start | bytes 196616 | tf_op jit(solution)/shard_map/ppermute | solution.py:29
  113.5 7.8 %collective-permute-start.14 = (f16[128,256]{1,0:T(8,128)(2,1)S(1)}, f16[128,256]{1,0:T(8,128)(2,1)S(1)}, u32[]{:S(2)}, u32[]{:S(2)}) collective-permute-start(f16[128,256]{1,0:T(8,128)(2,1)S(1)} %get-tuple-element.7), channel_id=1, source_target_pairs={{0,16},{2,18},{4,20},{6,22},{8,24},{10,26},{12,28},{14,30},{16,0},... | collective-permute-start | bytes 196616 | tf_op jit(solution)/shard_map/ppermute | solution.py:29
  114.5 6.8 %collective-permute-start.15 = (f16[128,256]{1,0:T(8,128)(2,1)S(1)}, f16[128,256]{1,0:T(8,128)(2,1)S(1)}, u32[]{:S(2)}, u32[]{:S(2)}) collective-permute-start(f16[128,256]{1,0:T(8,128)(2,1)S(1)} %get-tuple-element.7), channel_id=1, source_target_pairs={{0,8},{2,10},{4,12},{6,14},{8,0},{10,2},{12,4},{14,6},{16,24},{18,... | collective-permute-start | bytes 196616 | tf_op jit(solution)/shard_map/ppermute | solution.py:29
  115.9 6.2 %collective-permute-start.16 = (f16[128,256]{1,0:T(8,128)(2,1)S(1)}, f16[128,256]{1,0:T(8,128)(2,1)S(1)}, u32[]{:S(2)}, u32[]{:S(2)}) collective-permute-start(f16[128,256]{1,0:T(8,128)(2,1)S(1)} %get-tuple-element.7), channel_id=1, source_target_pairs={{0,24},{2,26},{4,28},{6,30},{8,16},{10,18},{12,20},{14,22},{16,8},... | collective-permute-start | bytes 196616 | tf_op jit(solution)/shard_map/ppermute | solution.py:29
  118.3 4.7 %collective-permute-start.29 = (f16[512,256]{1,0:T(8,128)(2,1)S(1)}, f16[512,256]{1,0:T(8,128)(2,1)S(1)}, u32[]{:S(2)}, u32[]{:S(2)}) collective-permute-start(f16[512,256]{1,0:T(8,128)(2,1)S(1)} %constant_dynamic-update-slice_fusion.5), channel_id=1, source_target_pairs={{0,2},{2,0},{4,6},{6,4},{8,10},{10,8},{12,14},{14,12},{16,18},{18,... | collective-permute-start | bytes 786440 | tf_op jit(solution)/shard_map/ppermute | solution.py:29
  122.1 1.6 %collective-permute-start.17 = (f16[512,256]{1,0:T(8,128)(2,1)S(1)}, f16[512,256]{1,0:T(8,128)(2,1)S(1)}, u32[]{:S(2)}, u32[]{:S(2)}) collective-permute-start(f16[512,256]{1,0:T(8,128)(2,1)S(1)} %constant_dynamic-update-slice_fusion.9), channel_id=1, source_target_pairs={{0,2},{2,0},{4,6},{6,4},{8,10},{10,8},{12,14},{14,12},{16,18},{18,... | collective-permute-start | bytes 786440 | tf_op jit(solution)/shard_map/ppermute | solution.py:29
  122.2 1.7 %copy-start.4 = (f32[1024,512]{1,0:T(8,128)S(1)}, f32[1024,512]{1,0:T(8,128)}, u32[]{:S(2)}) copy-start(f32[1024,512]{1,0:T(8,128)} %copy-done.3) | copy-start | bytes 6291460

commit v2 on v1

--- a/solution.py
+++ b/solution.py
@@ -3,6 +3,8 @@
 import jax
 import jax.numpy as jnp
 from jax import lax
+from jax.experimental import pallas as pl
+from jax.experimental.pallas import tpu as pltpu
 from jax.sharding import PartitionSpec as P
 
 D = 2048
@@ -140,7 +142,7 @@
     return lax.dot_general(a, b, (((0,), (0,)), ((), ())), preferred_element_type=f32)
 
 
-def shards(hidden, targets, valid, plan, outer_head, drift, ref_head):
+def shards_any(hidden, targets, valid, plan, outer_head, drift, ref_head):
     rows_local, width = outer_head.shape
     part = width // FRAGS
     fsdp = lax.axis_size("fsdp")
@@ -182,6 +184,361 @@
     return (new_outer, new_inner[None])
 
 
+def grant(**more):
+    return pltpu.CompilerParams(vmem_limit_bytes=40 * 1024 * 1024, **more)
+
+
+def anywhere(count):
+    return [pl.BlockSpec(memory_space=pl.ANY)] * count
+
+
+def after(value, *earlier):
+    def kernel(*refs):
+        pass
+
+    return pl.pallas_call(
+        kernel,
+        out_shape=jax.ShapeDtypeStruct(value.shape, value.dtype),
+        in_specs=anywhere(1 + len(earlier)),
+        out_specs=pl.BlockSpec(memory_space=pl.ANY),
+        input_output_aliases={0: 0},
+    )(value, *earlier)
+
+
+def normalized(hidden, step, spots):
+    tokens, width = hidden.shape[1:]
+    cols = width // 2
+    tile = tokens // 4
+
+    def kernel(spots_ref, hidden_ref, normed_ref, sent_ref):
+        normed_ref[...] = normalize(hidden_ref[0])
+        other = pl.multiple_of((1 - spots_ref[0]) * cols, cols)
+        sent_ref[...] = normed_ref[:, pl.ds(other, cols)]
+
+    return pl.pallas_call(
+        kernel,
+        out_shape=(
+            jax.ShapeDtypeStruct((tokens, width), bf16),
+            jax.ShapeDtypeStruct((tokens, cols), bf16),
+        ),
+        grid_spec=pltpu.PrefetchScalarGridSpec(
+            num_scalar_prefetch=1,
+            grid=(4,),
+            in_specs=[pl.BlockSpec((1, tile, width), lambda i, spots_ref: (step, i, 0))],
+            out_specs=(
+                pl.BlockSpec((tile, width), lambda i, spots_ref: (i, 0)),
+                pl.BlockSpec((tile, cols), lambda i, spots_ref: (i, 0)),
+            ),
+        ),
+        compiler_params=grant(),
+        cost_estimate=pl.CostEstimate(flops=4 * tokens * width, bytes_accessed=5 * tokens * width, transcendentals=0),
+    )(spots, hidden)
+
+
+def reference_logs(normed, stacks, spots):
+    tokens, width = normed[0].shape
+    entries = stacks[0].shape[1]
+    rows = width // (2 * 2 * CORES * MAJOR)
+
+    def kernel(spots_ref, first_ref, second_ref, *refs):
+        stack_refs = refs[:4]
+        out_ref, whole_ref, sems = refs[4:]
+        fsdp, me = spots_ref[0], spots_ref[4]
+        copies = []
+        for number, stack_ref in enumerate(stack_refs):
+            bit_core, bit_fsdp = number // 2, number % 2
+            for p in range(2 * MAJOR):
+                mask = bit_core + (p // MAJOR) * CORES + (p % MAJOR) * 2 * CORES
+                block = jnp.bitwise_xor(me, mask) * 2 + jnp.bitwise_xor(fsdp, bit_fsdp)
+                copies.append(
+                    pltpu.make_async_copy(
+                        stack_ref.at[pl.ds(p * rows, rows)],
+                        whole_ref.at[pl.ds(pl.multiple_of(block * rows, rows), rows)],
+                        sems.at[len(copies)],
+                    )
+                )
+        for copy in copies:
+            copy.start()
+        for copy in copies:
+            copy.wait()
+        for step, normed_ref in enumerate((first_ref, second_ref)):
+            for half in range(2):
+                at = pl.ds(half * (tokens // 2), tokens // 2)
+                out_ref[step, at, :] = log_softmax(capped(dot(normed_ref[at, :], whole_ref[...])))
+
+    whole = pl.BlockSpec(memory_space=pltpu.VMEM)
+    return pl.pallas_call(
+        kernel,
+        out_shape=jax.ShapeDtypeStruct((2, tokens, entries), f32),
+        in_specs=[pl.BlockSpec(memory_space=pltpu.SMEM), whole, whole] + anywhere(4),
+        out_specs=whole,
+        scratch_shapes=[pltpu.VMEM((width, entries), bf16), pltpu.SemaphoreType.DMA((32,))],
+        compiler_params=grant(),
+        cost_estimate=pl.CostEstimate(
+            flops=4 * tokens * width * entries, bytes_accessed=4 * width * entries, transcendentals=tokens * entries * 4
+        ),
+    )(spots, *normed, *stacks)
+
+
+def gradients(own, received, refer_log, step, target_ids, valid_rows, *earlier):
+    tokens, entries = own.shape
+    tile = tokens // 2
+
+    def kernel(own_ref, received_ref, refer_ref, target_ref, valid_ref, *refs):
+        raw = own_ref[...] + received_ref[...].astype(f32)
+        policy = capped(raw)
+        policy_log = log_softmax(policy)
+        policy_prob = jnp.exp(policy_log)
+        diverge = policy_log - refer_ref[0]
+        kl_value = jnp.sum(policy_prob * diverge, axis=-1, keepdims=True)
+        here = lax.broadcasted_iota(jnp.int32, policy.shape, 1)
+        onehot = jnp.where(target_ref[...] == here, 1.0, 0.0)
+        upstream = valid_ref[...].astype(f32) * (
+            policy_prob - onehot + kl_weight * policy_prob * (diverge - kl_value)
+        )
+        ratio = policy / soft_cap
+        refs[-1][...] = (upstream * (1.0 - ratio * ratio) * (4.0 / math.sqrt(D))).astype(bf16)
+
+    rows = pl.BlockSpec((tile, entries), lambda i: (i, 0))
+    single = pl.BlockSpec((tile, 1), lambda i: (i, 0))
+    return pl.pallas_call(
+        kernel,
+        out_shape=jax.ShapeDtypeStruct((tokens, entries), bf16),
+        grid=(2,),
+        in_specs=[rows, rows, pl.BlockSpec((1, tile, entries), lambda i: (step, i, 0)), single, single]
+        + anywhere(len(earlier)),
+        out_specs=rows,
+        compiler_params=grant(),
+        cost_estimate=pl.CostEstimate(
+            flops=20 * tokens * entries, bytes_accessed=14 * tokens * entries, transcendentals=3 * tokens * entries
+        ),
+    )(own, received, refer_log, target_ids[:, None], valid_rows[:, None], *earlier)
+
+
+def own_update(inner, normed, grads, spots, *earlier):
+    rows, entries = inner.shape
+    tokens = normed.shape[0]
+    tile = rows // 4
+
+    def kernel(spots_ref, inner_ref, normed_ref, grads_ref, *refs):
+        refs[-1][...] = inner_ref[...] - inner_rate * dot_rows(normed_ref[...], grads_ref[...])
+
+    return pl.pallas_call(
+        kernel,
+        out_shape=jax.ShapeDtypeStruct((rows, entries), f32),
+        grid_spec=pltpu.PrefetchScalarGridSpec(
+            num_scalar_prefetch=1,
+            grid=(4,),
+            in_specs=[
+                pl.BlockSpec((tile, entries), lambda i, spots_ref: (i, 0)),
+                pl.BlockSpec((tokens, tile), lambda i, spots_ref: (0, spots_ref[0] * 4 + i)),
+                pl.BlockSpec((tokens, entries), lambda i, spots_ref: (0, 0)),
+            ]
+            + anywhere(len(earlier)),
+            out_specs=pl.BlockSpec((tile, entries), lambda i, spots_ref: (i, 0)),
+        ),
+        compiler_params=grant(),
+        cost_estimate=pl.CostEstimate(
+            flops=2 * tokens * rows * entries, bytes_accessed=8 * rows * entries, transcendentals=0
+        ),
+    )(spots, inner, normed, grads, *earlier)
+
+
+def update(inner, features, grads, outer_head, spots, step, replicas, following=None):
+    rows, entries = inner.shape
+    tokens = features.shape[0]
+    part = entries // FRAGS
+    tile = rows // 4
+    more = following is not None
+
+    def kernel(spots_ref, inner_ref, features_ref, grads_ref, outer_ref, *refs):
+        if more:
+            following_ref, new_ref, sent_ref, kept_ref, weights_ref, partial_ref = refs
+        else:
+            new_ref, sent_ref, kept_ref = refs
+        i = pl.program_id(0)
+        new_ref[...] = inner_ref[...] - inner_rate * dot_rows(features_ref[...], grads_ref[...])
+        at = pl.ds(pl.multiple_of(spots_ref[2 + step] * part, part), part)
+        delta = (outer_ref[:, at] - new_ref[:, at]) * (1.0 / replicas)
+
+        @pl.when(i < 2)
+        def _():
+            sent_ref[...] = delta
+
+        @pl.when(i >= 2)
+        def _():
+            kept_ref[...] = delta
+
+        if more:
+            weights = new_ref[...].astype(bf16)
+            weights_ref[...] = weights
+            product = dot(following_ref[...], weights)
+
+            @pl.when(i == 0)
+            def _():
+                partial_ref[...] = product
+
+            @pl.when(i > 0)
+            def _():
+                partial_ref[...] += product
+
+    def row_tile(i, spots_ref):
+        return lax.rem(i + 2 * (1 - spots_ref[1]), 4)
+
+    rows_spec = pl.BlockSpec((tile, entries), lambda i, s: (row_tile(i, s), 0))
+    columns_spec = pl.BlockSpec((tokens, tile), lambda i, s: (0, row_tile(i, s)))
+    whole_spec = pl.BlockSpec((tokens, entries), lambda i, s: (0, 0))
+    in_specs = [rows_spec, columns_spec, whole_spec, rows_spec]
+    out_specs = [
+        rows_spec,
+        pl.BlockSpec((tile, part), lambda i, s: (jnp.minimum(i, 1), 0)),
+        pl.BlockSpec((tile, part), lambda i, s: (jnp.maximum(i - 2, 0), 0)),
+    ]
+    out_shape = [
+        jax.ShapeDtypeStruct((rows, entries), f32),
+        jax.ShapeDtypeStruct((rows // 2, part), f32),
+        jax.ShapeDtypeStruct((rows // 2, part), f32),
+    ]
+    operands = [inner, features, grads, outer_head]
+    if more:
+        in_specs += [columns_spec]
+        out_specs += [rows_spec, whole_spec]
+        out_shape += [
+            jax.ShapeDtypeStruct((rows, entries), bf16),
+            jax.ShapeDtypeStruct((tokens, entries), f32),
+        ]
+        operands += [following]
+    return pl.pallas_call(
+        kernel,
+        out_shape=out_shape,
+        grid_spec=pltpu.PrefetchScalarGridSpec(
+            num_scalar_prefetch=1, grid=(4,), in_specs=in_specs, out_specs=out_specs
+        ),
+        compiler_params=grant(),
+        cost_estimate=pl.CostEstimate(
+            flops=(4 if more else 2) * tokens * rows * entries, bytes_accessed=12 * rows * entries, transcendentals=0
+        ),
+    )(spots, *operands)
+
+
+def settled(outer_head, inner, means, spots):
+    rows, entries = inner.shape
+    part = entries // FRAGS
+    tile = rows // (CORES * MAJOR)
+
+    def kernel(spots_ref, outer_ref, inner_ref, own0, other0, own1, other1, new_outer_ref, new_inner_ref):
+        i = pl.program_id(0)
+        mine = i // MAJOR == spots_ref[1]
+        for f in range(FRAGS):
+            first = spots_ref[2] == f
+            at = slice(f * part, (f + 1) * part)
+            mean = jnp.where(
+                mine,
+                jnp.where(first, own0[...], own1[...]),
+                jnp.where(first, other0[...], other1[...]),
+            )
+            fresh = outer_ref[:, at] - outer_rate * mean
+            new_outer_ref[:, at] = fresh
+            new_inner_ref[:, at] = mix_weight * inner_ref[:, at] + (1.0 - mix_weight) * fresh
+
+    row_spec = pl.BlockSpec((tile, entries), lambda i, s: (i, 0))
+    piece_spec = pl.BlockSpec(
+        (tile, part), lambda i, s: (jnp.bitwise_xor(lax.rem(i, MAJOR), s[5]), 0)
+    )
+    return pl.pallas_call(
+        kernel,
+        out_shape=[jax.ShapeDtypeStruct((rows, entries), f32)] * 2,
+        grid_spec=pltpu.PrefetchScalarGridSpec(
+            num_scalar_prefetch=1,
+            grid=(CORES * MAJOR,),
+            in_specs=[row_spec, row_spec] + [piece_spec] * 4,
+            out_specs=[row_spec, row_spec],
+        ),
+        compiler_params=grant(),
+        cost_estimate=pl.CostEstimate(
+            flops=6 * rows * entries, bytes_accessed=20 * rows * entries, transcendentals=0
+        ),
+    )(spots, outer_head, inner, *means[0], *means[1])
+
+
+MASKS = (2, 1, 3)
+
+
+def gathered_stacks(ref_head):
+    step = 2 * CORES
+    stacks = []
+    for rows in (ref_head, swap(ref_head, "fsdp", 1)):
+        along = jnp.concatenate([rows] + [swap(rows, "replica", m * step) for m in range(1, MAJOR)], 0)
+        stacks.append(jnp.concatenate([along, swap(along, "replica", CORES)], 0))
+    return stacks + [swap(s, "replica", 1) for s in stacks]
+
+
+def quarters_sum(part, major):
+    step = 2 * CORES
+    quarter = part.shape[0] // MAJOR
+    sent = part.astype(f16)
+    own = rows_at(part, major, quarter)
+    for m in MASKS:
+        own = own + swap(rows_at(sent, major ^ m, quarter), "replica", m * step).astype(f32)
+    return own
+
+
+def quarters_gathered(own):
+    step = 2 * CORES
+    own = own.astype(f16)
+    got = {m: swap(own, "replica", m * step) for m in MASKS}
+    return jnp.concatenate([own, got[1], got[2], got[3]], 0).astype(f32)
+
+
+def shards_pair(hidden, targets, valid, plan, outer_head, drift, ref_head):
+    replicas = lax.axis_size("replica")
+    fsdp = lax.axis_index("fsdp")
+    replica = lax.axis_index("replica")
+    core = replica % CORES
+    major = replica // (2 * CORES)
+    spots = jnp.stack([fsdp, core, plan[0], plan[1], replica, major]).astype(jnp.int32)
+    rows = outer_head.shape[0]
+
+    normed, features = [], []
+    for s in range(STEPS):
+        whole, sent = normalized(hidden, s, spots)
+        normed.append(whole)
+        features.append(swap(sent, "fsdp", 1))
+    stacks = gathered_stacks(ref_head)
+    refer_log = reference_logs(normed, stacks, spots)
+
+    inner = outer_head + drift[0].astype(f32)
+    weights = inner.astype(bf16)
+    partial = dot(features[0], weights)
+    own = dot(columns_at(normed[0], fsdp, rows), weights)
+    grads = gradients(own, swap(partial.astype(logit_type), "fsdp", 1), refer_log, 0, targets[0], valid[0])
+    halfway = own_update(inner, normed[0], grads, spots)
+    inner, sent, kept, weights, partial = update(
+        halfway, features[0], swap(grads, "fsdp", 1), outer_head, spots, 0, replicas, features[1]
+    )
+
+    received = swap(partial.astype(logit_type), "fsdp", 1)
+    own = dot(columns_at(normed[1], fsdp, rows), weights)
+    summed = kept + swap(sent, "replica", 1)
+    grads = gradients(own, received, refer_log, 1, targets[1], valid[1], summed)
+    quarter = quarters_sum(summed, major)
+    partner_grads = swap(grads, "fsdp", 1)
+    halfway = own_update(inner, normed[1], grads, spots, quarter)
+    first = quarter + swap(quarter, "replica", CORES)
+    inner, sent, kept = update(
+        after(halfway, first), features[1], partner_grads, outer_head, spots, 1, replicas
+    )
+
+    summed = kept + swap(sent, "replica", 1)
+    quarter = quarters_sum(summed, major)
+    second = quarter + swap(quarter, "replica", CORES)
+    first = quarters_gathered(first)
+    second = quarters_gathered(after(second, first))
+    means = [(m, swap(m, "replica", 1)) for m in (first, second)]
+    new_outer, new_inner = settled(outer_head, inner, means, spots)
+    return (new_outer, new_inner[None])
+
+
 def solution(mesh):
     in_specs = (
         P(None, ("replica", "fsdp"), None),
@@ -193,4 +550,7 @@
         P(("replica", "fsdp"), None),
     )
     out_specs = (P("fsdp", None), P("replica", "fsdp", None))
+    chips = mesh.shape["replica"] // CORES
+    pairs = mesh.shape["fsdp"] == 2 and chips == 2 * MAJOR
+    shards = shards_pair if pairs else shards_any
     return jax.shard_map(shards, mesh=mesh, in_specs=in_specs, out_specs=out_specs, check_vma=False)

time: 127 us -> 151 us (1.19)
  Pallas kernels: 0 us -> 28.1 us
  local copies, waits for them, and re-layouts: 10.2 us -> 24.2 us
  matrix products: 13.9 us -> 6.14 us
  waiting for transfers between devices: 48.9 us -> 41.7 us
  other arithmetic: 14.1 us -> 9.63 us
  starting transfers between devices: 36.4 us -> 39.7 us
  between operations: 3.21 us -> 0.97 us
    pallas_call x0 -> x12, Pallas kernels: none -> 28.1 us  [the longest x2 8.62 us: update(): pl.pallas_call(kernel, out_shape=out_shape, grid_spec=pltpu.PrefetchScala...]
    unnamed x32 -> x62, local copies, waits for them, and re-layouts: 4.52 us -> 20 us
    ppermute x30 -> x35, waiting for transfers between devices: 48.9 us -> 41.7 us  [swap(): return lax.ppermute(value, axis, [(i, i ^ mask) for i in range(size)])]
    dot_general x4 -> x0, matrix products: 4.19 us -> none  [dot_rows(): lax.dot_general(a, b, (((0,), (0,)), ((), ())), preferred_element_type=f32)]
    reduce_sum x3 -> x0, other arithmetic: 3.71 us -> none  [the longest x1 2.02 us: normalize(): jnp.mean(values * values, axis=-1, keepdims=True) + norm_eps]
    dot_general x6 -> x3, matrix products: 9.68 us -> 6.14 us  [dot(): return jnp.dot(a, b, preferred_element_type=f32)]
    ppermute x30 -> x35, starting transfers between devices: 36.4 us -> 39.7 us  [swap(): return lax.ppermute(value, axis, [(i, i ^ mask) for i in range(size)])]
    add x2 -> x4, other arithmetic: 0.06 us -> 3.21 us  [the longest x1 1.57 us: shards_pair(): inner = outer_head + drift[0].astype(f32)]
  transfers between devices with their start and end apart: 30 -> 35, of which waited for: 15 -> 19; matrix products, arithmetic and copies ran while one was open for 17% -> 15% of each run, Pallas kernels for 0% -> 10%
where the time goes in v2:
time: 151 us; the launch traced here: 150 us
  waiting for transfers between devices  41.7 us (28%)
  starting transfers between devices  39.7 us (26%)
  Pallas kernels  28.1 us (19%)
  local copies, waits for them, and re-layouts  24.2 us (16%)
  other arithmetic  9.63 us (6%)
  matrix products  6.14 us (4%)
    ppermute x35, waiting for transfers between devices, swap(): return lax.ppermute(value, axis, [(i, i ^ mask) for i in range(size)])  41.7 us
    ppermute x35, starting transfers between devices, swap(): return lax.ppermute(value, axis, [(i, i ^ mask) for i in range(size)])  39.7 us
    unnamed x62, local copies, waits for them, and re-layouts  20 us
    pallas_call x2, Pallas kernels, update(): pl.pallas_call(kernel, out_shape=out_shape, grid_spec=pltpu.PrefetchScala...  8.62 us
    dot_general x3, matrix products, dot(): return jnp.dot(a, b, preferred_element_type=f32)  6.14 us
    pallas_call x2, Pallas kernels, normalized(): pl.pallas_call(kernel, out_shape=(jax.ShapeDtypeStruct((tokens, width), b...  4.68 us
    pallas_call x1, Pallas kernels, settled(): pl.pallas_call(kernel, out_shape=[jax.ShapeDtypeStruct((rows, entries), f...  4.27 us
    pallas_call x1, Pallas kernels, reference_logs(): pl.pallas_call(kernel, out_shape=jax.ShapeDtypeStruct((2, tokens, entries...  3.81 us
  transfers between devices with their start and end apart: 35, of which 19 were waited for; matrix products, arithmetic and copies ran while one was open for 15% of the time, Pallas kernels for 10%

profile of v2, /device:TPU:0, one launch (start us, length us, event | category | flops | bytes accessed | tf_op | source)
XLA Modules:
  0.0 150.4 jit_solution(2130589483524239400)
XLA Ops:
  0.6 3.0 %collective-permute-start.6 = (bf16[64,512]{1,0:T(8,128)(2,1)}, bf16[64,512]{1,0:T(8,128)(2,1)}, u32[]{:S(2)}, u32[]{:S(2)}) collective-permute-start(bf16[64,512]{1,0:T(8,128)(2,1)} %param.13), channel_id=1, source_target_pairs={{0,1},{1,0},{2,3},{3,2},{4,5},{5,4},{6,7},{7,6},{8,9},{9,8},{10,11... | collective-permute-start | bytes 196616 | tf_op jit(solution)/shard_map/ppermute | solution.py:31
  3.6 1.6 %collective-permute-start.2 = (bf16[64,512]{1,0:T(8,128)(2,1)}, bf16[64,512]{1,0:T(8,128)(2,1)S(1)}, u32[]{:S(2)}, u32[]{:S(2)}) collective-permute-start(bf16[64,512]{1,0:T(8,128)(2,1)} %param.13), channel_id=1, source_target_pairs={{0,8},{2,10},{4,12},{6,14},{8,0},{10,2},{12,4},{14,6},{16,24},{18,... | collective-permute-start | bytes 196616 | tf_op jit(solution)/shard_map/ppermute | solution.py:31
  5.2 2.6 %collective-permute-start.3 = (bf16[64,512]{1,0:T(8,128)(2,1)}, bf16[64,512]{1,0:T(8,128)(2,1)S(1)}, u32[]{:S(2)}, u32[]{:S(2)}) collective-permute-start(bf16[64,512]{1,0:T(8,128)(2,1)} %param.13), channel_id=1, source_target_pairs={{0,16},{2,18},{4,20},{6,22},{8,24},{10,26},{12,28},{14,30},{16,0},... | collective-permute-start | bytes 196616 | tf_op jit(solution)/shard_map/ppermute | solution.py:31
  8.8 1.6 %copy-done.5 = bf16[2,256,2048]{2,1,0:T(8,128)(2,1)S(1)} copy-done((bf16[2,256,2048]{2,1,0:T(8,128)(2,1)S(1)}, bf16[2,256,2048]{2,1,0:T(8,128)(2,1)}, u32[]{:S(2)}) %copy-start.5) | copy-done | bytes 2097176
  10.4 2.3 %shard_map.86 = (bf16[256,2048]{1,0:T(8,128)(2,1)S(1)}, bf16[256,1024]{1,0:T(8,128)(2,1)}) custom-call(s32[6]{0:T(128)S(1)} %stack.19.spots_ref, bf16[2,256,2048]{2,1,0:T(8,128)(2,1)S(1)} %copy-done.5), custom_call_target="tpu_custom_call" | custom-call | flops 2097152 | bytes 2621440 | tf_op jit(solution)/shard_map/pallas_call | solution.py:218
  13.0 2.3 %shard_map.87 = (bf16[256,2048]{1,0:T(8,128)(2,1)S(1)}, bf16[256,1024]{1,0:T(8,128)(2,1)}) custom-call(s32[6]{0:T(128)S(1)} %stack.19.spots_ref, bf16[2,256,2048]{2,1,0:T(8,128)(2,1)S(1)} %copy-done.5), custom_call_target="tpu_custom_call" | custom-call | flops 2097152 | bytes 2621440 | tf_op jit(solution)/shard_map/pallas_call | solution.py:218
  16.5 1.6 %convert_add_fusion.inner_ref = f32[1024,512]{1,0:T(8,128)S(1)} fusion(f32[1024,512]{1,0:T(8,128)S(1)} %copy-done, bf16[1,1024,512]{2,1,0:T(8,128)(2,1)} %param.12), kind=kLoop, calls=%fused_computation | loop fusion | flops 1048576 | bytes 5242880 | tf_op jit(solution)/shard_map/add | solution.py:510
  18.8 1.7 %collective-permute-start.14 = (bf16[256,1024]{1,0:T(8,128)(2,1)}, bf16[256,1024]{1,0:T(8,128)(2,1)}, u32[]{:S(2)}, u32[]{:S(2)}) collective-permute-start(bf16[256,1024]{1,0:T(8,128)(2,1)} %get-tuple-element.19), channel_id=1, source_target_pairs={{0,1},{1,0},{2,3},{3,2},{4,5},{5,4},{6,7},{7,6},{8,9},{9,8},{10,11... | collective-permute-start | bytes 1572872 | tf_op jit(solution)/shard_map/ppermute | solution.py:31
  20.5 1.5 constant_dynamic-update-slice_fusion.9
  23.3 3.5 %collective-permute-start.8 = (bf16[64,512]{1,0:T(8,128)(2,1)}, bf16[64,512]{1,0:T(8,128)(2,1)S(1)}, u32[]{:S(2)}, u32[]{:S(2)}) collective-permute-start(bf16[64,512]{1,0:T(8,128)(2,1)} %collective-permute-done.6), channel_id=1, source_target_pairs={{0,16},{2,18},{4,20},{6,22},{8,24},{10,26},{12,28},{14,30},{16,0},... | collective-permute-start | bytes 196616 | tf_op jit(solution)/shard_map/ppermute | solution.py:31
  29.2 1.5 constant_dynamic-update-slice_fusion.1
  30.7 1.5 %collective-permute-start.5 = (bf16[256,512]{1,0:T(8,128)(2,1)S(1)}, bf16[256,512]{1,0:T(8,128)(2,1)S(1)}, u32[]{:S(2)}, u32[]{:S(2)}) collective-permute-start(bf16[256,512]{1,0:T(8,128)(2,1)S(1)} %pad_maximum_fusion), channel_id=1, source_target_pairs={{0,4},{2,6},{4,0},{6,2},{8,12},{10,14},{12,8},{14,10},{16,20},{18,... | collective-permute-start | bytes 786440 | tf_op jit(solution)/shard_map/ppermute | solution.py:31
  32.2 2.1 %collective-permute-done.9 = bf16[64,512]{1,0:T(8,128)(2,1)S(1)} collective-permute-done((bf16[64,512]{1,0:T(8,128)(2,1)}, bf16[64,512]{1,0:T(8,128)(2,1)S(1)}, u32[]{:S(2)}, u32[]{:S(2)}) %collective-permute-start.9) | collective-permute-done | bytes 65568 | tf_op jit(solution)/shard_map/ppermute | solution.py:31
  35.2 1.6 %collective-permute-start.10 = (bf16[256,512]{1,0:T(8,128)(2,1)S(1)}, bf16[256,512]{1,0:T(8,128)(2,1)S(1)}, u32[]{:S(2)}, u32[]{:S(2)}) collective-permute-start(bf16[256,512]{1,0:T(8,128)(2,1)S(1)} %pad_maximum_fusion.1), channel_id=1, source_target_pairs={{0,4},{2,6},{4,0},{6,2},{8,12},{10,14},{12,8},{14,10},{16,20},{18,... | collective-permute-start | bytes 786440 | tf_op jit(solution)/shard_map/ppermute | solution.py:31
  40.5 2.2 %collective-permute-done.10 = bf16[256,512]{1,0:T(8,128)(2,1)S(1)} collective-permute-done((bf16[256,512]{1,0:T(8,128)(2,1)S(1)}, bf16[256,512]{1,0:T(8,128)(2,1)S(1)}, u32[]{:S(2)}, u32[]{:S(2)}) %collective-permute-start.10) | collective-permute-done | bytes 262176 | tf_op jit(solution)/shard_map/ppermute | solution.py:31
  43.4 2.3 %fusion.2 = f32[256,512]{1,0:T(8,128)} fusion(bf16[256,1024]{1,0:T(8,128)(2,1)} %collective-permute-done.features_ref, f32[1024,512]{1,0:T(8,128)S(1)} %convert_add_fusion.inner_ref), kind=kOutput, calls=%fused_computation.3 | convolution fusion | flops 268959744 | bytes 3145728 | tf_op jit(solution)/shard_map/dot_general | solution.py:138
  46.2 2.0 %fusion.4.own_ref = f32[256,512]{1,0:T(8,128)S(1)} fusion(f32[1024,512]{1,0:T(8,128)} %copy-done.1, bf16[256,2048]{1,0:T(8,128)(2,1)S(1)} %get-tuple-element.16.first_ref.normed_ref, s32[]{:T(128)S(6)} %select_n.33), kind=kOutput, calls=%fused_computation.5 | convolution fusion | flops 268959744 | bytes 3145732 | tf_op jit(solution)/shard_map/dot_general | solution.py:138
  50.7 3.8 %shard_map.88.refer_ref = f32[2,256,512]{2,1,0:T(8,128)S(1)} custom-call(s32[6]{0:T(128)S(1)} %stack.19.spots_ref, bf16[256,2048]{1,0:T(8,128)(2,1)S(1)} %copy-done.10, bf16[256,2048]{1,0:T(8,128)(2,1)S(1)} %copy-done.7, bf16[512,512]{1,0:T(8,128)(2,1)} %constant_dynamic-update-slice_fusion.refs_0_, ...), custom_call_target="tpu_custom_call" | custom-call | flops 1073741824 | bytes 4194304 | tf_op jit(solution)/shard_map/pallas_call | solution.py:270
  54.5 5.8 %collective-permute-done.1.received_ref = f32[256,512]{1,0:T(8,128)} collective-permute-done((f32[256,512]{1,0:T(8,128)}, f32[256,512]{1,0:T(8,128)}, u32[]{:S(2)}, u32[]{:S(2)}) %collective-permute-start.1) | collective-permute-done | bytes 524320 | tf_op jit(solution)/shard_map/ppermute | solution.py:31
  60.3 1.7 %shard_map.89.grads_ref = bf16[256,512]{1,0:T(8,128)(2,1)S(1)} custom-call(f32[256,512]{1,0:T(8,128)S(1)} %fusion.4.own_ref, f32[256,512]{1,0:T(8,128)} %collective-permute-done.1.received_ref, f32[2,256,512]{2,1,0:T(8,128)S(1)} %shard_map.88.refer_ref, s32[256,1]{1,0:T(8,128)S(1)} %copy.11.target_ref, s32[256,1]{1,0:T(8,128)S(1)} %copy.12.valid_ref), custom_call_target="tpu_custom_call" | custom-call | flops 2621440 | bytes 1835008 | tf_op jit(solution)/shard_map/pallas_call | solution.py:304
  62.4 1.7 %shard_map.90.inner_ref = f32[1024,512]{1,0:T(8,128)S(1)} custom-call(s32[6]{0:T(128)S(1)} %stack.19.spots_ref, f32[1024,512]{1,0:T(8,128)S(1)} %copy-done.2, bf16[256,2048]{1,0:T(8,128)(2,1)S(1)} %copy-done.11, bf16[256,512]{1,0:T(8,128)(2,1)S(1)} %shard_map.89.grads_ref), custom_call_target="tpu_custom_call" | custom-call | flops 268435456 | bytes 4194304 | tf_op jit(solution)/shard_map/pallas_call | solution.py:326
  64.1 5.9 %collective-permute-done.13.grads_ref = bf16[256,512]{1,0:T(8,128)(2,1)S(1)} collective-permute-done((bf16[256,512]{1,0:T(8,128)(2,1)S(1)}, bf16[256,512]{1,0:T(8,128)(2,1)S(1)}, u32[]{:S(2)}, u32[]{:S(2)}) %collective-permute-start.13) | collective-permute-done | bytes 262176 | tf_op jit(solution)/shard_map/ppermute | solution.py:31
  70.0 5.3 %shard_map.91 = (f32[1024,512]{1,0:T(8,128)S(1)}, f32[512,256]{1,0:T(8,128)}, f32[512,256]{1,0:T(8,128)S(1)}, bf16[1024,512]{1,0:T(8,128)(2,1)S(1)}, f32[256,512]{1,0:T(8,128)}) custom-call(s32[6]{0:T(128)S(1)} %stack.19.spots_ref, f32[1024,512]{1,0:T(8,128)S(1)} %shard_map.90.inner_ref, bf16[256,1024]{1,0:T(8,128)(2,1)} %collective-permute-done.features_ref, ...), custom_call_target="tpu_custom_call" | custom-call | flops 536870912 | bytes 6291456 | tf_op jit(solution)/shard_map/pallas_call | solution.py:411
  75.3 1.3 copy-done.16
  78.4 2.2 %collective-permute-done.16 = f32[512,256]{1,0:T(8,128)} collective-permute-done((f32[512,256]{1,0:T(8,128)}, f32[512,256]{1,0:T(8,128)}, u32[]{:S(2)}, u32[]{:S(2)}) %collective-permute-start.16) | collective-permute-done | bytes 524320 | tf_op jit(solution)/shard_map/ppermute | solution.py:31
  80.6 2.1 %fusion.11 = (f16[512,256]{1,0:T(8,128)(2,1)S(1)}, f32[512,256]{1,0:T(8,128)}) fusion(f32[512,256]{1,0:T(8,128)} %copy-done.19, f32[512,256]{1,0:T(8,128)} %collective-permute-done.16), kind=kLoop, calls=%fused_computation.38 | loop fusion | flops 262144 | bytes 1835008 | tf_op jit(solution)/shard_map/convert_element_type | solution.py:479
  84.1 2.6 %collective-permute-start.18 = (f16[128,256]{1,0:T(8,128)(2,1)}, f16[128,256]{1,0:T(8,128)(2,1)S(1)}, u32[]{:S(2)}, u32[]{:S(2)}) collective-permute-start(f16[128,256]{1,0:T(8,128)(2,1)} %get-tuple-element.41), channel_id=1, source_target_pairs={{0,8},{2,10},{4,12},{6,14},{8,0},{10,2},{12,4},{14,6},{16,24},{18,... | collective-permute-start | bytes 196616 | tf_op jit(solution)/shard_map/ppermute | solution.py:31
  90.3 2.6 %collective-permute-done.19 = f16[128,256]{1,0:T(8,128)(2,1)S(1)} collective-permute-done((f16[128,256]{1,0:T(8,128)(2,1)}, f16[128,256]{1,0:T(8,128)(2,1)S(1)}, u32[]{:S(2)}, u32[]{:S(2)}) %collective-permute-start.19) | collective-permute-done | bytes 65568 | tf_op jit(solution)/shard_map/ppermute | solution.py:31
  93.9 1.6 %collective-permute-start.20 = (f32[128,256]{1,0:T(8,128)S(1)}, f32[128,256]{1,0:T(8,128)S(1)}, u32[]{:S(2)}, u32[]{:S(2)}) collective-permute-start(f32[128,256]{1,0:T(8,128)S(1)} %convert_add_fusion.2.refs_0_), channel_id=1, source_target_pairs={{0,4},{2,6},{4,0},{6,2},{8,12},{10,14},{12,8},{14,10},{16,20},{18,... | collective-permute-start | bytes 393224 | tf_op jit(solution)/shard_map/ppermute | solution.py:31
  95.5 1.8 %fusion.own_ref = f32[256,512]{1,0:T(8,128)S(1)} fusion(bf16[1024,512]{1,0:T(8,128)(2,1)} %copy-done.18, bf16[256,2048]{1,0:T(8,128)(2,1)} %copy-done.6, s32[]{:T(128)S(6)} %select_n.33), kind=kOutput, calls=%fused_computation.1 | convolution fusion | flops 268435456 | bytes 2097156 | tf_op jit(solution)/shard_map/dot_general | solution.py:138
  97.3 3.9 %collective-permute-done.15.received_ref = f32[256,512]{1,0:T(8,128)} collective-permute-done((f32[256,512]{1,0:T(8,128)}, f32[256,512]{1,0:T(8,128)}, u32[]{:S(2)}, u32[]{:S(2)}) %collective-permute-start.15) | collective-permute-done | bytes 524320 | tf_op jit(solution)/shard_map/ppermute | solution.py:31
  101.2 1.7 %shard_map.92.grads_ref = bf16[256,512]{1,0:T(8,128)(2,1)S(1)} custom-call(f32[256,512]{1,0:T(8,128)S(1)} %fusion.own_ref, f32[256,512]{1,0:T(8,128)} %collective-permute-done.15.received_ref, f32[2,256,512]{2,1,0:T(8,128)S(1)} %shard_map.88.refer_ref, s32[256,1]{1,0:T(8,128)S(1)} %copy.13.target_ref, s32[256,1]{1,0:T(8,128)S(1)} %copy-done.20, ...), custom_call_target="tpu_custom_call" | custom-call | flops 2621440 | bytes 1835008 | tf_op jit(solution)/shard_map/pallas_call | solution.py:304
  103.3 1.7 %shard_map.93.refs_0_ = f32[1024,512]{1,0:T(8,128)S(1)} custom-call(s32[6]{0:T(128)S(1)} %stack.19.spots_ref, f32[1024,512]{1,0:T(8,128)S(1)} %copy-done.17, bf16[256,2048]{1,0:T(8,128)(2,1)S(1)} %copy-done.8, bf16[256,512]{1,0:T(8,128)(2,1)S(1)} %shard_map.92.grads_ref, f32[128,256]{1,0:T(8,128)S(1)} %convert_add_fusion.2.refs_0_), custom_call_target="tpu_custom_call" | custom-call | flops 268435456 | bytes 4194304 | tf_op jit(solution)/shard_map/pallas_call | solution.py:326
  105.0 1.3 copy-done.3
  107.0 2.5 %collective-permute-done.21.grads_ref = bf16[256,512]{1,0:T(8,128)(2,1)S(1)} collective-permute-done((bf16[256,512]{1,0:T(8,128)(2,1)S(1)}, bf16[256,512]{1,0:T(8,128)(2,1)S(1)}, u32[]{:S(2)}, u32[]{:S(2)}) %collective-permute-start.21) | collective-permute-done | bytes 262176 | tf_op jit(solution)/shard_map/ppermute | solution.py:31
  109.5 1.6 %copy-done.4 = f32[1024,512]{1,0:T(8,128)S(1)} copy-done((f32[1024,512]{1,0:T(8,128)S(1)}, f32[1024,512]{1,0:T(8,128)}, u32[]{:S(2)}) %copy-start.4) | copy-done | bytes 2097176
  111.1 3.3 %shard_map.95 = (f32[1024,512]{1,0:T(8,128)S(1)}, f32[512,256]{1,0:T(8,128)S(1)}, f32[512,256]{1,0:T(8,128)S(1)}) custom-call(s32[6]{0:T(128)S(1)} %stack.19.spots_ref, f32[1024,512]{1,0:T(8,128)S(1)} %copy-done.4, bf16[256,1024]{1,0:T(8,128)(2,1)} %collective-permute-done.14.refs_0_.features_ref, bf16[256,512]{1,0:T(8,128)(2,1)S(1)} %collective-permute-done.21.grads_ref, ...), custom_call_target="tpu_custom_call" | custom-call | flops 268435456 | bytes 6291456 | tf_op jit(solution)/shard_map/pallas_call | solution.py:411
  114.6 1.9 %collective-permute-done.26 = f32[512,256]{1,0:T(8,128)S(1)} collective-permute-done((f32[512,256]{1,0:T(8,128)S(1)}, f32[512,256]{1,0:T(8,128)S(1)}, u32[]{:S(2)}, u32[]{:S(2)}) %collective-permute-start.26) | collective-permute-done | bytes 524320 | tf_op jit(solution)/shard_map/ppermute | solution.py:31
  117.6 2.4 %collective-permute-start.28 = (f16[128,256]{1,0:T(8,128)(2,1)S(1)}, f16[128,256]{1,0:T(8,128)(2,1)S(1)}, u32[]{:S(2)}, u32[]{:S(2)}) collective-permute-start(f16[128,256]{1,0:T(8,128)(2,1)S(1)} %get-tuple-element.38), channel_id=1, source_target_pairs={{0,8},{2,10},{4,12},{6,14},{8,0},{10,2},{12,4},{14,6},{16,24},{18,... | collective-permute-start | bytes 196616 | tf_op jit(solution)/shard_map/ppermute | solution.py:31
  121.0 3.3 %collective-permute-start.23 = (f16[128,256]{1,0:T(8,128)(2,1)S(1)}, f16[128,256]{1,0:T(8,128)(2,1)S(1)}, u32[]{:S(2)}, u32[]{:S(2)}) collective-permute-start(f16[128,256]{1,0:T(8,128)(2,1)S(1)} %get-tuple-element.32), channel_id=1, source_target_pairs={{0,16},{2,18},{4,20},{6,22},{8,24},{10,26},{12,28},{14,30},{16,0},... | collective-permute-start | bytes 196616 | tf_op jit(solution)/shard_map/ppermute | solution.py:31
  124.4 1.5 %collective-permute-start.24 = (f16[128,256]{1,0:T(8,128)(2,1)S(1)}, f16[128,256]{1,0:T(8,128)(2,1)S(1)}, u32[]{:S(2)}, u32[]{:S(2)}) collective-permute-start(f16[128,256]{1,0:T(8,128)(2,1)S(1)} %get-tuple-element.32), channel_id=1, source_target_pairs={{0,24},{2,26},{4,28},{6,30},{8,16},{10,18},{12,20},{14,22},{16,8},... | collective-permute-start | bytes 196616 | tf_op jit(solution)/shard_map/ppermute | solution.py:31
  126.9 1.6 %collective-permute-start.30 = (f32[128,256]{1,0:T(8,128)S(1)}, f32[128,256]{1,0:T(8,128)S(1)}, u32[]{:S(2)}, u32[]{:S(2)}) collective-permute-start(f32[128,256]{1,0:T(8,128)S(1)} %convert_add_fusion.1), channel_id=1, source_target_pairs={{0,4},{2,6},{4,0},{6,2},{8,12},{10,14},{12,8},{14,10},{16,20},{18,... | collective-permute-start | bytes 393224 | tf_op jit(solution)/shard_map/ppermute | solution.py:31
  128.5 1.3 collective-permute-done.23
  135.5 2.5 %collective-permute-start.33 = (f16[128,256]{1,0:T(8,128)(2,1)S(1)}, f16[128,256]{1,0:T(8,128)(2,1)S(1)}, u32[]{:S(2)}, u32[]{:S(2)}) collective-permute-start(f16[128,256]{1,0:T(8,128)(2,1)S(1)} %convert_element_type.58), channel_id=1, source_target_pairs={{0,24},{2,26},{4,28},{6,30},{8,16},{10,18},{12,20},{14,22},{16,8},... | collective-permute-start | bytes 196616 | tf_op jit(solution)/shard_map/ppermute | solution.py:31
  138.1 4.4 %collective-permute-done.32 = f16[128,256]{1,0:T(8,128)(2,1)S(1)} collective-permute-done((f16[128,256]{1,0:T(8,128)(2,1)S(1)}, f16[128,256]{1,0:T(8,128)(2,1)S(1)}, u32[]{:S(2)}, u32[]{:S(2)}) %collective-permute-start.32) | collective-permute-done | bytes 65568 | tf_op jit(solution)/shard_map/ppermute | solution.py:31
  142.7 1.9 %collective-permute-done.34.other1 = f32[512,256]{1,0:T(8,128)S(1)} collective-permute-done((f32[512,256]{1,0:T(8,128)S(1)}, f32[512,256]{1,0:T(8,128)S(1)}, u32[]{:S(2)}, u32[]{:S(2)}) %collective-permute-start.34) | collective-permute-done | bytes 524320 | tf_op jit(solution)/shard_map/ppermute | solution.py:31
  144.6 1.6 %copy-done.15 = f32[1024,512]{1,0:T(8,128)S(1)} copy-done((f32[1024,512]{1,0:T(8,128)S(1)}, f32[1024,512]{1,0:T(8,128)}, u32[]{:S(2)}) %copy-start.15) | copy-done | bytes 2097176
  146.2 4.3 %shard_map.97 = (f32[1024,512]{1,0:T(8,128)}, f32[1024,512]{1,0:T(8,128)}) custom-call(s32[6]{0:T(128)S(1)} %stack.19.spots_ref, f32[1024,512]{1,0:T(8,128)S(1)} %copy-done, f32[1024,512]{1,0:T(8,128)S(1)} %copy-done.15, f32[512,256]{1,0:T(8,128)S(1)} %copy-done.12, f32[512,256]{1,0:T(8,128)S(1)} %collective-permute-done.25.other0, ...), custom_call_target="tpu_custom_call" | custom-call | flops 3145728 | bytes 10485760 | tf_op jit(solution)/shard_map/pallas_call | solution.py:448
  (122 shorter events, 33.6 us)
Async XLA Ops:
  0.6 18.2 %collective-permute-start.6 = (bf16[64,512]{1,0:T(8,128)(2,1)}, bf16[64,512]{1,0:T(8,128)(2,1)}, u32[]{:S(2)}, u32[]{:S(2)}) collective-permute-start(bf16[64,512]{1,0:T(8,128)(2,1)} %param.13), channel_id=1, source_target_pairs={{0,1},{1,0},{2,3},{3,2},{4,5},{5,4},{6,7},{7,6},{8,9},{9,8},{10,11... | collective-permute-start | bytes 196616 | tf_op jit(solution)/shard_map/ppermute | solution.py:31
  3.6 18.4 %collective-permute-start.2 = (bf16[64,512]{1,0:T(8,128)(2,1)}, bf16[64,512]{1,0:T(8,128)(2,1)S(1)}, u32[]{:S(2)}, u32[]{:S(2)}) collective-permute-start(bf16[64,512]{1,0:T(8,128)(2,1)} %param.13), channel_id=1, source_target_pairs={{0,8},{2,10},{4,12},{6,14},{8,0},{10,2},{12,4},{14,6},{16,24},{18,... | collective-permute-start | bytes 196616 | tf_op jit(solution)/shard_map/ppermute | solution.py:31
  5.2 18.1 %collective-permute-start.3 = (bf16[64,512]{1,0:T(8,128)(2,1)}, bf16[64,512]{1,0:T(8,128)(2,1)S(1)}, u32[]{:S(2)}, u32[]{:S(2)}) collective-permute-start(bf16[64,512]{1,0:T(8,128)(2,1)} %param.13), channel_id=1, source_target_pairs={{0,16},{2,18},{4,20},{6,22},{8,24},{10,26},{12,28},{14,30},{16,0},... | collective-permute-start | bytes 196616 | tf_op jit(solution)/shard_map/ppermute | solution.py:31
  7.8 19.6 %collective-permute-start.4 = (bf16[64,512]{1,0:T(8,128)(2,1)}, bf16[64,512]{1,0:T(8,128)(2,1)S(1)}, u32[]{:S(2)}, u32[]{:S(2)}) collective-permute-start(bf16[64,512]{1,0:T(8,128)(2,1)} %param.13), channel_id=1, source_target_pairs={{0,24},{2,26},{4,28},{6,30},{8,16},{10,18},{12,20},{14,22},{16,8},... | collective-permute-start | bytes 196616 | tf_op jit(solution)/shard_map/ppermute | solution.py:31
  10.3 6.0 %copy-start.25 = (s32[2,256]{1,0:T(2,128)S(1)}, s32[2,256]{1,0:T(2,128)}, u32[]{:S(2)}) copy-start(s32[2,256]{1,0:T(2,128)} %param.8) | copy-start | bytes 6148
  10.3 6.2 %copy-start = (f32[1024,512]{1,0:T(8,128)S(1)}, f32[1024,512]{1,0:T(8,128)}, u32[]{:S(2)}) copy-start(f32[1024,512]{1,0:T(8,128)} %outer_ref.5) | copy-start | bytes 6291460
  12.7 33.5 %copy-start.9 = (bf16[256,2048]{1,0:T(8,128)(2,1)}, bf16[256,2048]{1,0:T(8,128)(2,1)S(1)}, u32[]{:S(2)}) copy-start(bf16[256,2048]{1,0:T(8,128)(2,1)S(1)} %get-tuple-element.16.first_ref.normed_ref) | copy-start | bytes 3145732
  12.7 30.7 %collective-permute-start = (bf16[256,1024]{1,0:T(8,128)(2,1)}, bf16[256,1024]{1,0:T(8,128)(2,1)}, u32[]{:S(2)}, u32[]{:S(2)}) collective-permute-start(bf16[256,1024]{1,0:T(8,128)(2,1)} %get-tuple-element.17), channel_id=1, source_target_pairs={{0,1},{1,0},{2,3},{3,2},{4,5},{5,4},{6,7},{7,6},{8,9},{9,8},{10,11... | collective-permute-start | bytes 1572872 | tf_op jit(solution)/shard_map/ppermute | solution.py:31
  18.1 27.6 %copy-start.1 = (f32[1024,512]{1,0:T(8,128)}, f32[1024,512]{1,0:T(8,128)S(1)}, u32[]{:S(2)}) copy-start(f32[1024,512]{1,0:T(8,128)S(1)} %convert_add_fusion.inner_ref) | copy-start | bytes 6291460
  18.8 45.3 %collective-permute-start.14 = (bf16[256,1024]{1,0:T(8,128)(2,1)}, bf16[256,1024]{1,0:T(8,128)(2,1)}, u32[]{:S(2)}, u32[]{:S(2)}) collective-permute-start(bf16[256,1024]{1,0:T(8,128)(2,1)} %get-tuple-element.19), channel_id=1, source_target_pairs={{0,1},{1,0},{2,3},{3,2},{4,5},{5,4},{6,7},{7,6},{8,9},{9,8},{10,11... | collective-permute-start | bytes 1572872 | tf_op jit(solution)/shard_map/ppermute | solution.py:31
  22.0 8.7 %collective-permute-start.7 = (bf16[64,512]{1,0:T(8,128)(2,1)}, bf16[64,512]{1,0:T(8,128)(2,1)S(1)}, u32[]{:S(2)}, u32[]{:S(2)}) collective-permute-start(bf16[64,512]{1,0:T(8,128)(2,1)} %collective-permute-done.6), channel_id=1, source_target_pairs={{0,8},{2,10},{4,12},{6,14},{8,0},{10,2},{12,4},{14,6},{16,24},{18,... | collective-permute-start | bytes 196616 | tf_op jit(solution)/shard_map/ppermute | solution.py:31
  23.3 8.9 %collective-permute-start.8 = (bf16[64,512]{1,0:T(8,128)(2,1)}, bf16[64,512]{1,0:T(8,128)(2,1)S(1)}, u32[]{:S(2)}, u32[]{:S(2)}) collective-permute-start(bf16[64,512]{1,0:T(8,128)(2,1)} %collective-permute-done.6), channel_id=1, source_target_pairs={{0,16},{2,18},{4,20},{6,22},{8,24},{10,26},{12,28},{14,30},{16,0},... | collective-permute-start | bytes 196616 | tf_op jit(solution)/shard_map/ppermute | solution.py:31
  28.0 6.3 %collective-permute-start.9 = (bf16[64,512]{1,0:T(8,128)(2,1)}, bf16[64,512]{1,0:T(8,128)(2,1)S(1)}, u32[]{:S(2)}, u32[]{:S(2)}) collective-permute-start(bf16[64,512]{1,0:T(8,128)(2,1)} %collective-permute-done.6), channel_id=1, source_target_pairs={{0,24},{2,26},{4,28},{6,30},{8,16},{10,18},{12,20},{14,22},{16,8},... | collective-permute-start | bytes 196616 | tf_op jit(solution)/shard_map/ppermute | solution.py:31
  30.7 9.1 %collective-permute-start.5 = (bf16[256,512]{1,0:T(8,128)(2,1)S(1)}, bf16[256,512]{1,0:T(8,128)(2,1)S(1)}, u32[]{:S(2)}, u32[]{:S(2)}) collective-permute-start(bf16[256,512]{1,0:T(8,128)(2,1)S(1)} %pad_maximum_fusion), channel_id=1, source_target_pairs={{0,4},{2,6},{4,0},{6,2},{8,12},{10,14},{12,8},{14,10},{16,20},{18,... | collective-permute-start | bytes 786440 | tf_op jit(solution)/shard_map/ppermute | solution.py:31
  35.2 7.5 %collective-permute-start.10 = (bf16[256,512]{1,0:T(8,128)(2,1)S(1)}, bf16[256,512]{1,0:T(8,128)(2,1)S(1)}, u32[]{:S(2)}, u32[]{:S(2)}) collective-permute-start(bf16[256,512]{1,0:T(8,128)(2,1)S(1)} %pad_maximum_fusion.1), channel_id=1, source_target_pairs={{0,4},{2,6},{4,0},{6,2},{8,12},{10,14},{12,8},{14,10},{16,20},{18,... | collective-permute-start | bytes 786440 | tf_op jit(solution)/shard_map/ppermute | solution.py:31
  38.6 7.4 %copy-start.26 = (s32[2,256]{1,0:T(2,128)S(1)}, s32[2,256]{1,0:T(2,128)}, u32[]{:S(2)}) copy-start(s32[2,256]{1,0:T(2,128)} %param.9) | copy-start | bytes 6148
  40.5 7.7 %collective-permute-start.11 = (bf16[512,512]{1,0:T(8,128)(2,1)}, bf16[512,512]{1,0:T(8,128)(2,1)}, u32[]{:S(2)}, u32[]{:S(2)}) collective-permute-start(bf16[512,512]{1,0:T(8,128)(2,1)} %constant_dynamic-update-slice_fusion.refs_0_), channel_id=1, source_target_pairs={{0,2},{2,0},{4,6},{6,4},{8,10},{10,8},{12,14},{14,12},{16,18},{18,... | collective-permute-start | bytes 1572872 | tf_op jit(solution)/shard_map/ppermute | solution.py:31
  43.4 4.8 %collective-permute-start.12 = (bf16[512,512]{1,0:T(8,128)(2,1)}, bf16[512,512]{1,0:T(8,128)(2,1)}, u32[]{:S(2)}, u32[]{:S(2)}) collective-permute-start(bf16[512,512]{1,0:T(8,128)(2,1)} %constant_dynamic-update-slice_fusion.5.refs_1_), channel_id=1, source_target_pairs={{0,2},{2,0},{4,6},{6,4},{8,10},{10,8},{12,14},{14,12},{16,18},{18,... | collective-permute-start | bytes 1572872 | tf_op jit(solution)/shard_map/ppermute | solution.py:31
  45.7 14.7 %collective-permute-start.1 = (f32[256,512]{1,0:T(8,128)}, f32[256,512]{1,0:T(8,128)}, u32[]{:S(2)}, u32[]{:S(2)}) collective-permute-start(f32[256,512]{1,0:T(8,128)} %fusion.2), channel_id=1, source_target_pairs={{0,1},{1,0},{2,3},{3,2},{4,5},{5,4},{6,7},{7,6},{8,9},{9,8},{10,11... | collective-permute-start | bytes 1572872 | tf_op jit(solution)/shard_map/ppermute | solution.py:31
  50.7 11.7 %copy-start.11 = (bf16[256,2048]{1,0:T(8,128)(2,1)S(1)}, bf16[256,2048]{1,0:T(8,128)(2,1)}, u32[]{:S(2)}) copy-start(bf16[256,2048]{1,0:T(8,128)(2,1)} %copy-done.9) | copy-start | bytes 3145732
  54.5 7.9 %copy-start.2 = (f32[1024,512]{1,0:T(8,128)S(1)}, f32[1024,512]{1,0:T(8,128)}, u32[]{:S(2)}) copy-start(f32[1024,512]{1,0:T(8,128)} %copy-done.1) | copy-start | bytes 6291460
  62.0 8.0 %collective-permute-start.13 = (bf16[256,512]{1,0:T(8,128)(2,1)S(1)}, bf16[256,512]{1,0:T(8,128)(2,1)S(1)}, u32[]{:S(2)}, u32[]{:S(2)}) collective-permute-start(bf16[256,512]{1,0:T(8,128)(2,1)S(1)} %shard_map.89.grads_ref), channel_id=1, source_target_pairs={{0,1},{1,0},{2,3},{3,2},{4,5},{5,4},{6,7},{7,6},{8,9},{9,8},{10,11... | collective-permute-start | bytes 786440 | tf_op jit(solution)/shard_map/ppermute | solution.py:31
  78.4 2.3 %collective-permute-start.16 = (f32[512,256]{1,0:T(8,128)}, f32[512,256]{1,0:T(8,128)}, u32[]{:S(2)}, u32[]{:S(2)}) collective-permute-start(f32[512,256]{1,0:T(8,128)} %get-tuple-element.24), channel_id=1, source_target_pairs={{0,2},{2,0},{4,6},{6,4},{8,10},{10,8},{12,14},{14,12},{16,18},{18,... | collective-permute-start | bytes 1572872 | tf_op jit(solution)/shard_map/ppermute | solution.py:31
  83.4 6.9 %collective-permute-start.17 = (f16[128,256]{1,0:T(8,128)(2,1)}, f16[128,256]{1,0:T(8,128)(2,1)S(1)}, u32[]{:S(2)}, u32[]{:S(2)}) collective-permute-start(f16[128,256]{1,0:T(8,128)(2,1)} %get-tuple-element.39), channel_id=1, source_target_pairs={{0,16},{2,18},{4,20},{6,22},{8,24},{10,26},{12,28},{14,30},{16,0},... | collective-permute-start | bytes 196616 | tf_op jit(solution)/shard_map/ppermute | solution.py:31
  84.1 6.3 %collective-permute-start.18 = (f16[128,256]{1,0:T(8,128)(2,1)}, f16[128,256]{1,0:T(8,128)(2,1)S(1)}, u32[]{:S(2)}, u32[]{:S(2)}) collective-permute-start(f16[128,256]{1,0:T(8,128)(2,1)} %get-tuple-element.41), channel_id=1, source_target_pairs={{0,8},{2,10},{4,12},{6,14},{8,0},{10,2},{12,4},{14,6},{16,24},{18,... | collective-permute-start | bytes 196616 | tf_op jit(solution)/shard_map/ppermute | solution.py:31
  86.7 6.3 %collective-permute-start.19 = (f16[128,256]{1,0:T(8,128)(2,1)}, f16[128,256]{1,0:T(8,128)(2,1)S(1)}, u32[]{:S(2)}, u32[]{:S(2)}) collective-permute-start(f16[128,256]{1,0:T(8,128)(2,1)} %get-tuple-element.40), channel_id=1, source_target_pairs={{0,24},{2,26},{4,28},{6,30},{8,16},{10,18},{12,20},{14,22},{16,8},... | collective-permute-start | bytes 196616 | tf_op jit(solution)/shard_map/ppermute | solution.py:31
  87.8 13.4 %collective-permute-start.15 = (f32[256,512]{1,0:T(8,128)}, f32[256,512]{1,0:T(8,128)}, u32[]{:S(2)}, u32[]{:S(2)}) collective-permute-start(f32[256,512]{1,0:T(8,128)} %get-tuple-element.22), channel_id=1, source_target_pairs={{0,1},{1,0},{2,3},{3,2},{4,5},{5,4},{6,7},{7,6},{8,9},{9,8},{10,11... | collective-permute-start | bytes 1572872 | tf_op jit(solution)/shard_map/ppermute | solution.py:31
  89.0 12.2 %copy-start.13 = (f32[512,256]{1,0:T(8,128)S(1)}, f32[512,256]{1,0:T(8,128)}, u32[]{:S(2)}) copy-start(f32[512,256]{1,0:T(8,128)} %get-tuple-element.35.refs_0_) | copy-start | bytes 1572868
  89.0 12.2 %copy-start.20 = (s32[256,1]{1,0:T(8,128)S(1)}, s32[256,1]{1,0:T(8,128)}, u32[]{:S(2)}) copy-start(s32[256,1]{1,0:T(8,128)} %copy.14.valid_ref) | copy-start | bytes 3076
  93.9 12.4 %collective-permute-start.20 = (f32[128,256]{1,0:T(8,128)S(1)}, f32[128,256]{1,0:T(8,128)S(1)}, u32[]{:S(2)}, u32[]{:S(2)}) collective-permute-start(f32[128,256]{1,0:T(8,128)S(1)} %convert_add_fusion.2.refs_0_), channel_id=1, source_target_pairs={{0,4},{2,6},{4,0},{6,2},{8,12},{10,14},{12,8},{14,10},{16,20},{18,... | collective-permute-start | bytes 393224 | tf_op jit(solution)/shard_map/ppermute | solution.py:31
  97.3 6.0 %copy-start.8 = (bf16[256,2048]{1,0:T(8,128)(2,1)S(1)}, bf16[256,2048]{1,0:T(8,128)(2,1)}, u32[]{:S(2)}) copy-start(bf16[256,2048]{1,0:T(8,128)(2,1)} %copy-done.6) | copy-start | bytes 3145732
  97.3 5.9 %copy-start.17 = (f32[1024,512]{1,0:T(8,128)S(1)}, f32[1024,512]{1,0:T(8,128)}, u32[]{:S(2)}) copy-start(f32[1024,512]{1,0:T(8,128)} %copy-done.16) | copy-start | bytes 6291460
  102.9 6.6 %collective-permute-start.21 = (bf16[256,512]{1,0:T(8,128)(2,1)S(1)}, bf16[256,512]{1,0:T(8,128)(2,1)S(1)}, u32[]{:S(2)}, u32[]{:S(2)}) collective-permute-start(bf16[256,512]{1,0:T(8,128)(2,1)S(1)} %shard_map.92.grads_ref), channel_id=1, source_target_pairs={{0,1},{1,0},{2,3},{3,2},{4,5},{5,4},{6,7},{7,6},{8,9},{9,8},{10,11... | collective-permute-start | bytes 786440 | tf_op jit(solution)/shard_map/ppermute | solution.py:31
  114.5 16.1 %copy-start.14 = (f32[1024,512]{1,0:T(8,128)}, f32[1024,512]{1,0:T(8,128)S(1)}, u32[]{:S(2)}) copy-start(f32[1024,512]{1,0:T(8,128)S(1)} %get-tuple-element.25.inner_ref) | copy-start | bytes 6291460
  114.5 2.0 %collective-permute-start.26 = (f32[512,256]{1,0:T(8,128)S(1)}, f32[512,256]{1,0:T(8,128)S(1)}, u32[]{:S(2)}, u32[]{:S(2)}) collective-permute-start(f32[512,256]{1,0:T(8,128)S(1)} %get-tuple-element.27), channel_id=1, source_target_pairs={{0,2},{2,0},{4,6},{6,4},{8,10},{10,8},{12,14},{14,12},{16,18},{18,... | collective-permute-start | bytes 1572872 | tf_op jit(solution)/shard_map/ppermute | solution.py:31
  116.6 7.8 %collective-permute-start.27 = (f16[128,256]{1,0:T(8,128)(2,1)S(1)}, f16[128,256]{1,0:T(8,128)(2,1)S(1)}, u32[]{:S(2)}, u32[]{:S(2)}) collective-permute-start(f16[128,256]{1,0:T(8,128)(2,1)S(1)} %get-tuple-element.36), channel_id=1, source_target_pairs={{0,16},{2,18},{4,20},{6,22},{8,24},{10,26},{12,28},{14,30},{16,0},... | collective-permute-start | bytes 196616 | tf_op jit(solution)/shard_map/ppermute | solution.py:31
  117.6 8.3 %collective-permute-start.28 = (f16[128,256]{1,0:T(8,128)(2,1)S(1)}, f16[128,256]{1,0:T(8,128)(2,1)S(1)}, u32[]{:S(2)}, u32[]{:S(2)}) collective-permute-start(f16[128,256]{1,0:T(8,128)(2,1)S(1)} %get-tuple-element.38), channel_id=1, source_target_pairs={{0,8},{2,10},{4,12},{6,14},{8,0},{10,2},{12,4},{14,6},{16,24},{18,... | collective-permute-start | bytes 196616 | tf_op jit(solution)/shard_map/ppermute | solution.py:31
  120.0 6.9 %collective-permute-start.29 = (f16[128,256]{1,0:T(8,128)(2,1)S(1)}, f16[128,256]{1,0:T(8,128)(2,1)S(1)}, u32[]{:S(2)}, u32[]{:S(2)}) collective-permute-start(f16[128,256]{1,0:T(8,128)(2,1)S(1)} %get-tuple-element.37), channel_id=1, source_target_pairs={{0,24},{2,26},{4,28},{6,30},{8,16},{10,18},{12,20},{14,22},{16,8},... | collective-permute-start | bytes 196616 | tf_op jit(solution)/shard_map/ppermute | solution.py:31
  121.0 7.4 %collective-permute-start.22 = (f16[128,256]{1,0:T(8,128)(2,1)S(1)}, f16[128,256]{1,0:T(8,128)(2,1)S(1)}, u32[]{:S(2)}, u32[]{:S(2)}) collective-permute-start(f16[128,256]{1,0:T(8,128)(2,1)S(1)} %get-tuple-element.32), channel_id=1, source_target_pairs={{0,8},{2,10},{4,12},{6,14},{8,0},{10,2},{12,4},{14,6},{16,24},{18,... | collective-permute-start | bytes 196616 | tf_op jit(solution)/shard_map/ppermute | solution.py:31
  121.0 8.7 %collective-permute-start.23 = (f16[128,256]{1,0:T(8,128)(2,1)S(1)}, f16[128,256]{1,0:T(8,128)(2,1)S(1)}, u32[]{:S(2)}, u32[]{:S(2)}) collective-permute-start(f16[128,256]{1,0:T(8,128)(2,1)S(1)} %get-tuple-element.32), channel_id=1, source_target_pairs={{0,16},{2,18},{4,20},{6,22},{8,24},{10,26},{12,28},{14,30},{16,0},... | collective-permute-start | bytes 196616 | tf_op jit(solution)/shard_map/ppermute | solution.py:31
  124.4 6.2 %collective-permute-start.24 = (f16[128,256]{1,0:T(8,128)(2,1)S(1)}, f16[128,256]{1,0:T(8,128)(2,1)S(1)}, u32[]{:S(2)}, u32[]{:S(2)}) collective-permute-start(f16[128,256]{1,0:T(8,128)(2,1)S(1)} %get-tuple-element.32), channel_id=1, source_target_pairs={{0,24},{2,26},{4,28},{6,30},{8,16},{10,18},{12,20},{14,22},{16,8},... | collective-permute-start | bytes 196616 | tf_op jit(solution)/shard_map/ppermute | solution.py:31
  126.9 5.0 %collective-permute-start.30 = (f32[128,256]{1,0:T(8,128)S(1)}, f32[128,256]{1,0:T(8,128)S(1)}, u32[]{:S(2)}, u32[]{:S(2)}) collective-permute-start(f32[128,256]{1,0:T(8,128)S(1)} %convert_add_fusion.1), channel_id=1, source_target_pairs={{0,4},{2,6},{4,0},{6,2},{8,12},{10,14},{12,8},{14,10},{16,20},{18,... | collective-permute-start | bytes 393224 | tf_op jit(solution)/shard_map/ppermute | solution.py:31
  131.4 13.2 %copy-start.12 = (f32[512,256]{1,0:T(8,128)S(1)}, f32[512,256]{1,0:T(8,128)}, u32[]{:S(2)}) copy-start(f32[512,256]{1,0:T(8,128)} %maximum_convert_fusion.refs_1_.own0) | copy-start | bytes 1572868
  133.5 4.6 %collective-permute-start.31 = (f16[128,256]{1,0:T(8,128)(2,1)S(1)}, f16[128,256]{1,0:T(8,128)(2,1)S(1)}, u32[]{:S(2)}, u32[]{:S(2)}) collective-permute-start(f16[128,256]{1,0:T(8,128)(2,1)S(1)} %convert_element_type.58), channel_id=1, source_target_pairs={{0,8},{2,10},{4,12},{6,14},{8,0},{10,2},{12,4},{14,6},{16,24},{18,... | collective-permute-start | bytes 196616 | tf_op jit(solution)/shard_map/ppermute | solution.py:31
  134.6 7.9 %collective-permute-start.32 = (f16[128,256]{1,0:T(8,128)(2,1)S(1)}, f16[128,256]{1,0:T(8,128)(2,1)S(1)}, u32[]{:S(2)}, u32[]{:S(2)}) collective-permute-start(f16[128,256]{1,0:T(8,128)(2,1)S(1)} %convert_element_type.58), channel_id=1, source_target_pairs={{0,16},{2,18},{4,20},{6,22},{8,24},{10,26},{12,28},{14,30},{16,0},... | collective-permute-start | bytes 196616 | tf_op jit(solution)/shard_map/ppermute | solution.py:31
  135.5 7.1 %collective-permute-start.33 = (f16[128,256]{1,0:T(8,128)(2,1)S(1)}, f16[128,256]{1,0:T(8,128)(2,1)S(1)}, u32[]{:S(2)}, u32[]{:S(2)}) collective-permute-start(f16[128,256]{1,0:T(8,128)(2,1)S(1)} %convert_element_type.58), channel_id=1, source_target_pairs={{0,24},{2,26},{4,28},{6,30},{8,16},{10,18},{12,20},{14,22},{16,8},... | collective-permute-start | bytes 196616 | tf_op jit(solution)/shard_map/ppermute | solution.py:31
  138.0 4.7 %collective-permute-start.25 = (f32[512,256]{1,0:T(8,128)}, f32[512,256]{1,0:T(8,128)S(1)}, u32[]{:S(2)}, u32[]{:S(2)}) collective-permute-start(f32[512,256]{1,0:T(8,128)} %maximum_convert_fusion.refs_1_.own0), channel_id=1, source_target_pairs={{0,2},{2,0},{4,6},{6,4},{8,10},{10,8},{12,14},{14,12},{16,18},{18,... | collective-permute-start | bytes 1572872 | tf_op jit(solution)/shard_map/ppermute | solution.py:31
  142.6 2.0 %collective-permute-start.34 = (f32[512,256]{1,0:T(8,128)S(1)}, f32[512,256]{1,0:T(8,128)S(1)}, u32[]{:S(2)}, u32[]{:S(2)}) collective-permute-start(f32[512,256]{1,0:T(8,128)S(1)} %maximum_convert_fusion.1.own1), channel_id=1, source_target_pairs={{0,2},{2,0},{4,6},{6,4},{8,10},{10,8},{12,14},{14,12},{16,18},{18,... | collective-permute-start | bytes 1572872 | tf_op jit(solution)/shard_map/ppermute | solution.py:31
  (14 other events, 24.4 us)

commit v3 on v1

--- a/solution.py
+++ b/solution.py
@@ -3,6 +3,8 @@
 import jax
 import jax.numpy as jnp
 from jax import lax
+from jax.experimental import pallas as pl
+from jax.experimental.pallas import tpu as pltpu
 from jax.sharding import PartitionSpec as P
 
 D = 2048
@@ -21,7 +23,7 @@
 f32 = jnp.float32
 bf16 = jnp.bfloat16
 f16 = jnp.float16
-logit_type = jnp.float32
+logit_type = jnp.float16
 
 
 def swap(value, axis, mask):
@@ -140,7 +142,7 @@
     return lax.dot_general(a, b, (((0,), (0,)), ((), ())), preferred_element_type=f32)
 
 
-def shards(hidden, targets, valid, plan, outer_head, drift, ref_head):
+def shards_any(hidden, targets, valid, plan, outer_head, drift, ref_head):
     rows_local, width = outer_head.shape
     part = width // FRAGS
     fsdp = lax.axis_size("fsdp")
@@ -182,6 +184,397 @@
     return (new_outer, new_inner[None])
 
 
+MASKS = (2, 1, 3)
+VMEM = pl.BlockSpec(memory_space=pltpu.VMEM)
+SMEM = pl.BlockSpec(memory_space=pltpu.SMEM)
+ANY = pl.BlockSpec(memory_space=pl.ANY)
+HBM = pl.BlockSpec(memory_space=pltpu.HBM)
+
+
+def call(kernel, operands, in_specs, out_shape, out_specs, room, scratch=(), **more):
+    return pl.pallas_call(
+        kernel,
+        out_shape=out_shape,
+        in_specs=in_specs,
+        out_specs=out_specs,
+        scratch_shapes=scratch,
+        compiler_params=pltpu.CompilerParams(vmem_limit_bytes=room * 1024 * 1024),
+        cost_estimate=pl.CostEstimate(flops=1000, bytes_accessed=1000, transcendentals=0),
+        **more,
+    )(*operands)
+
+
+def like(shape, kind):
+    return jax.ShapeDtypeStruct(shape, kind)
+
+
+def after(value, *earlier):
+    def kernel(*refs):
+        pass
+
+    return call(
+        kernel,
+        (value,) + earlier,
+        [ANY] * (1 + len(earlier)),
+        like(value.shape, value.dtype),
+        ANY,
+        2,
+        input_output_aliases={0: 0},
+    )
+
+
+def stacked(pieces):
+    rows, cols = pieces[0].shape
+    count = len(pieces)
+
+    def kernel(*refs):
+        out_ref, sems = refs[count:]
+        copies = [
+            pltpu.make_async_copy(refs[k], out_ref.at[pl.ds(k * rows, rows)], sems.at[k])
+            for k in range(count)
+        ]
+        for copy in copies:
+            copy.start()
+        for copy in copies:
+            copy.wait()
+
+    return call(
+        kernel,
+        pieces,
+        [ANY] * count,
+        like((count * rows, cols), pieces[0].dtype),
+        ANY,
+        2,
+        [pltpu.SemaphoreType.DMA((count,))],
+    )
+
+
+def normalized(hidden, step, spots):
+    tokens, width = hidden.shape[1:]
+    cols = width // 2
+    parts = 4
+    tile = tokens // parts
+
+    def kernel(spots_ref, hidden_ref, normed_ref, sent_ref, held_ref, sems):
+        other = pl.multiple_of((1 - spots_ref[0]) * cols, cols)
+        copies = [
+            pltpu.make_async_copy(
+                hidden_ref.at[step, pl.ds(k * tile, tile)], held_ref.at[pl.ds(k * tile, tile)], sems.at[k]
+            )
+            for k in range(parts)
+        ]
+        for copy in copies:
+            copy.start()
+        for k, copy in enumerate(copies):
+            copy.wait()
+            at = pl.ds(k * tile, tile)
+            normed_ref[at, :] = normalize(held_ref[at, :])
+            sent_ref[at, :] = normed_ref[at, pl.ds(other, cols)]
+
+    return call(
+        kernel,
+        (spots, hidden),
+        [SMEM, HBM],
+        (like((tokens, width), bf16), like((tokens, cols), bf16)),
+        (VMEM, VMEM),
+        8,
+        [pltpu.VMEM((tokens, width), bf16), pltpu.SemaphoreType.DMA((parts,))],
+    )
+
+
+def reference_logs(normed, stacks, spots):
+    tokens, width = normed.shape
+    entries = stacks[0].shape[1]
+    rows = stacks[0].shape[0] // MAJOR
+    count = len(stacks)
+
+    def kernel(spots_ref, normed_ref, *refs):
+        out_ref, whole_ref, sems = refs[count:]
+        fsdp, me = spots_ref[0], spots_ref[4]
+        copies = []
+        for number in range(count):
+            bit_fsdp, bit_core, bit_y = number // 4, number // 2 % 2, number % 2
+            for p in range(MAJOR):
+                mask = bit_core + bit_y * CORES + p * 2 * CORES
+                block = jnp.bitwise_xor(me, mask) * 2 + jnp.bitwise_xor(fsdp, bit_fsdp)
+                copies.append(
+                    pltpu.make_async_copy(
+                        refs[number].at[pl.ds(p * rows, rows)],
+                        whole_ref.at[pl.ds(pl.multiple_of(block * rows, rows), rows)],
+                        sems.at[len(copies)],
+                    )
+                )
+        for copy in copies:
+            copy.start()
+        for copy in copies:
+            copy.wait()
+        out_ref[...] = log_softmax(capped(dot(normed_ref[...], whole_ref[...])))
+
+    return call(
+        kernel,
+        (spots, normed) + tuple(stacks),
+        [SMEM, VMEM] + [ANY] * count,
+        (like((tokens, entries), f32), like((width, entries), bf16)),
+        (VMEM, VMEM),
+        8,
+        [pltpu.SemaphoreType.DMA((count * MAJOR,))],
+    )
+
+
+def more_reference_logs(normed, whole, *earlier):
+    def kernel(normed_ref, whole_ref, *refs):
+        refs[-1][...] = log_softmax(capped(dot(normed_ref[...], whole_ref[...])))
+
+    return call(
+        kernel,
+        (normed, whole) + earlier,
+        [VMEM, VMEM] + [ANY] * len(earlier),
+        like((normed.shape[0], whole.shape[1]), f32),
+        VMEM,
+        8,
+    )
+
+
+def starting_weights(outer_head, drift):
+    rows, entries = outer_head.shape
+
+    def kernel(outer_ref, drift_ref, inner_ref, weights_ref):
+        inner = outer_ref[...] + drift_ref[0].astype(f32)
+        inner_ref[...] = inner
+        weights_ref[...] = inner.astype(bf16)
+
+    return call(
+        kernel,
+        (outer_head, drift),
+        [VMEM, VMEM],
+        (like((rows, entries), f32), like((rows, entries), bf16)),
+        (VMEM, VMEM),
+        10,
+    )
+
+
+def partial_logits(normed, weights, spots, own, *earlier):
+    tokens = normed.shape[0]
+    rows, entries = weights.shape
+
+    def kernel(spots_ref, normed_ref, weights_ref, *refs):
+        if own:
+            values = normed_ref[:, pl.ds(pl.multiple_of(spots_ref[0] * rows, rows), rows)]
+        else:
+            values = normed_ref[...]
+        refs[-1][...] = dot(values, weights_ref[...])
+
+    return call(
+        kernel,
+        (spots, normed, weights) + earlier,
+        [SMEM, VMEM, VMEM] + [ANY] * len(earlier),
+        like((tokens, entries), f32),
+        VMEM,
+        8,
+    )
+
+
+def gradients(own, received, refer_log, target_ids, valid_rows, *earlier):
+    tokens, entries = own.shape
+
+    def kernel(own_ref, received_ref, refer_ref, target_ref, valid_ref, *refs):
+        raw = own_ref[...] + received_ref[...].astype(f32)
+        policy = capped(raw)
+        policy_log = log_softmax(policy)
+        policy_prob = jnp.exp(policy_log)
+        diverge = policy_log - refer_ref[...]
+        kl_value = jnp.sum(policy_prob * diverge, axis=-1, keepdims=True)
+        here = lax.broadcasted_iota(jnp.int32, policy.shape, 1)
+        onehot = jnp.where(target_ref[...] == here, 1.0, 0.0)
+        upstream = valid_ref[...].astype(f32) * (
+            policy_prob - onehot + kl_weight * policy_prob * (diverge - kl_value)
+        )
+        ratio = policy / soft_cap
+        refs[-1][...] = (upstream * (1.0 - ratio * ratio) * (4.0 / math.sqrt(D))).astype(bf16)
+
+    return call(
+        kernel,
+        (own, received, refer_log, target_ids[:, None], valid_rows[:, None]) + earlier,
+        [VMEM] * 5 + [ANY] * len(earlier),
+        like((tokens, entries), bf16),
+        VMEM,
+        8,
+    )
+
+
+def own_update(inner, normed, grads, spots, *earlier):
+    rows, entries = inner.shape
+    tile = rows // 4
+
+    def kernel(spots_ref, inner_ref, normed_ref, grads_ref, *refs):
+        for k in range(4):
+            at = pl.ds(k * tile, tile)
+            columns = pl.ds(pl.multiple_of(spots_ref[0] * rows + k * tile, tile), tile)
+            refs[-1][at, :] = inner_ref[at, :] - inner_rate * dot_rows(normed_ref[:, columns], grads_ref[...])
+
+    return call(
+        kernel,
+        (spots, inner, normed, grads) + earlier,
+        [SMEM, VMEM, VMEM, VMEM] + [ANY] * len(earlier),
+        like((rows, entries), f32),
+        VMEM,
+        10,
+    )
+
+
+def update(inner, features, grads, outer_head, spots, step, replicas, following=None):
+    rows, entries = inner.shape
+    tokens = features.shape[0]
+    part = entries // FRAGS
+    half = rows // 2
+    tile = rows // 4
+    more = following is not None
+
+    def kernel(spots_ref, inner_ref, features_ref, grads_ref, outer_ref, *refs):
+        if more:
+            following_ref, new_ref, sent_ref, kept_ref, weights_ref, partial_ref = refs
+        else:
+            new_ref, sent_ref, kept_ref = refs
+        for k in range(4):
+            at = pl.ds(k * tile, tile)
+            new = inner_ref[at, :] - inner_rate * dot_rows(features_ref[:, at], grads_ref[...])
+            new_ref[at, :] = new
+            if more:
+                weights_ref[at, :] = new.astype(bf16)
+        if more:
+            partial_ref[...] = dot(following_ref[...], weights_ref[...])
+        columns = pl.ds(pl.multiple_of(spots_ref[2 + step] * part, part), part)
+        core = spots_ref[1]
+        for place_ref, which in ((sent_ref, 1 - core), (kept_ref, core)):
+            at = pl.ds(pl.multiple_of(which * half, half), half)
+            place_ref[...] = (outer_ref[at, columns] - new_ref[at, columns]) * (1.0 / replicas)
+
+    operands = (spots, inner, features, grads, outer_head)
+    out_shape = [like((rows, entries), f32), like((half, part), f32), like((half, part), f32)]
+    if more:
+        operands += (following,)
+        out_shape += [like((rows, entries), bf16), like((tokens, entries), f32)]
+    return call(
+        kernel,
+        operands,
+        [SMEM] + [VMEM] * (len(operands) - 1),
+        out_shape,
+        [VMEM] * len(out_shape),
+        14,
+    )
+
+
+def settled(outer_head, inner, means, spots):
+    rows, entries = inner.shape
+    part = entries // FRAGS
+    tile = rows // (CORES * MAJOR)
+    steps = 4
+    each = CORES * MAJOR // steps
+
+    def kernel(spots_ref, outer_ref, inner_ref, own0, other0, own1, other1, new_outer_ref, new_inner_ref):
+        for k in range(each):
+            i = pl.program_id(0) * each + k
+            mine = i // MAJOR == spots_ref[1]
+            there = jnp.bitwise_xor(lax.rem(i, MAJOR), spots_ref[5])
+            source = pl.ds(pl.multiple_of(there * tile, tile), tile)
+            at = pl.ds(pl.multiple_of(i * tile, tile), tile)
+            to = pl.ds(k * tile, tile)
+            mean0 = jnp.where(mine, own0[source, :], other0[source, :])
+            mean1 = jnp.where(mine, own1[source, :], other1[source, :])
+            for f in range(FRAGS):
+                columns = pl.ds(f * part, part)
+                mean = jnp.where(spots_ref[2] == f, mean0, mean1)
+                fresh = outer_ref[at, columns] - outer_rate * mean
+                new_outer_ref[to, columns] = fresh
+                new_inner_ref[to, columns] = mix_weight * inner_ref[at, columns] + (1.0 - mix_weight) * fresh
+
+    block = pl.BlockSpec((each * tile, entries), lambda i: (i, 0))
+    return call(
+        kernel,
+        (spots, outer_head, inner) + tuple(means[0]) + tuple(means[1]),
+        [SMEM] + [VMEM] * 6,
+        [like((rows, entries), f32)] * 2,
+        [block, block],
+        14,
+        grid=(steps,),
+    )
+
+
+def gathered_stacks(ref_head, sent, normed):
+    step = 2 * CORES
+    stacks = []
+    for rows in (after(ref_head, normed), swap(after(ref_head, sent), "fsdp", 1)):
+        along = stacked([rows] + [swap(rows, "replica", m * step) for m in range(1, MAJOR)])
+        both = [along, swap(along, "replica", CORES)]
+        stacks += both + [swap(s, "replica", 1) for s in both]
+    return stacks
+
+
+def quarters_sum(part, major):
+    step = 2 * CORES
+    quarter = part.shape[0] // MAJOR
+    sent = part.astype(f16)
+    own = rows_at(part, major, quarter)
+    for m in MASKS:
+        own = own + swap(rows_at(sent, major ^ m, quarter), "replica", m * step).astype(f32)
+    return own
+
+
+def quarters_gathered(own):
+    step = 2 * CORES
+    got = {m: swap(own, "replica", m * step) for m in MASKS}
+    return jnp.concatenate([own, got[1], got[2], got[3]], 0).astype(f32)
+
+
+def shards_pair(hidden, targets, valid, plan, outer_head, drift, ref_head):
+    replicas = lax.axis_size("replica")
+    fsdp = lax.axis_index("fsdp")
+    replica = lax.axis_index("replica")
+    core = replica % CORES
+    major = replica // (2 * CORES)
+    spots = jnp.stack([fsdp, core, plan[0], plan[1], replica, major]).astype(jnp.int32)
+
+    normed0, sent0 = normalized(hidden, 0, spots)
+    features0 = swap(sent0, "fsdp", 1)
+    normed1, sent1 = normalized(hidden, 1, spots)
+    stacks = gathered_stacks(ref_head, sent0, normed1)
+
+    inner, weights = starting_weights(outer_head, drift)
+    partial = partial_logits(features0, weights, spots, False)
+    received = swap(partial.astype(logit_type), "fsdp", 1).astype(f32)
+    own = partial_logits(normed0, weights, spots, True)
+    features1 = swap(after(sent1, received), "fsdp", 1)
+    refer_log, whole = reference_logs(normed0, stacks, spots)
+    grads = gradients(own, received, refer_log, targets[0], valid[0])
+    partner_grads = swap(grads, "fsdp", 1)
+    halfway = own_update(inner, normed0, grads, spots)
+    refer_log = more_reference_logs(normed1, whole, halfway)
+    inner, sent, kept, weights, partial = update(
+        halfway, features0, partner_grads, outer_head, spots, 0, replicas, features1
+    )
+
+    received = swap(partial.astype(logit_type), "fsdp", 1).astype(f32)
+    own = partial_logits(normed1, weights, spots, True)
+    summed = kept + swap(sent, "replica", 1)
+    grads = gradients(own, received, refer_log, targets[1], valid[1], summed)
+    quarter = quarters_sum(summed, major)
+    partner_grads = swap(grads, "fsdp", 1)
+    halfway = own_update(inner, normed1, grads, spots, quarter)
+    first = quarter + swap(quarter, "replica", CORES)
+    inner, sent, kept = update(
+        halfway, features1, after(partner_grads, first), outer_head, spots, 1, replicas
+    )
+
+    summed = kept + swap(sent, "replica", 1)
+    quarter = quarters_sum(summed, major)
+    second = quarter + swap(quarter, "replica", CORES)
+    first = quarters_gathered(first.astype(f16))
+    second = quarters_gathered(second.astype(f16))
+    means = [(m, swap(m, "replica", 1)) for m in (first, second)]
+    new_outer, new_inner = settled(outer_head, inner, means, spots)
+    return (new_outer, new_inner[None])
+
+
 def solution(mesh):
     in_specs = (
         P(None, ("replica", "fsdp"), None),
@@ -193,4 +586,7 @@
         P(("replica", "fsdp"), None),
     )
     out_specs = (P("fsdp", None), P("replica", "fsdp", None))
+    chips = mesh.shape["replica"] // CORES
+    pairs = mesh.shape["fsdp"] == 2 and chips == 2 * MAJOR
+    shards = shards_pair if pairs else shards_any
     return jax.shard_map(shards, mesh=mesh, in_specs=in_specs, out_specs=out_specs, check_vma=False)

time: 127 us -> 134 us (1.055)
  Pallas kernels: 0 us -> 23 us
  matrix products: 13.9 us -> 0 us
  local copies, waits for them, and re-layouts: 10.2 us -> 19.3 us
  other arithmetic: 14.1 us -> 7.23 us
  waiting for transfers between devices: 48.9 us -> 42.8 us
  starting transfers between devices: 36.4 us -> 40.2 us
  between operations: 3.21 us -> 1.11 us
    pallas_call x0 -> x21, Pallas kernels: none -> 23 us  [call(): pl.pallas_call(kernel, out_shape=out_shape, in_specs=in_specs, out_specs=...]
    dot_general x10 -> x0, matrix products: 13.9 us -> none  [the longest x6 9.68 us: dot(): return jnp.dot(a, b, preferred_element_type=f32)]
    unnamed x32 -> x62, local copies, waits for them, and re-layouts: 4.52 us -> 16.6 us
    ppermute x30 -> x37, waiting for transfers between devices: 48.9 us -> 42.8 us  [swap(): return lax.ppermute(value, axis, [(i, i ^ mask) for i in range(size)])]
    ppermute x30 -> x37, starting transfers between devices: 36.4 us -> 40.2 us  [swap(): return lax.ppermute(value, axis, [(i, i ^ mask) for i in range(size)])]
    reduce_sum x3 -> x0, other arithmetic: 3.71 us -> none  [the longest x1 2.02 us: normalize(): jnp.mean(values * values, axis=-1, keepdims=True) + norm_eps]
    broadcast_in_dim x1 -> x0, other arithmetic: 2.87 us -> none  [shards(): return (new_outer, new_inner[None])]
    dynamic_slice x2 -> x0, local copies, waits for them, and re-layouts: 2.74 us -> none  [columns_at(): return lax.dynamic_slice_in_dim(value, block * count, count, 1)]
  transfers between devices with their start and end apart: 30 -> 37, of which waited for: 15 -> 20; matrix products, arithmetic and copies ran while one was open for 17% -> 5% of each run, Pallas kernels for 0% -> 11%
where the time goes in v3:
time: 134 us
  waiting for transfers between devices  42.8 us (32%)
  starting transfers between devices  40.2 us (30%)
  Pallas kernels  23 us (17%)
  local copies, waits for them, and re-layouts  19.3 us (14%)
  other arithmetic  7.23 us (5%)
    ppermute x37, waiting for transfers between devices, swap(): return lax.ppermute(value, axis, [(i, i ^ mask) for i in range(size)])  42.8 us
    ppermute x37, starting transfers between devices, swap(): return lax.ppermute(value, axis, [(i, i ^ mask) for i in range(size)])  40.2 us
    pallas_call x21, Pallas kernels, call(): pl.pallas_call(kernel, out_shape=out_shape, in_specs=in_specs, out_specs=...  23 us
    unnamed x62, local copies, waits for them, and re-layouts  16.6 us
    convert_element_type x4, other arithmetic, shards_pair(): received = swap(partial.astype(logit_type), 'fsdp', 1).astype(f32)  3.04 us
  transfers between devices with their start and end apart: 37, of which 20 were waited for; matrix products, arithmetic and copies ran while one was open for 5% of the time, Pallas kernels for 11%

profile of v3, /device:TPU:0, one launch (start us, length us, event | category | flops | bytes accessed | tf_op | source)
XLA Modules:
  0.0 133.5 jit_solution(9136195410917035160)
XLA Ops:
  2.2 1.6 %copy-done.6 = bf16[2,256,2048]{2,1,0:T(8,128)(2,1)S(1)} copy-done((bf16[2,256,2048]{2,1,0:T(8,128)(2,1)S(1)}, bf16[2,256,2048]{2,1,0:T(8,128)(2,1)}, u32[]{:S(2)}) %copy-start.6) | copy-done | bytes 2097176
  3.8 1.3 shard_map.87
  5.1 3.0 %collective-permute-start = (bf16[256,1024]{1,0:T(8,128)(2,1)S(1)}, bf16[256,1024]{1,0:T(8,128)(2,1)S(1)}, u32[]{:S(2)}, u32[]{:S(2)}) collective-permute-start(bf16[256,1024]{1,0:T(8,128)(2,1)S(1)} %get-tuple-element.23.refs_1_), channel_id=1, source_target_pairs={{0,1},{1,0},{2,3},{3,2},{4,5},{5,4},{6,7},{7,6},{8,9},{9,8},{10,11... | collective-permute-start | bytes 1572872 | tf_op jit(solution)/shard_map/ppermute | solution.py:31
  8.2 2.1 %shard_map.90 = (bf16[256,2048]{1,0:T(8,128)(2,1)S(1)}, bf16[256,1024]{1,0:T(8,128)(2,1)}) custom-call(s32[6]{0:T(128)S(1)} %stack.19.spots_ref, bf16[2,256,2048]{2,1,0:T(8,128)(2,1)S(1)} %copy-done.7), custom_call_target="tpu_custom_call" | custom-call | flops 1000 | bytes 1000 | tf_op jit(solution)/shard_map/pallas_call | solution.py:195
  10.4 4.1 %collective-permute-start.4 = (bf16[64,512]{1,0:T(8,128)(2,1)S(1)}, bf16[64,512]{1,0:T(8,128)(2,1)S(1)}, u32[]{:S(2)}, u32[]{:S(2)}) collective-permute-start(bf16[64,512]{1,0:T(8,128)(2,1)S(1)} %shard_map.91.refs_0_), channel_id=1, source_target_pairs={{0,24},{2,26},{4,28},{6,30},{8,16},{10,18},{12,20},{14,22},{16,8},... | collective-permute-start | bytes 196616 | tf_op jit(solution)/shard_map/ppermute | solution.py:31
  15.1 6.4 %collective-permute-done.8.refs_0_ = bf16[64,512]{1,0:T(8,128)(2,1)S(1)} collective-permute-done((bf16[64,512]{1,0:T(8,128)(2,1)S(1)}, bf16[64,512]{1,0:T(8,128)(2,1)S(1)}, u32[]{:S(2)}, u32[]{:S(2)}) %collective-permute-start.8) | collective-permute-done | bytes 65568 | tf_op jit(solution)/shard_map/ppermute | solution.py:31
  21.5 3.9 %collective-permute-start.11 = (bf16[64,512]{1,0:T(8,128)(2,1)S(1)}, bf16[64,512]{1,0:T(8,128)(2,1)S(1)}, u32[]{:S(2)}, u32[]{:S(2)}) collective-permute-start(bf16[64,512]{1,0:T(8,128)(2,1)S(1)} %collective-permute-done.8.refs_0_), channel_id=1, source_target_pairs={{0,24},{2,26},{4,28},{6,30},{8,16},{10,18},{12,20},{14,22},{16,8},... | collective-permute-start | bytes 196616 | tf_op jit(solution)/shard_map/ppermute | solution.py:31
  26.2 1.3 copy-done.13
  27.9 1.8 %collective-permute-start.5 = (bf16[256,512]{1,0:T(8,128)(2,1)S(1)}, bf16[256,512]{1,0:T(8,128)(2,1)}, u32[]{:S(2)}, u32[]{:S(2)}) collective-permute-start(bf16[256,512]{1,0:T(8,128)(2,1)S(1)} %shard_map.92.refs_0_), channel_id=1, source_target_pairs={{0,4},{2,6},{4,0},{6,2},{8,12},{10,14},{12,8},{14,10},{16,20},{18,... | collective-permute-start | bytes 786440 | tf_op jit(solution)/shard_map/ppermute | solution.py:31
  29.7 1.0 collective-permute-done.10.refs_2_
  31.4 1.6 %collective-permute-start.12 = (bf16[256,512]{1,0:T(8,128)(2,1)}, bf16[256,512]{1,0:T(8,128)(2,1)}, u32[]{:S(2)}, u32[]{:S(2)}) collective-permute-start(bf16[256,512]{1,0:T(8,128)(2,1)} %shard_map.94.refs_4_), channel_id=1, source_target_pairs={{0,4},{2,6},{4,0},{6,2},{8,12},{10,14},{12,8},{14,10},{16,20},{18,... | collective-permute-start | bytes 786440 | tf_op jit(solution)/shard_map/ppermute | solution.py:31
  34.0 1.6 %collective-permute-start.1 = (f16[256,512]{1,0:T(8,128)(2,1)S(1)}, f16[256,512]{1,0:T(8,128)(2,1)S(1)}, u32[]{:S(2)}, u32[]{:S(2)}) collective-permute-start(f16[256,512]{1,0:T(8,128)(2,1)S(1)} %convert_element_type.48), channel_id=1, source_target_pairs={{0,1},{1,0},{2,3},{3,2},{4,5},{5,4},{6,7},{7,6},{8,9},{9,8},{10,11... | collective-permute-start | bytes 786440 | tf_op jit(solution)/shard_map/ppermute | solution.py:31
  36.3 4.0 %collective-permute-done.12.refs_5_ = bf16[256,512]{1,0:T(8,128)(2,1)} collective-permute-done((bf16[256,512]{1,0:T(8,128)(2,1)}, bf16[256,512]{1,0:T(8,128)(2,1)}, u32[]{:S(2)}, u32[]{:S(2)}) %collective-permute-start.12) | collective-permute-done | bytes 262176 | tf_op jit(solution)/shard_map/ppermute | solution.py:31
  40.7 1.6 %collective-permute-start.16 = (bf16[256,1024]{1,0:T(8,128)(2,1)}, bf16[256,1024]{1,0:T(8,128)(2,1)}, u32[]{:S(2)}, u32[]{:S(2)}) collective-permute-start(bf16[256,1024]{1,0:T(8,128)(2,1)} %shard_map.98), channel_id=1, source_target_pairs={{0,1},{1,0},{2,3},{3,2},{4,5},{5,4},{6,7},{7,6},{8,9},{9,8},{10,11... | collective-permute-start | bytes 1572872 | tf_op jit(solution)/shard_map/ppermute | solution.py:31
  45.7 1.2 copy-done.4
  46.9 3.7 %shard_map.95 = (f32[256,512]{1,0:T(8,128)S(1)}, bf16[2048,512]{1,0:T(8,128)(2,1)S(1)}) custom-call(s32[6]{0:T(128)S(1)} %stack.19.spots_ref, bf16[256,2048]{1,0:T(8,128)(2,1)S(1)} %copy-done.4, bf16[256,512]{1,0:T(8,128)(2,1)S(1)} %shard_map.92.refs_0_, bf16[256,512]{1,0:T(8,128)(2,1)} %collective-permute-done.5.refs_1_, ...), custom_call_target="tpu_custom_call" | custom-call | flops 1000 | bytes 1000 | tf_op jit(solution)/shard_map/pallas_call | solution.py:195
  50.7 1.4 %copy-done.20 = f32[256,512]{1,0:T(8,128)S(1)} copy-done((f32[256,512]{1,0:T(8,128)S(1)}, f32[256,512]{1,0:T(8,128)}, u32[]{:S(2)}) %copy-start.20) | copy-done | bytes 524312
  55.2 1.0 shard_map.97.inner_ref.refs_0_
  56.2 6.5 %collective-permute-done.15.grads_ref = bf16[256,512]{1,0:T(8,128)(2,1)S(1)} collective-permute-done((bf16[256,512]{1,0:T(8,128)(2,1)S(1)}, bf16[256,512]{1,0:T(8,128)(2,1)S(1)}, u32[]{:S(2)}, u32[]{:S(2)}) %collective-permute-start.15) | collective-permute-done | bytes 262176 | tf_op jit(solution)/shard_map/ppermute | solution.py:31
  62.7 2.6 %shard_map.99 = (f32[1024,512]{1,0:T(8,128)S(1)}, f32[512,256]{1,0:T(8,128)}, f32[512,256]{1,0:T(8,128)S(1)}, bf16[1024,512]{1,0:T(8,128)(2,1)S(1)}, f32[256,512]{1,0:T(8,128)S(1)}) custom-call(s32[6]{0:T(128)S(1)} %stack.19.spots_ref, f32[1024,512]{1,0:T(8,128)S(1)} %shard_map.97.inner_ref.refs_0_, bf16[256,1024]{1,0:T(8,128)(2,1)S(1)} %copy-done.18, ...), custom_call_target="tpu_custom_call" | custom-call | flops 1000 | bytes 1000 | tf_op jit(solution)/shard_map/pallas_call | solution.py:195
  65.3 1.3 copy-done.11
  66.7 1.0 copy-done.22
  69.3 2.2 %collective-permute-done.18 = f32[512,256]{1,0:T(8,128)} collective-permute-done((f32[512,256]{1,0:T(8,128)}, f32[512,256]{1,0:T(8,128)}, u32[]{:S(2)}, u32[]{:S(2)}) %collective-permute-start.18) | collective-permute-done | bytes 524320 | tf_op jit(solution)/shard_map/ppermute | solution.py:31
  71.6 2.1 %fusion.2 = (f16[512,256]{1,0:T(8,128)(2,1)S(1)}, f32[512,256]{1,0:T(8,128)}) fusion(f32[512,256]{1,0:T(8,128)} %copy-done.24, f32[512,256]{1,0:T(8,128)} %collective-permute-done.18), kind=kLoop, calls=%fused_computation.17 | loop fusion | flops 262144 | bytes 1835008 | tf_op jit(solution)/shard_map/convert_element_type | solution.py:516
  73.7 2.4 %collective-permute-start.19 = (f16[128,256]{1,0:T(8,128)(2,1)S(1)}, f16[128,256]{1,0:T(8,128)(2,1)S(1)}, u32[]{:S(2)}, u32[]{:S(2)}) collective-permute-start(f16[128,256]{1,0:T(8,128)(2,1)S(1)} %get-tuple-element.47), channel_id=1, source_target_pairs={{0,16},{2,18},{4,20},{6,22},{8,24},{10,26},{12,28},{14,30},{16,0},... | collective-permute-start | bytes 196616 | tf_op jit(solution)/shard_map/ppermute | solution.py:31
  76.1 1.5 %collective-permute-start.21 = (f16[128,256]{1,0:T(8,128)(2,1)S(1)}, f16[128,256]{1,0:T(8,128)(2,1)S(1)}, u32[]{:S(2)}, u32[]{:S(2)}) collective-permute-start(f16[128,256]{1,0:T(8,128)(2,1)S(1)} %get-tuple-element.48), channel_id=1, source_target_pairs={{0,24},{2,26},{4,28},{6,30},{8,16},{10,18},{12,20},{14,22},{16,8},... | collective-permute-start | bytes 196616 | tf_op jit(solution)/shard_map/ppermute | solution.py:31
  77.9 1.8 %convert_element_type.50 = f16[256,512]{1,0:T(8,128)(2,1)} convert(f32[256,512]{1,0:T(8,128)} %copy-done.27) | non-fusion elementwise | flops 131072 | bytes 786432 | tf_op jit(solution)/shard_map/convert_element_type | solution.py:556
  80.2 1.3 collective-permute-done.19
  81.5 1.1 collective-permute-done.21
  84.0 1.6 %collective-permute-start.23 = (f32[128,256]{1,0:T(8,128)S(1)}, f32[128,256]{1,0:T(8,128)}, u32[]{:S(2)}, u32[]{:S(2)}) collective-permute-start(f32[128,256]{1,0:T(8,128)S(1)} %convert_add_fusion.1.refs_0_), channel_id=1, source_target_pairs={{0,4},{2,6},{4,0},{6,2},{8,12},{10,14},{12,8},{14,10},{16,20},{18,... | collective-permute-start | bytes 393224 | tf_op jit(solution)/shard_map/ppermute | solution.py:31
  85.9 1.6 %copy-done.2 = f32[1024,512]{1,0:T(8,128)S(1)} copy-done((f32[1024,512]{1,0:T(8,128)S(1)}, f32[1024,512]{1,0:T(8,128)}, u32[]{:S(2)}) %copy-start.2) | copy-done | bytes 2097176
  87.5 1.6 %copy-done.16 = bf16[2048,512]{1,0:T(8,128)(2,1)S(1)} copy-done((bf16[2048,512]{1,0:T(8,128)(2,1)S(1)}, bf16[2048,512]{1,0:T(8,128)(2,1)}, u32[]{:S(2)}) %copy-start.16) | copy-done | bytes 2097176
  91.3 1.1 convert_element_type.51.received_ref
  93.7 1.0 shard_map.103.inner_ref
  95.6 5.1 %collective-permute-done.22.refs_0_ = bf16[256,512]{1,0:T(8,128)(2,1)S(1)} collective-permute-done((bf16[256,512]{1,0:T(8,128)(2,1)S(1)}, bf16[256,512]{1,0:T(8,128)(2,1)S(1)}, u32[]{:S(2)}, u32[]{:S(2)}) %collective-permute-start.22) | collective-permute-done | bytes 262176 | tf_op jit(solution)/shard_map/ppermute | solution.py:31
  100.7 1.8 %shard_map.105 = (f32[1024,512]{1,0:T(8,128)S(1)}, f32[512,256]{1,0:T(8,128)S(1)}, f32[512,256]{1,0:T(8,128)S(1)}) custom-call(s32[6]{0:T(128)S(1)} %stack.19.spots_ref, f32[1024,512]{1,0:T(8,128)S(1)} %shard_map.103.inner_ref, bf16[256,1024]{1,0:T(8,128)(2,1)} %collective-permute-done.16.refs_0_.features_ref, bf16[256,512]{1,0:T(8,128)(2,1)S(1)} %shard_map.104.grads_ref, ...), custom_call_target="tpu_custom_call" | custom-call | flops 1000 | bytes 1000 | tf_op jit(solution)/shard_map/pallas_call | solution.py:195
  102.5 1.9 %collective-permute-done.28 = f32[512,256]{1,0:T(8,128)S(1)} collective-permute-done((f32[512,256]{1,0:T(8,128)S(1)}, f32[512,256]{1,0:T(8,128)S(1)}, u32[]{:S(2)}, u32[]{:S(2)}) %collective-permute-start.28) | collective-permute-done | bytes 524320 | tf_op jit(solution)/shard_map/ppermute | solution.py:31
  104.6 2.7 %collective-permute-start.29 = (f16[128,256]{1,0:T(8,128)(2,1)S(1)}, f16[128,256]{1,0:T(8,128)(2,1)S(1)}, u32[]{:S(2)}, u32[]{:S(2)}) collective-permute-start(f16[128,256]{1,0:T(8,128)(2,1)S(1)} %get-tuple-element.44), channel_id=1, source_target_pairs={{0,16},{2,18},{4,20},{6,22},{8,24},{10,26},{12,28},{14,30},{16,0},... | collective-permute-start | bytes 196616 | tf_op jit(solution)/shard_map/ppermute | solution.py:31
  108.3 3.3 %collective-permute-done.29 = f16[128,256]{1,0:T(8,128)(2,1)S(1)} collective-permute-done((f16[128,256]{1,0:T(8,128)(2,1)S(1)}, f16[128,256]{1,0:T(8,128)(2,1)S(1)}, u32[]{:S(2)}, u32[]{:S(2)}) %collective-permute-start.29) | collective-permute-done | bytes 65568 | tf_op jit(solution)/shard_map/ppermute | solution.py:31
  111.6 2.1 %collective-permute-done.31 = f16[128,256]{1,0:T(8,128)(2,1)S(1)} collective-permute-done((f16[128,256]{1,0:T(8,128)(2,1)S(1)}, f16[128,256]{1,0:T(8,128)(2,1)S(1)}, u32[]{:S(2)}, u32[]{:S(2)}) %collective-permute-start.31) | collective-permute-done | bytes 65568 | tf_op jit(solution)/shard_map/ppermute | solution.py:31
  114.5 2.7 %collective-permute-start.26 = (f16[128,256]{1,0:T(8,128)(2,1)S(1)}, f16[128,256]{1,0:T(8,128)(2,1)S(1)}, u32[]{:S(2)}, u32[]{:S(2)}) collective-permute-start(f16[128,256]{1,0:T(8,128)(2,1)S(1)} %get-tuple-element.40), channel_id=1, source_target_pairs={{0,24},{2,26},{4,28},{6,30},{8,16},{10,18},{12,20},{14,22},{16,8},... | collective-permute-start | bytes 196616 | tf_op jit(solution)/shard_map/ppermute | solution.py:31
  117.2 1.7 %collective-permute-start.24 = (f16[128,256]{1,0:T(8,128)(2,1)S(1)}, f16[128,256]{1,0:T(8,128)(2,1)S(1)}, u32[]{:S(2)}, u32[]{:S(2)}) collective-permute-start(f16[128,256]{1,0:T(8,128)(2,1)S(1)} %get-tuple-element.40), channel_id=1, source_target_pairs={{0,8},{2,10},{4,12},{6,14},{8,0},{10,2},{12,4},{14,6},{16,24},{18,... | collective-permute-start | bytes 196616 | tf_op jit(solution)/shard_map/ppermute | solution.py:31
  119.0 2.7 %collective-permute-start.35 = (f16[128,256]{1,0:T(8,128)(2,1)S(1)}, f16[128,256]{1,0:T(8,128)(2,1)S(1)}, u32[]{:S(2)}, u32[]{:S(2)}) collective-permute-start(f16[128,256]{1,0:T(8,128)(2,1)S(1)} %add_convert_fusion), channel_id=1, source_target_pairs={{0,24},{2,26},{4,28},{6,30},{8,16},{10,18},{12,20},{14,22},{16,8},... | collective-permute-start | bytes 196616 | tf_op jit(solution)/shard_map/ppermute | solution.py:31
  121.8 1.7 %collective-permute-start.33 = (f16[128,256]{1,0:T(8,128)(2,1)S(1)}, f16[128,256]{1,0:T(8,128)(2,1)S(1)}, u32[]{:S(2)}, u32[]{:S(2)}) collective-permute-start(f16[128,256]{1,0:T(8,128)(2,1)S(1)} %add_convert_fusion), channel_id=1, source_target_pairs={{0,8},{2,10},{4,12},{6,14},{8,0},{10,2},{12,4},{14,6},{16,24},{18,... | collective-permute-start | bytes 196616 | tf_op jit(solution)/shard_map/ppermute | solution.py:31
  123.5 2.0 %collective-permute-done.25 = f16[128,256]{1,0:T(8,128)(2,1)S(1)} collective-permute-done((f16[128,256]{1,0:T(8,128)(2,1)S(1)}, f16[128,256]{1,0:T(8,128)(2,1)S(1)}, u32[]{:S(2)}, u32[]{:S(2)}) %collective-permute-start.25) | collective-permute-done | bytes 65568 | tf_op jit(solution)/shard_map/ppermute | solution.py:31
  125.8 2.5 %collective-permute-done.34 = f16[128,256]{1,0:T(8,128)(2,1)S(1)} collective-permute-done((f16[128,256]{1,0:T(8,128)(2,1)S(1)}, f16[128,256]{1,0:T(8,128)(2,1)S(1)}, u32[]{:S(2)}, u32[]{:S(2)}) %collective-permute-start.34) | collective-permute-done | bytes 65568 | tf_op jit(solution)/shard_map/ppermute | solution.py:31
  128.5 1.9 %collective-permute-done.36.other1 = f32[512,256]{1,0:T(8,128)S(1)} collective-permute-done((f32[512,256]{1,0:T(8,128)S(1)}, f32[512,256]{1,0:T(8,128)S(1)}, u32[]{:S(2)}, u32[]{:S(2)}) %collective-permute-start.36) | collective-permute-done | bytes 524320 | tf_op jit(solution)/shard_map/ppermute | solution.py:31
  130.4 3.1 %shard_map.106 = (f32[1024,512]{1,0:T(8,128)}, f32[1024,512]{1,0:T(8,128)}) custom-call(s32[6]{0:T(128)S(1)} %stack.19.spots_ref, f32[1024,512]{1,0:T(8,128)S(1)} %copy-done, f32[1024,512]{1,0:T(8,128)S(1)} %get-tuple-element.33.inner_ref, f32[512,256]{1,0:T(8,128)S(1)} %maximum_convert_fusion.own0, f32[512,256]{1,0:T(8,128)S(1)} %collective-permute-done.27.other0, ...), custom_call_target="tpu_custom_call" | custom-call | flops 1000 | bytes 1000 | tf_op jit(solution)/shard_map/pallas_call | solution.py:195
  (130 shorter events, 23.9 us)
Async XLA Ops:
  3.8 4.4 %copy-start.7 = (bf16[2,256,2048]{2,1,0:T(8,128)(2,1)S(1)}, bf16[2,256,2048]{2,1,0:T(8,128)(2,1)}, u32[]{:S(2)}) copy-start(bf16[2,256,2048]{2,1,0:T(8,128)(2,1)} %hidden_ref.3) | copy-start | bytes 6291460
  5.1 37.2 %copy-start.3 = (bf16[256,2048]{1,0:T(8,128)(2,1)}, bf16[256,2048]{1,0:T(8,128)(2,1)S(1)}, u32[]{:S(2)}) copy-start(bf16[256,2048]{1,0:T(8,128)(2,1)S(1)} %get-tuple-element.21.normed_ref) | copy-start | bytes 3145732
  5.1 20.8 %copy-start = (f32[1024,512]{1,0:T(8,128)S(1)}, f32[1024,512]{1,0:T(8,128)}, u32[]{:S(2)}) copy-start(f32[1024,512]{1,0:T(8,128)} %outer_ref.7) | copy-start | bytes 6291460
  5.1 20.8 %copy-start.21 = (bf16[1,1024,512]{2,1,0:T(8,128)(2,1)S(1)}, bf16[1,1024,512]{2,1,0:T(8,128)(2,1)}, u32[]{:S(2)}) copy-start(bf16[1,1024,512]{2,1,0:T(8,128)(2,1)} %drift_ref.1) | copy-start | bytes 3145732
  5.1 27.9 %collective-permute-start = (bf16[256,1024]{1,0:T(8,128)(2,1)S(1)}, bf16[256,1024]{1,0:T(8,128)(2,1)S(1)}, u32[]{:S(2)}, u32[]{:S(2)}) collective-permute-start(bf16[256,1024]{1,0:T(8,128)(2,1)S(1)} %get-tuple-element.23.refs_1_), channel_id=1, source_target_pairs={{0,1},{1,0},{2,3},{3,2},{4,5},{5,4},{6,7},{7,6},{8,9},{9,8},{10,11... | collective-permute-start | bytes 1572872 | tf_op jit(solution)/shard_map/ppermute | solution.py:31
  8.1 13.3 %collective-permute-start.8 = (bf16[64,512]{1,0:T(8,128)(2,1)S(1)}, bf16[64,512]{1,0:T(8,128)(2,1)S(1)}, u32[]{:S(2)}, u32[]{:S(2)}) collective-permute-start(bf16[64,512]{1,0:T(8,128)(2,1)S(1)} %shard_map.93), channel_id=1, source_target_pairs={{0,1},{1,0},{2,3},{3,2},{4,5},{5,4},{6,7},{7,6},{8,9},{9,8},{10,11... | collective-permute-start | bytes 196616 | tf_op jit(solution)/shard_map/ppermute | solution.py:31
  10.4 15.0 %collective-permute-start.4 = (bf16[64,512]{1,0:T(8,128)(2,1)S(1)}, bf16[64,512]{1,0:T(8,128)(2,1)S(1)}, u32[]{:S(2)}, u32[]{:S(2)}) collective-permute-start(bf16[64,512]{1,0:T(8,128)(2,1)S(1)} %shard_map.91.refs_0_), channel_id=1, source_target_pairs={{0,24},{2,26},{4,28},{6,30},{8,16},{10,18},{12,20},{14,22},{16,8},... | collective-permute-start | bytes 196616 | tf_op jit(solution)/shard_map/ppermute | solution.py:31
  14.5 10.9 %collective-permute-start.3 = (bf16[64,512]{1,0:T(8,128)(2,1)S(1)}, bf16[64,512]{1,0:T(8,128)(2,1)S(1)}, u32[]{:S(2)}, u32[]{:S(2)}) collective-permute-start(bf16[64,512]{1,0:T(8,128)(2,1)S(1)} %shard_map.91.refs_0_), channel_id=1, source_target_pairs={{0,16},{2,18},{4,20},{6,22},{8,24},{10,26},{12,28},{14,30},{16,0},... | collective-permute-start | bytes 196616 | tf_op jit(solution)/shard_map/ppermute | solution.py:31
  14.5 13.0 %collective-permute-start.2 = (bf16[64,512]{1,0:T(8,128)(2,1)S(1)}, bf16[64,512]{1,0:T(8,128)(2,1)S(1)}, u32[]{:S(2)}, u32[]{:S(2)}) collective-permute-start(bf16[64,512]{1,0:T(8,128)(2,1)S(1)} %shard_map.91.refs_0_), channel_id=1, source_target_pairs={{0,8},{2,10},{4,12},{6,14},{8,0},{10,2},{12,4},{14,6},{16,24},{18,... | collective-permute-start | bytes 196616 | tf_op jit(solution)/shard_map/ppermute | solution.py:31
  21.5 8.2 %collective-permute-start.11 = (bf16[64,512]{1,0:T(8,128)(2,1)S(1)}, bf16[64,512]{1,0:T(8,128)(2,1)S(1)}, u32[]{:S(2)}, u32[]{:S(2)}) collective-permute-start(bf16[64,512]{1,0:T(8,128)(2,1)S(1)} %collective-permute-done.8.refs_0_), channel_id=1, source_target_pairs={{0,24},{2,26},{4,28},{6,30},{8,16},{10,18},{12,20},{14,22},{16,8},... | collective-permute-start | bytes 196616 | tf_op jit(solution)/shard_map/ppermute | solution.py:31
  25.3 5.4 %collective-permute-start.10 = (bf16[64,512]{1,0:T(8,128)(2,1)S(1)}, bf16[64,512]{1,0:T(8,128)(2,1)S(1)}, u32[]{:S(2)}, u32[]{:S(2)}) collective-permute-start(bf16[64,512]{1,0:T(8,128)(2,1)S(1)} %collective-permute-done.8.refs_0_), channel_id=1, source_target_pairs={{0,16},{2,18},{4,20},{6,22},{8,24},{10,26},{12,28},{14,30},{16,0},... | collective-permute-start | bytes 196616 | tf_op jit(solution)/shard_map/ppermute | solution.py:31
  25.3 5.4 %collective-permute-start.9 = (bf16[64,512]{1,0:T(8,128)(2,1)S(1)}, bf16[64,512]{1,0:T(8,128)(2,1)S(1)}, u32[]{:S(2)}, u32[]{:S(2)}) collective-permute-start(bf16[64,512]{1,0:T(8,128)(2,1)S(1)} %collective-permute-done.8.refs_0_), channel_id=1, source_target_pairs={{0,8},{2,10},{4,12},{6,14},{8,0},{10,2},{12,4},{14,6},{16,24},{18,... | collective-permute-start | bytes 196616 | tf_op jit(solution)/shard_map/ppermute | solution.py:31
  27.9 8.4 %collective-permute-start.5 = (bf16[256,512]{1,0:T(8,128)(2,1)S(1)}, bf16[256,512]{1,0:T(8,128)(2,1)}, u32[]{:S(2)}, u32[]{:S(2)}) collective-permute-start(bf16[256,512]{1,0:T(8,128)(2,1)S(1)} %shard_map.92.refs_0_), channel_id=1, source_target_pairs={{0,4},{2,6},{4,0},{6,2},{8,12},{10,14},{12,8},{14,10},{16,20},{18,... | collective-permute-start | bytes 786440 | tf_op jit(solution)/shard_map/ppermute | solution.py:31
  31.4 8.9 %collective-permute-start.12 = (bf16[256,512]{1,0:T(8,128)(2,1)}, bf16[256,512]{1,0:T(8,128)(2,1)}, u32[]{:S(2)}, u32[]{:S(2)}) collective-permute-start(bf16[256,512]{1,0:T(8,128)(2,1)} %shard_map.94.refs_4_), channel_id=1, source_target_pairs={{0,4},{2,6},{4,0},{6,2},{8,12},{10,14},{12,8},{14,10},{16,20},{18,... | collective-permute-start | bytes 786440 | tf_op jit(solution)/shard_map/ppermute | solution.py:31
  33.0 7.7 %copy-start.17 = (bf16[256,1024]{1,0:T(8,128)(2,1)}, bf16[256,1024]{1,0:T(8,128)(2,1)S(1)}, u32[]{:S(2)}) copy-start(bf16[256,1024]{1,0:T(8,128)(2,1)S(1)} %collective-permute-done.normed_ref.features_ref) | copy-start | bytes 1572868
  34.0 8.3 %copy-start.28 = (s32[2,256]{1,0:T(2,128)S(1)}, s32[2,256]{1,0:T(2,128)}, u32[]{:S(2)}) copy-start(s32[2,256]{1,0:T(2,128)} %param.9) | copy-start | bytes 6148
  34.0 6.6 %collective-permute-start.1 = (f16[256,512]{1,0:T(8,128)(2,1)S(1)}, f16[256,512]{1,0:T(8,128)(2,1)S(1)}, u32[]{:S(2)}, u32[]{:S(2)}) collective-permute-start(f16[256,512]{1,0:T(8,128)(2,1)S(1)} %convert_element_type.48), channel_id=1, source_target_pairs={{0,1},{1,0},{2,3},{3,2},{4,5},{5,4},{6,7},{7,6},{8,9},{9,8},{10,11... | collective-permute-start | bytes 786440 | tf_op jit(solution)/shard_map/ppermute | solution.py:31
  35.6 10.1 %collective-permute-start.6 = (bf16[256,512]{1,0:T(8,128)(2,1)S(1)}, bf16[256,512]{1,0:T(8,128)(2,1)}, u32[]{:S(2)}, u32[]{:S(2)}) collective-permute-start(bf16[256,512]{1,0:T(8,128)(2,1)S(1)} %shard_map.92.refs_0_), channel_id=1, source_target_pairs={{0,2},{2,0},{4,6},{6,4},{8,10},{10,8},{12,14},{14,12},{16,18},{18,... | collective-permute-start | bytes 786440 | tf_op jit(solution)/shard_map/ppermute | solution.py:31
  35.6 10.1 %collective-permute-start.13 = (bf16[256,512]{1,0:T(8,128)(2,1)}, bf16[256,512]{1,0:T(8,128)(2,1)}, u32[]{:S(2)}, u32[]{:S(2)}) collective-permute-start(bf16[256,512]{1,0:T(8,128)(2,1)} %shard_map.94.refs_4_), channel_id=1, source_target_pairs={{0,2},{2,0},{4,6},{6,4},{8,10},{10,8},{12,14},{14,12},{16,18},{18,... | collective-permute-start | bytes 786440 | tf_op jit(solution)/shard_map/ppermute | solution.py:31
  36.3 9.4 %collective-permute-start.7 = (bf16[256,512]{1,0:T(8,128)(2,1)}, bf16[256,512]{1,0:T(8,128)(2,1)}, u32[]{:S(2)}, u32[]{:S(2)}) collective-permute-start(bf16[256,512]{1,0:T(8,128)(2,1)} %collective-permute-done.5.refs_1_), channel_id=1, source_target_pairs={{0,2},{2,0},{4,6},{6,4},{8,10},{10,8},{12,14},{14,12},{16,18},{18,... | collective-permute-start | bytes 786440 | tf_op jit(solution)/shard_map/ppermute | solution.py:31
  40.3 5.4 %collective-permute-start.14 = (bf16[256,512]{1,0:T(8,128)(2,1)}, bf16[256,512]{1,0:T(8,128)(2,1)}, u32[]{:S(2)}, u32[]{:S(2)}) collective-permute-start(bf16[256,512]{1,0:T(8,128)(2,1)} %collective-permute-done.12.refs_5_), channel_id=1, source_target_pairs={{0,2},{2,0},{4,6},{6,4},{8,10},{10,8},{12,14},{14,12},{16,18},{18,... | collective-permute-start | bytes 786440 | tf_op jit(solution)/shard_map/ppermute | solution.py:31
  40.7 22.0 %collective-permute-start.16 = (bf16[256,1024]{1,0:T(8,128)(2,1)}, bf16[256,1024]{1,0:T(8,128)(2,1)}, u32[]{:S(2)}, u32[]{:S(2)}) collective-permute-start(bf16[256,1024]{1,0:T(8,128)(2,1)} %shard_map.98), channel_id=1, source_target_pairs={{0,1},{1,0},{2,3},{3,2},{4,5},{5,4},{6,7},{7,6},{8,9},{9,8},{10,11... | collective-permute-start | bytes 1572872 | tf_op jit(solution)/shard_map/ppermute | solution.py:31
  46.9 8.2 %copy-start.5 = (bf16[256,2048]{1,0:T(8,128)(2,1)S(1)}, bf16[256,2048]{1,0:T(8,128)(2,1)}, u32[]{:S(2)}) copy-start(bf16[256,2048]{1,0:T(8,128)(2,1)} %copy-done.3) | copy-start | bytes 3145732
  46.9 8.2 %copy-start.14 = (f32[1024,512]{1,0:T(8,128)S(1)}, f32[1024,512]{1,0:T(8,128)}, u32[]{:S(2)}) copy-start(f32[1024,512]{1,0:T(8,128)} %copy-done.13) | copy-start | bytes 6291460
  50.7 5.5 %copy-start.15 = (bf16[2048,512]{1,0:T(8,128)(2,1)}, bf16[2048,512]{1,0:T(8,128)(2,1)S(1)}, u32[]{:S(2)}) copy-start(bf16[2048,512]{1,0:T(8,128)(2,1)S(1)} %get-tuple-element.30.whole_ref) | copy-start | bytes 6291460
  54.5 8.2 %collective-permute-start.15 = (bf16[256,512]{1,0:T(8,128)(2,1)S(1)}, bf16[256,512]{1,0:T(8,128)(2,1)S(1)}, u32[]{:S(2)}, u32[]{:S(2)}) collective-permute-start(bf16[256,512]{1,0:T(8,128)(2,1)S(1)} %shard_map.96.grads_ref), channel_id=1, source_target_pairs={{0,1},{1,0},{2,3},{3,2},{4,5},{5,4},{6,7},{7,6},{8,9},{9,8},{10,11... | collective-permute-start | bytes 786440 | tf_op jit(solution)/shard_map/ppermute | solution.py:31
  55.1 7.6 %copy-start.18 = (bf16[256,1024]{1,0:T(8,128)(2,1)S(1)}, bf16[256,1024]{1,0:T(8,128)(2,1)}, u32[]{:S(2)}) copy-start(bf16[256,1024]{1,0:T(8,128)(2,1)} %copy-done.17) | copy-start | bytes 1572868
  56.2 9.2 %copy-start.1 = (f32[1024,512]{1,0:T(8,128)}, f32[1024,512]{1,0:T(8,128)S(1)}, u32[]{:S(2)}) copy-start(f32[1024,512]{1,0:T(8,128)S(1)} %shard_map.97.inner_ref.refs_0_) | copy-start | bytes 6291460
  69.3 2.3 %collective-permute-start.18 = (f32[512,256]{1,0:T(8,128)}, f32[512,256]{1,0:T(8,128)}, u32[]{:S(2)}, u32[]{:S(2)}) collective-permute-start(f32[512,256]{1,0:T(8,128)} %get-tuple-element.32), channel_id=1, source_target_pairs={{0,2},{2,0},{4,6},{6,4},{8,10},{10,8},{12,14},{14,12},{16,18},{18,... | collective-permute-start | bytes 1572872 | tf_op jit(solution)/shard_map/ppermute | solution.py:31
  73.7 7.8 %collective-permute-start.19 = (f16[128,256]{1,0:T(8,128)(2,1)S(1)}, f16[128,256]{1,0:T(8,128)(2,1)S(1)}, u32[]{:S(2)}, u32[]{:S(2)}) collective-permute-start(f16[128,256]{1,0:T(8,128)(2,1)S(1)} %get-tuple-element.47), channel_id=1, source_target_pairs={{0,16},{2,18},{4,20},{6,22},{8,24},{10,26},{12,28},{14,30},{16,0},... | collective-permute-start | bytes 196616 | tf_op jit(solution)/shard_map/ppermute | solution.py:31
  76.1 6.4 %collective-permute-start.21 = (f16[128,256]{1,0:T(8,128)(2,1)S(1)}, f16[128,256]{1,0:T(8,128)(2,1)S(1)}, u32[]{:S(2)}, u32[]{:S(2)}) collective-permute-start(f16[128,256]{1,0:T(8,128)(2,1)S(1)} %get-tuple-element.48), channel_id=1, source_target_pairs={{0,24},{2,26},{4,28},{6,30},{8,16},{10,18},{12,20},{14,22},{16,8},... | collective-permute-start | bytes 196616 | tf_op jit(solution)/shard_map/ppermute | solution.py:31
  77.6 5.4 %collective-permute-start.20 = (f16[128,256]{1,0:T(8,128)(2,1)S(1)}, f16[128,256]{1,0:T(8,128)(2,1)S(1)}, u32[]{:S(2)}, u32[]{:S(2)}) collective-permute-start(f16[128,256]{1,0:T(8,128)(2,1)S(1)} %get-tuple-element.49), channel_id=1, source_target_pairs={{0,8},{2,10},{4,12},{6,14},{8,0},{10,2},{12,4},{14,6},{16,24},{18,... | collective-permute-start | bytes 196616 | tf_op jit(solution)/shard_map/ppermute | solution.py:31
  79.7 11.6 %collective-permute-start.17 = (f16[256,512]{1,0:T(8,128)(2,1)}, f16[256,512]{1,0:T(8,128)(2,1)}, u32[]{:S(2)}, u32[]{:S(2)}) collective-permute-start(f16[256,512]{1,0:T(8,128)(2,1)} %convert_element_type.50), channel_id=1, source_target_pairs={{0,1},{1,0},{2,3},{3,2},{4,5},{5,4},{6,7},{7,6},{8,9},{9,8},{10,11... | collective-permute-start | bytes 786440 | tf_op jit(solution)/shard_map/ppermute | solution.py:31
  84.0 10.7 %collective-permute-start.23 = (f32[128,256]{1,0:T(8,128)S(1)}, f32[128,256]{1,0:T(8,128)}, u32[]{:S(2)}, u32[]{:S(2)}) collective-permute-start(f32[128,256]{1,0:T(8,128)S(1)} %convert_add_fusion.1.refs_0_), channel_id=1, source_target_pairs={{0,4},{2,6},{4,0},{6,2},{8,12},{10,14},{12,8},{14,10},{16,20},{18,... | collective-permute-start | bytes 393224 | tf_op jit(solution)/shard_map/ppermute | solution.py:31
  93.1 7.7 %collective-permute-start.22 = (bf16[256,512]{1,0:T(8,128)(2,1)S(1)}, bf16[256,512]{1,0:T(8,128)(2,1)S(1)}, u32[]{:S(2)}, u32[]{:S(2)}) collective-permute-start(bf16[256,512]{1,0:T(8,128)(2,1)S(1)} %shard_map.102.grads_ref), channel_id=1, source_target_pairs={{0,1},{1,0},{2,3},{3,2},{4,5},{5,4},{6,7},{7,6},{8,9},{9,8},{10,11... | collective-permute-start | bytes 786440 | tf_op jit(solution)/shard_map/ppermute | solution.py:31
  102.5 2.0 %collective-permute-start.28 = (f32[512,256]{1,0:T(8,128)S(1)}, f32[512,256]{1,0:T(8,128)S(1)}, u32[]{:S(2)}, u32[]{:S(2)}) collective-permute-start(f32[512,256]{1,0:T(8,128)S(1)} %get-tuple-element.35), channel_id=1, source_target_pairs={{0,2},{2,0},{4,6},{6,4},{8,10},{10,8},{12,14},{14,12},{16,18},{18,... | collective-permute-start | bytes 1572872 | tf_op jit(solution)/shard_map/ppermute | solution.py:31
  104.6 7.1 %collective-permute-start.29 = (f16[128,256]{1,0:T(8,128)(2,1)S(1)}, f16[128,256]{1,0:T(8,128)(2,1)S(1)}, u32[]{:S(2)}, u32[]{:S(2)}) collective-permute-start(f16[128,256]{1,0:T(8,128)(2,1)S(1)} %get-tuple-element.44), channel_id=1, source_target_pairs={{0,16},{2,18},{4,20},{6,22},{8,24},{10,26},{12,28},{14,30},{16,0},... | collective-permute-start | bytes 196616 | tf_op jit(solution)/shard_map/ppermute | solution.py:31
  107.3 6.4 %collective-permute-start.31 = (f16[128,256]{1,0:T(8,128)(2,1)S(1)}, f16[128,256]{1,0:T(8,128)(2,1)S(1)}, u32[]{:S(2)}, u32[]{:S(2)}) collective-permute-start(f16[128,256]{1,0:T(8,128)(2,1)S(1)} %get-tuple-element.45), channel_id=1, source_target_pairs={{0,24},{2,26},{4,28},{6,30},{8,16},{10,18},{12,20},{14,22},{16,8},... | collective-permute-start | bytes 196616 | tf_op jit(solution)/shard_map/ppermute | solution.py:31
  107.8 6.1 %collective-permute-start.30 = (f16[128,256]{1,0:T(8,128)(2,1)S(1)}, f16[128,256]{1,0:T(8,128)(2,1)S(1)}, u32[]{:S(2)}, u32[]{:S(2)}) collective-permute-start(f16[128,256]{1,0:T(8,128)(2,1)S(1)} %get-tuple-element.46), channel_id=1, source_target_pairs={{0,8},{2,10},{4,12},{6,14},{8,0},{10,2},{12,4},{14,6},{16,24},{18,... | collective-permute-start | bytes 196616 | tf_op jit(solution)/shard_map/ppermute | solution.py:31
  114.0 5.0 %collective-permute-start.32 = (f32[128,256]{1,0:T(8,128)S(1)}, f32[128,256]{1,0:T(8,128)S(1)}, u32[]{:S(2)}, u32[]{:S(2)}) collective-permute-start(f32[128,256]{1,0:T(8,128)S(1)} %convert_add_fusion), channel_id=1, source_target_pairs={{0,4},{2,6},{4,0},{6,2},{8,12},{10,14},{12,8},{14,10},{16,20},{18,... | collective-permute-start | bytes 393224 | tf_op jit(solution)/shard_map/ppermute | solution.py:31
  114.5 7.2 %collective-permute-start.26 = (f16[128,256]{1,0:T(8,128)(2,1)S(1)}, f16[128,256]{1,0:T(8,128)(2,1)S(1)}, u32[]{:S(2)}, u32[]{:S(2)}) collective-permute-start(f16[128,256]{1,0:T(8,128)(2,1)S(1)} %get-tuple-element.40), channel_id=1, source_target_pairs={{0,24},{2,26},{4,28},{6,30},{8,16},{10,18},{12,20},{14,22},{16,8},... | collective-permute-start | bytes 196616 | tf_op jit(solution)/shard_map/ppermute | solution.py:31
  117.2 8.3 %collective-permute-start.25 = (f16[128,256]{1,0:T(8,128)(2,1)S(1)}, f16[128,256]{1,0:T(8,128)(2,1)S(1)}, u32[]{:S(2)}, u32[]{:S(2)}) collective-permute-start(f16[128,256]{1,0:T(8,128)(2,1)S(1)} %get-tuple-element.40), channel_id=1, source_target_pairs={{0,16},{2,18},{4,20},{6,22},{8,24},{10,26},{12,28},{14,30},{16,0},... | collective-permute-start | bytes 196616 | tf_op jit(solution)/shard_map/ppermute | solution.py:31
  117.2 8.3 %collective-permute-start.24 = (f16[128,256]{1,0:T(8,128)(2,1)S(1)}, f16[128,256]{1,0:T(8,128)(2,1)S(1)}, u32[]{:S(2)}, u32[]{:S(2)}) collective-permute-start(f16[128,256]{1,0:T(8,128)(2,1)S(1)} %get-tuple-element.40), channel_id=1, source_target_pairs={{0,8},{2,10},{4,12},{6,14},{8,0},{10,2},{12,4},{14,6},{16,24},{18,... | collective-permute-start | bytes 196616 | tf_op jit(solution)/shard_map/ppermute | solution.py:31
  119.0 6.8 %collective-permute-start.35 = (f16[128,256]{1,0:T(8,128)(2,1)S(1)}, f16[128,256]{1,0:T(8,128)(2,1)S(1)}, u32[]{:S(2)}, u32[]{:S(2)}) collective-permute-start(f16[128,256]{1,0:T(8,128)(2,1)S(1)} %add_convert_fusion), channel_id=1, source_target_pairs={{0,24},{2,26},{4,28},{6,30},{8,16},{10,18},{12,20},{14,22},{16,8},... | collective-permute-start | bytes 196616 | tf_op jit(solution)/shard_map/ppermute | solution.py:31
  121.7 6.6 %collective-permute-start.34 = (f16[128,256]{1,0:T(8,128)(2,1)S(1)}, f16[128,256]{1,0:T(8,128)(2,1)S(1)}, u32[]{:S(2)}, u32[]{:S(2)}) collective-permute-start(f16[128,256]{1,0:T(8,128)(2,1)S(1)} %add_convert_fusion), channel_id=1, source_target_pairs={{0,16},{2,18},{4,20},{6,22},{8,24},{10,26},{12,28},{14,30},{16,0},... | collective-permute-start | bytes 196616 | tf_op jit(solution)/shard_map/ppermute | solution.py:31
  121.8 6.6 %collective-permute-start.33 = (f16[128,256]{1,0:T(8,128)(2,1)S(1)}, f16[128,256]{1,0:T(8,128)(2,1)S(1)}, u32[]{:S(2)}, u32[]{:S(2)}) collective-permute-start(f16[128,256]{1,0:T(8,128)(2,1)S(1)} %add_convert_fusion), channel_id=1, source_target_pairs={{0,8},{2,10},{4,12},{6,14},{8,0},{10,2},{12,4},{14,6},{16,24},{18,... | collective-permute-start | bytes 196616 | tf_op jit(solution)/shard_map/ppermute | solution.py:31
  125.5 3.0 %collective-permute-start.27 = (f32[512,256]{1,0:T(8,128)S(1)}, f32[512,256]{1,0:T(8,128)S(1)}, u32[]{:S(2)}, u32[]{:S(2)}) collective-permute-start(f32[512,256]{1,0:T(8,128)S(1)} %maximum_convert_fusion.own0), channel_id=1, source_target_pairs={{0,2},{2,0},{4,6},{6,4},{8,10},{10,8},{12,14},{14,12},{16,18},{18,... | collective-permute-start | bytes 1572872 | tf_op jit(solution)/shard_map/ppermute | solution.py:31
  128.4 2.0 %collective-permute-start.36 = (f32[512,256]{1,0:T(8,128)S(1)}, f32[512,256]{1,0:T(8,128)S(1)}, u32[]{:S(2)}, u32[]{:S(2)}) collective-permute-start(f32[512,256]{1,0:T(8,128)S(1)} %maximum_convert_fusion.1.own1), channel_id=1, source_target_pairs={{0,2},{2,0},{4,6},{6,4},{8,10},{10,8},{12,14},{14,12},{16,18},{18,... | collective-permute-start | bytes 1572872 | tf_op jit(solution)/shard_map/ppermute | solution.py:31
  (19 other events, 32.0 us)

commit v4 on v3

--- a/solution.py
+++ b/solution.py
@@ -23,7 +23,7 @@
 f32 = jnp.float32
 bf16 = jnp.bfloat16
 f16 = jnp.float16
-logit_type = jnp.float16
+logit_type = jnp.float32
 
 
 def swap(value, axis, mask):
@@ -249,14 +249,61 @@
     )
 
 
-def normalized(hidden, step, spots):
+def positions():
+    replica = lax.axis_index("replica")
+    return lax.axis_index("fsdp"), replica, lax.rem(replica, CORES), replica // (2 * CORES)
+
+
+LEVEL = math.log(2.0) / 64.0
+
+
+def scale_of(code):
+    return jnp.exp(code.astype(f32) * LEVEL)
+
+
+def packed_rows(rows):
+    return rows + 8
+
+
+def pack(out_ref, first, second):
+    rows = first.shape[0]
+    codes, values = [], []
+    for x in (first, second):
+        top = jnp.maximum(jnp.max(jnp.abs(x), axis=0, keepdims=True), 1e-30)
+        code = jnp.ceil(jnp.log(top) * (1.0 / LEVEL)).astype(jnp.int32) + 1
+        codes.append(code)
+        values.append(jnp.round(x * (32767.0 / scale_of(code))).astype(jnp.int32))
+    out_ref[0:rows, :] = (values[0] << 16) | (values[1] & 0xFFFF)
+    row = lax.broadcasted_iota(jnp.int32, (8, first.shape[1]), 0)
+    out_ref[rows : rows + 8, :] = jnp.where(row == 0, codes[0], codes[1])
+
+
+def unpack(ref, start=0, rows=None):
+    rows = ref.shape[0] - 8 if rows is None else rows
+    both = ref[pl.ds(start, rows), :]
+    codes = ref[pl.ds(start + rows, 8), :]
+    unit = scale_of(codes) * (1.0 / 32767.0)
+    return (both >> 16).astype(f32) * unit[0:1, :], ((both << 16) >> 16).astype(f32) * unit[1:2, :]
+
+
+def column(ref, step):
+    row = ref[step : step + 1, :]
+    return jnp.broadcast_to(row, (128, row.shape[1])).T[:, 0:1]
+
+
+def normalized(hidden, step, pieces, room, passed=(), earlier=()):
     tokens, width = hidden.shape[1:]
     cols = width // 2
     parts = 4
     tile = tokens // parts
-
-    def kernel(spots_ref, hidden_ref, normed_ref, sent_ref, held_ref, sems):
-        other = pl.multiple_of((1 - spots_ref[0]) * cols, cols)
+    each = tokens // pieces
+
+    def kernel(hidden_ref, *refs):
+        passed_refs, refs = refs[: len(passed)], refs[len(passed) + len(earlier) :]
+        normed_ref, refs = refs[0], refs[1:]
+        sent_refs, refs = refs[:pieces], refs[pieces:]
+        copy_refs, (held_ref, sems) = refs[: len(passed)], refs[len(passed) :]
+        other = pl.multiple_of((1 - lax.axis_index("fsdp")) * cols, cols)
         copies = [
             pltpu.make_async_copy(
                 hidden_ref.at[step, pl.ds(k * tile, tile)], held_ref.at[pl.ds(k * tile, tile)], sems.at[k]
@@ -265,59 +312,52 @@
         ]
         for copy in copies:
             copy.start()
+        for source, target in zip(passed_refs, copy_refs):
+            target[...] = source[...]
         for k, copy in enumerate(copies):
             copy.wait()
             at = pl.ds(k * tile, tile)
             normed_ref[at, :] = normalize(held_ref[at, :])
-            sent_ref[at, :] = normed_ref[at, pl.ds(other, cols)]
-
-    return call(
-        kernel,
-        (spots, hidden),
-        [SMEM, HBM],
-        (like((tokens, width), bf16), like((tokens, cols), bf16)),
-        (VMEM, VMEM),
-        8,
+            sent_refs[k * tile // each][pl.ds(k * tile % each, tile), :] = normed_ref[at, pl.ds(other, cols)]
+
+    return call(
+        kernel,
+        (hidden,) + passed + earlier,
+        [HBM] + [VMEM] * len(passed) + [ANY] * len(earlier),
+        [like((tokens, width), bf16)]
+        + [like((each, cols), bf16)] * pieces
+        + [like(p.shape, p.dtype) for p in passed],
+        [VMEM] * (1 + pieces + len(passed)),
+        room,
         [pltpu.VMEM((tokens, width), bf16), pltpu.SemaphoreType.DMA((parts,))],
     )
 
 
-def reference_logs(normed, stacks, spots):
+def reference_logs(normed, stacks, *earlier):
     tokens, width = normed.shape
     entries = stacks[0].shape[1]
     rows = stacks[0].shape[0] // MAJOR
     count = len(stacks)
 
-    def kernel(spots_ref, normed_ref, *refs):
-        out_ref, whole_ref, sems = refs[count:]
-        fsdp, me = spots_ref[0], spots_ref[4]
-        copies = []
+    def kernel(normed_ref, *refs):
+        out_ref, whole_ref = refs[count + len(earlier) :]
+        fsdp, me, _, _ = positions()
         for number in range(count):
             bit_fsdp, bit_core, bit_y = number // 4, number // 2 % 2, number % 2
             for p in range(MAJOR):
                 mask = bit_core + bit_y * CORES + p * 2 * CORES
                 block = jnp.bitwise_xor(me, mask) * 2 + jnp.bitwise_xor(fsdp, bit_fsdp)
-                copies.append(
-                    pltpu.make_async_copy(
-                        refs[number].at[pl.ds(p * rows, rows)],
-                        whole_ref.at[pl.ds(pl.multiple_of(block * rows, rows), rows)],
-                        sems.at[len(copies)],
-                    )
-                )
-        for copy in copies:
-            copy.start()
-        for copy in copies:
-            copy.wait()
+                to = pl.ds(pl.multiple_of(block * rows, rows), rows)
+                whole_ref[to, :] = refs[number][p * rows : (p + 1) * rows, :]
         out_ref[...] = log_softmax(capped(dot(normed_ref[...], whole_ref[...])))
 
     return call(
         kernel,
-        (spots, normed) + tuple(stacks),
-        [SMEM, VMEM] + [ANY] * count,
+        (normed,) + tuple(stacks) + earlier,
+        [VMEM] * (1 + count) + [ANY] * len(earlier),
         (like((tokens, entries), f32), like((width, entries), bf16)),
         (VMEM, VMEM),
-        8,
-        [pltpu.SemaphoreType.DMA((count * MAJOR,))],
+        10,
     )
 
 
@@ -335,58 +375,78 @@
     )
 
 
-def starting_weights(outer_head, drift):
+def starting_weights(outer_head, drift, *earlier):
     rows, entries = outer_head.shape
 
-    def kernel(outer_ref, drift_ref, inner_ref, weights_ref):
+    def kernel(outer_ref, drift_ref, *refs):
+        inner_ref, weights_ref = refs[-2:]
         inner = outer_ref[...] + drift_ref[0].astype(f32)
         inner_ref[...] = inner
         weights_ref[...] = inner.astype(bf16)
 
     return call(
         kernel,
-        (outer_head, drift),
-        [VMEM, VMEM],
+        (outer_head, drift) + earlier,
+        [VMEM, VMEM] + [ANY] * len(earlier),
         (like((rows, entries), f32), like((rows, entries), bf16)),
         (VMEM, VMEM),
         10,
     )
 
 
-def partial_logits(normed, weights, spots, own, *earlier):
+def pack_logits(out_ref, logits):
+    half = logits.shape[1] // 2
+    pack(out_ref, logits[:, :half], logits[:, half:])
+
+
+def partner_logits(features, weights):
+    tokens = features.shape[0]
+    entries = weights.shape[1]
+
+    def kernel(features_ref, weights_ref, out_ref):
+        pack_logits(out_ref, dot(features_ref[...], weights_ref[...]))
+
+    return call(
+        kernel,
+        (features, weights),
+        [VMEM, VMEM],
+        like((packed_rows(tokens), entries // 2), jnp.int32),
+        VMEM,
+        8,
+    )
+
+
+def own_logits(normed, weights, *earlier):
     tokens = normed.shape[0]
     rows, entries = weights.shape
 
-    def kernel(spots_ref, normed_ref, weights_ref, *refs):
-        if own:
-            values = normed_ref[:, pl.ds(pl.multiple_of(spots_ref[0] * rows, rows), rows)]
-        else:
-            values = normed_ref[...]
-        refs[-1][...] = dot(values, weights_ref[...])
-
-    return call(
-        kernel,
-        (spots, normed, weights) + earlier,
-        [SMEM, VMEM, VMEM] + [ANY] * len(earlier),
+    def kernel(normed_ref, weights_ref, *refs):
+        at = pl.ds(pl.multiple_of(lax.axis_index("fsdp") * rows, rows), rows)
+        refs[-1][...] = dot(normed_ref[:, at], weights_ref[...])
+
+    return call(
+        kernel,
+        (normed, weights) + earlier,
+        [VMEM, VMEM] + [ANY] * len(earlier),
         like((tokens, entries), f32),
         VMEM,
         8,
     )
 
 
-def gradients(own, received, refer_log, target_ids, valid_rows, *earlier):
+def gradients(own, received, refer_log, targets, valid, step, *earlier):
     tokens, entries = own.shape
 
-    def kernel(own_ref, received_ref, refer_ref, target_ref, valid_ref, *refs):
-        raw = own_ref[...] + received_ref[...].astype(f32)
+    def kernel(own_ref, received_ref, refer_ref, targets_ref, valid_ref, *refs):
+        raw = own_ref[...] + jnp.concatenate(unpack(received_ref), axis=1)
         policy = capped(raw)
         policy_log = log_softmax(policy)
         policy_prob = jnp.exp(policy_log)
         diverge = policy_log - refer_ref[...]
         kl_value = jnp.sum(policy_prob * diverge, axis=-1, keepdims=True)
         here = lax.broadcasted_iota(jnp.int32, policy.shape, 1)
-        onehot = jnp.where(target_ref[...] == here, 1.0, 0.0)
-        upstream = valid_ref[...].astype(f32) * (
+        onehot = jnp.where(column(targets_ref, step) == here, 1.0, 0.0)
+        upstream = column(valid_ref, step).astype(f32) * (
             policy_prob - onehot + kl_weight * policy_prob * (diverge - kl_value)
         )
         ratio = policy / soft_cap
@@ -394,7 +454,7 @@
 
     return call(
         kernel,
-        (own, received, refer_log, target_ids[:, None], valid_rows[:, None]) + earlier,
+        (own, received, refer_log, targets, valid) + earlier,
         [VMEM] * 5 + [ANY] * len(earlier),
         like((tokens, entries), bf16),
         VMEM,
@@ -402,176 +462,248 @@
     )
 
 
-def own_update(inner, normed, grads, spots, *earlier):
+def own_update(inner, normed, grads, *earlier):
     rows, entries = inner.shape
     tile = rows // 4
 
-    def kernel(spots_ref, inner_ref, normed_ref, grads_ref, *refs):
+    def kernel(inner_ref, normed_ref, grads_ref, *refs):
         for k in range(4):
             at = pl.ds(k * tile, tile)
-            columns = pl.ds(pl.multiple_of(spots_ref[0] * rows + k * tile, tile), tile)
+            columns = pl.ds(pl.multiple_of(lax.axis_index("fsdp") * rows + k * tile, tile), tile)
             refs[-1][at, :] = inner_ref[at, :] - inner_rate * dot_rows(normed_ref[:, columns], grads_ref[...])
 
     return call(
         kernel,
-        (spots, inner, normed, grads) + earlier,
-        [SMEM, VMEM, VMEM, VMEM] + [ANY] * len(earlier),
+        (inner, normed, grads) + earlier,
+        [VMEM] * 3 + [ANY] * len(earlier),
         like((rows, entries), f32),
         VMEM,
         10,
     )
 
 
-def update(inner, features, grads, outer_head, spots, step, replicas, following=None):
+def update(inner, features, grads, outer_head, plan, step, replicas, following=(), earlier=()):
     rows, entries = inner.shape
     tokens = features.shape[0]
     part = entries // FRAGS
     half = rows // 2
     tile = rows // 4
-    more = following is not None
-
-    def kernel(spots_ref, inner_ref, features_ref, grads_ref, outer_ref, *refs):
-        if more:
-            following_ref, new_ref, sent_ref, kept_ref, weights_ref, partial_ref = refs
-        else:
-            new_ref, sent_ref, kept_ref = refs
+    pieces = len(following)
+
+    def kernel(plan_ref, inner_ref, features_ref, grads_ref, outer_ref, *refs):
+        following_refs, refs = refs[:pieces], refs[pieces + len(earlier) :]
+        new_ref, sent_ref, kept_ref = refs[:3]
         for k in range(4):
             at = pl.ds(k * tile, tile)
             new = inner_ref[at, :] - inner_rate * dot_rows(features_ref[:, at], grads_ref[...])
             new_ref[at, :] = new
-            if more:
-                weights_ref[at, :] = new.astype(bf16)
-        if more:
-            partial_ref[...] = dot(following_ref[...], weights_ref[...])
-        columns = pl.ds(pl.multiple_of(spots_ref[2 + step] * part, part), part)
-        core = spots_ref[1]
+            if pieces:
+                refs[4][at, :] = new.astype(bf16)
+        if pieces:
+            next_ref, weights_ref, partial_ref = refs[3:]
+            each = tokens // pieces
+            for k, piece_ref in enumerate(following_refs):
+                next_ref[k * each : (k + 1) * each, :] = piece_ref[...]
+            pack_logits(partial_ref, dot(next_ref[...], weights_ref[...]))
+        columns = pl.ds(pl.multiple_of(plan_ref[step] * part, part), part)
+        core = positions()[2]
         for place_ref, which in ((sent_ref, 1 - core), (kept_ref, core)):
             at = pl.ds(pl.multiple_of(which * half, half), half)
             place_ref[...] = (outer_ref[at, columns] - new_ref[at, columns]) * (1.0 / replicas)
 
-    operands = (spots, inner, features, grads, outer_head)
+    operands = (plan, inner, features, grads, outer_head) + tuple(following)
     out_shape = [like((rows, entries), f32), like((half, part), f32), like((half, part), f32)]
-    if more:
-        operands += (following,)
-        out_shape += [like((rows, entries), bf16), like((tokens, entries), f32)]
-    return call(
-        kernel,
-        operands,
-        [SMEM] + [VMEM] * (len(operands) - 1),
+    if pieces:
+        out_shape += [
+            like((tokens, rows), bf16),
+            like((rows, entries), bf16),
+            like((packed_rows(tokens), entries // 2), jnp.int32),
+        ]
+    return call(
+        kernel,
+        operands + tuple(earlier),
+        [SMEM] + [VMEM] * (len(operands) - 1) + [ANY] * len(earlier),
         out_shape,
         [VMEM] * len(out_shape),
-        14,
-    )
-
-
-def settled(outer_head, inner, means, spots):
+        16,
+    )
+
+
+def pack_quarter(out_ref, quarter):
+    half = quarter.shape[0] // 2
+    pack(out_ref, quarter[:half], quarter[half:])
+
+
+def unpack_quarter(ref, start=0, rows=None):
+    return jnp.concatenate(unpack(ref, start, rows), axis=0)
+
+
+def quarters(kept, received):
+    rows, cols = kept.shape
+    quarter = rows // MAJOR
+
+    def kernel(kept_ref, received_ref, own_ref, *refs):
+        major = positions()[3]
+
+        def piece(mask):
+            at = pl.ds(pl.multiple_of(jnp.bitwise_xor(major, mask) * quarter, quarter), quarter)
+            return kept_ref[at, :] + received_ref[at, :]
+
+        for mask, out_ref in zip(MASKS, refs):
+            pack_quarter(out_ref, piece(mask))
+        own_ref[...] = piece(0)
+
+    small = like((packed_rows(quarter // 2), cols), jnp.int32)
+    return call(
+        kernel,
+        (kept, received),
+        [VMEM] * 2,
+        [like((quarter, cols), f32)] + [small] * len(MASKS),
+        [VMEM] * (1 + len(MASKS)),
+        6,
+    )
+
+
+def quarter_sum(own, pieces, *earlier):
+    def kernel(own_ref, *refs):
+        total = own_ref[...]
+        for ref in refs[: len(pieces)]:
+            total = total + unpack_quarter(ref)
+        pack_quarter(refs[-1], total)
+
+    return call(
+        kernel,
+        (own,) + tuple(pieces) + earlier,
+        [VMEM] * (1 + len(pieces)) + [ANY] * len(earlier),
+        like(pieces[0].shape, jnp.int32),
+        VMEM,
+        4,
+    )
+
+
+def pair_sum(one, other):
+    def kernel(one_ref, other_ref, out_ref):
+        pack_quarter(out_ref, unpack_quarter(one_ref) + unpack_quarter(other_ref))
+
+    return call(kernel, (one, other), [VMEM] * 2, like(one.shape, jnp.int32), VMEM, 4)
+
+
+def settled(outer_head, inner, means, plan):
     rows, entries = inner.shape
     part = entries // FRAGS
     tile = rows // (CORES * MAJOR)
-    steps = 4
-    each = CORES * MAJOR // steps
-
-    def kernel(spots_ref, outer_ref, inner_ref, own0, other0, own1, other1, new_outer_ref, new_inner_ref):
-        for k in range(each):
-            i = pl.program_id(0) * each + k
-            mine = i // MAJOR == spots_ref[1]
-            there = jnp.bitwise_xor(lax.rem(i, MAJOR), spots_ref[5])
-            source = pl.ds(pl.multiple_of(there * tile, tile), tile)
-            at = pl.ds(pl.multiple_of(i * tile, tile), tile)
-            to = pl.ds(k * tile, tile)
-            mean0 = jnp.where(mine, own0[source, :], other0[source, :])
-            mean1 = jnp.where(mine, own1[source, :], other1[source, :])
+    steps = CORES * MAJOR
+    small = packed_rows(tile // 2)
+
+    def kernel(plan_ref, outer_ref, inner_ref, own0, other0, own1, other1, new_outer_ref, new_inner_ref, *scratch):
+        mean_ref, outer_held, inner_held, sems = scratch
+        _, _, core, major = positions()
+        copies = []
+        for i in range(steps):
+            start = pl.multiple_of(jnp.bitwise_xor(i % MAJOR, major) * small, small)
+            at = pl.ds(i * tile, tile)
+
+            @pl.when(i // MAJOR == core)
+            def _():
+                mean_ref[0] = unpack_quarter(own0, start, tile // 2)
+                mean_ref[1] = unpack_quarter(own1, start, tile // 2)
+
+            @pl.when(i // MAJOR != core)
+            def _():
+                mean_ref[0] = unpack_quarter(other0, start, tile // 2)
+                mean_ref[1] = unpack_quarter(other1, start, tile // 2)
+
             for f in range(FRAGS):
                 columns = pl.ds(f * part, part)
-                mean = jnp.where(spots_ref[2] == f, mean0, mean1)
+                mean = mean_ref[jnp.where(plan_ref[0] == f, 0, 1)]
                 fresh = outer_ref[at, columns] - outer_rate * mean
-                new_outer_ref[to, columns] = fresh
-                new_inner_ref[to, columns] = mix_weight * inner_ref[at, columns] + (1.0 - mix_weight) * fresh
-
-    block = pl.BlockSpec((each * tile, entries), lambda i: (i, 0))
-    return call(
-        kernel,
-        (spots, outer_head, inner) + tuple(means[0]) + tuple(means[1]),
+                outer_held[at, columns] = fresh
+                inner_held[at, columns] = mix_weight * inner_ref[at, columns] + (1.0 - mix_weight) * fresh
+            for k, (held, out) in enumerate(((outer_held, new_outer_ref), (inner_held, new_inner_ref))):
+                copies.append(pltpu.make_async_copy(held.at[at], out.at[at], sems.at[2 * i + k]))
+                copies[-1].start()
+        for copy in copies:
+            copy.wait()
+
+    return call(
+        kernel,
+        (plan, outer_head, inner) + tuple(means[0]) + tuple(means[1]),
         [SMEM] + [VMEM] * 6,
         [like((rows, entries), f32)] * 2,
-        [block, block],
+        [HBM, HBM],
         14,
-        grid=(steps,),
-    )
-
-
-def gathered_stacks(ref_head, sent, normed):
+        [
+            pltpu.VMEM((2, tile, part), f32),
+            pltpu.VMEM((rows, entries), f32),
+            pltpu.VMEM((rows, entries), f32),
+            pltpu.SemaphoreType.DMA((2 * steps,)),
+        ],
+    )
+
+
+def gathered_stacks(ref_own, ref_partner):
     step = 2 * CORES
     stacks = []
-    for rows in (after(ref_head, normed), swap(after(ref_head, sent), "fsdp", 1)):
+    for rows in (ref_own, ref_partner):
         along = stacked([rows] + [swap(rows, "replica", m * step) for m in range(1, MAJOR)])
         both = [along, swap(along, "replica", CORES)]
         stacks += both + [swap(s, "replica", 1) for s in both]
     return stacks
 
 
-def quarters_sum(part, major):
-    step = 2 * CORES
-    quarter = part.shape[0] // MAJOR
-    sent = part.astype(f16)
-    own = rows_at(part, major, quarter)
-    for m in MASKS:
-        own = own + swap(rows_at(sent, major ^ m, quarter), "replica", m * step).astype(f32)
-    return own
-
-
-def quarters_gathered(own):
+def gathered_quarters(own):
     step = 2 * CORES
     got = {m: swap(own, "replica", m * step) for m in MASKS}
-    return jnp.concatenate([own, got[1], got[2], got[3]], 0).astype(f32)
+    stack = stacked([own, got[1], got[2], got[3]])
+    return stack, swap(stack, "replica", 1)
+
+
+def chip_quarters(sent, kept):
+    own, *pieces = quarters(kept, swap(sent, "replica", 1))
+    return own, [swap(p, "replica", m * 2 * CORES) for p, m in zip(pieces, MASKS)]
 
 
 def shards_pair(hidden, targets, valid, plan, outer_head, drift, ref_head):
     replicas = lax.axis_size("replica")
-    fsdp = lax.axis_index("fsdp")
-    replica = lax.axis_index("replica")
-    core = replica % CORES
-    major = replica // (2 * CORES)
-    spots = jnp.stack([fsdp, core, plan[0], plan[1], replica, major]).astype(jnp.int32)
-
-    normed0, sent0 = normalized(hidden, 0, spots)
-    features0 = swap(sent0, "fsdp", 1)
-    normed1, sent1 = normalized(hidden, 1, spots)
-    stacks = gathered_stacks(ref_head, sent0, normed1)
+
+    ref_partner = swap(ref_head, "fsdp", 1)
+    normed0, sent0 = normalized(hidden, 0, 1, 60)
+    features0 = swap(after(sent0, ref_partner), "fsdp", 1)
+    normed1, sent1a, sent1b, *pieces = normalized(hidden, 1, 2, 8, (ref_head, ref_partner), (sent0,))
+    features1a = swap(sent1a, "fsdp", 1)
+    stacks = gathered_stacks(*pieces)
 
     inner, weights = starting_weights(outer_head, drift)
-    partial = partial_logits(features0, weights, spots, False)
-    received = swap(partial.astype(logit_type), "fsdp", 1).astype(f32)
-    own = partial_logits(normed0, weights, spots, True)
-    features1 = swap(after(sent1, received), "fsdp", 1)
-    refer_log, whole = reference_logs(normed0, stacks, spots)
-    grads = gradients(own, received, refer_log, targets[0], valid[0])
+    partial = partner_logits(features0, weights)
+    received = swap(partial, "fsdp", 1)
+    own = own_logits(normed0, weights, partial)
+    features1b = swap(after(sent1b, own), "fsdp", 1)
+    refer_log, whole = reference_logs(normed0, stacks, features1a)
+    grads = gradients(own, received, refer_log, targets, valid, 0)
     partner_grads = swap(grads, "fsdp", 1)
-    halfway = own_update(inner, normed0, grads, spots)
+    halfway = own_update(inner, normed0, grads, features1b)
     refer_log = more_reference_logs(normed1, whole, halfway)
-    inner, sent, kept, weights, partial = update(
-        halfway, features0, partner_grads, outer_head, spots, 0, replicas, features1
-    )
-
-    received = swap(partial.astype(logit_type), "fsdp", 1).astype(f32)
-    own = partial_logits(normed1, weights, spots, True)
-    summed = kept + swap(sent, "replica", 1)
-    grads = gradients(own, received, refer_log, targets[1], valid[1], summed)
-    quarter = quarters_sum(summed, major)
+    inner, sent, kept, features1, weights, partial = update(
+        halfway, features0, partner_grads, outer_head, plan, 0, replicas, (features1a, features1b), (refer_log,)
+    )
+
+    received = swap(partial, "fsdp", 1)
+    own = own_logits(normed1, weights)
+    quarter, pieces = chip_quarters(sent, kept)
+    grads = gradients(own, received, refer_log, targets, valid, 1, *pieces)
     partner_grads = swap(grads, "fsdp", 1)
-    halfway = own_update(inner, normed1, grads, spots, quarter)
-    first = quarter + swap(quarter, "replica", CORES)
+    halfway = own_update(inner, normed1, grads)
+    quarter = quarter_sum(quarter, pieces, halfway)
+    first = pair_sum(quarter, swap(quarter, "replica", CORES))
     inner, sent, kept = update(
-        halfway, features1, after(partner_grads, first), outer_head, spots, 1, replicas
-    )
-
-    summed = kept + swap(sent, "replica", 1)
-    quarter = quarters_sum(summed, major)
-    second = quarter + swap(quarter, "replica", CORES)
-    first = quarters_gathered(first.astype(f16))
-    second = quarters_gathered(second.astype(f16))
-    means = [(m, swap(m, "replica", 1)) for m in (first, second)]
-    new_outer, new_inner = settled(outer_head, inner, means, spots)
+        halfway, features1, partner_grads, outer_head, plan, 1, replicas, (), (first,)
+    )
+
+    quarter, pieces = chip_quarters(sent, kept)
+    quarter = quarter_sum(quarter, pieces)
+    second = pair_sum(quarter, swap(quarter, "replica", CORES))
+    means = [gathered_quarters(m) for m in (first, second)]
+    new_outer, new_inner = settled(outer_head, inner, means, plan)
     return (new_outer, new_inner[None])
 
 

time: 134 us -> 105 us (0.78)
  local copies, waits for them, and re-layouts: 19.3 us -> 0.87 us
  other arithmetic: 7.23 us -> 0 us
  starting transfers between devices: 40.2 us -> 46.8 us
  Pallas kernels: 23 us -> 17.2 us
  waiting for transfers between devices: 42.8 us -> 38.8 us
    unnamed x62 -> x16, local copies, waits for them, and re-layouts: 16.6 us -> 0.87 us
    ppermute x37 -> x38, starting transfers between devices: 40.2 us -> 46.8 us  [swap(): return lax.ppermute(value, axis, [(i, i ^ mask) for i in range(size)])]
    convert_element_type x10 -> x0, other arithmetic: 6.26 us -> none  [the longest x4 3.04 us: shards_pair(): received = swap(partial.astype(logit_type), 'fsdp', 1).astype(f32)]
    pallas_call x21 -> x27, Pallas kernels: 23 us -> 17.2 us  [call(): pl.pallas_call(kernel, out_shape=out_shape, in_specs=in_specs, out_specs=...]
    ppermute x37 -> x38, waiting for transfers between devices: 42.8 us -> 38.8 us  [swap(): return lax.ppermute(value, axis, [(i, i ^ mask) for i in range(size)])]
    another operation x7 -> x0, local copies, waits for them, and re-layouts: 2.61 us -> none  [the longest x3 0.94 us: gradients(): valid_rows[:, None]]
  transfers between devices with their start and end apart: 37 -> 38, of which waited for: 20 -> 21; matrix products, arithmetic and copies ran while one was open for 5% -> 0% of each run, Pallas kernels for 11% -> 9%
where the time goes in v4:
time: 105 us
  starting transfers between devices  46.8 us (45%)
  waiting for transfers between devices  38.8 us (37%)
  Pallas kernels  17.2 us (16%)
    ppermute x38, starting transfers between devices, swap(): return lax.ppermute(value, axis, [(i, i ^ mask) for i in range(size)])  46.8 us
    ppermute x38, waiting for transfers between devices, swap(): return lax.ppermute(value, axis, [(i, i ^ mask) for i in range(size)])  38.8 us
    pallas_call x27, Pallas kernels, call(): pl.pallas_call(kernel, out_shape=out_shape, in_specs=in_specs, out_specs=...  17.2 us
  transfers between devices with their start and end apart: 38, of which 21 were waited for; matrix products, arithmetic and copies ran while one was open for 0% of the time, Pallas kernels for 9%

profile of v4, /device:TPU:0, one launch (start us, length us, event | category | flops | bytes accessed | tf_op | source)
XLA Modules:
  0.0 104.7 jit_solution(18055071686221358499)
XLA Ops:
  0.6 3.0 %collective-permute-start = (bf16[64,512]{1,0:T(8,128)(2,1)}, bf16[64,512]{1,0:T(8,128)(2,1)S(1)}, u32[]{:S(2)}, u32[]{:S(2)}) collective-permute-start(bf16[64,512]{1,0:T(8,128)(2,1)} %refs_0_.1), channel_id=1, source_target_pairs={{0,1},{1,0},{2,3},{3,2},{4,5},{5,4},{6,7},{7,6},{8,9},{9,8},{10,11... | collective-permute-start | bytes 196616 | tf_op jit(solution)/shard_map/ppermute | solution.py:31
  3.6 2.7 %shard_map.87 = (bf16[256,2048]{1,0:T(8,128)(2,1)}, bf16[256,1024]{1,0:T(8,128)(2,1)}) custom-call(bf16[2,256,2048]{2,1,0:T(8,128)(2,1)} %hidden_ref.3), custom_call_target="tpu_custom_call" | custom-call | flops 1000 | bytes 1000 | tf_op jit(solution)/shard_map/pallas_call | solution.py:195
  6.4 0.8 copy-done.4
  8.0 1.8 %collective-permute-start.1 = (bf16[256,1024]{1,0:T(8,128)(2,1)}, bf16[256,1024]{1,0:T(8,128)(2,1)S(1)}, u32[]{:S(2)}, u32[]{:S(2)}) collective-permute-start(bf16[256,1024]{1,0:T(8,128)(2,1)} %shard_map.88), channel_id=1, source_target_pairs={{0,1},{1,0},{2,3},{3,2},{4,5},{5,4},{6,7},{7,6},{8,9},{9,8},{10,11... | collective-permute-start | bytes 1572872 | tf_op jit(solution)/shard_map/ppermute | solution.py:31
  9.8 3.6 %collective-permute-start.11 = (bf16[64,512]{1,0:T(8,128)(2,1)S(1)}, bf16[64,512]{1,0:T(8,128)(2,1)S(1)}, u32[]{:S(2)}, u32[]{:S(2)}) collective-permute-start(bf16[64,512]{1,0:T(8,128)(2,1)S(1)} %get-tuple-element.37.refs_0_), channel_id=1, source_target_pairs={{0,24},{2,26},{4,28},{6,30},{8,16},{10,18},{12,20},{14,22},{16,8},... | collective-permute-start | bytes 196616 | tf_op jit(solution)/shard_map/ppermute | solution.py:31
  14.2 3.6 %collective-permute-start.5 = (bf16[64,512]{1,0:T(8,128)(2,1)S(1)}, bf16[64,512]{1,0:T(8,128)(2,1)S(1)}, u32[]{:S(2)}, u32[]{:S(2)}) collective-permute-start(bf16[64,512]{1,0:T(8,128)(2,1)S(1)} %get-tuple-element.36.refs_0_), channel_id=1, source_target_pairs={{0,24},{2,26},{4,28},{6,30},{8,16},{10,18},{12,20},{14,22},{16,8},... | collective-permute-start | bytes 196616 | tf_op jit(solution)/shard_map/ppermute | solution.py:31
  17.8 2.2 %collective-permute-start.4 = (bf16[64,512]{1,0:T(8,128)(2,1)S(1)}, bf16[64,512]{1,0:T(8,128)(2,1)S(1)}, u32[]{:S(2)}, u32[]{:S(2)}) collective-permute-start(bf16[64,512]{1,0:T(8,128)(2,1)S(1)} %get-tuple-element.36.refs_0_), channel_id=1, source_target_pairs={{0,16},{2,18},{4,20},{6,22},{8,24},{10,26},{12,28},{14,30},{16,0},... | collective-permute-start | bytes 196616 | tf_op jit(solution)/shard_map/ppermute | solution.py:31
  20.8 1.4 %collective-permute-start.15 = (bf16[128,1024]{1,0:T(8,128)(2,1)S(1)}, bf16[128,1024]{1,0:T(8,128)(2,1)S(1)}, u32[]{:S(2)}, u32[]{:S(2)}) collective-permute-start(bf16[128,1024]{1,0:T(8,128)(2,1)S(1)} %get-tuple-element.38), channel_id=1, source_target_pairs={{0,1},{1,0},{2,3},{3,2},{4,5},{5,4},{6,7},{7,6},{8,9},{9,8},{10,11... | collective-permute-start | bytes 786440 | tf_op jit(solution)/shard_map/ppermute | solution.py:31
  22.5 1.6 %collective-permute-start.12 = (bf16[256,512]{1,0:T(8,128)(2,1)S(1)}, bf16[256,512]{1,0:T(8,128)(2,1)S(1)}, u32[]{:S(2)}, u32[]{:S(2)}) collective-permute-start(bf16[256,512]{1,0:T(8,128)(2,1)S(1)} %shard_map.93.refs_4_), channel_id=1, source_target_pairs={{0,4},{2,6},{4,0},{6,2},{8,12},{10,14},{12,8},{14,10},{16,20},{18,... | collective-permute-start | bytes 786440 | tf_op jit(solution)/shard_map/ppermute | solution.py:31
  24.1 0.9 collective-permute-done.3.refs_1_
  25.4 1.6 %collective-permute-start.6 = (bf16[256,512]{1,0:T(8,128)(2,1)S(1)}, bf16[256,512]{1,0:T(8,128)(2,1)S(1)}, u32[]{:S(2)}, u32[]{:S(2)}) collective-permute-start(bf16[256,512]{1,0:T(8,128)(2,1)S(1)} %shard_map.92.refs_0_), channel_id=1, source_target_pairs={{0,4},{2,6},{4,0},{6,2},{8,12},{10,14},{12,8},{14,10},{16,20},{18,... | collective-permute-start | bytes 786440 | tf_op jit(solution)/shard_map/ppermute | solution.py:31
  27.8 1.4 %collective-permute-start.2 = (s32[264,256]{1,0:T(8,128)S(1)}, s32[264,256]{1,0:T(8,128)S(1)}, u32[]{:S(2)}, u32[]{:S(2)}) collective-permute-start(s32[264,256]{1,0:T(8,128)S(1)} %shard_map.89.refs_0_), channel_id=1, source_target_pairs={{0,1},{1,0},{2,3},{3,2},{4,5},{5,4},{6,7},{7,6},{8,9},{9,8},{10,11... | collective-permute-start | bytes 811016 | tf_op jit(solution)/shard_map/ppermute | solution.py:31
  29.8 1.6 %collective-permute-done.12.refs_5_ = bf16[256,512]{1,0:T(8,128)(2,1)S(1)} collective-permute-done((bf16[256,512]{1,0:T(8,128)(2,1)S(1)}, bf16[256,512]{1,0:T(8,128)(2,1)S(1)}, u32[]{:S(2)}, u32[]{:S(2)}) %collective-permute-start.12) | collective-permute-done | bytes 262176 | tf_op jit(solution)/shard_map/ppermute | solution.py:31
  31.4 2.8 %collective-permute-done.6.refs_1_ = bf16[256,512]{1,0:T(8,128)(2,1)S(1)} collective-permute-done((bf16[256,512]{1,0:T(8,128)(2,1)S(1)}, bf16[256,512]{1,0:T(8,128)(2,1)S(1)}, u32[]{:S(2)}, u32[]{:S(2)}) %collective-permute-start.6) | collective-permute-done | bytes 262176 | tf_op jit(solution)/shard_map/ppermute | solution.py:31
  34.7 1.0 collective-permute-start.16
  35.7 1.0 shard_map.94
  37.4 1.1 %collective-permute-start.17 = (bf16[256,512]{1,0:T(8,128)(2,1)S(1)}, bf16[256,512]{1,0:T(8,128)(2,1)S(1)}, u32[]{:S(2)}, u32[]{:S(2)}) collective-permute-start(bf16[256,512]{1,0:T(8,128)(2,1)S(1)} %shard_map.95.grads_ref), channel_id=1, source_target_pairs={{0,1},{1,0},{2,3},{3,2},{4,5},{5,4},{6,7},{7,6},{8,9},{9,8},{10,11... | collective-permute-start | bytes 786440 | tf_op jit(solution)/shard_map/ppermute | solution.py:31
  38.6 5.3 %collective-permute-done.16.refs_0_.refs_1_ = bf16[128,1024]{1,0:T(8,128)(2,1)S(1)} collective-permute-done((bf16[128,1024]{1,0:T(8,128)(2,1)S(1)}, bf16[128,1024]{1,0:T(8,128)(2,1)S(1)}, u32[]{:S(2)}, u32[]{:S(2)}) %collective-permute-start.16) | collective-permute-done | bytes 262176 | tf_op jit(solution)/shard_map/ppermute | solution.py:31
  44.4 0.9 shard_map.98.refs_2_.refer_ref
  45.2 3.9 %collective-permute-done.17.grads_ref = bf16[256,512]{1,0:T(8,128)(2,1)S(1)} collective-permute-done((bf16[256,512]{1,0:T(8,128)(2,1)S(1)}, bf16[256,512]{1,0:T(8,128)(2,1)S(1)}, u32[]{:S(2)}, u32[]{:S(2)}) %collective-permute-start.17) | collective-permute-done | bytes 262176 | tf_op jit(solution)/shard_map/ppermute | solution.py:31
  49.1 1.7 %shard_map.99 = (f32[1024,512]{1,0:T(8,128)S(1)}, f32[512,256]{1,0:T(8,128)S(1)}, f32[512,256]{1,0:T(8,128)S(1)}, bf16[256,1024]{1,0:T(8,128)(2,1)S(1)}, bf16[10...) custom-call(s32[2]{0:T(128)S(1)} %copy-done.7, f32[1024,512]{1,0:T(8,128)S(1)} %shard_map.97.refs_0_.inner_ref, ...), custom_call_target="tpu_custom_call" | custom-call | flops 1000 | bytes 1000 | tf_op jit(solution)/shard_map/pallas_call | solution.py:195
  50.9 1.0 collective-permute-start.18
  51.8 0.9 collective-permute-done.19.received_ref
  52.9 1.0 collective-permute-start.20
  54.7 2.6 %collective-permute-start.22 = (s32[72,256]{1,0:T(8,128)S(1)}, s32[72,256]{1,0:T(8,128)S(1)}, u32[]{:S(2)}, u32[]{:S(2)}) collective-permute-start(s32[72,256]{1,0:T(8,128)S(1)} %get-tuple-element.50), channel_id=1, source_target_pairs={{0,24},{2,26},{4,28},{6,30},{8,16},{10,18},{12,20},{14,22},{16,8},... | collective-permute-start | bytes 221192 | tf_op jit(solution)/shard_map/ppermute | solution.py:31
  57.8 2.0 %collective-permute-done.18.received_ref = s32[264,256]{1,0:T(8,128)S(1)} collective-permute-done((s32[264,256]{1,0:T(8,128)S(1)}, s32[264,256]{1,0:T(8,128)S(1)}, u32[]{:S(2)}, u32[]{:S(2)}) %collective-permute-start.18) | collective-permute-done | bytes 270368 | tf_op jit(solution)/shard_map/ppermute | solution.py:31
  59.8 1.5 %collective-permute-done.20.refs_0_ = s32[72,256]{1,0:T(8,128)S(1)} collective-permute-done((s32[72,256]{1,0:T(8,128)S(1)}, s32[72,256]{1,0:T(8,128)S(1)}, u32[]{:S(2)}, u32[]{:S(2)}) %collective-permute-start.20) | collective-permute-done | bytes 73760 | tf_op jit(solution)/shard_map/ppermute | solution.py:31
  62.0 1.0 collective-permute-start.23
  63.7 1.6 %collective-permute-start.24 = (s32[72,256]{1,0:T(8,128)S(1)}, s32[72,256]{1,0:T(8,128)S(1)}, u32[]{:S(2)}, u32[]{:S(2)}) collective-permute-start(s32[72,256]{1,0:T(8,128)S(1)} %shard_map.104.one_ref), channel_id=1, source_target_pairs={{0,4},{2,6},{4,0},{6,2},{8,12},{10,14},{12,8},{14,10},{16,20},{18,... | collective-permute-start | bytes 221192 | tf_op jit(solution)/shard_map/ppermute | solution.py:31
  65.2 2.8 %collective-permute-done.24.other_ref = s32[72,256]{1,0:T(8,128)S(1)} collective-permute-done((s32[72,256]{1,0:T(8,128)S(1)}, s32[72,256]{1,0:T(8,128)S(1)}, u32[]{:S(2)}, u32[]{:S(2)}) %collective-permute-start.24) | collective-permute-done | bytes 73760 | tf_op jit(solution)/shard_map/ppermute | solution.py:31
  68.2 1.1 %collective-permute-done.23.grads_ref = bf16[256,512]{1,0:T(8,128)(2,1)S(1)} collective-permute-done((bf16[256,512]{1,0:T(8,128)(2,1)S(1)}, bf16[256,512]{1,0:T(8,128)(2,1)S(1)}, u32[]{:S(2)}, u32[]{:S(2)}) %collective-permute-start.23) | collective-permute-done | bytes 262176 | tf_op jit(solution)/shard_map/ppermute | solution.py:31
  69.3 1.3 %shard_map.106 = (f32[1024,512]{1,0:T(8,128)S(1)}, f32[512,256]{1,0:T(8,128)S(1)}, f32[512,256]{1,0:T(8,128)S(1)}) custom-call(s32[2]{0:T(128)S(1)} %copy-done.7, f32[1024,512]{1,0:T(8,128)S(1)} %shard_map.103.refs_3_.inner_ref, bf16[256,1024]{1,0:T(8,128)(2,1)S(1)} %get-tuple-element.51.features_ref, ...), custom_call_target="tpu_custom_call" | custom-call | flops 1000 | bytes 1000 | tf_op jit(solution)/shard_map/pallas_call | solution.py:195
  70.6 1.9 %collective-permute-done.29.received_ref = f32[512,256]{1,0:T(8,128)S(1)} collective-permute-done((f32[512,256]{1,0:T(8,128)S(1)}, f32[512,256]{1,0:T(8,128)S(1)}, u32[]{:S(2)}, u32[]{:S(2)}) %collective-permute-start.29) | collective-permute-done | bytes 524320 | tf_op jit(solution)/shard_map/ppermute | solution.py:31
  72.6 2.0 %collective-permute-start.30 = (s32[72,256]{1,0:T(8,128)S(1)}, s32[72,256]{1,0:T(8,128)S(1)}, u32[]{:S(2)}, u32[]{:S(2)}) collective-permute-start(s32[72,256]{1,0:T(8,128)S(1)} %get-tuple-element.57), channel_id=1, source_target_pairs={{0,16},{2,18},{4,20},{6,22},{8,24},{10,26},{12,28},{14,30},{16,0},... | collective-permute-start | bytes 221192 | tf_op jit(solution)/shard_map/ppermute | solution.py:31
  74.7 1.1 %collective-permute-start.31 = (s32[72,256]{1,0:T(8,128)S(1)}, s32[72,256]{1,0:T(8,128)S(1)}, u32[]{:S(2)}, u32[]{:S(2)}) collective-permute-start(s32[72,256]{1,0:T(8,128)S(1)} %get-tuple-element.58), channel_id=1, source_target_pairs={{0,8},{2,10},{4,12},{6,14},{8,0},{10,2},{12,4},{14,6},{16,24},{18,... | collective-permute-start | bytes 221192 | tf_op jit(solution)/shard_map/ppermute | solution.py:31
  75.8 2.3 %collective-permute-start.32 = (s32[72,256]{1,0:T(8,128)S(1)}, s32[72,256]{1,0:T(8,128)S(1)}, u32[]{:S(2)}, u32[]{:S(2)}) collective-permute-start(s32[72,256]{1,0:T(8,128)S(1)} %get-tuple-element.59), channel_id=1, source_target_pairs={{0,24},{2,26},{4,28},{6,30},{8,16},{10,18},{12,20},{14,22},{16,8},... | collective-permute-start | bytes 221192 | tf_op jit(solution)/shard_map/ppermute | solution.py:31
  78.1 1.4 %collective-permute-done.31.refs_1_ = s32[72,256]{1,0:T(8,128)S(1)} collective-permute-done((s32[72,256]{1,0:T(8,128)S(1)}, s32[72,256]{1,0:T(8,128)S(1)}, u32[]{:S(2)}, u32[]{:S(2)}) %collective-permute-start.31) | collective-permute-done | bytes 73760 | tf_op jit(solution)/shard_map/ppermute | solution.py:31
  79.5 4.0 %collective-permute-done.32.refs_2_ = s32[72,256]{1,0:T(8,128)S(1)} collective-permute-done((s32[72,256]{1,0:T(8,128)S(1)}, s32[72,256]{1,0:T(8,128)S(1)}, u32[]{:S(2)}, u32[]{:S(2)}) %collective-permute-start.32) | collective-permute-done | bytes 73760 | tf_op jit(solution)/shard_map/ppermute | solution.py:31
  83.6 1.6 %collective-permute-start.33 = (s32[72,256]{1,0:T(8,128)S(1)}, s32[72,256]{1,0:T(8,128)S(1)}, u32[]{:S(2)}, u32[]{:S(2)}) collective-permute-start(s32[72,256]{1,0:T(8,128)S(1)} %shard_map.109.one_ref), channel_id=1, source_target_pairs={{0,4},{2,6},{4,0},{6,2},{8,12},{10,14},{12,8},{14,10},{16,20},{18,... | collective-permute-start | bytes 221192 | tf_op jit(solution)/shard_map/ppermute | solution.py:31
  85.2 1.4 %collective-permute-start.27 = (s32[72,256]{1,0:T(8,128)S(1)}, s32[72,256]{1,0:T(8,128)S(1)}, u32[]{:S(2)}, u32[]{:S(2)}) collective-permute-start(s32[72,256]{1,0:T(8,128)S(1)} %shard_map.105.refs_0_), channel_id=1, source_target_pairs={{0,24},{2,26},{4,28},{6,30},{8,16},{10,18},{12,20},{14,22},{16,8},... | collective-permute-start | bytes 221192 | tf_op jit(solution)/shard_map/ppermute | solution.py:31
  86.7 2.9 %collective-permute-start.25 = (s32[72,256]{1,0:T(8,128)S(1)}, s32[72,256]{1,0:T(8,128)S(1)}, u32[]{:S(2)}, u32[]{:S(2)}) collective-permute-start(s32[72,256]{1,0:T(8,128)S(1)} %shard_map.105.refs_0_), channel_id=1, source_target_pairs={{0,8},{2,10},{4,12},{6,14},{8,0},{10,2},{12,4},{14,6},{16,24},{18,... | collective-permute-start | bytes 221192 | tf_op jit(solution)/shard_map/ppermute | solution.py:31
  89.7 1.5 %collective-permute-start.36 = (s32[72,256]{1,0:T(8,128)S(1)}, s32[72,256]{1,0:T(8,128)S(1)}, u32[]{:S(2)}, u32[]{:S(2)}) collective-permute-start(s32[72,256]{1,0:T(8,128)S(1)} %shard_map.110.refs_0_), channel_id=1, source_target_pairs={{0,24},{2,26},{4,28},{6,30},{8,16},{10,18},{12,20},{14,22},{16,8},... | collective-permute-start | bytes 221192 | tf_op jit(solution)/shard_map/ppermute | solution.py:31
  91.2 0.9 collective-permute-done.27.refs_3_
  92.1 2.0 %collective-permute-start.34 = (s32[72,256]{1,0:T(8,128)S(1)}, s32[72,256]{1,0:T(8,128)S(1)}, u32[]{:S(2)}, u32[]{:S(2)}) collective-permute-start(s32[72,256]{1,0:T(8,128)S(1)} %shard_map.110.refs_0_), channel_id=1, source_target_pairs={{0,8},{2,10},{4,12},{6,14},{8,0},{10,2},{12,4},{14,6},{16,24},{18,... | collective-permute-start | bytes 221192 | tf_op jit(solution)/shard_map/ppermute | solution.py:31
  94.2 1.9 %collective-permute-done.26.refs_2_ = s32[72,256]{1,0:T(8,128)S(1)} collective-permute-done((s32[72,256]{1,0:T(8,128)S(1)}, s32[72,256]{1,0:T(8,128)S(1)}, u32[]{:S(2)}, u32[]{:S(2)}) %collective-permute-start.26) | collective-permute-done | bytes 73760 | tf_op jit(solution)/shard_map/ppermute | solution.py:31
  96.7 3.1 %collective-permute-done.35.refs_2_ = s32[72,256]{1,0:T(8,128)S(1)} collective-permute-done((s32[72,256]{1,0:T(8,128)S(1)}, s32[72,256]{1,0:T(8,128)S(1)}, u32[]{:S(2)}, u32[]{:S(2)}) %collective-permute-start.35) | collective-permute-done | bytes 73760 | tf_op jit(solution)/shard_map/ppermute | solution.py:31
  100.3 1.6 %collective-permute-done.37.other1 = s32[288,256]{1,0:T(8,128)S(1)} collective-permute-done((s32[288,256]{1,0:T(8,128)S(1)}, s32[288,256]{1,0:T(8,128)S(1)}, u32[]{:S(2)}, u32[]{:S(2)}) %collective-permute-start.37) | collective-permute-done | bytes 294944 | tf_op jit(solution)/shard_map/ppermute | solution.py:31
  101.9 2.8 %shard_map.112 = (f32[1024,512]{1,0:T(8,128)}, f32[1024,512]{1,0:T(8,128)}) custom-call(s32[2]{0:T(128)S(1)} %copy-done.7, f32[1024,512]{1,0:T(8,128)S(1)} %copy-done, f32[1024,512]{1,0:T(8,128)S(1)} %get-tuple-element.53.inner_ref, s32[288,256]{1,0:T(8,128)S(1)} %shard_map.107.own0, s32[288,256]{1,0:T(8,128)S(1)} %collective-permute-done.28.other0, ...), custom_call_target="tpu_custom_call" | custom-call | flops 1000 | bytes 1000 | tf_op jit(solution)/shard_map/pallas_call | solution.py:195
  (71 shorter events, 10.4 us)
Async XLA Ops:
  0.6 5.8 %copy-start.2 = (bf16[2,256,2048]{2,1,0:T(8,128)(2,1)S(1)}, bf16[2,256,2048]{2,1,0:T(8,128)(2,1)}, u32[]{:S(2)}) copy-start(bf16[2,256,2048]{2,1,0:T(8,128)(2,1)} %hidden_ref.3) | copy-start | bytes 6291460
  0.6 5.8 %collective-permute-start = (bf16[64,512]{1,0:T(8,128)(2,1)}, bf16[64,512]{1,0:T(8,128)(2,1)S(1)}, u32[]{:S(2)}, u32[]{:S(2)}) collective-permute-start(bf16[64,512]{1,0:T(8,128)(2,1)} %refs_0_.1), channel_id=1, source_target_pairs={{0,1},{1,0},{2,3},{3,2},{4,5},{5,4},{6,7},{7,6},{8,9},{9,8},{10,11... | collective-permute-start | bytes 196616 | tf_op jit(solution)/shard_map/ppermute | solution.py:31
  6.4 0.8 copy-start.4
  7.3 19.7 %copy-start = (f32[1024,512]{1,0:T(8,128)S(1)}, f32[1024,512]{1,0:T(8,128)}, u32[]{:S(2)}) copy-start(f32[1024,512]{1,0:T(8,128)} %outer_ref.7) | copy-start | bytes 6291460
  7.3 19.7 %copy-start.3 = (bf16[1,1024,512]{2,1,0:T(8,128)(2,1)S(1)}, bf16[1,1024,512]{2,1,0:T(8,128)(2,1)}, u32[]{:S(2)}) copy-start(bf16[1,1024,512]{2,1,0:T(8,128)(2,1)} %drift_ref.1) | copy-start | bytes 3145732
  8.0 19.2 %collective-permute-start.1 = (bf16[256,1024]{1,0:T(8,128)(2,1)}, bf16[256,1024]{1,0:T(8,128)(2,1)S(1)}, u32[]{:S(2)}, u32[]{:S(2)}) collective-permute-start(bf16[256,1024]{1,0:T(8,128)(2,1)} %shard_map.88), channel_id=1, source_target_pairs={{0,1},{1,0},{2,3},{3,2},{4,5},{5,4},{6,7},{7,6},{8,9},{9,8},{10,11... | collective-permute-start | bytes 1572872 | tf_op jit(solution)/shard_map/ppermute | solution.py:31
  9.8 8.0 %collective-permute-start.11 = (bf16[64,512]{1,0:T(8,128)(2,1)S(1)}, bf16[64,512]{1,0:T(8,128)(2,1)S(1)}, u32[]{:S(2)}, u32[]{:S(2)}) collective-permute-start(bf16[64,512]{1,0:T(8,128)(2,1)S(1)} %get-tuple-element.37.refs_0_), channel_id=1, source_target_pairs={{0,24},{2,26},{4,28},{6,30},{8,16},{10,18},{12,20},{14,22},{16,8},... | collective-permute-start | bytes 196616 | tf_op jit(solution)/shard_map/ppermute | solution.py:31
  13.4 7.4 %collective-permute-start.10 = (bf16[64,512]{1,0:T(8,128)(2,1)S(1)}, bf16[64,512]{1,0:T(8,128)(2,1)S(1)}, u32[]{:S(2)}, u32[]{:S(2)}) collective-permute-start(bf16[64,512]{1,0:T(8,128)(2,1)S(1)} %get-tuple-element.37.refs_0_), channel_id=1, source_target_pairs={{0,16},{2,18},{4,20},{6,22},{8,24},{10,26},{12,28},{14,30},{16,0},... | collective-permute-start | bytes 196616 | tf_op jit(solution)/shard_map/ppermute | solution.py:31
  13.4 7.4 %collective-permute-start.9 = (bf16[64,512]{1,0:T(8,128)(2,1)S(1)}, bf16[64,512]{1,0:T(8,128)(2,1)S(1)}, u32[]{:S(2)}, u32[]{:S(2)}) collective-permute-start(bf16[64,512]{1,0:T(8,128)(2,1)S(1)} %get-tuple-element.37.refs_0_), channel_id=1, source_target_pairs={{0,8},{2,10},{4,12},{6,14},{8,0},{10,2},{12,4},{14,6},{16,24},{18,... | collective-permute-start | bytes 196616 | tf_op jit(solution)/shard_map/ppermute | solution.py:31
  14.2 8.3 %collective-permute-start.5 = (bf16[64,512]{1,0:T(8,128)(2,1)S(1)}, bf16[64,512]{1,0:T(8,128)(2,1)S(1)}, u32[]{:S(2)}, u32[]{:S(2)}) collective-permute-start(bf16[64,512]{1,0:T(8,128)(2,1)S(1)} %get-tuple-element.36.refs_0_), channel_id=1, source_target_pairs={{0,24},{2,26},{4,28},{6,30},{8,16},{10,18},{12,20},{14,22},{16,8},... | collective-permute-start | bytes 196616 | tf_op jit(solution)/shard_map/ppermute | solution.py:31
  17.8 6.3 %collective-permute-start.4 = (bf16[64,512]{1,0:T(8,128)(2,1)S(1)}, bf16[64,512]{1,0:T(8,128)(2,1)S(1)}, u32[]{:S(2)}, u32[]{:S(2)}) collective-permute-start(bf16[64,512]{1,0:T(8,128)(2,1)S(1)} %get-tuple-element.36.refs_0_), channel_id=1, source_target_pairs={{0,16},{2,18},{4,20},{6,22},{8,24},{10,26},{12,28},{14,30},{16,0},... | collective-permute-start | bytes 196616 | tf_op jit(solution)/shard_map/ppermute | solution.py:31
  20.8 4.3 %collective-permute-start.3 = (bf16[64,512]{1,0:T(8,128)(2,1)S(1)}, bf16[64,512]{1,0:T(8,128)(2,1)S(1)}, u32[]{:S(2)}, u32[]{:S(2)}) collective-permute-start(bf16[64,512]{1,0:T(8,128)(2,1)S(1)} %get-tuple-element.36.refs_0_), channel_id=1, source_target_pairs={{0,8},{2,10},{4,12},{6,14},{8,0},{10,2},{12,4},{14,6},{16,24},{18,... | collective-permute-start | bytes 196616 | tf_op jit(solution)/shard_map/ppermute | solution.py:31
  20.8 8.5 %collective-permute-start.15 = (bf16[128,1024]{1,0:T(8,128)(2,1)S(1)}, bf16[128,1024]{1,0:T(8,128)(2,1)S(1)}, u32[]{:S(2)}, u32[]{:S(2)}) collective-permute-start(bf16[128,1024]{1,0:T(8,128)(2,1)S(1)} %get-tuple-element.38), channel_id=1, source_target_pairs={{0,1},{1,0},{2,3},{3,2},{4,5},{5,4},{6,7},{7,6},{8,9},{9,8},{10,11... | collective-permute-start | bytes 786440 | tf_op jit(solution)/shard_map/ppermute | solution.py:31
  22.5 8.9 %collective-permute-start.12 = (bf16[256,512]{1,0:T(8,128)(2,1)S(1)}, bf16[256,512]{1,0:T(8,128)(2,1)S(1)}, u32[]{:S(2)}, u32[]{:S(2)}) collective-permute-start(bf16[256,512]{1,0:T(8,128)(2,1)S(1)} %shard_map.93.refs_4_), channel_id=1, source_target_pairs={{0,4},{2,6},{4,0},{6,2},{8,12},{10,14},{12,8},{14,10},{16,20},{18,... | collective-permute-start | bytes 786440 | tf_op jit(solution)/shard_map/ppermute | solution.py:31
  25.4 8.8 %copy-start.1 = (bf16[256,2048]{1,0:T(8,128)(2,1)S(1)}, bf16[256,2048]{1,0:T(8,128)(2,1)}, u32[]{:S(2)}) copy-start(bf16[256,2048]{1,0:T(8,128)(2,1)} %get-tuple-element.33.normed_ref) | copy-start | bytes 3145732
  25.4 8.8 %collective-permute-start.6 = (bf16[256,512]{1,0:T(8,128)(2,1)S(1)}, bf16[256,512]{1,0:T(8,128)(2,1)S(1)}, u32[]{:S(2)}, u32[]{:S(2)}) collective-permute-start(bf16[256,512]{1,0:T(8,128)(2,1)S(1)} %shard_map.92.refs_0_), channel_id=1, source_target_pairs={{0,4},{2,6},{4,0},{6,2},{8,12},{10,14},{12,8},{14,10},{16,20},{18,... | collective-permute-start | bytes 786440 | tf_op jit(solution)/shard_map/ppermute | solution.py:31
  27.8 9.0 %collective-permute-start.2 = (s32[264,256]{1,0:T(8,128)S(1)}, s32[264,256]{1,0:T(8,128)S(1)}, u32[]{:S(2)}, u32[]{:S(2)}) collective-permute-start(s32[264,256]{1,0:T(8,128)S(1)} %shard_map.89.refs_0_), channel_id=1, source_target_pairs={{0,1},{1,0},{2,3},{3,2},{4,5},{5,4},{6,7},{7,6},{8,9},{9,8},{10,11... | collective-permute-start | bytes 811016 | tf_op jit(solution)/shard_map/ppermute | solution.py:31
  29.3 5.4 %collective-permute-start.13 = (bf16[256,512]{1,0:T(8,128)(2,1)S(1)}, bf16[256,512]{1,0:T(8,128)(2,1)S(1)}, u32[]{:S(2)}, u32[]{:S(2)}) collective-permute-start(bf16[256,512]{1,0:T(8,128)(2,1)S(1)} %shard_map.93.refs_4_), channel_id=1, source_target_pairs={{0,2},{2,0},{4,6},{6,4},{8,10},{10,8},{12,14},{14,12},{16,18},{18,... | collective-permute-start | bytes 786440 | tf_op jit(solution)/shard_map/ppermute | solution.py:31
  29.3 6.4 %collective-permute-start.7 = (bf16[256,512]{1,0:T(8,128)(2,1)S(1)}, bf16[256,512]{1,0:T(8,128)(2,1)S(1)}, u32[]{:S(2)}, u32[]{:S(2)}) collective-permute-start(bf16[256,512]{1,0:T(8,128)(2,1)S(1)} %shard_map.92.refs_0_), channel_id=1, source_target_pairs={{0,2},{2,0},{4,6},{6,4},{8,10},{10,8},{12,14},{14,12},{16,18},{18,... | collective-permute-start | bytes 786440 | tf_op jit(solution)/shard_map/ppermute | solution.py:31
  31.4 4.3 %collective-permute-start.14 = (bf16[256,512]{1,0:T(8,128)(2,1)S(1)}, bf16[256,512]{1,0:T(8,128)(2,1)S(1)}, u32[]{:S(2)}, u32[]{:S(2)}) collective-permute-start(bf16[256,512]{1,0:T(8,128)(2,1)S(1)} %collective-permute-done.12.refs_5_), channel_id=1, source_target_pairs={{0,2},{2,0},{4,6},{6,4},{8,10},{10,8},{12,14},{14,12},{16,18},{18,... | collective-permute-start | bytes 786440 | tf_op jit(solution)/shard_map/ppermute | solution.py:31
  34.2 1.5 %collective-permute-start.8 = (bf16[256,512]{1,0:T(8,128)(2,1)S(1)}, bf16[256,512]{1,0:T(8,128)(2,1)S(1)}, u32[]{:S(2)}, u32[]{:S(2)}) collective-permute-start(bf16[256,512]{1,0:T(8,128)(2,1)S(1)} %collective-permute-done.6.refs_1_), channel_id=1, source_target_pairs={{0,2},{2,0},{4,6},{6,4},{8,10},{10,8},{12,14},{14,12},{16,18},{18,... | collective-permute-start | bytes 786440 | tf_op jit(solution)/shard_map/ppermute | solution.py:31
  34.6 2.1 %copy-start.5 = (s32[2,256]{1,0:T(2,128)S(1)}, s32[2,256]{1,0:T(2,128)}, u32[]{:S(2)}) copy-start(s32[2,256]{1,0:T(2,128)} %targets_ref.3) | copy-start | bytes 6148
  34.7 2.1 %copy-start.6 = (s32[2,256]{1,0:T(2,128)S(1)}, s32[2,256]{1,0:T(2,128)}, u32[]{:S(2)}) copy-start(s32[2,256]{1,0:T(2,128)} %valid_ref.3) | copy-start | bytes 6148
  34.7 9.2 %collective-permute-start.16 = (bf16[128,1024]{1,0:T(8,128)(2,1)S(1)}, bf16[128,1024]{1,0:T(8,128)(2,1)S(1)}, u32[]{:S(2)}, u32[]{:S(2)}) collective-permute-start(bf16[128,1024]{1,0:T(8,128)(2,1)S(1)} %shard_map.96), channel_id=1, source_target_pairs={{0,1},{1,0},{2,3},{3,2},{4,5},{5,4},{6,7},{7,6},{8,9},{9,8},{10,11... | collective-permute-start | bytes 786440 | tf_op jit(solution)/shard_map/ppermute | solution.py:31
  37.4 11.6 %collective-permute-start.17 = (bf16[256,512]{1,0:T(8,128)(2,1)S(1)}, bf16[256,512]{1,0:T(8,128)(2,1)S(1)}, u32[]{:S(2)}, u32[]{:S(2)}) collective-permute-start(bf16[256,512]{1,0:T(8,128)(2,1)S(1)} %shard_map.95.grads_ref), channel_id=1, source_target_pairs={{0,1},{1,0},{2,3},{3,2},{4,5},{5,4},{6,7},{7,6},{8,9},{9,8},{10,11... | collective-permute-start | bytes 786440 | tf_op jit(solution)/shard_map/ppermute | solution.py:31
  44.4 4.7 %copy-start.7 = (s32[2]{0:T(128)S(1)}, s32[2]{0:T(128)}, u32[]{:S(2)}) copy-start(s32[2]{0:T(128)} %plan_ref.5) | copy-start | bytes 28
  50.8 2.0 %collective-permute-start.19 = (f32[512,256]{1,0:T(8,128)S(1)}, f32[512,256]{1,0:T(8,128)S(1)}, u32[]{:S(2)}, u32[]{:S(2)}) collective-permute-start(f32[512,256]{1,0:T(8,128)S(1)} %get-tuple-element.47), channel_id=1, source_target_pairs={{0,2},{2,0},{4,6},{6,4},{8,10},{10,8},{12,14},{14,12},{16,18},{18,... | collective-permute-start | bytes 1572872 | tf_op jit(solution)/shard_map/ppermute | solution.py:31
  50.9 8.9 %collective-permute-start.18 = (s32[264,256]{1,0:T(8,128)S(1)}, s32[264,256]{1,0:T(8,128)S(1)}, u32[]{:S(2)}, u32[]{:S(2)}) collective-permute-start(s32[264,256]{1,0:T(8,128)S(1)} %get-tuple-element.45), channel_id=1, source_target_pairs={{0,1},{1,0},{2,3},{3,2},{4,5},{5,4},{6,7},{7,6},{8,9},{9,8},{10,11... | collective-permute-start | bytes 811016 | tf_op jit(solution)/shard_map/ppermute | solution.py:31
  52.9 8.4 %collective-permute-start.20 = (s32[72,256]{1,0:T(8,128)S(1)}, s32[72,256]{1,0:T(8,128)S(1)}, u32[]{:S(2)}, u32[]{:S(2)}) collective-permute-start(s32[72,256]{1,0:T(8,128)S(1)} %get-tuple-element.48), channel_id=1, source_target_pairs={{0,16},{2,18},{4,20},{6,22},{8,24},{10,26},{12,28},{14,30},{16,0},... | collective-permute-start | bytes 221192 | tf_op jit(solution)/shard_map/ppermute | solution.py:31
  53.9 7.4 %collective-permute-start.21 = (s32[72,256]{1,0:T(8,128)S(1)}, s32[72,256]{1,0:T(8,128)S(1)}, u32[]{:S(2)}, u32[]{:S(2)}) collective-permute-start(s32[72,256]{1,0:T(8,128)S(1)} %get-tuple-element.49), channel_id=1, source_target_pairs={{0,8},{2,10},{4,12},{6,14},{8,0},{10,2},{12,4},{14,6},{16,24},{18,... | collective-permute-start | bytes 221192 | tf_op jit(solution)/shard_map/ppermute | solution.py:31
  54.7 6.6 %collective-permute-start.22 = (s32[72,256]{1,0:T(8,128)S(1)}, s32[72,256]{1,0:T(8,128)S(1)}, u32[]{:S(2)}, u32[]{:S(2)}) collective-permute-start(s32[72,256]{1,0:T(8,128)S(1)} %get-tuple-element.50), channel_id=1, source_target_pairs={{0,24},{2,26},{4,28},{6,30},{8,16},{10,18},{12,20},{14,22},{16,8},... | collective-permute-start | bytes 221192 | tf_op jit(solution)/shard_map/ppermute | solution.py:31
  62.0 7.2 %collective-permute-start.23 = (bf16[256,512]{1,0:T(8,128)(2,1)S(1)}, bf16[256,512]{1,0:T(8,128)(2,1)S(1)}, u32[]{:S(2)}, u32[]{:S(2)}) collective-permute-start(bf16[256,512]{1,0:T(8,128)(2,1)S(1)} %shard_map.102.grads_ref), channel_id=1, source_target_pairs={{0,1},{1,0},{2,3},{3,2},{4,5},{5,4},{6,7},{7,6},{8,9},{9,8},{10,11... | collective-permute-start | bytes 786440 | tf_op jit(solution)/shard_map/ppermute | solution.py:31
  63.7 4.4 %collective-permute-start.24 = (s32[72,256]{1,0:T(8,128)S(1)}, s32[72,256]{1,0:T(8,128)S(1)}, u32[]{:S(2)}, u32[]{:S(2)}) collective-permute-start(s32[72,256]{1,0:T(8,128)S(1)} %shard_map.104.one_ref), channel_id=1, source_target_pairs={{0,4},{2,6},{4,0},{6,2},{8,12},{10,14},{12,8},{14,10},{16,20},{18,... | collective-permute-start | bytes 221192 | tf_op jit(solution)/shard_map/ppermute | solution.py:31
  70.5 2.0 %collective-permute-start.29 = (f32[512,256]{1,0:T(8,128)S(1)}, f32[512,256]{1,0:T(8,128)S(1)}, u32[]{:S(2)}, u32[]{:S(2)}) collective-permute-start(f32[512,256]{1,0:T(8,128)S(1)} %get-tuple-element.55), channel_id=1, source_target_pairs={{0,2},{2,0},{4,6},{6,4},{8,10},{10,8},{12,14},{14,12},{16,18},{18,... | collective-permute-start | bytes 1572872 | tf_op jit(solution)/shard_map/ppermute | solution.py:31
  72.6 5.4 %collective-permute-start.30 = (s32[72,256]{1,0:T(8,128)S(1)}, s32[72,256]{1,0:T(8,128)S(1)}, u32[]{:S(2)}, u32[]{:S(2)}) collective-permute-start(s32[72,256]{1,0:T(8,128)S(1)} %get-tuple-element.57), channel_id=1, source_target_pairs={{0,16},{2,18},{4,20},{6,22},{8,24},{10,26},{12,28},{14,30},{16,0},... | collective-permute-start | bytes 221192 | tf_op jit(solution)/shard_map/ppermute | solution.py:31
  74.7 4.8 %collective-permute-start.31 = (s32[72,256]{1,0:T(8,128)S(1)}, s32[72,256]{1,0:T(8,128)S(1)}, u32[]{:S(2)}, u32[]{:S(2)}) collective-permute-start(s32[72,256]{1,0:T(8,128)S(1)} %get-tuple-element.58), channel_id=1, source_target_pairs={{0,8},{2,10},{4,12},{6,14},{8,0},{10,2},{12,4},{14,6},{16,24},{18,... | collective-permute-start | bytes 221192 | tf_op jit(solution)/shard_map/ppermute | solution.py:31
  75.8 7.7 %collective-permute-start.32 = (s32[72,256]{1,0:T(8,128)S(1)}, s32[72,256]{1,0:T(8,128)S(1)}, u32[]{:S(2)}, u32[]{:S(2)}) collective-permute-start(s32[72,256]{1,0:T(8,128)S(1)} %get-tuple-element.59), channel_id=1, source_target_pairs={{0,24},{2,26},{4,28},{6,30},{8,16},{10,18},{12,20},{14,22},{16,8},... | collective-permute-start | bytes 221192 | tf_op jit(solution)/shard_map/ppermute | solution.py:31
  83.6 6.0 %collective-permute-start.33 = (s32[72,256]{1,0:T(8,128)S(1)}, s32[72,256]{1,0:T(8,128)S(1)}, u32[]{:S(2)}, u32[]{:S(2)}) collective-permute-start(s32[72,256]{1,0:T(8,128)S(1)} %shard_map.109.one_ref), channel_id=1, source_target_pairs={{0,4},{2,6},{4,0},{6,2},{8,12},{10,14},{12,8},{14,10},{16,20},{18,... | collective-permute-start | bytes 221192 | tf_op jit(solution)/shard_map/ppermute | solution.py:31
  85.2 6.9 %collective-permute-start.27 = (s32[72,256]{1,0:T(8,128)S(1)}, s32[72,256]{1,0:T(8,128)S(1)}, u32[]{:S(2)}, u32[]{:S(2)}) collective-permute-start(s32[72,256]{1,0:T(8,128)S(1)} %shard_map.105.refs_0_), channel_id=1, source_target_pairs={{0,24},{2,26},{4,28},{6,30},{8,16},{10,18},{12,20},{14,22},{16,8},... | collective-permute-start | bytes 221192 | tf_op jit(solution)/shard_map/ppermute | solution.py:31
  86.7 9.4 %collective-permute-start.26 = (s32[72,256]{1,0:T(8,128)S(1)}, s32[72,256]{1,0:T(8,128)S(1)}, u32[]{:S(2)}, u32[]{:S(2)}) collective-permute-start(s32[72,256]{1,0:T(8,128)S(1)} %shard_map.105.refs_0_), channel_id=1, source_target_pairs={{0,16},{2,18},{4,20},{6,22},{8,24},{10,26},{12,28},{14,30},{16,0},... | collective-permute-start | bytes 221192 | tf_op jit(solution)/shard_map/ppermute | solution.py:31
  86.7 9.4 %collective-permute-start.25 = (s32[72,256]{1,0:T(8,128)S(1)}, s32[72,256]{1,0:T(8,128)S(1)}, u32[]{:S(2)}, u32[]{:S(2)}) collective-permute-start(s32[72,256]{1,0:T(8,128)S(1)} %shard_map.105.refs_0_), channel_id=1, source_target_pairs={{0,8},{2,10},{4,12},{6,14},{8,0},{10,2},{12,4},{14,6},{16,24},{18,... | collective-permute-start | bytes 221192 | tf_op jit(solution)/shard_map/ppermute | solution.py:31
  89.7 7.0 %collective-permute-start.36 = (s32[72,256]{1,0:T(8,128)S(1)}, s32[72,256]{1,0:T(8,128)S(1)}, u32[]{:S(2)}, u32[]{:S(2)}) collective-permute-start(s32[72,256]{1,0:T(8,128)S(1)} %shard_map.110.refs_0_), channel_id=1, source_target_pairs={{0,24},{2,26},{4,28},{6,30},{8,16},{10,18},{12,20},{14,22},{16,8},... | collective-permute-start | bytes 221192 | tf_op jit(solution)/shard_map/ppermute | solution.py:31
  91.2 8.6 %collective-permute-start.35 = (s32[72,256]{1,0:T(8,128)S(1)}, s32[72,256]{1,0:T(8,128)S(1)}, u32[]{:S(2)}, u32[]{:S(2)}) collective-permute-start(s32[72,256]{1,0:T(8,128)S(1)} %shard_map.110.refs_0_), channel_id=1, source_target_pairs={{0,16},{2,18},{4,20},{6,22},{8,24},{10,26},{12,28},{14,30},{16,0},... | collective-permute-start | bytes 221192 | tf_op jit(solution)/shard_map/ppermute | solution.py:31
  92.1 7.7 %collective-permute-start.34 = (s32[72,256]{1,0:T(8,128)S(1)}, s32[72,256]{1,0:T(8,128)S(1)}, u32[]{:S(2)}, u32[]{:S(2)}) collective-permute-start(s32[72,256]{1,0:T(8,128)S(1)} %shard_map.110.refs_0_), channel_id=1, source_target_pairs={{0,8},{2,10},{4,12},{6,14},{8,0},{10,2},{12,4},{14,6},{16,24},{18,... | collective-permute-start | bytes 221192 | tf_op jit(solution)/shard_map/ppermute | solution.py:31
  96.5 3.8 %collective-permute-start.28 = (s32[288,256]{1,0:T(8,128)S(1)}, s32[288,256]{1,0:T(8,128)S(1)}, u32[]{:S(2)}, u32[]{:S(2)}) collective-permute-start(s32[288,256]{1,0:T(8,128)S(1)} %shard_map.107.own0), channel_id=1, source_target_pairs={{0,2},{2,0},{4,6},{6,4},{8,10},{10,8},{12,14},{14,12},{16,18},{18,... | collective-permute-start | bytes 884744 | tf_op jit(solution)/shard_map/ppermute | solution.py:31
  100.3 1.6 %collective-permute-start.37 = (s32[288,256]{1,0:T(8,128)S(1)}, s32[288,256]{1,0:T(8,128)S(1)}, u32[]{:S(2)}, u32[]{:S(2)}) collective-permute-start(s32[288,256]{1,0:T(8,128)S(1)} %shard_map.111.own1), channel_id=1, source_target_pairs={{0,2},{2,0},{4,6},{6,4},{8,10},{10,8},{12,14},{14,12},{16,18},{18,... | collective-permute-start | bytes 884744 | tf_op jit(solution)/shard_map/ppermute | solution.py:31

commit v5 on v4

--- a/solution.py
+++ b/solution.py
@@ -291,61 +291,65 @@
     return jnp.broadcast_to(row, (128, row.shape[1])).T[:, 0:1]
 
 
-def normalized(hidden, step, pieces, room, passed=(), earlier=()):
-    tokens, width = hidden.shape[1:]
+def normalized(hidden, sizes, passed=(), folded=(), earlier=()):
+    tokens, width = hidden.shape
     cols = width // 2
-    parts = 4
-    tile = tokens // parts
-    each = tokens // pieces
+    tile = 64
+    extra = [f.shape[0] * f.shape[1] // cols for f in folded]
+    starts = [sum(sizes[:k]) for k in range(len(sizes))]
+    lengths = [size + sum(extra) * (k == 0) for k, size in enumerate(sizes)]
 
     def kernel(hidden_ref, *refs):
-        passed_refs, refs = refs[: len(passed)], refs[len(passed) + len(earlier) :]
-        normed_ref, refs = refs[0], refs[1:]
-        sent_refs, refs = refs[:pieces], refs[pieces:]
-        copy_refs, (held_ref, sems) = refs[: len(passed)], refs[len(passed) :]
+        passed_refs, refs = refs[: len(passed)], refs[len(passed) :]
+        folded_refs, refs = refs[: len(folded)], refs[len(folded) + len(earlier) :]
+        normed_ref, sent_refs, copy_refs = refs[0], refs[1 : 1 + len(sizes)], refs[1 + len(sizes) :]
         other = pl.multiple_of((1 - lax.axis_index("fsdp")) * cols, cols)
-        copies = [
-            pltpu.make_async_copy(
-                hidden_ref.at[step, pl.ds(k * tile, tile)], held_ref.at[pl.ds(k * tile, tile)], sems.at[k]
-            )
-            for k in range(parts)
-        ]
-        for copy in copies:
-            copy.start()
         for source, target in zip(passed_refs, copy_refs):
             target[...] = source[...]
-        for k, copy in enumerate(copies):
-            copy.wait()
-            at = pl.ds(k * tile, tile)
-            normed_ref[at, :] = normalize(held_ref[at, :])
-            sent_refs[k * tile // each][pl.ds(k * tile % each, tile), :] = normed_ref[at, pl.ds(other, cols)]
-
-    return call(
-        kernel,
-        (hidden,) + passed + earlier,
-        [HBM] + [VMEM] * len(passed) + [ANY] * len(earlier),
+        for ref, rows in zip(folded_refs, extra):
+            part = ref.shape[1]
+            for k in range(cols // part):
+                sent_refs[0][sizes[0] : sizes[0] + rows, k * part : (k + 1) * part] = ref[k * rows : (k + 1) * rows, :]
+        for start, size, sent_ref in zip(starts, sizes, sent_refs):
+            for k in range(0, size, tile):
+                at = pl.ds(start + k, tile)
+                normed_ref[at, :] = normalize(hidden_ref[at, :])
+                sent_ref[k : k + tile, :] = normed_ref[at, pl.ds(other, cols)]
+
+    return call(
+        kernel,
+        (hidden,) + passed + folded + earlier,
+        [VMEM] * (1 + len(passed) + len(folded)) + [ANY] * len(earlier),
         [like((tokens, width), bf16)]
-        + [like((each, cols), bf16)] * pieces
+        + [like((length, cols), bf16) for length in lengths]
         + [like(p.shape, p.dtype) for p in passed],
-        [VMEM] * (1 + pieces + len(passed)),
-        room,
-        [pltpu.VMEM((tokens, width), bf16), pltpu.SemaphoreType.DMA((parts,))],
-    )
+        [VMEM] * (1 + len(sizes) + len(passed)),
+        8,
+    )
+
+
+def unfolded(message, start, shape):
+    def kernel(message_ref, out_ref):
+        rows = message.shape[0] - start
+        for k in range(shape[0] // rows):
+            out_ref[k * rows : (k + 1) * rows, :] = message_ref[start:, k * shape[1] : (k + 1) * shape[1]]
+
+    return call(kernel, (message,), [VMEM], like(shape, message.dtype), VMEM, 4)
 
 
 def reference_logs(normed, stacks, *earlier):
     tokens, width = normed.shape
-    entries = stacks[0].shape[1]
-    rows = stacks[0].shape[0] // MAJOR
+    entries = stacks[0][0].shape[1]
+    marks = [m for _, m in stacks]
+    stacks = tuple(a for a, _ in stacks)
+    rows = stacks[0].shape[0] // len(marks[0])
     count = len(stacks)
 
     def kernel(normed_ref, *refs):
         out_ref, whole_ref = refs[count + len(earlier) :]
         fsdp, me, _, _ = positions()
         for number in range(count):
-            bit_fsdp, bit_core, bit_y = number // 4, number // 2 % 2, number % 2
-            for p in range(MAJOR):
-                mask = bit_core + bit_y * CORES + p * 2 * CORES
+            for p, (mask, bit_fsdp) in enumerate(marks[number]):
                 block = jnp.bitwise_xor(me, mask) * 2 + jnp.bitwise_xor(fsdp, bit_fsdp)
                 to = pl.ds(pl.multiple_of(block * rows, rows), rows)
                 whole_ref[to, :] = refs[number][p * rows : (p + 1) * rows, :]
@@ -399,20 +403,29 @@
     pack(out_ref, logits[:, :half], logits[:, half:])
 
 
-def partner_logits(features, weights):
-    tokens = features.shape[0]
+def put_together(out_ref, refs, sizes):
+    start = 0
+    for ref, size in zip(refs, sizes):
+        out_ref[start : start + size, :] = ref[0:size, :]
+        start += size
+
+
+def partner_logits(pieces, sizes, weights):
+    tokens, cols = sum(sizes), pieces[0].shape[1]
     entries = weights.shape[1]
 
-    def kernel(features_ref, weights_ref, out_ref):
+    def kernel(weights_ref, *refs):
+        features_ref, out_ref = refs[-2:]
+        put_together(features_ref, refs[:-2], sizes)
         pack_logits(out_ref, dot(features_ref[...], weights_ref[...]))
 
     return call(
         kernel,
-        (features, weights),
-        [VMEM, VMEM],
-        like((packed_rows(tokens), entries // 2), jnp.int32),
-        VMEM,
-        8,
+        (weights,) + tuple(pieces),
+        [VMEM] * (1 + len(pieces)),
+        (like((tokens, cols), bf16), like((packed_rows(tokens), entries // 2), jnp.int32)),
+        (VMEM, VMEM),
+        10,
     )
 
 
@@ -501,9 +514,7 @@
                 refs[4][at, :] = new.astype(bf16)
         if pieces:
             next_ref, weights_ref, partial_ref = refs[3:]
-            each = tokens // pieces
-            for k, piece_ref in enumerate(following_refs):
-                next_ref[k * each : (k + 1) * each, :] = piece_ref[...]
+            put_together(next_ref, following_refs, [f.shape[0] for f in following])
             pack_logits(partial_ref, dot(next_ref[...], weights_ref[...]))
         columns = pl.ds(pl.multiple_of(plan_ref[step] * part, part), part)
         core = positions()[2]
@@ -581,11 +592,18 @@
     )
 
 
-def pair_sum(one, other):
-    def kernel(one_ref, other_ref, out_ref):
-        pack_quarter(out_ref, unpack_quarter(one_ref) + unpack_quarter(other_ref))
-
-    return call(kernel, (one, other), [VMEM] * 2, like(one.shape, jnp.int32), VMEM, 4)
+def pair_sum(one, other, *earlier):
+    def kernel(one_ref, other_ref, *refs):
+        pack_quarter(refs[-1], unpack_quarter(one_ref) + unpack_quarter(other_ref))
+
+    return call(
+        kernel,
+        (one, other) + earlier,
+        [VMEM] * 2 + [ANY] * len(earlier),
+        like(one.shape, jnp.int32),
+        VMEM,
+        4,
+    )
 
 
 def settled(outer_head, inner, means, plan):
@@ -641,20 +659,35 @@
     )
 
 
+def along(stack, *masks):
+    array, marks = stack
+    return (
+        stacked([array] + [swap(array, "replica", m) for m in masks]),
+        [(mark ^ m, bit) for m in (0,) + masks for mark, bit in marks],
+    )
+
+
+def across(stack, mask):
+    array, marks = stack
+    return swap(array, "replica", mask), [(mark ^ mask, bit) for mark, bit in marks]
+
+
 def gathered_stacks(ref_own, ref_partner):
-    step = 2 * CORES
+    along_z = [m * 2 * CORES for m in range(1, MAJOR)]
     stacks = []
-    for rows in (ref_own, ref_partner):
-        along = stacked([rows] + [swap(rows, "replica", m * step) for m in range(1, MAJOR)])
-        both = [along, swap(along, "replica", CORES)]
-        stacks += both + [swap(s, "replica", 1) for s in both]
+    for piece in ((ref_own, [(0, 0)]), (ref_partner, [(0, 1)])):
+        first = along(piece, *along_z)
+        second = across(first, CORES)
+        stacks += [first, second, across(first, 1), across(second, 1)]
     return stacks
 
 
-def gathered_quarters(own):
-    step = 2 * CORES
-    got = {m: swap(own, "replica", m * step) for m in MASKS}
-    stack = stacked([own, got[1], got[2], got[3]])
+def quarters_along(own):
+    return [own] + [swap(own, "replica", m * 2 * CORES) for m in range(1, MAJOR)]
+
+
+def gathered_quarters(pieces):
+    stack = stacked(pieces)
     return stack, swap(stack, "replica", 1)
 
 
@@ -666,18 +699,21 @@
 def shards_pair(hidden, targets, valid, plan, outer_head, drift, ref_head):
     replicas = lax.axis_size("replica")
 
-    ref_partner = swap(ref_head, "fsdp", 1)
-    normed0, sent0 = normalized(hidden, 0, 1, 60)
-    features0 = swap(after(sent0, ref_partner), "fsdp", 1)
-    normed1, sent1a, sent1b, *pieces = normalized(hidden, 1, 2, 8, (ref_head, ref_partner), (sent0,))
+    tokens = hidden.shape[1]
+    sizes0 = (tokens // 4, 3 * tokens // 4)
+    sizes1 = (tokens // 2, tokens // 2)
+
+    normed0, *sent0 = normalized(hidden[0], sizes0, (), (ref_head,))
+    features0 = [swap(s, "fsdp", 1) for s in sent0]
+    normed1, sent1a, sent1b, ref_own = normalized(hidden[1], sizes1, (ref_head,), (), tuple(sent0))
     features1a = swap(sent1a, "fsdp", 1)
-    stacks = gathered_stacks(*pieces)
-
-    inner, weights = starting_weights(outer_head, drift)
-    partial = partner_logits(features0, weights)
+    stacks = gathered_stacks(ref_own, unfolded(features0[0], sizes0[0], ref_head.shape))
+
+    inner, weights = starting_weights(outer_head, drift, normed1)
+    features0, partial = partner_logits(features0, sizes0, weights)
     received = swap(partial, "fsdp", 1)
     own = own_logits(normed0, weights, partial)
-    features1b = swap(after(sent1b, own), "fsdp", 1)
+    features1b = swap(after(sent1b, partial), "fsdp", 1)
     refer_log, whole = reference_logs(normed0, stacks, features1a)
     grads = gradients(own, received, refer_log, targets, valid, 0)
     partner_grads = swap(grads, "fsdp", 1)
@@ -701,8 +737,9 @@
 
     quarter, pieces = chip_quarters(sent, kept)
     quarter = quarter_sum(quarter, pieces)
-    second = pair_sum(quarter, swap(quarter, "replica", CORES))
-    means = [gathered_quarters(m) for m in (first, second)]
+    first = quarters_along(first)
+    second = pair_sum(quarter, swap(quarter, "replica", CORES), first[1], first[2])
+    means = [gathered_quarters(m) for m in (first, quarters_along(second))]
     new_outer, new_inner = settled(outer_head, inner, means, plan)
     return (new_outer, new_inner[None])
 

time: 105 us -> 101 us (0.962)
  Pallas kernels: 17.2 us -> 14.6 us
  waiting for transfers between devices: 38.8 us -> 37.2 us
    pallas_call x27, Pallas kernels: 17.2 us -> 14.6 us  [call(): pl.pallas_call(kernel, out_shape=out_shape, in_specs=in_specs, out_specs=...]
    squeeze x0 -> x1, local copies, waits for them, and re-layouts: none -> 1.71 us  [shards_pair(): normed0, *sent0 = normalized(hidden[0], sizes0, (), (ref_head,))]
    ppermute x38, waiting for transfers between devices: 38.8 us -> 37.2 us  [swap(): return lax.ppermute(value, axis, [(i, i ^ mask) for i in range(size)])]
  transfers between devices with their start and end apart: 38 -> 38, of which waited for: 21 -> 20; matrix products, arithmetic and copies ran while one was open for 0% -> 0% of each run, Pallas kernels for 9% -> 8%
where the time goes in v5:
time: 101 us
  starting transfers between devices  46.7 us (46%)
  waiting for transfers between devices  37.2 us (37%)
  Pallas kernels  14.6 us (14%)
  local copies, waits for them, and re-layouts  1.74 us (2%)
    ppermute x38, starting transfers between devices, swap(): return lax.ppermute(value, axis, [(i, i ^ mask) for i in range(size)])  46.7 us
    ppermute x38, waiting for transfers between devices, swap(): return lax.ppermute(value, axis, [(i, i ^ mask) for i in range(size)])  37.2 us
    pallas_call x27, Pallas kernels, call(): pl.pallas_call(kernel, out_shape=out_shape, in_specs=in_specs, out_specs=...  14.6 us
  transfers between devices with their start and end apart: 38, of which 20 were waited for; matrix products, arithmetic and copies ran while one was open for 0% of the time, Pallas kernels for 8%

profile of v5, /device:TPU:0, one launch (start us, length us, event | category | flops | bytes accessed | tf_op | source)
XLA Modules:
  0.0 101.2 jit_solution(17358774912275750622)
XLA Ops:
  0.6 1.7 %slice_bitcast_fusion = (bf16[256,2048]{1,0:T(8,128)(2,1)S(1)}, bf16[256,2048]{1,0:T(8,128)(2,1)S(1)}) fusion(bf16[2,256,2048]{2,1,0:T(8,128)(2,1)} %param.7), kind=kLoop, calls=%fused_computation | loop fusion | bytes 4194304 | tf_op jit(solution)/shard_map/squeeze | solution.py:706
  2.8 3.0 %collective-permute-start = (bf16[96,1024]{1,0:T(8,128)(2,1)S(1)}, bf16[96,1024]{1,0:T(8,128)(2,1)S(1)}, u32[]{:S(2)}, u32[]{:S(2)}) collective-permute-start(bf16[96,1024]{1,0:T(8,128)(2,1)S(1)} %get-tuple-element.34.refs_1_), channel_id=1, source_target_pairs={{0,1},{1,0},{2,3},{3,2},{4,5},{5,4},{6,7},{7,6},{8,9},{9,8},{10,11... | collective-permute-start | bytes 589832 | tf_op jit(solution)/shard_map/ppermute | solution.py:31
  6.4 4.1 %collective-permute-start.5 = (bf16[64,512]{1,0:T(8,128)(2,1)S(1)}, bf16[64,512]{1,0:T(8,128)(2,1)S(1)}, u32[]{:S(2)}, u32[]{:S(2)}) collective-permute-start(bf16[64,512]{1,0:T(8,128)(2,1)S(1)} %get-tuple-element.41.refs_0_), channel_id=1, source_target_pairs={{0,24},{2,26},{4,28},{6,30},{8,16},{10,18},{12,20},{14,22},{16,8},... | collective-permute-start | bytes 196616 | tf_op jit(solution)/shard_map/ppermute | solution.py:31
  10.5 0.6 collective-permute-start.3
  11.6 4.2 %collective-permute-start.11 = (bf16[64,512]{1,0:T(8,128)(2,1)S(1)}, bf16[64,512]{1,0:T(8,128)(2,1)S(1)}, u32[]{:S(2)}, u32[]{:S(2)}) collective-permute-start(bf16[64,512]{1,0:T(8,128)(2,1)S(1)} %shard_map.92.refs_0_), channel_id=1, source_target_pairs={{0,24},{2,26},{4,28},{6,30},{8,16},{10,18},{12,20},{14,22},{16,8},... | collective-permute-start | bytes 196616 | tf_op jit(solution)/shard_map/ppermute | solution.py:31
  15.7 2.9 %collective-permute-done.4.refs_2_ = bf16[64,512]{1,0:T(8,128)(2,1)S(1)} collective-permute-done((bf16[64,512]{1,0:T(8,128)(2,1)S(1)}, bf16[64,512]{1,0:T(8,128)(2,1)S(1)}, u32[]{:S(2)}, u32[]{:S(2)}) %collective-permute-start.4) | collective-permute-done | bytes 65568 | tf_op jit(solution)/shard_map/ppermute | solution.py:31
  18.6 1.5 %collective-permute-start.15 = (bf16[128,1024]{1,0:T(8,128)(2,1)S(1)}, bf16[128,1024]{1,0:T(8,128)(2,1)S(1)}, u32[]{:S(2)}, u32[]{:S(2)}) collective-permute-start(bf16[128,1024]{1,0:T(8,128)(2,1)S(1)} %get-tuple-element.42), channel_id=1, source_target_pairs={{0,1},{1,0},{2,3},{3,2},{4,5},{5,4},{6,7},{7,6},{8,9},{9,8},{10,11... | collective-permute-start | bytes 786440 | tf_op jit(solution)/shard_map/ppermute | solution.py:31
  20.5 1.6 %collective-permute-start.6 = (bf16[256,512]{1,0:T(8,128)(2,1)S(1)}, bf16[256,512]{1,0:T(8,128)(2,1)S(1)}, u32[]{:S(2)}, u32[]{:S(2)}) collective-permute-start(bf16[256,512]{1,0:T(8,128)(2,1)S(1)} %shard_map.91.refs_0_), channel_id=1, source_target_pairs={{0,4},{2,6},{4,0},{6,2},{8,12},{10,14},{12,8},{14,10},{16,20},{18,... | collective-permute-start | bytes 786440 | tf_op jit(solution)/shard_map/ppermute | solution.py:31
  22.1 0.8 collective-permute-done.9.refs_1_
  23.3 1.6 %collective-permute-start.12 = (bf16[256,512]{1,0:T(8,128)(2,1)S(1)}, bf16[256,512]{1,0:T(8,128)(2,1)S(1)}, u32[]{:S(2)}, u32[]{:S(2)}) collective-permute-start(bf16[256,512]{1,0:T(8,128)(2,1)S(1)} %shard_map.93.refs_4_), channel_id=1, source_target_pairs={{0,4},{2,6},{4,0},{6,2},{8,12},{10,14},{12,8},{14,10},{16,20},{18,... | collective-permute-start | bytes 786440 | tf_op jit(solution)/shard_map/ppermute | solution.py:31
  25.7 1.6 %collective-permute-start.2 = (s32[264,256]{1,0:T(8,128)S(1)}, s32[264,256]{1,0:T(8,128)S(1)}, u32[]{:S(2)}, u32[]{:S(2)}) collective-permute-start(s32[264,256]{1,0:T(8,128)S(1)} %get-tuple-element.40.refs_0_.refs_1_), channel_id=1, source_target_pairs={{0,1},{1,0},{2,3},{3,2},{4,5},{5,4},{6,7},{7,6},{8,9},{9,8},{10,11... | collective-permute-start | bytes 811016 | tf_op jit(solution)/shard_map/ppermute | solution.py:31
  27.8 1.2 %collective-permute-done.6.refs_1_ = bf16[256,512]{1,0:T(8,128)(2,1)S(1)} collective-permute-done((bf16[256,512]{1,0:T(8,128)(2,1)S(1)}, bf16[256,512]{1,0:T(8,128)(2,1)S(1)}, u32[]{:S(2)}, u32[]{:S(2)}) %collective-permute-start.6) | collective-permute-done | bytes 262176 | tf_op jit(solution)/shard_map/ppermute | solution.py:31
  28.9 2.8 %collective-permute-done.12.refs_5_ = bf16[256,512]{1,0:T(8,128)(2,1)S(1)} collective-permute-done((bf16[256,512]{1,0:T(8,128)(2,1)S(1)}, bf16[256,512]{1,0:T(8,128)(2,1)S(1)}, u32[]{:S(2)}, u32[]{:S(2)}) %collective-permute-start.12) | collective-permute-done | bytes 262176 | tf_op jit(solution)/shard_map/ppermute | solution.py:31
  32.2 1.4 %collective-permute-start.16 = (bf16[128,1024]{1,0:T(8,128)(2,1)S(1)}, bf16[128,1024]{1,0:T(8,128)(2,1)S(1)}, u32[]{:S(2)}, u32[]{:S(2)}) collective-permute-start(bf16[128,1024]{1,0:T(8,128)(2,1)S(1)} %shard_map.96), channel_id=1, source_target_pairs={{0,1},{1,0},{2,3},{3,2},{4,5},{5,4},{6,7},{7,6},{8,9},{9,8},{10,11... | collective-permute-start | bytes 786440 | tf_op jit(solution)/shard_map/ppermute | solution.py:31
  33.6 1.0 %shard_map.94 = (f32[256,512]{1,0:T(8,128)S(1)}, bf16[2048,512]{1,0:T(8,128)(2,1)S(1)}) custom-call(bf16[256,2048]{1,0:T(8,128)(2,1)S(1)} %get-tuple-element.38.normed_ref, bf16[256,512]{1,0:T(8,128)(2,1)S(1)} %shard_map.91.refs_0_, bf16[256,512]{1,0:T(8,128)(2,1)S(1)} %collective-permute-done.6.refs_1_, ...), custom_call_target="tpu_custom_call" | custom-call | flops 1000 | bytes 1000 | tf_op jit(solution)/shard_map/pallas_call | solution.py:195
  34.7 0.6 shard_map.95.grads_ref
  35.4 1.0 %collective-permute-start.17 = (bf16[256,512]{1,0:T(8,128)(2,1)S(1)}, bf16[256,512]{1,0:T(8,128)(2,1)S(1)}, u32[]{:S(2)}, u32[]{:S(2)}) collective-permute-start(bf16[256,512]{1,0:T(8,128)(2,1)S(1)} %shard_map.95.grads_ref), channel_id=1, source_target_pairs={{0,1},{1,0},{2,3},{3,2},{4,5},{5,4},{6,7},{7,6},{8,9},{9,8},{10,11... | collective-permute-start | bytes 786440 | tf_op jit(solution)/shard_map/ppermute | solution.py:31
  36.4 5.0 %collective-permute-done.16.refs_0_.refs_1_ = bf16[128,1024]{1,0:T(8,128)(2,1)S(1)} collective-permute-done((bf16[128,1024]{1,0:T(8,128)(2,1)S(1)}, bf16[128,1024]{1,0:T(8,128)(2,1)S(1)}, u32[]{:S(2)}, u32[]{:S(2)}) %collective-permute-start.16) | collective-permute-done | bytes 262176 | tf_op jit(solution)/shard_map/ppermute | solution.py:31
  41.9 0.9 shard_map.98.refs_2_.refer_ref
  42.8 3.8 %collective-permute-done.17.grads_ref = bf16[256,512]{1,0:T(8,128)(2,1)S(1)} collective-permute-done((bf16[256,512]{1,0:T(8,128)(2,1)S(1)}, bf16[256,512]{1,0:T(8,128)(2,1)S(1)}, u32[]{:S(2)}, u32[]{:S(2)}) %collective-permute-start.17) | collective-permute-done | bytes 262176 | tf_op jit(solution)/shard_map/ppermute | solution.py:31
  46.6 1.6 %shard_map.99 = (f32[1024,512]{1,0:T(8,128)S(1)}, f32[512,256]{1,0:T(8,128)S(1)}, f32[512,256]{1,0:T(8,128)S(1)}, bf16[256,1024]{1,0:T(8,128)(2,1)S(1)}, bf16[10...) custom-call(s32[2]{0:T(128)S(1)} %copy-done.5, f32[1024,512]{1,0:T(8,128)S(1)} %shard_map.97.refs_0_.inner_ref, ...), custom_call_target="tpu_custom_call" | custom-call | flops 1000 | bytes 1000 | tf_op jit(solution)/shard_map/pallas_call | solution.py:195
  48.4 1.4 %collective-permute-start.18 = (s32[264,256]{1,0:T(8,128)S(1)}, s32[264,256]{1,0:T(8,128)S(1)}, u32[]{:S(2)}, u32[]{:S(2)}) collective-permute-start(s32[264,256]{1,0:T(8,128)S(1)} %get-tuple-element.49), channel_id=1, source_target_pairs={{0,1},{1,0},{2,3},{3,2},{4,5},{5,4},{6,7},{7,6},{8,9},{9,8},{10,11... | collective-permute-start | bytes 811016 | tf_op jit(solution)/shard_map/ppermute | solution.py:31
  50.4 1.6 %collective-permute-start.20 = (s32[72,256]{1,0:T(8,128)S(1)}, s32[72,256]{1,0:T(8,128)S(1)}, u32[]{:S(2)}, u32[]{:S(2)}) collective-permute-start(s32[72,256]{1,0:T(8,128)S(1)} %get-tuple-element.52), channel_id=1, source_target_pairs={{0,16},{2,18},{4,20},{6,22},{8,24},{10,26},{12,28},{14,30},{16,0},... | collective-permute-start | bytes 221192 | tf_op jit(solution)/shard_map/ppermute | solution.py:31
  52.0 1.6 %collective-permute-start.21 = (s32[72,256]{1,0:T(8,128)S(1)}, s32[72,256]{1,0:T(8,128)S(1)}, u32[]{:S(2)}, u32[]{:S(2)}) collective-permute-start(s32[72,256]{1,0:T(8,128)S(1)} %get-tuple-element.53), channel_id=1, source_target_pairs={{0,8},{2,10},{4,12},{6,14},{8,0},{10,2},{12,4},{14,6},{16,24},{18,... | collective-permute-start | bytes 221192 | tf_op jit(solution)/shard_map/ppermute | solution.py:31
  53.6 1.2 %collective-permute-start.22 = (s32[72,256]{1,0:T(8,128)S(1)}, s32[72,256]{1,0:T(8,128)S(1)}, u32[]{:S(2)}, u32[]{:S(2)}) collective-permute-start(s32[72,256]{1,0:T(8,128)S(1)} %get-tuple-element.54), channel_id=1, source_target_pairs={{0,24},{2,26},{4,28},{6,30},{8,16},{10,18},{12,20},{14,22},{16,8},... | collective-permute-start | bytes 221192 | tf_op jit(solution)/shard_map/ppermute | solution.py:31
  55.3 2.0 %collective-permute-done.18.received_ref = s32[264,256]{1,0:T(8,128)S(1)} collective-permute-done((s32[264,256]{1,0:T(8,128)S(1)}, s32[264,256]{1,0:T(8,128)S(1)}, u32[]{:S(2)}, u32[]{:S(2)}) %collective-permute-start.18) | collective-permute-done | bytes 270368 | tf_op jit(solution)/shard_map/ppermute | solution.py:31
  57.3 0.8 collective-permute-done.20.refs_0_
  58.0 1.8 %collective-permute-done.22.refs_2_ = s32[72,256]{1,0:T(8,128)S(1)} collective-permute-done((s32[72,256]{1,0:T(8,128)S(1)}, s32[72,256]{1,0:T(8,128)S(1)}, u32[]{:S(2)}, u32[]{:S(2)}) %collective-permute-start.22) | collective-permute-done | bytes 73760 | tf_op jit(solution)/shard_map/ppermute | solution.py:31
  59.8 0.6 shard_map.102.grads_ref
  60.5 1.1 %collective-permute-start.23 = (bf16[256,512]{1,0:T(8,128)(2,1)S(1)}, bf16[256,512]{1,0:T(8,128)(2,1)S(1)}, u32[]{:S(2)}, u32[]{:S(2)}) collective-permute-start(bf16[256,512]{1,0:T(8,128)(2,1)S(1)} %shard_map.102.grads_ref), channel_id=1, source_target_pairs={{0,1},{1,0},{2,3},{3,2},{4,5},{5,4},{6,7},{7,6},{8,9},{9,8},{10,11... | collective-permute-start | bytes 786440 | tf_op jit(solution)/shard_map/ppermute | solution.py:31
  62.2 1.6 %collective-permute-start.24 = (s32[72,256]{1,0:T(8,128)S(1)}, s32[72,256]{1,0:T(8,128)S(1)}, u32[]{:S(2)}, u32[]{:S(2)}) collective-permute-start(s32[72,256]{1,0:T(8,128)S(1)} %shard_map.104.one_ref), channel_id=1, source_target_pairs={{0,4},{2,6},{4,0},{6,2},{8,12},{10,14},{12,8},{14,10},{16,20},{18,... | collective-permute-start | bytes 221192 | tf_op jit(solution)/shard_map/ppermute | solution.py:31
  63.8 2.8 %collective-permute-done.24.other_ref = s32[72,256]{1,0:T(8,128)S(1)} collective-permute-done((s32[72,256]{1,0:T(8,128)S(1)}, s32[72,256]{1,0:T(8,128)S(1)}, u32[]{:S(2)}, u32[]{:S(2)}) %collective-permute-start.24) | collective-permute-done | bytes 73760 | tf_op jit(solution)/shard_map/ppermute | solution.py:31
  66.8 0.7 collective-permute-done.23.grads_ref
  67.5 1.2 %shard_map.106 = (f32[1024,512]{1,0:T(8,128)S(1)}, f32[512,256]{1,0:T(8,128)S(1)}, f32[512,256]{1,0:T(8,128)S(1)}) custom-call(s32[2]{0:T(128)S(1)} %copy-done.5, f32[1024,512]{1,0:T(8,128)S(1)} %shard_map.103.refs_3_.inner_ref, bf16[256,1024]{1,0:T(8,128)(2,1)S(1)} %get-tuple-element.55.features_ref, ...), custom_call_target="tpu_custom_call" | custom-call | flops 1000 | bytes 1000 | tf_op jit(solution)/shard_map/pallas_call | solution.py:195
  68.8 1.9 %collective-permute-done.29.received_ref = f32[512,256]{1,0:T(8,128)S(1)} collective-permute-done((f32[512,256]{1,0:T(8,128)S(1)}, f32[512,256]{1,0:T(8,128)S(1)}, u32[]{:S(2)}, u32[]{:S(2)}) %collective-permute-start.29) | collective-permute-done | bytes 524320 | tf_op jit(solution)/shard_map/ppermute | solution.py:31
  70.8 3.5 %collective-permute-start.30 = (s32[72,256]{1,0:T(8,128)S(1)}, s32[72,256]{1,0:T(8,128)S(1)}, u32[]{:S(2)}, u32[]{:S(2)}) collective-permute-start(s32[72,256]{1,0:T(8,128)S(1)} %get-tuple-element.61), channel_id=1, source_target_pairs={{0,16},{2,18},{4,20},{6,22},{8,24},{10,26},{12,28},{14,30},{16,0},... | collective-permute-start | bytes 221192 | tf_op jit(solution)/shard_map/ppermute | solution.py:31
  74.4 1.5 %collective-permute-start.32 = (s32[72,256]{1,0:T(8,128)S(1)}, s32[72,256]{1,0:T(8,128)S(1)}, u32[]{:S(2)}, u32[]{:S(2)}) collective-permute-start(s32[72,256]{1,0:T(8,128)S(1)} %get-tuple-element.63), channel_id=1, source_target_pairs={{0,24},{2,26},{4,28},{6,30},{8,16},{10,18},{12,20},{14,22},{16,8},... | collective-permute-start | bytes 221192 | tf_op jit(solution)/shard_map/ppermute | solution.py:31
  75.9 1.9 %collective-permute-start.26 = (s32[72,256]{1,0:T(8,128)S(1)}, s32[72,256]{1,0:T(8,128)S(1)}, u32[]{:S(2)}, u32[]{:S(2)}) collective-permute-start(s32[72,256]{1,0:T(8,128)S(1)} %shard_map.105.refs_0_), channel_id=1, source_target_pairs={{0,16},{2,18},{4,20},{6,22},{8,24},{10,26},{12,28},{14,30},{16,0},... | collective-permute-start | bytes 221192 | tf_op jit(solution)/shard_map/ppermute | solution.py:31
  77.9 0.9 collective-permute-start.25
  78.9 2.9 %collective-permute-done.31.refs_1_ = s32[72,256]{1,0:T(8,128)S(1)} collective-permute-done((s32[72,256]{1,0:T(8,128)S(1)}, s32[72,256]{1,0:T(8,128)S(1)}, u32[]{:S(2)}, u32[]{:S(2)}) %collective-permute-start.31) | collective-permute-done | bytes 73760 | tf_op jit(solution)/shard_map/ppermute | solution.py:31
  81.9 1.2 %collective-permute-start.33 = (s32[72,256]{1,0:T(8,128)S(1)}, s32[72,256]{1,0:T(8,128)S(1)}, u32[]{:S(2)}, u32[]{:S(2)}) collective-permute-start(s32[72,256]{1,0:T(8,128)S(1)} %shard_map.109.one_ref), channel_id=1, source_target_pairs={{0,4},{2,6},{4,0},{6,2},{8,12},{10,14},{12,8},{14,10},{16,20},{18,... | collective-permute-start | bytes 221192 | tf_op jit(solution)/shard_map/ppermute | solution.py:31
  83.1 3.0 %collective-permute-start.27 = (s32[72,256]{1,0:T(8,128)S(1)}, s32[72,256]{1,0:T(8,128)S(1)}, u32[]{:S(2)}, u32[]{:S(2)}) collective-permute-start(s32[72,256]{1,0:T(8,128)S(1)} %shard_map.105.refs_0_), channel_id=1, source_target_pairs={{0,24},{2,26},{4,28},{6,30},{8,16},{10,18},{12,20},{14,22},{16,8},... | collective-permute-start | bytes 221192 | tf_op jit(solution)/shard_map/ppermute | solution.py:31
  86.4 2.7 %collective-permute-start.36 = (s32[72,256]{1,0:T(8,128)S(1)}, s32[72,256]{1,0:T(8,128)S(1)}, u32[]{:S(2)}, u32[]{:S(2)}) collective-permute-start(s32[72,256]{1,0:T(8,128)S(1)} %shard_map.110.refs_0_), channel_id=1, source_target_pairs={{0,24},{2,26},{4,28},{6,30},{8,16},{10,18},{12,20},{14,22},{16,8},... | collective-permute-start | bytes 221192 | tf_op jit(solution)/shard_map/ppermute | solution.py:31
  89.1 1.2 %collective-permute-start.35 = (s32[72,256]{1,0:T(8,128)S(1)}, s32[72,256]{1,0:T(8,128)S(1)}, u32[]{:S(2)}, u32[]{:S(2)}) collective-permute-start(s32[72,256]{1,0:T(8,128)S(1)} %shard_map.110.refs_0_), channel_id=1, source_target_pairs={{0,16},{2,18},{4,20},{6,22},{8,24},{10,26},{12,28},{14,30},{16,0},... | collective-permute-start | bytes 221192 | tf_op jit(solution)/shard_map/ppermute | solution.py:31
  91.4 1.4 %collective-permute-done.36.refs_3_ = s32[72,256]{1,0:T(8,128)S(1)} collective-permute-done((s32[72,256]{1,0:T(8,128)S(1)}, s32[72,256]{1,0:T(8,128)S(1)}, u32[]{:S(2)}, u32[]{:S(2)}) %collective-permute-start.36) | collective-permute-done | bytes 73760 | tf_op jit(solution)/shard_map/ppermute | solution.py:31
  92.8 3.6 %collective-permute-done.35.refs_2_ = s32[72,256]{1,0:T(8,128)S(1)} collective-permute-done((s32[72,256]{1,0:T(8,128)S(1)}, s32[72,256]{1,0:T(8,128)S(1)}, u32[]{:S(2)}, u32[]{:S(2)}) %collective-permute-start.35) | collective-permute-done | bytes 73760 | tf_op jit(solution)/shard_map/ppermute | solution.py:31
  96.9 1.6 %collective-permute-done.37.other1 = s32[288,256]{1,0:T(8,128)S(1)} collective-permute-done((s32[288,256]{1,0:T(8,128)S(1)}, s32[288,256]{1,0:T(8,128)S(1)}, u32[]{:S(2)}, u32[]{:S(2)}) %collective-permute-start.37) | collective-permute-done | bytes 294944 | tf_op jit(solution)/shard_map/ppermute | solution.py:31
  98.4 2.8 %shard_map.112 = (f32[1024,512]{1,0:T(8,128)}, f32[1024,512]{1,0:T(8,128)}) custom-call(s32[2]{0:T(128)S(1)} %copy-done.5, f32[1024,512]{1,0:T(8,128)S(1)} %copy-done, f32[1024,512]{1,0:T(8,128)S(1)} %get-tuple-element.57.inner_ref, s32[288,256]{1,0:T(8,128)S(1)} %shard_map.107.own0, s32[288,256]{1,0:T(8,128)S(1)} %collective-permute-done.28.other0, ...), custom_call_target="tpu_custom_call" | custom-call | flops 1000 | bytes 1000 | tf_op jit(solution)/shard_map/pallas_call | solution.py:195
  (68 shorter events, 8.4 us)
Async XLA Ops:
  0.6 1.7 %copy-start.2 = (bf16[64,512]{1,0:T(8,128)(2,1)S(1)}, bf16[64,512]{1,0:T(8,128)(2,1)}, u32[]{:S(2)}) copy-start(bf16[64,512]{1,0:T(8,128)(2,1)} %refs_0_.3) | copy-start | bytes 196612
  2.4 22.5 %copy-start = (f32[1024,512]{1,0:T(8,128)S(1)}, f32[1024,512]{1,0:T(8,128)}, u32[]{:S(2)}) copy-start(f32[1024,512]{1,0:T(8,128)} %outer_ref.7) | copy-start | bytes 6291460
  2.4 22.5 %copy-start.1 = (bf16[1,1024,512]{2,1,0:T(8,128)(2,1)S(1)}, bf16[1,1024,512]{2,1,0:T(8,128)(2,1)}, u32[]{:S(2)}) copy-start(bf16[1,1024,512]{2,1,0:T(8,128)(2,1)} %drift_ref.1) | copy-start | bytes 3145732
  2.8 8.7 %collective-permute-start = (bf16[96,1024]{1,0:T(8,128)(2,1)S(1)}, bf16[96,1024]{1,0:T(8,128)(2,1)S(1)}, u32[]{:S(2)}, u32[]{:S(2)}) collective-permute-start(bf16[96,1024]{1,0:T(8,128)(2,1)S(1)} %get-tuple-element.34.refs_1_), channel_id=1, source_target_pairs={{0,1},{1,0},{2,3},{3,2},{4,5},{5,4},{6,7},{7,6},{8,9},{9,8},{10,11... | collective-permute-start | bytes 589832 | tf_op jit(solution)/shard_map/ppermute | solution.py:31
  5.8 19.3 %collective-permute-start.1 = (bf16[192,1024]{1,0:T(8,128)(2,1)S(1)}, bf16[192,1024]{1,0:T(8,128)(2,1)S(1)}, u32[]{:S(2)}, u32[]{:S(2)}) collective-permute-start(bf16[192,1024]{1,0:T(8,128)(2,1)S(1)} %get-tuple-element.35.refs_2_), channel_id=1, source_target_pairs={{0,1},{1,0},{2,3},{3,2},{4,5},{5,4},{6,7},{7,6},{8,9},{9,8},{10,11... | collective-permute-start | bytes 1179656 | tf_op jit(solution)/shard_map/ppermute | solution.py:31
  6.4 9.4 %collective-permute-start.5 = (bf16[64,512]{1,0:T(8,128)(2,1)S(1)}, bf16[64,512]{1,0:T(8,128)(2,1)S(1)}, u32[]{:S(2)}, u32[]{:S(2)}) collective-permute-start(bf16[64,512]{1,0:T(8,128)(2,1)S(1)} %get-tuple-element.41.refs_0_), channel_id=1, source_target_pairs={{0,24},{2,26},{4,28},{6,30},{8,16},{10,18},{12,20},{14,22},{16,8},... | collective-permute-start | bytes 196616 | tf_op jit(solution)/shard_map/ppermute | solution.py:31
  10.5 8.1 %collective-permute-start.4 = (bf16[64,512]{1,0:T(8,128)(2,1)S(1)}, bf16[64,512]{1,0:T(8,128)(2,1)S(1)}, u32[]{:S(2)}, u32[]{:S(2)}) collective-permute-start(bf16[64,512]{1,0:T(8,128)(2,1)S(1)} %get-tuple-element.41.refs_0_), channel_id=1, source_target_pairs={{0,16},{2,18},{4,20},{6,22},{8,24},{10,26},{12,28},{14,30},{16,0},... | collective-permute-start | bytes 196616 | tf_op jit(solution)/shard_map/ppermute | solution.py:31
  10.5 8.2 %collective-permute-start.3 = (bf16[64,512]{1,0:T(8,128)(2,1)S(1)}, bf16[64,512]{1,0:T(8,128)(2,1)S(1)}, u32[]{:S(2)}, u32[]{:S(2)}) collective-permute-start(bf16[64,512]{1,0:T(8,128)(2,1)S(1)} %get-tuple-element.41.refs_0_), channel_id=1, source_target_pairs={{0,8},{2,10},{4,12},{6,14},{8,0},{10,2},{12,4},{14,6},{16,24},{18,... | collective-permute-start | bytes 196616 | tf_op jit(solution)/shard_map/ppermute | solution.py:31
  11.6 8.9 %collective-permute-start.11 = (bf16[64,512]{1,0:T(8,128)(2,1)S(1)}, bf16[64,512]{1,0:T(8,128)(2,1)S(1)}, u32[]{:S(2)}, u32[]{:S(2)}) collective-permute-start(bf16[64,512]{1,0:T(8,128)(2,1)S(1)} %shard_map.92.refs_0_), channel_id=1, source_target_pairs={{0,24},{2,26},{4,28},{6,30},{8,16},{10,18},{12,20},{14,22},{16,8},... | collective-permute-start | bytes 196616 | tf_op jit(solution)/shard_map/ppermute | solution.py:31
  15.7 6.4 %collective-permute-start.10 = (bf16[64,512]{1,0:T(8,128)(2,1)S(1)}, bf16[64,512]{1,0:T(8,128)(2,1)S(1)}, u32[]{:S(2)}, u32[]{:S(2)}) collective-permute-start(bf16[64,512]{1,0:T(8,128)(2,1)S(1)} %shard_map.92.refs_0_), channel_id=1, source_target_pairs={{0,16},{2,18},{4,20},{6,22},{8,24},{10,26},{12,28},{14,30},{16,0},... | collective-permute-start | bytes 196616 | tf_op jit(solution)/shard_map/ppermute | solution.py:31
  18.6 4.3 %collective-permute-start.9 = (bf16[64,512]{1,0:T(8,128)(2,1)S(1)}, bf16[64,512]{1,0:T(8,128)(2,1)S(1)}, u32[]{:S(2)}, u32[]{:S(2)}) collective-permute-start(bf16[64,512]{1,0:T(8,128)(2,1)S(1)} %shard_map.92.refs_0_), channel_id=1, source_target_pairs={{0,8},{2,10},{4,12},{6,14},{8,0},{10,2},{12,4},{14,6},{16,24},{18,... | collective-permute-start | bytes 196616 | tf_op jit(solution)/shard_map/ppermute | solution.py:31
  18.6 8.6 %collective-permute-start.15 = (bf16[128,1024]{1,0:T(8,128)(2,1)S(1)}, bf16[128,1024]{1,0:T(8,128)(2,1)S(1)}, u32[]{:S(2)}, u32[]{:S(2)}) collective-permute-start(bf16[128,1024]{1,0:T(8,128)(2,1)S(1)} %get-tuple-element.42), channel_id=1, source_target_pairs={{0,1},{1,0},{2,3},{3,2},{4,5},{5,4},{6,7},{7,6},{8,9},{9,8},{10,11... | collective-permute-start | bytes 786440 | tf_op jit(solution)/shard_map/ppermute | solution.py:31
  20.5 8.4 %collective-permute-start.6 = (bf16[256,512]{1,0:T(8,128)(2,1)S(1)}, bf16[256,512]{1,0:T(8,128)(2,1)S(1)}, u32[]{:S(2)}, u32[]{:S(2)}) collective-permute-start(bf16[256,512]{1,0:T(8,128)(2,1)S(1)} %shard_map.91.refs_0_), channel_id=1, source_target_pairs={{0,4},{2,6},{4,0},{6,2},{8,12},{10,14},{12,8},{14,10},{16,20},{18,... | collective-permute-start | bytes 786440 | tf_op jit(solution)/shard_map/ppermute | solution.py:31
  23.3 8.5 %collective-permute-start.12 = (bf16[256,512]{1,0:T(8,128)(2,1)S(1)}, bf16[256,512]{1,0:T(8,128)(2,1)S(1)}, u32[]{:S(2)}, u32[]{:S(2)}) collective-permute-start(bf16[256,512]{1,0:T(8,128)(2,1)S(1)} %shard_map.93.refs_4_), channel_id=1, source_target_pairs={{0,4},{2,6},{4,0},{6,2},{8,12},{10,14},{12,8},{14,10},{16,20},{18,... | collective-permute-start | bytes 786440 | tf_op jit(solution)/shard_map/ppermute | solution.py:31
  25.7 9.0 %collective-permute-start.2 = (s32[264,256]{1,0:T(8,128)S(1)}, s32[264,256]{1,0:T(8,128)S(1)}, u32[]{:S(2)}, u32[]{:S(2)}) collective-permute-start(s32[264,256]{1,0:T(8,128)S(1)} %get-tuple-element.40.refs_0_.refs_1_), channel_id=1, source_target_pairs={{0,1},{1,0},{2,3},{3,2},{4,5},{5,4},{6,7},{7,6},{8,9},{9,8},{10,11... | collective-permute-start | bytes 811016 | tf_op jit(solution)/shard_map/ppermute | solution.py:31
  27.3 5.0 %collective-permute-start.7 = (bf16[256,512]{1,0:T(8,128)(2,1)S(1)}, bf16[256,512]{1,0:T(8,128)(2,1)S(1)}, u32[]{:S(2)}, u32[]{:S(2)}) collective-permute-start(bf16[256,512]{1,0:T(8,128)(2,1)S(1)} %shard_map.91.refs_0_), channel_id=1, source_target_pairs={{0,2},{2,0},{4,6},{6,4},{8,10},{10,8},{12,14},{14,12},{16,18},{18,... | collective-permute-start | bytes 786440 | tf_op jit(solution)/shard_map/ppermute | solution.py:31
  27.3 6.4 %collective-permute-start.13 = (bf16[256,512]{1,0:T(8,128)(2,1)S(1)}, bf16[256,512]{1,0:T(8,128)(2,1)S(1)}, u32[]{:S(2)}, u32[]{:S(2)}) collective-permute-start(bf16[256,512]{1,0:T(8,128)(2,1)S(1)} %shard_map.93.refs_4_), channel_id=1, source_target_pairs={{0,2},{2,0},{4,6},{6,4},{8,10},{10,8},{12,14},{14,12},{16,18},{18,... | collective-permute-start | bytes 786440 | tf_op jit(solution)/shard_map/ppermute | solution.py:31
  28.9 4.7 %collective-permute-start.8 = (bf16[256,512]{1,0:T(8,128)(2,1)S(1)}, bf16[256,512]{1,0:T(8,128)(2,1)S(1)}, u32[]{:S(2)}, u32[]{:S(2)}) collective-permute-start(bf16[256,512]{1,0:T(8,128)(2,1)S(1)} %collective-permute-done.6.refs_1_), channel_id=1, source_target_pairs={{0,2},{2,0},{4,6},{6,4},{8,10},{10,8},{12,14},{14,12},{16,18},{18,... | collective-permute-start | bytes 786440 | tf_op jit(solution)/shard_map/ppermute | solution.py:31
  31.7 1.9 %collective-permute-start.14 = (bf16[256,512]{1,0:T(8,128)(2,1)S(1)}, bf16[256,512]{1,0:T(8,128)(2,1)S(1)}, u32[]{:S(2)}, u32[]{:S(2)}) collective-permute-start(bf16[256,512]{1,0:T(8,128)(2,1)S(1)} %collective-permute-done.12.refs_5_), channel_id=1, source_target_pairs={{0,2},{2,0},{4,6},{6,4},{8,10},{10,8},{12,14},{14,12},{16,18},{18,... | collective-permute-start | bytes 786440 | tf_op jit(solution)/shard_map/ppermute | solution.py:31
  32.2 2.5 %copy-start.3 = (s32[2,256]{1,0:T(2,128)S(1)}, s32[2,256]{1,0:T(2,128)}, u32[]{:S(2)}) copy-start(s32[2,256]{1,0:T(2,128)} %targets_ref.3) | copy-start | bytes 6148
  32.2 2.5 %copy-start.4 = (s32[2,256]{1,0:T(2,128)S(1)}, s32[2,256]{1,0:T(2,128)}, u32[]{:S(2)}) copy-start(s32[2,256]{1,0:T(2,128)} %valid_ref.3) | copy-start | bytes 6148
  32.2 9.2 %collective-permute-start.16 = (bf16[128,1024]{1,0:T(8,128)(2,1)S(1)}, bf16[128,1024]{1,0:T(8,128)(2,1)S(1)}, u32[]{:S(2)}, u32[]{:S(2)}) collective-permute-start(bf16[128,1024]{1,0:T(8,128)(2,1)S(1)} %shard_map.96), channel_id=1, source_target_pairs={{0,1},{1,0},{2,3},{3,2},{4,5},{5,4},{6,7},{7,6},{8,9},{9,8},{10,11... | collective-permute-start | bytes 786440 | tf_op jit(solution)/shard_map/ppermute | solution.py:31
  35.4 11.3 %collective-permute-start.17 = (bf16[256,512]{1,0:T(8,128)(2,1)S(1)}, bf16[256,512]{1,0:T(8,128)(2,1)S(1)}, u32[]{:S(2)}, u32[]{:S(2)}) collective-permute-start(bf16[256,512]{1,0:T(8,128)(2,1)S(1)} %shard_map.95.grads_ref), channel_id=1, source_target_pairs={{0,1},{1,0},{2,3},{3,2},{4,5},{5,4},{6,7},{7,6},{8,9},{9,8},{10,11... | collective-permute-start | bytes 786440 | tf_op jit(solution)/shard_map/ppermute | solution.py:31
  41.9 4.7 %copy-start.5 = (s32[2]{0:T(128)S(1)}, s32[2]{0:T(128)}, u32[]{:S(2)}) copy-start(s32[2]{0:T(128)} %plan_ref.5) | copy-start | bytes 28
  48.3 2.0 %collective-permute-start.19 = (f32[512,256]{1,0:T(8,128)S(1)}, f32[512,256]{1,0:T(8,128)S(1)}, u32[]{:S(2)}, u32[]{:S(2)}) collective-permute-start(f32[512,256]{1,0:T(8,128)S(1)} %get-tuple-element.51), channel_id=1, source_target_pairs={{0,2},{2,0},{4,6},{6,4},{8,10},{10,8},{12,14},{14,12},{16,18},{18,... | collective-permute-start | bytes 1572872 | tf_op jit(solution)/shard_map/ppermute | solution.py:31
  48.4 8.9 %collective-permute-start.18 = (s32[264,256]{1,0:T(8,128)S(1)}, s32[264,256]{1,0:T(8,128)S(1)}, u32[]{:S(2)}, u32[]{:S(2)}) collective-permute-start(s32[264,256]{1,0:T(8,128)S(1)} %get-tuple-element.49), channel_id=1, source_target_pairs={{0,1},{1,0},{2,3},{3,2},{4,5},{5,4},{6,7},{7,6},{8,9},{9,8},{10,11... | collective-permute-start | bytes 811016 | tf_op jit(solution)/shard_map/ppermute | solution.py:31
  50.4 7.6 %collective-permute-start.20 = (s32[72,256]{1,0:T(8,128)S(1)}, s32[72,256]{1,0:T(8,128)S(1)}, u32[]{:S(2)}, u32[]{:S(2)}) collective-permute-start(s32[72,256]{1,0:T(8,128)S(1)} %get-tuple-element.52), channel_id=1, source_target_pairs={{0,16},{2,18},{4,20},{6,22},{8,24},{10,26},{12,28},{14,30},{16,0},... | collective-permute-start | bytes 221192 | tf_op jit(solution)/shard_map/ppermute | solution.py:31
  52.0 6.0 %collective-permute-start.21 = (s32[72,256]{1,0:T(8,128)S(1)}, s32[72,256]{1,0:T(8,128)S(1)}, u32[]{:S(2)}, u32[]{:S(2)}) collective-permute-start(s32[72,256]{1,0:T(8,128)S(1)} %get-tuple-element.53), channel_id=1, source_target_pairs={{0,8},{2,10},{4,12},{6,14},{8,0},{10,2},{12,4},{14,6},{16,24},{18,... | collective-permute-start | bytes 221192 | tf_op jit(solution)/shard_map/ppermute | solution.py:31
  53.6 6.2 %collective-permute-start.22 = (s32[72,256]{1,0:T(8,128)S(1)}, s32[72,256]{1,0:T(8,128)S(1)}, u32[]{:S(2)}, u32[]{:S(2)}) collective-permute-start(s32[72,256]{1,0:T(8,128)S(1)} %get-tuple-element.54), channel_id=1, source_target_pairs={{0,24},{2,26},{4,28},{6,30},{8,16},{10,18},{12,20},{14,22},{16,8},... | collective-permute-start | bytes 221192 | tf_op jit(solution)/shard_map/ppermute | solution.py:31
  60.5 7.0 %collective-permute-start.23 = (bf16[256,512]{1,0:T(8,128)(2,1)S(1)}, bf16[256,512]{1,0:T(8,128)(2,1)S(1)}, u32[]{:S(2)}, u32[]{:S(2)}) collective-permute-start(bf16[256,512]{1,0:T(8,128)(2,1)S(1)} %shard_map.102.grads_ref), channel_id=1, source_target_pairs={{0,1},{1,0},{2,3},{3,2},{4,5},{5,4},{6,7},{7,6},{8,9},{9,8},{10,11... | collective-permute-start | bytes 786440 | tf_op jit(solution)/shard_map/ppermute | solution.py:31
  62.2 4.4 %collective-permute-start.24 = (s32[72,256]{1,0:T(8,128)S(1)}, s32[72,256]{1,0:T(8,128)S(1)}, u32[]{:S(2)}, u32[]{:S(2)}) collective-permute-start(s32[72,256]{1,0:T(8,128)S(1)} %shard_map.104.one_ref), channel_id=1, source_target_pairs={{0,4},{2,6},{4,0},{6,2},{8,12},{10,14},{12,8},{14,10},{16,20},{18,... | collective-permute-start | bytes 221192 | tf_op jit(solution)/shard_map/ppermute | solution.py:31
  68.7 2.0 %collective-permute-start.29 = (f32[512,256]{1,0:T(8,128)S(1)}, f32[512,256]{1,0:T(8,128)S(1)}, u32[]{:S(2)}, u32[]{:S(2)}) collective-permute-start(f32[512,256]{1,0:T(8,128)S(1)} %get-tuple-element.59), channel_id=1, source_target_pairs={{0,2},{2,0},{4,6},{6,4},{8,10},{10,8},{12,14},{14,12},{16,18},{18,... | collective-permute-start | bytes 1572872 | tf_op jit(solution)/shard_map/ppermute | solution.py:31
  70.8 8.0 %collective-permute-start.30 = (s32[72,256]{1,0:T(8,128)S(1)}, s32[72,256]{1,0:T(8,128)S(1)}, u32[]{:S(2)}, u32[]{:S(2)}) collective-permute-start(s32[72,256]{1,0:T(8,128)S(1)} %get-tuple-element.61), channel_id=1, source_target_pairs={{0,16},{2,18},{4,20},{6,22},{8,24},{10,26},{12,28},{14,30},{16,0},... | collective-permute-start | bytes 221192 | tf_op jit(solution)/shard_map/ppermute | solution.py:31
  74.4 7.4 %collective-permute-start.31 = (s32[72,256]{1,0:T(8,128)S(1)}, s32[72,256]{1,0:T(8,128)S(1)}, u32[]{:S(2)}, u32[]{:S(2)}) collective-permute-start(s32[72,256]{1,0:T(8,128)S(1)} %get-tuple-element.62), channel_id=1, source_target_pairs={{0,8},{2,10},{4,12},{6,14},{8,0},{10,2},{12,4},{14,6},{16,24},{18,... | collective-permute-start | bytes 221192 | tf_op jit(solution)/shard_map/ppermute | solution.py:31
  74.4 7.4 %collective-permute-start.32 = (s32[72,256]{1,0:T(8,128)S(1)}, s32[72,256]{1,0:T(8,128)S(1)}, u32[]{:S(2)}, u32[]{:S(2)}) collective-permute-start(s32[72,256]{1,0:T(8,128)S(1)} %get-tuple-element.63), channel_id=1, source_target_pairs={{0,24},{2,26},{4,28},{6,30},{8,16},{10,18},{12,20},{14,22},{16,8},... | collective-permute-start | bytes 221192 | tf_op jit(solution)/shard_map/ppermute | solution.py:31
  75.9 10.2 %collective-permute-start.26 = (s32[72,256]{1,0:T(8,128)S(1)}, s32[72,256]{1,0:T(8,128)S(1)}, u32[]{:S(2)}, u32[]{:S(2)}) collective-permute-start(s32[72,256]{1,0:T(8,128)S(1)} %shard_map.105.refs_0_), channel_id=1, source_target_pairs={{0,16},{2,18},{4,20},{6,22},{8,24},{10,26},{12,28},{14,30},{16,0},... | collective-permute-start | bytes 221192 | tf_op jit(solution)/shard_map/ppermute | solution.py:31
  77.9 8.3 %collective-permute-start.25 = (s32[72,256]{1,0:T(8,128)S(1)}, s32[72,256]{1,0:T(8,128)S(1)}, u32[]{:S(2)}, u32[]{:S(2)}) collective-permute-start(s32[72,256]{1,0:T(8,128)S(1)} %shard_map.105.refs_0_), channel_id=1, source_target_pairs={{0,8},{2,10},{4,12},{6,14},{8,0},{10,2},{12,4},{14,6},{16,24},{18,... | collective-permute-start | bytes 221192 | tf_op jit(solution)/shard_map/ppermute | solution.py:31
  81.9 4.4 %collective-permute-start.33 = (s32[72,256]{1,0:T(8,128)S(1)}, s32[72,256]{1,0:T(8,128)S(1)}, u32[]{:S(2)}, u32[]{:S(2)}) collective-permute-start(s32[72,256]{1,0:T(8,128)S(1)} %shard_map.109.one_ref), channel_id=1, source_target_pairs={{0,4},{2,6},{4,0},{6,2},{8,12},{10,14},{12,8},{14,10},{16,20},{18,... | collective-permute-start | bytes 221192 | tf_op jit(solution)/shard_map/ppermute | solution.py:31
  83.1 7.8 %collective-permute-start.27 = (s32[72,256]{1,0:T(8,128)S(1)}, s32[72,256]{1,0:T(8,128)S(1)}, u32[]{:S(2)}, u32[]{:S(2)}) collective-permute-start(s32[72,256]{1,0:T(8,128)S(1)} %shard_map.105.refs_0_), channel_id=1, source_target_pairs={{0,24},{2,26},{4,28},{6,30},{8,16},{10,18},{12,20},{14,22},{16,8},... | collective-permute-start | bytes 221192 | tf_op jit(solution)/shard_map/ppermute | solution.py:31
  86.4 6.4 %collective-permute-start.36 = (s32[72,256]{1,0:T(8,128)S(1)}, s32[72,256]{1,0:T(8,128)S(1)}, u32[]{:S(2)}, u32[]{:S(2)}) collective-permute-start(s32[72,256]{1,0:T(8,128)S(1)} %shard_map.110.refs_0_), channel_id=1, source_target_pairs={{0,24},{2,26},{4,28},{6,30},{8,16},{10,18},{12,20},{14,22},{16,8},... | collective-permute-start | bytes 221192 | tf_op jit(solution)/shard_map/ppermute | solution.py:31
  89.1 7.2 %collective-permute-start.35 = (s32[72,256]{1,0:T(8,128)S(1)}, s32[72,256]{1,0:T(8,128)S(1)}, u32[]{:S(2)}, u32[]{:S(2)}) collective-permute-start(s32[72,256]{1,0:T(8,128)S(1)} %shard_map.110.refs_0_), channel_id=1, source_target_pairs={{0,16},{2,18},{4,20},{6,22},{8,24},{10,26},{12,28},{14,30},{16,0},... | collective-permute-start | bytes 221192 | tf_op jit(solution)/shard_map/ppermute | solution.py:31
  90.4 6.0 %collective-permute-start.34 = (s32[72,256]{1,0:T(8,128)S(1)}, s32[72,256]{1,0:T(8,128)S(1)}, u32[]{:S(2)}, u32[]{:S(2)}) collective-permute-start(s32[72,256]{1,0:T(8,128)S(1)} %shard_map.110.refs_0_), channel_id=1, source_target_pairs={{0,8},{2,10},{4,12},{6,14},{8,0},{10,2},{12,4},{14,6},{16,24},{18,... | collective-permute-start | bytes 221192 | tf_op jit(solution)/shard_map/ppermute | solution.py:31
  91.3 5.6 %collective-permute-start.28 = (s32[288,256]{1,0:T(8,128)S(1)}, s32[288,256]{1,0:T(8,128)S(1)}, u32[]{:S(2)}, u32[]{:S(2)}) collective-permute-start(s32[288,256]{1,0:T(8,128)S(1)} %shard_map.107.own0), channel_id=1, source_target_pairs={{0,2},{2,0},{4,6},{6,4},{8,10},{10,8},{12,14},{14,12},{16,18},{18,... | collective-permute-start | bytes 884744 | tf_op jit(solution)/shard_map/ppermute | solution.py:31
  96.8 1.6 %collective-permute-start.37 = (s32[288,256]{1,0:T(8,128)S(1)}, s32[288,256]{1,0:T(8,128)S(1)}, u32[]{:S(2)}, u32[]{:S(2)}) collective-permute-start(s32[288,256]{1,0:T(8,128)S(1)} %shard_map.111.own1), channel_id=1, source_target_pairs={{0,2},{2,0},{4,6},{6,4},{8,10},{10,8},{12,14},{14,12},{16,18},{18,... | collective-permute-start | bytes 884744 | tf_op jit(solution)/shard_map/ppermute | solution.py:31

commit v6 on v5

--- a/solution.py
+++ b/solution.py
@@ -184,7 +184,7 @@
     return (new_outer, new_inner[None])
 
 
-MASKS = (2, 1, 3)
+MASKS = (3, 1, 2)
 VMEM = pl.BlockSpec(memory_space=pltpu.VMEM)
 SMEM = pl.BlockSpec(memory_space=pltpu.SMEM)
 ANY = pl.BlockSpec(memory_space=pl.ANY)
@@ -726,13 +726,13 @@
     received = swap(partial, "fsdp", 1)
     own = own_logits(normed1, weights)
     quarter, pieces = chip_quarters(sent, kept)
-    grads = gradients(own, received, refer_log, targets, valid, 1, *pieces)
+    grads = gradients(own, received, refer_log, targets, valid, 1, pieces[0])
     partner_grads = swap(grads, "fsdp", 1)
     halfway = own_update(inner, normed1, grads)
     quarter = quarter_sum(quarter, pieces, halfway)
     first = pair_sum(quarter, swap(quarter, "replica", CORES))
     inner, sent, kept = update(
-        halfway, features1, partner_grads, outer_head, plan, 1, replicas, (), (first,)
+        halfway, features1, partner_grads, outer_head, plan, 1, replicas, (), (quarter,)
     )
 
     quarter, pieces = chip_quarters(sent, kept)

time: 101 us -> 98.9 us (0.979)
  waiting for transfers between devices: 37.2 us -> 35 us
    ppermute x38, waiting for transfers between devices: 37.2 us -> 35 us  [swap(): return lax.ppermute(value, axis, [(i, i ^ mask) for i in range(size)])]
  transfers between devices with their start and end apart: 38 -> 38, of which waited for: 20 -> 18; matrix products, arithmetic and copies ran while one was open for 0% -> 0% of each run, Pallas kernels for 8% -> 8%
where the time goes in v6:
time: 98.9 us; the launch traced here: 98.7 us
  starting transfers between devices  46.4 us (47%)
  waiting for transfers between devices  35 us (35%)
  Pallas kernels  14.6 us (15%)
  local copies, waits for them, and re-layouts  1.74 us (2%)
    ppermute x38, starting transfers between devices, swap(): return lax.ppermute(value, axis, [(i, i ^ mask) for i in range(size)])  46.4 us
    ppermute x38, waiting for transfers between devices, swap(): return lax.ppermute(value, axis, [(i, i ^ mask) for i in range(size)])  35 us
    pallas_call x27, Pallas kernels, call(): pl.pallas_call(kernel, out_shape=out_shape, in_specs=in_specs, out_specs=...  14.6 us
  transfers between devices with their start and end apart: 38, of which 18 were waited for; matrix products, arithmetic and copies ran while one was open for 0% of the time, Pallas kernels for 8%

profile of v6, /device:TPU:0, one launch (start us, length us, event | category | flops | bytes accessed | tf_op | source)
XLA Modules:
  0.0 98.7 jit_solution(13085510392319051349)
XLA Ops:
  0.6 1.7 %slice_bitcast_fusion = (bf16[256,2048]{1,0:T(8,128)(2,1)S(1)}, bf16[256,2048]{1,0:T(8,128)(2,1)S(1)}) fusion(bf16[2,256,2048]{2,1,0:T(8,128)(2,1)} %param.7), kind=kLoop, calls=%fused_computation | loop fusion | bytes 4194304 | tf_op jit(solution)/shard_map/squeeze | solution.py:706
  2.8 3.0 %collective-permute-start = (bf16[96,1024]{1,0:T(8,128)(2,1)S(1)}, bf16[96,1024]{1,0:T(8,128)(2,1)S(1)}, u32[]{:S(2)}, u32[]{:S(2)}) collective-permute-start(bf16[96,1024]{1,0:T(8,128)(2,1)S(1)} %get-tuple-element.34.refs_1_), channel_id=1, source_target_pairs={{0,1},{1,0},{2,3},{3,2},{4,5},{5,4},{6,7},{7,6},{8,9},{9,8},{10,11... | collective-permute-start | bytes 589832 | tf_op jit(solution)/shard_map/ppermute | solution.py:31
  6.4 4.1 %collective-permute-start.5 = (bf16[64,512]{1,0:T(8,128)(2,1)S(1)}, bf16[64,512]{1,0:T(8,128)(2,1)S(1)}, u32[]{:S(2)}, u32[]{:S(2)}) collective-permute-start(bf16[64,512]{1,0:T(8,128)(2,1)S(1)} %get-tuple-element.41.refs_0_), channel_id=1, source_target_pairs={{0,24},{2,26},{4,28},{6,30},{8,16},{10,18},{12,20},{14,22},{16,8},... | collective-permute-start | bytes 196616 | tf_op jit(solution)/shard_map/ppermute | solution.py:31
  10.5 0.6 collective-permute-start.3
  11.6 4.2 %collective-permute-start.11 = (bf16[64,512]{1,0:T(8,128)(2,1)S(1)}, bf16[64,512]{1,0:T(8,128)(2,1)S(1)}, u32[]{:S(2)}, u32[]{:S(2)}) collective-permute-start(bf16[64,512]{1,0:T(8,128)(2,1)S(1)} %shard_map.92.refs_0_), channel_id=1, source_target_pairs={{0,24},{2,26},{4,28},{6,30},{8,16},{10,18},{12,20},{14,22},{16,8},... | collective-permute-start | bytes 196616 | tf_op jit(solution)/shard_map/ppermute | solution.py:31
  15.7 2.9 %collective-permute-done.4.refs_2_ = bf16[64,512]{1,0:T(8,128)(2,1)S(1)} collective-permute-done((bf16[64,512]{1,0:T(8,128)(2,1)S(1)}, bf16[64,512]{1,0:T(8,128)(2,1)S(1)}, u32[]{:S(2)}, u32[]{:S(2)}) %collective-permute-start.4) | collective-permute-done | bytes 65568 | tf_op jit(solution)/shard_map/ppermute | solution.py:31
  18.6 1.5 %collective-permute-start.15 = (bf16[128,1024]{1,0:T(8,128)(2,1)S(1)}, bf16[128,1024]{1,0:T(8,128)(2,1)S(1)}, u32[]{:S(2)}, u32[]{:S(2)}) collective-permute-start(bf16[128,1024]{1,0:T(8,128)(2,1)S(1)} %get-tuple-element.42), channel_id=1, source_target_pairs={{0,1},{1,0},{2,3},{3,2},{4,5},{5,4},{6,7},{7,6},{8,9},{9,8},{10,11... | collective-permute-start | bytes 786440 | tf_op jit(solution)/shard_map/ppermute | solution.py:31
  20.5 1.6 %collective-permute-start.6 = (bf16[256,512]{1,0:T(8,128)(2,1)S(1)}, bf16[256,512]{1,0:T(8,128)(2,1)S(1)}, u32[]{:S(2)}, u32[]{:S(2)}) collective-permute-start(bf16[256,512]{1,0:T(8,128)(2,1)S(1)} %shard_map.91.refs_0_), channel_id=1, source_target_pairs={{0,4},{2,6},{4,0},{6,2},{8,12},{10,14},{12,8},{14,10},{16,20},{18,... | collective-permute-start | bytes 786440 | tf_op jit(solution)/shard_map/ppermute | solution.py:31
  22.1 0.8 collective-permute-done.9.refs_1_
  23.3 1.6 %collective-permute-start.12 = (bf16[256,512]{1,0:T(8,128)(2,1)S(1)}, bf16[256,512]{1,0:T(8,128)(2,1)S(1)}, u32[]{:S(2)}, u32[]{:S(2)}) collective-permute-start(bf16[256,512]{1,0:T(8,128)(2,1)S(1)} %shard_map.93.refs_4_), channel_id=1, source_target_pairs={{0,4},{2,6},{4,0},{6,2},{8,12},{10,14},{12,8},{14,10},{16,20},{18,... | collective-permute-start | bytes 786440 | tf_op jit(solution)/shard_map/ppermute | solution.py:31
  25.2 0.5 shard_map.89
  25.7 1.6 %collective-permute-start.2 = (s32[264,256]{1,0:T(8,128)S(1)}, s32[264,256]{1,0:T(8,128)S(1)}, u32[]{:S(2)}, u32[]{:S(2)}) collective-permute-start(s32[264,256]{1,0:T(8,128)S(1)} %get-tuple-element.40.refs_0_.refs_1_), channel_id=1, source_target_pairs={{0,1},{1,0},{2,3},{3,2},{4,5},{5,4},{6,7},{7,6},{8,9},{9,8},{10,11... | collective-permute-start | bytes 811016 | tf_op jit(solution)/shard_map/ppermute | solution.py:31
  27.8 1.2 %collective-permute-done.6.refs_1_ = bf16[256,512]{1,0:T(8,128)(2,1)S(1)} collective-permute-done((bf16[256,512]{1,0:T(8,128)(2,1)S(1)}, bf16[256,512]{1,0:T(8,128)(2,1)S(1)}, u32[]{:S(2)}, u32[]{:S(2)}) %collective-permute-start.6) | collective-permute-done | bytes 262176 | tf_op jit(solution)/shard_map/ppermute | solution.py:31
  28.9 2.8 %collective-permute-done.12.refs_5_ = bf16[256,512]{1,0:T(8,128)(2,1)S(1)} collective-permute-done((bf16[256,512]{1,0:T(8,128)(2,1)S(1)}, bf16[256,512]{1,0:T(8,128)(2,1)S(1)}, u32[]{:S(2)}, u32[]{:S(2)}) %collective-permute-start.12) | collective-permute-done | bytes 262176 | tf_op jit(solution)/shard_map/ppermute | solution.py:31
  32.2 1.4 %collective-permute-start.16 = (bf16[128,1024]{1,0:T(8,128)(2,1)S(1)}, bf16[128,1024]{1,0:T(8,128)(2,1)S(1)}, u32[]{:S(2)}, u32[]{:S(2)}) collective-permute-start(bf16[128,1024]{1,0:T(8,128)(2,1)S(1)} %shard_map.96), channel_id=1, source_target_pairs={{0,1},{1,0},{2,3},{3,2},{4,5},{5,4},{6,7},{7,6},{8,9},{9,8},{10,11... | collective-permute-start | bytes 786440 | tf_op jit(solution)/shard_map/ppermute | solution.py:31
  33.6 1.0 %shard_map.94 = (f32[256,512]{1,0:T(8,128)S(1)}, bf16[2048,512]{1,0:T(8,128)(2,1)S(1)}) custom-call(bf16[256,2048]{1,0:T(8,128)(2,1)S(1)} %get-tuple-element.38.normed_ref, bf16[256,512]{1,0:T(8,128)(2,1)S(1)} %shard_map.91.refs_0_, bf16[256,512]{1,0:T(8,128)(2,1)S(1)} %collective-permute-done.6.refs_1_, ...), custom_call_target="tpu_custom_call" | custom-call | flops 1000 | bytes 1000 | tf_op jit(solution)/shard_map/pallas_call | solution.py:195
  34.7 0.6 shard_map.95.grads_ref
  35.4 1.0 %collective-permute-start.17 = (bf16[256,512]{1,0:T(8,128)(2,1)S(1)}, bf16[256,512]{1,0:T(8,128)(2,1)S(1)}, u32[]{:S(2)}, u32[]{:S(2)}) collective-permute-start(bf16[256,512]{1,0:T(8,128)(2,1)S(1)} %shard_map.95.grads_ref), channel_id=1, source_target_pairs={{0,1},{1,0},{2,3},{3,2},{4,5},{5,4},{6,7},{7,6},{8,9},{9,8},{10,11... | collective-permute-start | bytes 786440 | tf_op jit(solution)/shard_map/ppermute | solution.py:31
  36.4 5.0 %collective-permute-done.16.refs_0_.refs_1_ = bf16[128,1024]{1,0:T(8,128)(2,1)S(1)} collective-permute-done((bf16[128,1024]{1,0:T(8,128)(2,1)S(1)}, bf16[128,1024]{1,0:T(8,128)(2,1)S(1)}, u32[]{:S(2)}, u32[]{:S(2)}) %collective-permute-start.16) | collective-permute-done | bytes 262176 | tf_op jit(solution)/shard_map/ppermute | solution.py:31
  41.9 0.9 shard_map.98.refs_2_.refer_ref
  42.8 3.8 %collective-permute-done.17.grads_ref = bf16[256,512]{1,0:T(8,128)(2,1)S(1)} collective-permute-done((bf16[256,512]{1,0:T(8,128)(2,1)S(1)}, bf16[256,512]{1,0:T(8,128)(2,1)S(1)}, u32[]{:S(2)}, u32[]{:S(2)}) %collective-permute-start.17) | collective-permute-done | bytes 262176 | tf_op jit(solution)/shard_map/ppermute | solution.py:31
  46.6 1.6 %shard_map.99 = (f32[1024,512]{1,0:T(8,128)S(1)}, f32[512,256]{1,0:T(8,128)S(1)}, f32[512,256]{1,0:T(8,128)S(1)}, bf16[256,1024]{1,0:T(8,128)(2,1)S(1)}, bf16[10...) custom-call(s32[2]{0:T(128)S(1)} %copy-done.5, f32[1024,512]{1,0:T(8,128)S(1)} %shard_map.97.refs_0_.inner_ref, ...), custom_call_target="tpu_custom_call" | custom-call | flops 1000 | bytes 1000 | tf_op jit(solution)/shard_map/pallas_call | solution.py:195
  48.4 1.4 %collective-permute-start.18 = (s32[264,256]{1,0:T(8,128)S(1)}, s32[264,256]{1,0:T(8,128)S(1)}, u32[]{:S(2)}, u32[]{:S(2)}) collective-permute-start(s32[264,256]{1,0:T(8,128)S(1)} %get-tuple-element.49), channel_id=1, source_target_pairs={{0,1},{1,0},{2,3},{3,2},{4,5},{5,4},{6,7},{7,6},{8,9},{9,8},{10,11... | collective-permute-start | bytes 811016 | tf_op jit(solution)/shard_map/ppermute | solution.py:31
  50.4 2.7 %collective-permute-start.20 = (s32[72,256]{1,0:T(8,128)S(1)}, s32[72,256]{1,0:T(8,128)S(1)}, u32[]{:S(2)}, u32[]{:S(2)}) collective-permute-start(s32[72,256]{1,0:T(8,128)S(1)} %get-tuple-element.52), channel_id=1, source_target_pairs={{0,24},{2,26},{4,28},{6,30},{8,16},{10,18},{12,20},{14,22},{16,8},... | collective-permute-start | bytes 221192 | tf_op jit(solution)/shard_map/ppermute | solution.py:31
  53.5 3.8 %collective-permute-done.18.received_ref = s32[264,256]{1,0:T(8,128)S(1)} collective-permute-done((s32[264,256]{1,0:T(8,128)S(1)}, s32[264,256]{1,0:T(8,128)S(1)}, u32[]{:S(2)}, u32[]{:S(2)}) %collective-permute-start.18) | collective-permute-done | bytes 270368 | tf_op jit(solution)/shard_map/ppermute | solution.py:31
  57.3 0.6 shard_map.102.grads_ref
  57.9 1.4 %collective-permute-start.21 = (bf16[256,512]{1,0:T(8,128)(2,1)S(1)}, bf16[256,512]{1,0:T(8,128)(2,1)S(1)}, u32[]{:S(2)}, u32[]{:S(2)}) collective-permute-start(bf16[256,512]{1,0:T(8,128)(2,1)S(1)} %shard_map.102.grads_ref), channel_id=1, source_target_pairs={{0,1},{1,0},{2,3},{3,2},{4,5},{5,4},{6,7},{7,6},{8,9},{9,8},{10,11... | collective-permute-start | bytes 786440 | tf_op jit(solution)/shard_map/ppermute | solution.py:31
  59.3 1.1 %collective-permute-start.22 = (s32[72,256]{1,0:T(8,128)S(1)}, s32[72,256]{1,0:T(8,128)S(1)}, u32[]{:S(2)}, u32[]{:S(2)}) collective-permute-start(s32[72,256]{1,0:T(8,128)S(1)} %get-tuple-element.55), channel_id=1, source_target_pairs={{0,8},{2,10},{4,12},{6,14},{8,0},{10,2},{12,4},{14,6},{16,24},{18,... | collective-permute-start | bytes 221192 | tf_op jit(solution)/shard_map/ppermute | solution.py:31
  60.4 1.8 %collective-permute-start.23 = (s32[72,256]{1,0:T(8,128)S(1)}, s32[72,256]{1,0:T(8,128)S(1)}, u32[]{:S(2)}, u32[]{:S(2)}) collective-permute-start(s32[72,256]{1,0:T(8,128)S(1)} %get-tuple-element.56), channel_id=1, source_target_pairs={{0,16},{2,18},{4,20},{6,22},{8,24},{10,26},{12,28},{14,30},{16,0},... | collective-permute-start | bytes 221192 | tf_op jit(solution)/shard_map/ppermute | solution.py:31
  62.7 1.5 %collective-permute-done.22.refs_1_ = s32[72,256]{1,0:T(8,128)S(1)} collective-permute-done((s32[72,256]{1,0:T(8,128)S(1)}, s32[72,256]{1,0:T(8,128)S(1)}, u32[]{:S(2)}, u32[]{:S(2)}) %collective-permute-start.22) | collective-permute-done | bytes 73760 | tf_op jit(solution)/shard_map/ppermute | solution.py:31
  64.2 2.3 %collective-permute-done.23.refs_2_ = s32[72,256]{1,0:T(8,128)S(1)} collective-permute-done((s32[72,256]{1,0:T(8,128)S(1)}, s32[72,256]{1,0:T(8,128)S(1)}, u32[]{:S(2)}, u32[]{:S(2)}) %collective-permute-start.23) | collective-permute-done | bytes 73760 | tf_op jit(solution)/shard_map/ppermute | solution.py:31
  66.6 1.2 %shard_map.105 = (f32[1024,512]{1,0:T(8,128)S(1)}, f32[512,256]{1,0:T(8,128)S(1)}, f32[512,256]{1,0:T(8,128)S(1)}) custom-call(s32[2]{0:T(128)S(1)} %copy-done.5, f32[1024,512]{1,0:T(8,128)S(1)} %shard_map.103.refs_3_.inner_ref, bf16[256,1024]{1,0:T(8,128)(2,1)S(1)} %get-tuple-element.53.features_ref, ...), custom_call_target="tpu_custom_call" | custom-call | flops 1000 | bytes 1000 | tf_op jit(solution)/shard_map/pallas_call | solution.py:195
  67.9 1.6 %collective-permute-start.24 = (s32[72,256]{1,0:T(8,128)S(1)}, s32[72,256]{1,0:T(8,128)S(1)}, u32[]{:S(2)}, u32[]{:S(2)}) collective-permute-start(s32[72,256]{1,0:T(8,128)S(1)} %shard_map.104.refs_0_.one_ref), channel_id=1, source_target_pairs={{0,4},{2,6},{4,0},{6,2},{8,12},{10,14},{12,8},{14,10},{16,20},{18,... | collective-permute-start | bytes 221192 | tf_op jit(solution)/shard_map/ppermute | solution.py:31
  70.0 2.3 %collective-permute-start.30 = (s32[72,256]{1,0:T(8,128)S(1)}, s32[72,256]{1,0:T(8,128)S(1)}, u32[]{:S(2)}, u32[]{:S(2)}) collective-permute-start(s32[72,256]{1,0:T(8,128)S(1)} %get-tuple-element.61), channel_id=1, source_target_pairs={{0,24},{2,26},{4,28},{6,30},{8,16},{10,18},{12,20},{14,22},{16,8},... | collective-permute-start | bytes 221192 | tf_op jit(solution)/shard_map/ppermute | solution.py:31
  72.2 2.2 %collective-permute-start.32 = (s32[72,256]{1,0:T(8,128)S(1)}, s32[72,256]{1,0:T(8,128)S(1)}, u32[]{:S(2)}, u32[]{:S(2)}) collective-permute-start(s32[72,256]{1,0:T(8,128)S(1)} %get-tuple-element.63), channel_id=1, source_target_pairs={{0,16},{2,18},{4,20},{6,22},{8,24},{10,26},{12,28},{14,30},{16,0},... | collective-permute-start | bytes 221192 | tf_op jit(solution)/shard_map/ppermute | solution.py:31
  74.5 0.8 collective-permute-start.26
  75.3 2.0 %collective-permute-start.25 = (s32[72,256]{1,0:T(8,128)S(1)}, s32[72,256]{1,0:T(8,128)S(1)}, u32[]{:S(2)}, u32[]{:S(2)}) collective-permute-start(s32[72,256]{1,0:T(8,128)S(1)} %shard_map.106.refs_0_), channel_id=1, source_target_pairs={{0,8},{2,10},{4,12},{6,14},{8,0},{10,2},{12,4},{14,6},{16,24},{18,... | collective-permute-start | bytes 221192 | tf_op jit(solution)/shard_map/ppermute | solution.py:31
  77.3 2.0 %collective-permute-done.31.refs_1_ = s32[72,256]{1,0:T(8,128)S(1)} collective-permute-done((s32[72,256]{1,0:T(8,128)S(1)}, s32[72,256]{1,0:T(8,128)S(1)}, u32[]{:S(2)}, u32[]{:S(2)}) %collective-permute-start.31) | collective-permute-done | bytes 73760 | tf_op jit(solution)/shard_map/ppermute | solution.py:31
  79.3 2.1 %collective-permute-done.32.refs_2_ = s32[72,256]{1,0:T(8,128)S(1)} collective-permute-done((s32[72,256]{1,0:T(8,128)S(1)}, s32[72,256]{1,0:T(8,128)S(1)}, u32[]{:S(2)}, u32[]{:S(2)}) %collective-permute-start.32) | collective-permute-done | bytes 73760 | tf_op jit(solution)/shard_map/ppermute | solution.py:31
  81.6 1.6 %collective-permute-start.33 = (s32[72,256]{1,0:T(8,128)S(1)}, s32[72,256]{1,0:T(8,128)S(1)}, u32[]{:S(2)}, u32[]{:S(2)}) collective-permute-start(s32[72,256]{1,0:T(8,128)S(1)} %shard_map.109.one_ref), channel_id=1, source_target_pairs={{0,4},{2,6},{4,0},{6,2},{8,12},{10,14},{12,8},{14,10},{16,20},{18,... | collective-permute-start | bytes 221192 | tf_op jit(solution)/shard_map/ppermute | solution.py:31
  83.1 1.6 %collective-permute-start.27 = (s32[72,256]{1,0:T(8,128)S(1)}, s32[72,256]{1,0:T(8,128)S(1)}, u32[]{:S(2)}, u32[]{:S(2)}) collective-permute-start(s32[72,256]{1,0:T(8,128)S(1)} %shard_map.106.refs_0_), channel_id=1, source_target_pairs={{0,24},{2,26},{4,28},{6,30},{8,16},{10,18},{12,20},{14,22},{16,8},... | collective-permute-start | bytes 221192 | tf_op jit(solution)/shard_map/ppermute | solution.py:31
  84.8 1.2 %collective-permute-done.33.other_ref = s32[72,256]{1,0:T(8,128)S(1)} collective-permute-done((s32[72,256]{1,0:T(8,128)S(1)}, s32[72,256]{1,0:T(8,128)S(1)}, u32[]{:S(2)}, u32[]{:S(2)}) %collective-permute-start.33) | collective-permute-done | bytes 73760 | tf_op jit(solution)/shard_map/ppermute | solution.py:31
  86.1 1.7 %collective-permute-start.36 = (s32[72,256]{1,0:T(8,128)S(1)}, s32[72,256]{1,0:T(8,128)S(1)}, u32[]{:S(2)}, u32[]{:S(2)}) collective-permute-start(s32[72,256]{1,0:T(8,128)S(1)} %shard_map.110.refs_0_), channel_id=1, source_target_pairs={{0,24},{2,26},{4,28},{6,30},{8,16},{10,18},{12,20},{14,22},{16,8},... | collective-permute-start | bytes 221192 | tf_op jit(solution)/shard_map/ppermute | solution.py:31
  87.8 2.7 %collective-permute-start.34 = (s32[72,256]{1,0:T(8,128)S(1)}, s32[72,256]{1,0:T(8,128)S(1)}, u32[]{:S(2)}, u32[]{:S(2)}) collective-permute-start(s32[72,256]{1,0:T(8,128)S(1)} %shard_map.110.refs_0_), channel_id=1, source_target_pairs={{0,8},{2,10},{4,12},{6,14},{8,0},{10,2},{12,4},{14,6},{16,24},{18,... | collective-permute-start | bytes 221192 | tf_op jit(solution)/shard_map/ppermute | solution.py:31
  91.0 1.3 %collective-permute-done.36.refs_3_ = s32[72,256]{1,0:T(8,128)S(1)} collective-permute-done((s32[72,256]{1,0:T(8,128)S(1)}, s32[72,256]{1,0:T(8,128)S(1)}, u32[]{:S(2)}, u32[]{:S(2)}) %collective-permute-start.36) | collective-permute-done | bytes 73760 | tf_op jit(solution)/shard_map/ppermute | solution.py:31
  92.3 1.6 %collective-permute-done.35.refs_2_ = s32[72,256]{1,0:T(8,128)S(1)} collective-permute-done((s32[72,256]{1,0:T(8,128)S(1)}, s32[72,256]{1,0:T(8,128)S(1)}, u32[]{:S(2)}, u32[]{:S(2)}) %collective-permute-start.35) | collective-permute-done | bytes 73760 | tf_op jit(solution)/shard_map/ppermute | solution.py:31
  94.4 1.6 %collective-permute-done.37.other1 = s32[288,256]{1,0:T(8,128)S(1)} collective-permute-done((s32[288,256]{1,0:T(8,128)S(1)}, s32[288,256]{1,0:T(8,128)S(1)}, u32[]{:S(2)}, u32[]{:S(2)}) %collective-permute-start.37) | collective-permute-done | bytes 294944 | tf_op jit(solution)/shard_map/ppermute | solution.py:31
  95.9 2.8 %shard_map.112 = (f32[1024,512]{1,0:T(8,128)}, f32[1024,512]{1,0:T(8,128)}) custom-call(s32[2]{0:T(128)S(1)} %copy-done.5, f32[1024,512]{1,0:T(8,128)S(1)} %copy-done, f32[1024,512]{1,0:T(8,128)S(1)} %get-tuple-element.57.inner_ref, s32[288,256]{1,0:T(8,128)S(1)} %shard_map.107.own0, s32[288,256]{1,0:T(8,128)S(1)} %collective-permute-done.28.other0, ...), custom_call_target="tpu_custom_call" | custom-call | flops 1000 | bytes 1000 | tf_op jit(solution)/shard_map/pallas_call | solution.py:195
  (68 shorter events, 7.4 us)
Async XLA Ops:
  0.6 1.7 %copy-start.2 = (bf16[64,512]{1,0:T(8,128)(2,1)S(1)}, bf16[64,512]{1,0:T(8,128)(2,1)}, u32[]{:S(2)}) copy-start(bf16[64,512]{1,0:T(8,128)(2,1)} %refs_0_.3) | copy-start | bytes 196612
  2.4 22.5 %copy-start = (f32[1024,512]{1,0:T(8,128)S(1)}, f32[1024,512]{1,0:T(8,128)}, u32[]{:S(2)}) copy-start(f32[1024,512]{1,0:T(8,128)} %outer_ref.7) | copy-start | bytes 6291460
  2.4 22.5 %copy-start.1 = (bf16[1,1024,512]{2,1,0:T(8,128)(2,1)S(1)}, bf16[1,1024,512]{2,1,0:T(8,128)(2,1)}, u32[]{:S(2)}) copy-start(bf16[1,1024,512]{2,1,0:T(8,128)(2,1)} %drift_ref.1) | copy-start | bytes 3145732
  2.8 8.7 %collective-permute-start = (bf16[96,1024]{1,0:T(8,128)(2,1)S(1)}, bf16[96,1024]{1,0:T(8,128)(2,1)S(1)}, u32[]{:S(2)}, u32[]{:S(2)}) collective-permute-start(bf16[96,1024]{1,0:T(8,128)(2,1)S(1)} %get-tuple-element.34.refs_1_), channel_id=1, source_target_pairs={{0,1},{1,0},{2,3},{3,2},{4,5},{5,4},{6,7},{7,6},{8,9},{9,8},{10,11... | collective-permute-start | bytes 589832 | tf_op jit(solution)/shard_map/ppermute | solution.py:31
  5.8 19.3 %collective-permute-start.1 = (bf16[192,1024]{1,0:T(8,128)(2,1)S(1)}, bf16[192,1024]{1,0:T(8,128)(2,1)S(1)}, u32[]{:S(2)}, u32[]{:S(2)}) collective-permute-start(bf16[192,1024]{1,0:T(8,128)(2,1)S(1)} %get-tuple-element.35.refs_2_), channel_id=1, source_target_pairs={{0,1},{1,0},{2,3},{3,2},{4,5},{5,4},{6,7},{7,6},{8,9},{9,8},{10,11... | collective-permute-start | bytes 1179656 | tf_op jit(solution)/shard_map/ppermute | solution.py:31
  6.4 9.4 %collective-permute-start.5 = (bf16[64,512]{1,0:T(8,128)(2,1)S(1)}, bf16[64,512]{1,0:T(8,128)(2,1)S(1)}, u32[]{:S(2)}, u32[]{:S(2)}) collective-permute-start(bf16[64,512]{1,0:T(8,128)(2,1)S(1)} %get-tuple-element.41.refs_0_), channel_id=1, source_target_pairs={{0,24},{2,26},{4,28},{6,30},{8,16},{10,18},{12,20},{14,22},{16,8},... | collective-permute-start | bytes 196616 | tf_op jit(solution)/shard_map/ppermute | solution.py:31
  10.5 8.1 %collective-permute-start.4 = (bf16[64,512]{1,0:T(8,128)(2,1)S(1)}, bf16[64,512]{1,0:T(8,128)(2,1)S(1)}, u32[]{:S(2)}, u32[]{:S(2)}) collective-permute-start(bf16[64,512]{1,0:T(8,128)(2,1)S(1)} %get-tuple-element.41.refs_0_), channel_id=1, source_target_pairs={{0,16},{2,18},{4,20},{6,22},{8,24},{10,26},{12,28},{14,30},{16,0},... | collective-permute-start | bytes 196616 | tf_op jit(solution)/shard_map/ppermute | solution.py:31
  10.5 8.2 %collective-permute-start.3 = (bf16[64,512]{1,0:T(8,128)(2,1)S(1)}, bf16[64,512]{1,0:T(8,128)(2,1)S(1)}, u32[]{:S(2)}, u32[]{:S(2)}) collective-permute-start(bf16[64,512]{1,0:T(8,128)(2,1)S(1)} %get-tuple-element.41.refs_0_), channel_id=1, source_target_pairs={{0,8},{2,10},{4,12},{6,14},{8,0},{10,2},{12,4},{14,6},{16,24},{18,... | collective-permute-start | bytes 196616 | tf_op jit(solution)/shard_map/ppermute | solution.py:31
  11.6 8.9 %collective-permute-start.11 = (bf16[64,512]{1,0:T(8,128)(2,1)S(1)}, bf16[64,512]{1,0:T(8,128)(2,1)S(1)}, u32[]{:S(2)}, u32[]{:S(2)}) collective-permute-start(bf16[64,512]{1,0:T(8,128)(2,1)S(1)} %shard_map.92.refs_0_), channel_id=1, source_target_pairs={{0,24},{2,26},{4,28},{6,30},{8,16},{10,18},{12,20},{14,22},{16,8},... | collective-permute-start | bytes 196616 | tf_op jit(solution)/shard_map/ppermute | solution.py:31
  15.7 6.4 %collective-permute-start.10 = (bf16[64,512]{1,0:T(8,128)(2,1)S(1)}, bf16[64,512]{1,0:T(8,128)(2,1)S(1)}, u32[]{:S(2)}, u32[]{:S(2)}) collective-permute-start(bf16[64,512]{1,0:T(8,128)(2,1)S(1)} %shard_map.92.refs_0_), channel_id=1, source_target_pairs={{0,16},{2,18},{4,20},{6,22},{8,24},{10,26},{12,28},{14,30},{16,0},... | collective-permute-start | bytes 196616 | tf_op jit(solution)/shard_map/ppermute | solution.py:31
  18.6 4.3 %collective-permute-start.9 = (bf16[64,512]{1,0:T(8,128)(2,1)S(1)}, bf16[64,512]{1,0:T(8,128)(2,1)S(1)}, u32[]{:S(2)}, u32[]{:S(2)}) collective-permute-start(bf16[64,512]{1,0:T(8,128)(2,1)S(1)} %shard_map.92.refs_0_), channel_id=1, source_target_pairs={{0,8},{2,10},{4,12},{6,14},{8,0},{10,2},{12,4},{14,6},{16,24},{18,... | collective-permute-start | bytes 196616 | tf_op jit(solution)/shard_map/ppermute | solution.py:31
  18.6 8.6 %collective-permute-start.15 = (bf16[128,1024]{1,0:T(8,128)(2,1)S(1)}, bf16[128,1024]{1,0:T(8,128)(2,1)S(1)}, u32[]{:S(2)}, u32[]{:S(2)}) collective-permute-start(bf16[128,1024]{1,0:T(8,128)(2,1)S(1)} %get-tuple-element.42), channel_id=1, source_target_pairs={{0,1},{1,0},{2,3},{3,2},{4,5},{5,4},{6,7},{7,6},{8,9},{9,8},{10,11... | collective-permute-start | bytes 786440 | tf_op jit(solution)/shard_map/ppermute | solution.py:31
  20.5 8.4 %collective-permute-start.6 = (bf16[256,512]{1,0:T(8,128)(2,1)S(1)}, bf16[256,512]{1,0:T(8,128)(2,1)S(1)}, u32[]{:S(2)}, u32[]{:S(2)}) collective-permute-start(bf16[256,512]{1,0:T(8,128)(2,1)S(1)} %shard_map.91.refs_0_), channel_id=1, source_target_pairs={{0,4},{2,6},{4,0},{6,2},{8,12},{10,14},{12,8},{14,10},{16,20},{18,... | collective-permute-start | bytes 786440 | tf_op jit(solution)/shard_map/ppermute | solution.py:31
  23.3 8.5 %collective-permute-start.12 = (bf16[256,512]{1,0:T(8,128)(2,1)S(1)}, bf16[256,512]{1,0:T(8,128)(2,1)S(1)}, u32[]{:S(2)}, u32[]{:S(2)}) collective-permute-start(bf16[256,512]{1,0:T(8,128)(2,1)S(1)} %shard_map.93.refs_4_), channel_id=1, source_target_pairs={{0,4},{2,6},{4,0},{6,2},{8,12},{10,14},{12,8},{14,10},{16,20},{18,... | collective-permute-start | bytes 786440 | tf_op jit(solution)/shard_map/ppermute | solution.py:31
  25.7 9.0 %collective-permute-start.2 = (s32[264,256]{1,0:T(8,128)S(1)}, s32[264,256]{1,0:T(8,128)S(1)}, u32[]{:S(2)}, u32[]{:S(2)}) collective-permute-start(s32[264,256]{1,0:T(8,128)S(1)} %get-tuple-element.40.refs_0_.refs_1_), channel_id=1, source_target_pairs={{0,1},{1,0},{2,3},{3,2},{4,5},{5,4},{6,7},{7,6},{8,9},{9,8},{10,11... | collective-permute-start | bytes 811016 | tf_op jit(solution)/shard_map/ppermute | solution.py:31
  27.3 5.0 %collective-permute-start.7 = (bf16[256,512]{1,0:T(8,128)(2,1)S(1)}, bf16[256,512]{1,0:T(8,128)(2,1)S(1)}, u32[]{:S(2)}, u32[]{:S(2)}) collective-permute-start(bf16[256,512]{1,0:T(8,128)(2,1)S(1)} %shard_map.91.refs_0_), channel_id=1, source_target_pairs={{0,2},{2,0},{4,6},{6,4},{8,10},{10,8},{12,14},{14,12},{16,18},{18,... | collective-permute-start | bytes 786440 | tf_op jit(solution)/shard_map/ppermute | solution.py:31
  27.3 6.4 %collective-permute-start.13 = (bf16[256,512]{1,0:T(8,128)(2,1)S(1)}, bf16[256,512]{1,0:T(8,128)(2,1)S(1)}, u32[]{:S(2)}, u32[]{:S(2)}) collective-permute-start(bf16[256,512]{1,0:T(8,128)(2,1)S(1)} %shard_map.93.refs_4_), channel_id=1, source_target_pairs={{0,2},{2,0},{4,6},{6,4},{8,10},{10,8},{12,14},{14,12},{16,18},{18,... | collective-permute-start | bytes 786440 | tf_op jit(solution)/shard_map/ppermute | solution.py:31
  28.9 4.7 %collective-permute-start.8 = (bf16[256,512]{1,0:T(8,128)(2,1)S(1)}, bf16[256,512]{1,0:T(8,128)(2,1)S(1)}, u32[]{:S(2)}, u32[]{:S(2)}) collective-permute-start(bf16[256,512]{1,0:T(8,128)(2,1)S(1)} %collective-permute-done.6.refs_1_), channel_id=1, source_target_pairs={{0,2},{2,0},{4,6},{6,4},{8,10},{10,8},{12,14},{14,12},{16,18},{18,... | collective-permute-start | bytes 786440 | tf_op jit(solution)/shard_map/ppermute | solution.py:31
  31.7 1.9 %collective-permute-start.14 = (bf16[256,512]{1,0:T(8,128)(2,1)S(1)}, bf16[256,512]{1,0:T(8,128)(2,1)S(1)}, u32[]{:S(2)}, u32[]{:S(2)}) collective-permute-start(bf16[256,512]{1,0:T(8,128)(2,1)S(1)} %collective-permute-done.12.refs_5_), channel_id=1, source_target_pairs={{0,2},{2,0},{4,6},{6,4},{8,10},{10,8},{12,14},{14,12},{16,18},{18,... | collective-permute-start | bytes 786440 | tf_op jit(solution)/shard_map/ppermute | solution.py:31
  32.2 2.5 %copy-start.3 = (s32[2,256]{1,0:T(2,128)S(1)}, s32[2,256]{1,0:T(2,128)}, u32[]{:S(2)}) copy-start(s32[2,256]{1,0:T(2,128)} %targets_ref.3) | copy-start | bytes 6148
  32.2 2.5 %copy-start.4 = (s32[2,256]{1,0:T(2,128)S(1)}, s32[2,256]{1,0:T(2,128)}, u32[]{:S(2)}) copy-start(s32[2,256]{1,0:T(2,128)} %valid_ref.3) | copy-start | bytes 6148
  32.2 9.2 %collective-permute-start.16 = (bf16[128,1024]{1,0:T(8,128)(2,1)S(1)}, bf16[128,1024]{1,0:T(8,128)(2,1)S(1)}, u32[]{:S(2)}, u32[]{:S(2)}) collective-permute-start(bf16[128,1024]{1,0:T(8,128)(2,1)S(1)} %shard_map.96), channel_id=1, source_target_pairs={{0,1},{1,0},{2,3},{3,2},{4,5},{5,4},{6,7},{7,6},{8,9},{9,8},{10,11... | collective-permute-start | bytes 786440 | tf_op jit(solution)/shard_map/ppermute | solution.py:31
  35.4 11.3 %collective-permute-start.17 = (bf16[256,512]{1,0:T(8,128)(2,1)S(1)}, bf16[256,512]{1,0:T(8,128)(2,1)S(1)}, u32[]{:S(2)}, u32[]{:S(2)}) collective-permute-start(bf16[256,512]{1,0:T(8,128)(2,1)S(1)} %shard_map.95.grads_ref), channel_id=1, source_target_pairs={{0,1},{1,0},{2,3},{3,2},{4,5},{5,4},{6,7},{7,6},{8,9},{9,8},{10,11... | collective-permute-start | bytes 786440 | tf_op jit(solution)/shard_map/ppermute | solution.py:31
  41.9 4.7 %copy-start.5 = (s32[2]{0:T(128)S(1)}, s32[2]{0:T(128)}, u32[]{:S(2)}) copy-start(s32[2]{0:T(128)} %plan_ref.5) | copy-start | bytes 28
  48.3 2.0 %collective-permute-start.19 = (f32[512,256]{1,0:T(8,128)S(1)}, f32[512,256]{1,0:T(8,128)S(1)}, u32[]{:S(2)}, u32[]{:S(2)}) collective-permute-start(f32[512,256]{1,0:T(8,128)S(1)} %get-tuple-element.51), channel_id=1, source_target_pairs={{0,2},{2,0},{4,6},{6,4},{8,10},{10,8},{12,14},{14,12},{16,18},{18,... | collective-permute-start | bytes 1572872 | tf_op jit(solution)/shard_map/ppermute | solution.py:31
  48.4 8.9 %collective-permute-start.18 = (s32[264,256]{1,0:T(8,128)S(1)}, s32[264,256]{1,0:T(8,128)S(1)}, u32[]{:S(2)}, u32[]{:S(2)}) collective-permute-start(s32[264,256]{1,0:T(8,128)S(1)} %get-tuple-element.49), channel_id=1, source_target_pairs={{0,1},{1,0},{2,3},{3,2},{4,5},{5,4},{6,7},{7,6},{8,9},{9,8},{10,11... | collective-permute-start | bytes 811016 | tf_op jit(solution)/shard_map/ppermute | solution.py:31
  50.4 6.9 %collective-permute-start.20 = (s32[72,256]{1,0:T(8,128)S(1)}, s32[72,256]{1,0:T(8,128)S(1)}, u32[]{:S(2)}, u32[]{:S(2)}) collective-permute-start(s32[72,256]{1,0:T(8,128)S(1)} %get-tuple-element.52), channel_id=1, source_target_pairs={{0,24},{2,26},{4,28},{6,30},{8,16},{10,18},{12,20},{14,22},{16,8},... | collective-permute-start | bytes 221192 | tf_op jit(solution)/shard_map/ppermute | solution.py:31
  57.9 8.7 %collective-permute-start.21 = (bf16[256,512]{1,0:T(8,128)(2,1)S(1)}, bf16[256,512]{1,0:T(8,128)(2,1)S(1)}, u32[]{:S(2)}, u32[]{:S(2)}) collective-permute-start(bf16[256,512]{1,0:T(8,128)(2,1)S(1)} %shard_map.102.grads_ref), channel_id=1, source_target_pairs={{0,1},{1,0},{2,3},{3,2},{4,5},{5,4},{6,7},{7,6},{8,9},{9,8},{10,11... | collective-permute-start | bytes 786440 | tf_op jit(solution)/shard_map/ppermute | solution.py:31
  59.3 4.8 %collective-permute-start.22 = (s32[72,256]{1,0:T(8,128)S(1)}, s32[72,256]{1,0:T(8,128)S(1)}, u32[]{:S(2)}, u32[]{:S(2)}) collective-permute-start(s32[72,256]{1,0:T(8,128)S(1)} %get-tuple-element.55), channel_id=1, source_target_pairs={{0,8},{2,10},{4,12},{6,14},{8,0},{10,2},{12,4},{14,6},{16,24},{18,... | collective-permute-start | bytes 221192 | tf_op jit(solution)/shard_map/ppermute | solution.py:31
  60.4 6.0 %collective-permute-start.23 = (s32[72,256]{1,0:T(8,128)S(1)}, s32[72,256]{1,0:T(8,128)S(1)}, u32[]{:S(2)}, u32[]{:S(2)}) collective-permute-start(s32[72,256]{1,0:T(8,128)S(1)} %get-tuple-element.56), channel_id=1, source_target_pairs={{0,16},{2,18},{4,20},{6,22},{8,24},{10,26},{12,28},{14,30},{16,0},... | collective-permute-start | bytes 221192 | tf_op jit(solution)/shard_map/ppermute | solution.py:31
  67.8 2.0 %collective-permute-start.29 = (f32[512,256]{1,0:T(8,128)S(1)}, f32[512,256]{1,0:T(8,128)S(1)}, u32[]{:S(2)}, u32[]{:S(2)}) collective-permute-start(f32[512,256]{1,0:T(8,128)S(1)} %get-tuple-element.59), channel_id=1, source_target_pairs={{0,2},{2,0},{4,6},{6,4},{8,10},{10,8},{12,14},{14,12},{16,18},{18,... | collective-permute-start | bytes 1572872 | tf_op jit(solution)/shard_map/ppermute | solution.py:31
  67.9 6.5 %collective-permute-start.24 = (s32[72,256]{1,0:T(8,128)S(1)}, s32[72,256]{1,0:T(8,128)S(1)}, u32[]{:S(2)}, u32[]{:S(2)}) collective-permute-start(s32[72,256]{1,0:T(8,128)S(1)} %shard_map.104.refs_0_.one_ref), channel_id=1, source_target_pairs={{0,4},{2,6},{4,0},{6,2},{8,12},{10,14},{12,8},{14,10},{16,20},{18,... | collective-permute-start | bytes 221192 | tf_op jit(solution)/shard_map/ppermute | solution.py:31
  70.0 7.4 %collective-permute-start.30 = (s32[72,256]{1,0:T(8,128)S(1)}, s32[72,256]{1,0:T(8,128)S(1)}, u32[]{:S(2)}, u32[]{:S(2)}) collective-permute-start(s32[72,256]{1,0:T(8,128)S(1)} %get-tuple-element.61), channel_id=1, source_target_pairs={{0,24},{2,26},{4,28},{6,30},{8,16},{10,18},{12,20},{14,22},{16,8},... | collective-permute-start | bytes 221192 | tf_op jit(solution)/shard_map/ppermute | solution.py:31
  72.2 7.1 %collective-permute-start.31 = (s32[72,256]{1,0:T(8,128)S(1)}, s32[72,256]{1,0:T(8,128)S(1)}, u32[]{:S(2)}, u32[]{:S(2)}) collective-permute-start(s32[72,256]{1,0:T(8,128)S(1)} %get-tuple-element.62), channel_id=1, source_target_pairs={{0,8},{2,10},{4,12},{6,14},{8,0},{10,2},{12,4},{14,6},{16,24},{18,... | collective-permute-start | bytes 221192 | tf_op jit(solution)/shard_map/ppermute | solution.py:31
  72.2 9.2 %collective-permute-start.32 = (s32[72,256]{1,0:T(8,128)S(1)}, s32[72,256]{1,0:T(8,128)S(1)}, u32[]{:S(2)}, u32[]{:S(2)}) collective-permute-start(s32[72,256]{1,0:T(8,128)S(1)} %get-tuple-element.63), channel_id=1, source_target_pairs={{0,16},{2,18},{4,20},{6,22},{8,24},{10,26},{12,28},{14,30},{16,0},... | collective-permute-start | bytes 221192 | tf_op jit(solution)/shard_map/ppermute | solution.py:31
  74.5 10.3 %collective-permute-start.26 = (s32[72,256]{1,0:T(8,128)S(1)}, s32[72,256]{1,0:T(8,128)S(1)}, u32[]{:S(2)}, u32[]{:S(2)}) collective-permute-start(s32[72,256]{1,0:T(8,128)S(1)} %shard_map.106.refs_0_), channel_id=1, source_target_pairs={{0,16},{2,18},{4,20},{6,22},{8,24},{10,26},{12,28},{14,30},{16,0},... | collective-permute-start | bytes 221192 | tf_op jit(solution)/shard_map/ppermute | solution.py:31
  75.3 9.5 %collective-permute-start.25 = (s32[72,256]{1,0:T(8,128)S(1)}, s32[72,256]{1,0:T(8,128)S(1)}, u32[]{:S(2)}, u32[]{:S(2)}) collective-permute-start(s32[72,256]{1,0:T(8,128)S(1)} %shard_map.106.refs_0_), channel_id=1, source_target_pairs={{0,8},{2,10},{4,12},{6,14},{8,0},{10,2},{12,4},{14,6},{16,24},{18,... | collective-permute-start | bytes 221192 | tf_op jit(solution)/shard_map/ppermute | solution.py:31
  81.6 4.4 %collective-permute-start.33 = (s32[72,256]{1,0:T(8,128)S(1)}, s32[72,256]{1,0:T(8,128)S(1)}, u32[]{:S(2)}, u32[]{:S(2)}) collective-permute-start(s32[72,256]{1,0:T(8,128)S(1)} %shard_map.109.one_ref), channel_id=1, source_target_pairs={{0,4},{2,6},{4,0},{6,2},{8,12},{10,14},{12,8},{14,10},{16,20},{18,... | collective-permute-start | bytes 221192 | tf_op jit(solution)/shard_map/ppermute | solution.py:31
  83.1 7.4 %collective-permute-start.27 = (s32[72,256]{1,0:T(8,128)S(1)}, s32[72,256]{1,0:T(8,128)S(1)}, u32[]{:S(2)}, u32[]{:S(2)}) collective-permute-start(s32[72,256]{1,0:T(8,128)S(1)} %shard_map.106.refs_0_), channel_id=1, source_target_pairs={{0,24},{2,26},{4,28},{6,30},{8,16},{10,18},{12,20},{14,22},{16,8},... | collective-permute-start | bytes 221192 | tf_op jit(solution)/shard_map/ppermute | solution.py:31
  86.1 6.2 %collective-permute-start.36 = (s32[72,256]{1,0:T(8,128)S(1)}, s32[72,256]{1,0:T(8,128)S(1)}, u32[]{:S(2)}, u32[]{:S(2)}) collective-permute-start(s32[72,256]{1,0:T(8,128)S(1)} %shard_map.110.refs_0_), channel_id=1, source_target_pairs={{0,24},{2,26},{4,28},{6,30},{8,16},{10,18},{12,20},{14,22},{16,8},... | collective-permute-start | bytes 221192 | tf_op jit(solution)/shard_map/ppermute | solution.py:31
  87.8 6.1 %collective-permute-start.35 = (s32[72,256]{1,0:T(8,128)S(1)}, s32[72,256]{1,0:T(8,128)S(1)}, u32[]{:S(2)}, u32[]{:S(2)}) collective-permute-start(s32[72,256]{1,0:T(8,128)S(1)} %shard_map.110.refs_0_), channel_id=1, source_target_pairs={{0,16},{2,18},{4,20},{6,22},{8,24},{10,26},{12,28},{14,30},{16,0},... | collective-permute-start | bytes 221192 | tf_op jit(solution)/shard_map/ppermute | solution.py:31
  87.8 6.1 %collective-permute-start.34 = (s32[72,256]{1,0:T(8,128)S(1)}, s32[72,256]{1,0:T(8,128)S(1)}, u32[]{:S(2)}, u32[]{:S(2)}) collective-permute-start(s32[72,256]{1,0:T(8,128)S(1)} %shard_map.110.refs_0_), channel_id=1, source_target_pairs={{0,8},{2,10},{4,12},{6,14},{8,0},{10,2},{12,4},{14,6},{16,24},{18,... | collective-permute-start | bytes 221192 | tf_op jit(solution)/shard_map/ppermute | solution.py:31
  90.9 3.4 %collective-permute-start.28 = (s32[288,256]{1,0:T(8,128)S(1)}, s32[288,256]{1,0:T(8,128)S(1)}, u32[]{:S(2)}, u32[]{:S(2)}) collective-permute-start(s32[288,256]{1,0:T(8,128)S(1)} %shard_map.107.own0), channel_id=1, source_target_pairs={{0,2},{2,0},{4,6},{6,4},{8,10},{10,8},{12,14},{14,12},{16,18},{18,... | collective-permute-start | bytes 884744 | tf_op jit(solution)/shard_map/ppermute | solution.py:31
  94.3 1.6 %collective-permute-start.37 = (s32[288,256]{1,0:T(8,128)S(1)}, s32[288,256]{1,0:T(8,128)S(1)}, u32[]{:S(2)}, u32[]{:S(2)}) collective-permute-start(s32[288,256]{1,0:T(8,128)S(1)} %shard_map.111.own1), channel_id=1, source_target_pairs={{0,2},{2,0},{4,6},{6,4},{8,10},{10,8},{12,14},{14,12},{16,18},{18,... | collective-permute-start | bytes 884744 | tf_op jit(solution)/shard_map/ppermute | solution.py:31

commit v7 on v6

--- a/solution.py
+++ b/solution.py
@@ -184,7 +184,14 @@
     return (new_outer, new_inner[None])
 
 
-MASKS = (3, 1, 2)
+MASKS = (3, 2, 1)
+COST = {
+    "stacked": 5000000000,
+    "more_reference_logs": 100000000,
+    "own_logits": 100000000,
+    "own_update": 5000000000,
+    "update": 1000000000,
+}
 VMEM = pl.BlockSpec(memory_space=pltpu.VMEM)
 SMEM = pl.BlockSpec(memory_space=pltpu.SMEM)
 ANY = pl.BlockSpec(memory_space=pl.ANY)
@@ -199,7 +206,7 @@
         out_specs=out_specs,
         scratch_shapes=scratch,
         compiler_params=pltpu.CompilerParams(vmem_limit_bytes=room * 1024 * 1024),
-        cost_estimate=pl.CostEstimate(flops=1000, bytes_accessed=1000, transcendentals=0),
+        cost_estimate=pl.CostEstimate(flops=COST.get(kernel.__qualname__.split(".")[0], 1000), bytes_accessed=1000, transcendentals=0),
         **more,
     )(*operands)
 
@@ -294,7 +301,7 @@
 def normalized(hidden, sizes, passed=(), folded=(), earlier=()):
     tokens, width = hidden.shape
     cols = width // 2
-    tile = 64
+    tile = 16
     extra = [f.shape[0] * f.shape[1] // cols for f in folded]
     starts = [sum(sizes[:k]) for k in range(len(sizes))]
     lengths = [size + sum(extra) * (k == 0) for k, size in enumerate(sizes)]
@@ -673,7 +680,7 @@
 
 
 def gathered_stacks(ref_own, ref_partner):
-    along_z = [m * 2 * CORES for m in range(1, MAJOR)]
+    along_z = [m * 2 * CORES for m in (1, 2, 3)]
     stacks = []
     for piece in ((ref_own, [(0, 0)]), (ref_partner, [(0, 1)])):
         first = along(piece, *along_z)
@@ -682,8 +689,9 @@
     return stacks
 
 
-def quarters_along(own):
-    return [own] + [swap(own, "replica", m * 2 * CORES) for m in range(1, MAJOR)]
+def quarters_along(own, order):
+    got = {m: swap(own, "replica", m * 2 * CORES) for m in order}
+    return [own] + [got[m] for m in range(1, MAJOR)]
 
 
 def gathered_quarters(pieces):
@@ -700,8 +708,8 @@
     replicas = lax.axis_size("replica")
 
     tokens = hidden.shape[1]
-    sizes0 = (tokens // 4, 3 * tokens // 4)
-    sizes1 = (tokens // 2, tokens // 2)
+    sizes0 = (4 * tokens // 16, tokens - 4 * tokens // 16)
+    sizes1 = (9 * tokens // 16, tokens - 9 * tokens // 16)
 
     normed0, *sent0 = normalized(hidden[0], sizes0, (), (ref_head,))
     features0 = [swap(s, "fsdp", 1) for s in sent0]
@@ -715,7 +723,7 @@
     own = own_logits(normed0, weights, partial)
     features1b = swap(after(sent1b, partial), "fsdp", 1)
     refer_log, whole = reference_logs(normed0, stacks, features1a)
-    grads = gradients(own, received, refer_log, targets, valid, 0)
+    grads = gradients(own, received, refer_log, targets, valid, 0, features1a)
     partner_grads = swap(grads, "fsdp", 1)
     halfway = own_update(inner, normed0, grads, features1b)
     refer_log = more_reference_logs(normed1, whole, halfway)
@@ -737,9 +745,9 @@
 
     quarter, pieces = chip_quarters(sent, kept)
     quarter = quarter_sum(quarter, pieces)
-    first = quarters_along(first)
+    first = quarters_along(first, (3, 1, 2))
     second = pair_sum(quarter, swap(quarter, "replica", CORES), first[1], first[2])
-    means = [gathered_quarters(m) for m in (first, quarters_along(second))]
+    means = [gathered_quarters(m) for m in (first, quarters_along(second, (1, 2, 3)))]
     new_outer, new_inner = settled(outer_head, inner, means, plan)
     return (new_outer, new_inner[None])
 

time: 98.9 us -> 96.1 us (0.972)
  starting transfers between devices: 46.4 us -> 44.4 us
    ppermute x38, starting transfers between devices: 46.4 us -> 44.4 us  [swap(): return lax.ppermute(value, axis, [(i, i ^ mask) for i in range(size)])]
  transfers between devices with their start and end apart: 38 -> 38, of which waited for: 18 -> 19; matrix products, arithmetic and copies ran while one was open for 0% -> 0% of each run, Pallas kernels for 8% -> 9%
where the time goes in v7:
time: 96.1 us; the launch traced here: 96 us
  starting transfers between devices  44.4 us (46%)
  waiting for transfers between devices  34.3 us (36%)
  Pallas kernels  14.5 us (15%)
  local copies, waits for them, and re-layouts  1.74 us (2%)
  between operations  0.99 us (1%)
    ppermute x38, starting transfers between devices, swap(): return lax.ppermute(value, axis, [(i, i ^ mask) for i in range(size)])  44.4 us
    ppermute x38, waiting for transfers between devices, swap(): return lax.ppermute(value, axis, [(i, i ^ mask) for i in range(size)])  34.3 us
    pallas_call x27, Pallas kernels, call(): pl.pallas_call(kernel, out_shape=out_shape, in_specs=in_specs, out_specs=...  14.5 us
  transfers between devices with their start and end apart: 38, of which 19 were waited for; matrix products, arithmetic and copies ran while one was open for 0% of the time, Pallas kernels for 9%

profile of v7, /device:TPU:0, one launch (start us, length us, event | category | flops | bytes accessed | tf_op | source)
XLA Modules:
  0.0 96.0 jit_solution(2224210221003691469)
XLA Ops:
  0.6 1.7 %slice_bitcast_fusion = (bf16[256,2048]{1,0:T(8,128)(2,1)S(1)}, bf16[256,2048]{1,0:T(8,128)(2,1)S(1)}) fusion(bf16[2,256,2048]{2,1,0:T(8,128)(2,1)} %param.7), kind=kLoop, calls=%fused_computation | loop fusion | bytes 4194304 | tf_op jit(solution)/shard_map/squeeze | solution.py:714
  2.8 3.0 %collective-permute-start = (bf16[96,1024]{1,0:T(8,128)(2,1)S(1)}, bf16[96,1024]{1,0:T(8,128)(2,1)S(1)}, u32[]{:S(2)}, u32[]{:S(2)}) collective-permute-start(bf16[96,1024]{1,0:T(8,128)(2,1)S(1)} %get-tuple-element.34.refs_1_), channel_id=1, source_target_pairs={{0,1},{1,0},{2,3},{3,2},{4,5},{5,4},{6,7},{7,6},{8,9},{9,8},{10,11... | collective-permute-start | bytes 589832 | tf_op jit(solution)/shard_map/ppermute | solution.py:31
  6.2 3.7 %collective-permute-start.5 = (bf16[64,512]{1,0:T(8,128)(2,1)S(1)}, bf16[64,512]{1,0:T(8,128)(2,1)S(1)}, u32[]{:S(2)}, u32[]{:S(2)}) collective-permute-start(bf16[64,512]{1,0:T(8,128)(2,1)S(1)} %get-tuple-element.41.refs_0_), channel_id=1, source_target_pairs={{0,24},{2,26},{4,28},{6,30},{8,16},{10,18},{12,20},{14,22},{16,8},... | collective-permute-start | bytes 196616 | tf_op jit(solution)/shard_map/ppermute | solution.py:31
  9.9 0.8 collective-permute-start.3
  11.1 1.6 %collective-permute-start.15 = (bf16[144,1024]{1,0:T(8,128)(2,1)S(1)}, bf16[144,1024]{1,0:T(8,128)(2,1)S(1)}, u32[]{:S(2)}, u32[]{:S(2)}) collective-permute-start(bf16[144,1024]{1,0:T(8,128)(2,1)S(1)} %get-tuple-element.42), channel_id=1, source_target_pairs={{0,1},{1,0},{2,3},{3,2},{4,5},{5,4},{6,7},{7,6},{8,9},{9,8},{10,11... | collective-permute-start | bytes 884744 | tf_op jit(solution)/shard_map/ppermute | solution.py:31
  13.1 3.6 %collective-permute-start.11 = (bf16[64,512]{1,0:T(8,128)(2,1)S(1)}, bf16[64,512]{1,0:T(8,128)(2,1)S(1)}, u32[]{:S(2)}, u32[]{:S(2)}) collective-permute-start(bf16[64,512]{1,0:T(8,128)(2,1)S(1)} %shard_map.92.refs_0_), channel_id=1, source_target_pairs={{0,24},{2,26},{4,28},{6,30},{8,16},{10,18},{12,20},{14,22},{16,8},... | collective-permute-start | bytes 196616 | tf_op jit(solution)/shard_map/ppermute | solution.py:31
  16.8 2.2 %collective-permute-start.9 = (bf16[64,512]{1,0:T(8,128)(2,1)S(1)}, bf16[64,512]{1,0:T(8,128)(2,1)S(1)}, u32[]{:S(2)}, u32[]{:S(2)}) collective-permute-start(bf16[64,512]{1,0:T(8,128)(2,1)S(1)} %shard_map.92.refs_0_), channel_id=1, source_target_pairs={{0,8},{2,10},{4,12},{6,14},{8,0},{10,2},{12,4},{14,6},{16,24},{18,... | collective-permute-start | bytes 196616 | tf_op jit(solution)/shard_map/ppermute | solution.py:31
  19.3 1.6 %collective-permute-start.6 = (bf16[256,512]{1,0:T(8,128)(2,1)S(1)}, bf16[256,512]{1,0:T(8,128)(2,1)S(1)}, u32[]{:S(2)}, u32[]{:S(2)}) collective-permute-start(bf16[256,512]{1,0:T(8,128)(2,1)S(1)} %shard_map.91.refs_0_), channel_id=1, source_target_pairs={{0,4},{2,6},{4,0},{6,2},{8,12},{10,14},{12,8},{14,10},{16,20},{18,... | collective-permute-start | bytes 786440 | tf_op jit(solution)/shard_map/ppermute | solution.py:31
  20.9 1.0 %collective-permute-done.10.refs_2_ = bf16[64,512]{1,0:T(8,128)(2,1)S(1)} collective-permute-done((bf16[64,512]{1,0:T(8,128)(2,1)S(1)}, bf16[64,512]{1,0:T(8,128)(2,1)S(1)}, u32[]{:S(2)}, u32[]{:S(2)}) %collective-permute-start.10) | collective-permute-done | bytes 65568 | tf_op jit(solution)/shard_map/ppermute | solution.py:31
  22.3 1.6 %collective-permute-start.12 = (bf16[256,512]{1,0:T(8,128)(2,1)S(1)}, bf16[256,512]{1,0:T(8,128)(2,1)S(1)}, u32[]{:S(2)}, u32[]{:S(2)}) collective-permute-start(bf16[256,512]{1,0:T(8,128)(2,1)S(1)} %shard_map.93.refs_4_), channel_id=1, source_target_pairs={{0,4},{2,6},{4,0},{6,2},{8,12},{10,14},{12,8},{14,10},{16,20},{18,... | collective-permute-start | bytes 786440 | tf_op jit(solution)/shard_map/ppermute | solution.py:31
  24.2 0.5 shard_map.89
  24.7 0.6 collective-permute-start.2
  25.3 1.5 %collective-permute-done.15.refs_8_.refs_0_ = bf16[144,1024]{1,0:T(8,128)(2,1)S(1)} collective-permute-done((bf16[144,1024]{1,0:T(8,128)(2,1)S(1)}, bf16[144,1024]{1,0:T(8,128)(2,1)S(1)}, u32[]{:S(2)}, u32[]{:S(2)}) %collective-permute-start.15) | collective-permute-done | bytes 294944 | tf_op jit(solution)/shard_map/ppermute | solution.py:31
  26.9 1.5 %collective-permute-done.6.refs_1_ = bf16[256,512]{1,0:T(8,128)(2,1)S(1)} collective-permute-done((bf16[256,512]{1,0:T(8,128)(2,1)S(1)}, bf16[256,512]{1,0:T(8,128)(2,1)S(1)}, u32[]{:S(2)}, u32[]{:S(2)}) %collective-permute-start.6) | collective-permute-done | bytes 262176 | tf_op jit(solution)/shard_map/ppermute | solution.py:31
  28.3 2.8 %collective-permute-done.12.refs_5_ = bf16[256,512]{1,0:T(8,128)(2,1)S(1)} collective-permute-done((bf16[256,512]{1,0:T(8,128)(2,1)S(1)}, bf16[256,512]{1,0:T(8,128)(2,1)S(1)}, u32[]{:S(2)}, u32[]{:S(2)}) %collective-permute-start.12) | collective-permute-done | bytes 262176 | tf_op jit(solution)/shard_map/ppermute | solution.py:31
  31.1 0.6 collective-permute-start.16
  32.7 1.0 %shard_map.94 = (f32[256,512]{1,0:T(8,128)S(1)}, bf16[2048,512]{1,0:T(8,128)(2,1)S(1)}) custom-call(bf16[256,2048]{1,0:T(8,128)(2,1)S(1)} %get-tuple-element.38.normed_ref, bf16[256,512]{1,0:T(8,128)(2,1)S(1)} %shard_map.91.refs_0_, bf16[256,512]{1,0:T(8,128)(2,1)S(1)} %collective-permute-done.6.refs_1_, ...), custom_call_target="tpu_custom_call" | custom-call | flops 1000 | bytes 1000 | tf_op jit(solution)/shard_map/pallas_call | solution.py:202
  33.7 0.6 shard_map.95.grads_ref
  34.4 1.1 %collective-permute-start.17 = (bf16[256,512]{1,0:T(8,128)(2,1)S(1)}, bf16[256,512]{1,0:T(8,128)(2,1)S(1)}, u32[]{:S(2)}, u32[]{:S(2)}) collective-permute-start(bf16[256,512]{1,0:T(8,128)(2,1)S(1)} %shard_map.95.grads_ref), channel_id=1, source_target_pairs={{0,1},{1,0},{2,3},{3,2},{4,5},{5,4},{6,7},{7,6},{8,9},{9,8},{10,11... | collective-permute-start | bytes 786440 | tf_op jit(solution)/shard_map/ppermute | solution.py:31
  35.5 4.1 %collective-permute-done.16.refs_0_.refs_1_ = bf16[112,1024]{1,0:T(8,128)(2,1)S(1)} collective-permute-done((bf16[112,1024]{1,0:T(8,128)(2,1)S(1)}, bf16[112,1024]{1,0:T(8,128)(2,1)S(1)}, u32[]{:S(2)}, u32[]{:S(2)}) %collective-permute-start.16) | collective-permute-done | bytes 229408 | tf_op jit(solution)/shard_map/ppermute | solution.py:31
  39.6 0.5 shard_map.97.refs_0_.inner_ref
  40.1 0.9 shard_map.98.refs_2_.refer_ref
  41.0 3.8 %collective-permute-done.17.grads_ref = bf16[256,512]{1,0:T(8,128)(2,1)S(1)} collective-permute-done((bf16[256,512]{1,0:T(8,128)(2,1)S(1)}, bf16[256,512]{1,0:T(8,128)(2,1)S(1)}, u32[]{:S(2)}, u32[]{:S(2)}) %collective-permute-start.17) | collective-permute-done | bytes 262176 | tf_op jit(solution)/shard_map/ppermute | solution.py:31
  44.8 1.6 %shard_map.99 = (f32[1024,512]{1,0:T(8,128)S(1)}, f32[512,256]{1,0:T(8,128)S(1)}, f32[512,256]{1,0:T(8,128)S(1)}, bf16[256,1024]{1,0:T(8,128)(2,1)S(1)}, bf16[10...) custom-call(s32[2]{0:T(128)S(1)} %copy-done.5, f32[1024,512]{1,0:T(8,128)S(1)} %shard_map.97.refs_0_.inner_ref, ...), custom_call_target="tpu_custom_call" | custom-call | flops 1000000000 | bytes 1000 | tf_op jit(solution)/shard_map/pallas_call | solution.py:202
  46.5 0.6 collective-permute-start.18
  47.1 1.3 %collective-permute-done.19.received_ref = f32[512,256]{1,0:T(8,128)S(1)} collective-permute-done((f32[512,256]{1,0:T(8,128)S(1)}, f32[512,256]{1,0:T(8,128)S(1)}, u32[]{:S(2)}, u32[]{:S(2)}) %collective-permute-start.19) | collective-permute-done | bytes 524320 | tf_op jit(solution)/shard_map/ppermute | solution.py:31
  48.5 2.5 %collective-permute-start.20 = (s32[72,256]{1,0:T(8,128)S(1)}, s32[72,256]{1,0:T(8,128)S(1)}, u32[]{:S(2)}, u32[]{:S(2)}) collective-permute-start(s32[72,256]{1,0:T(8,128)S(1)} %get-tuple-element.52), channel_id=1, source_target_pairs={{0,24},{2,26},{4,28},{6,30},{8,16},{10,18},{12,20},{14,22},{16,8},... | collective-permute-start | bytes 221192 | tf_op jit(solution)/shard_map/ppermute | solution.py:31
  51.6 1.9 %collective-permute-start.23 = (s32[72,256]{1,0:T(8,128)S(1)}, s32[72,256]{1,0:T(8,128)S(1)}, u32[]{:S(2)}, u32[]{:S(2)}) collective-permute-start(s32[72,256]{1,0:T(8,128)S(1)} %get-tuple-element.56), channel_id=1, source_target_pairs={{0,8},{2,10},{4,12},{6,14},{8,0},{10,2},{12,4},{14,6},{16,24},{18,... | collective-permute-start | bytes 221192 | tf_op jit(solution)/shard_map/ppermute | solution.py:31
  53.5 1.9 %collective-permute-done.18.received_ref = s32[264,256]{1,0:T(8,128)S(1)} collective-permute-done((s32[264,256]{1,0:T(8,128)S(1)}, s32[264,256]{1,0:T(8,128)S(1)}, u32[]{:S(2)}, u32[]{:S(2)}) %collective-permute-start.18) | collective-permute-done | bytes 270368 | tf_op jit(solution)/shard_map/ppermute | solution.py:31
  55.6 0.6 shard_map.102.grads_ref
  56.2 0.6 collective-permute-start.21
  57.3 0.7 collective-permute-done.22.refs_1_
  58.1 5.9 %collective-permute-done.21.grads_ref = bf16[256,512]{1,0:T(8,128)(2,1)S(1)} collective-permute-done((bf16[256,512]{1,0:T(8,128)(2,1)S(1)}, bf16[256,512]{1,0:T(8,128)(2,1)S(1)}, u32[]{:S(2)}, u32[]{:S(2)}) %collective-permute-start.21) | collective-permute-done | bytes 262176 | tf_op jit(solution)/shard_map/ppermute | solution.py:31
  64.0 1.3 %shard_map.105 = (f32[1024,512]{1,0:T(8,128)S(1)}, f32[512,256]{1,0:T(8,128)S(1)}, f32[512,256]{1,0:T(8,128)S(1)}) custom-call(s32[2]{0:T(128)S(1)} %copy-done.5, f32[1024,512]{1,0:T(8,128)S(1)} %shard_map.103.refs_3_.inner_ref, bf16[256,1024]{1,0:T(8,128)(2,1)S(1)} %get-tuple-element.53.features_ref, ...), custom_call_target="tpu_custom_call" | custom-call | flops 1000000000 | bytes 1000 | tf_op jit(solution)/shard_map/pallas_call | solution.py:202
  65.3 1.6 %collective-permute-start.24 = (s32[72,256]{1,0:T(8,128)S(1)}, s32[72,256]{1,0:T(8,128)S(1)}, u32[]{:S(2)}, u32[]{:S(2)}) collective-permute-start(s32[72,256]{1,0:T(8,128)S(1)} %shard_map.104.refs_0_.one_ref), channel_id=1, source_target_pairs={{0,4},{2,6},{4,0},{6,2},{8,12},{10,14},{12,8},{14,10},{16,20},{18,... | collective-permute-start | bytes 221192 | tf_op jit(solution)/shard_map/ppermute | solution.py:31
  67.4 2.5 %collective-permute-start.30 = (s32[72,256]{1,0:T(8,128)S(1)}, s32[72,256]{1,0:T(8,128)S(1)}, u32[]{:S(2)}, u32[]{:S(2)}) collective-permute-start(s32[72,256]{1,0:T(8,128)S(1)} %get-tuple-element.61), channel_id=1, source_target_pairs={{0,24},{2,26},{4,28},{6,30},{8,16},{10,18},{12,20},{14,22},{16,8},... | collective-permute-start | bytes 221192 | tf_op jit(solution)/shard_map/ppermute | solution.py:31
  69.9 1.9 %collective-permute-start.32 = (s32[72,256]{1,0:T(8,128)S(1)}, s32[72,256]{1,0:T(8,128)S(1)}, u32[]{:S(2)}, u32[]{:S(2)}) collective-permute-start(s32[72,256]{1,0:T(8,128)S(1)} %get-tuple-element.63), channel_id=1, source_target_pairs={{0,8},{2,10},{4,12},{6,14},{8,0},{10,2},{12,4},{14,6},{16,24},{18,... | collective-permute-start | bytes 221192 | tf_op jit(solution)/shard_map/ppermute | solution.py:31
  71.9 1.1 %collective-permute-start.26 = (s32[72,256]{1,0:T(8,128)S(1)}, s32[72,256]{1,0:T(8,128)S(1)}, u32[]{:S(2)}, u32[]{:S(2)}) collective-permute-start(s32[72,256]{1,0:T(8,128)S(1)} %shard_map.106.refs_0_), channel_id=1, source_target_pairs={{0,16},{2,18},{4,20},{6,22},{8,24},{10,26},{12,28},{14,30},{16,0},... | collective-permute-start | bytes 221192 | tf_op jit(solution)/shard_map/ppermute | solution.py:31
  73.0 2.0 %collective-permute-start.25 = (s32[72,256]{1,0:T(8,128)S(1)}, s32[72,256]{1,0:T(8,128)S(1)}, u32[]{:S(2)}, u32[]{:S(2)}) collective-permute-start(s32[72,256]{1,0:T(8,128)S(1)} %shard_map.106.refs_0_), channel_id=1, source_target_pairs={{0,8},{2,10},{4,12},{6,14},{8,0},{10,2},{12,4},{14,6},{16,24},{18,... | collective-permute-start | bytes 221192 | tf_op jit(solution)/shard_map/ppermute | solution.py:31
  75.1 2.7 %collective-permute-done.31.refs_1_ = s32[72,256]{1,0:T(8,128)S(1)} collective-permute-done((s32[72,256]{1,0:T(8,128)S(1)}, s32[72,256]{1,0:T(8,128)S(1)}, u32[]{:S(2)}, u32[]{:S(2)}) %collective-permute-start.31) | collective-permute-done | bytes 73760 | tf_op jit(solution)/shard_map/ppermute | solution.py:31
  77.8 1.6 %collective-permute-start.33 = (s32[72,256]{1,0:T(8,128)S(1)}, s32[72,256]{1,0:T(8,128)S(1)}, u32[]{:S(2)}, u32[]{:S(2)}) collective-permute-start(s32[72,256]{1,0:T(8,128)S(1)} %shard_map.109.one_ref), channel_id=1, source_target_pairs={{0,4},{2,6},{4,0},{6,2},{8,12},{10,14},{12,8},{14,10},{16,20},{18,... | collective-permute-start | bytes 221192 | tf_op jit(solution)/shard_map/ppermute | solution.py:31
  79.4 2.4 %collective-permute-start.27 = (s32[72,256]{1,0:T(8,128)S(1)}, s32[72,256]{1,0:T(8,128)S(1)}, u32[]{:S(2)}, u32[]{:S(2)}) collective-permute-start(s32[72,256]{1,0:T(8,128)S(1)} %shard_map.106.refs_0_), channel_id=1, source_target_pairs={{0,24},{2,26},{4,28},{6,30},{8,16},{10,18},{12,20},{14,22},{16,8},... | collective-permute-start | bytes 221192 | tf_op jit(solution)/shard_map/ppermute | solution.py:31
  82.3 2.5 %collective-permute-start.36 = (s32[72,256]{1,0:T(8,128)S(1)}, s32[72,256]{1,0:T(8,128)S(1)}, u32[]{:S(2)}, u32[]{:S(2)}) collective-permute-start(s32[72,256]{1,0:T(8,128)S(1)} %shard_map.110.refs_0_), channel_id=1, source_target_pairs={{0,24},{2,26},{4,28},{6,30},{8,16},{10,18},{12,20},{14,22},{16,8},... | collective-permute-start | bytes 221192 | tf_op jit(solution)/shard_map/ppermute | solution.py:31
  84.8 2.0 %collective-permute-start.34 = (s32[72,256]{1,0:T(8,128)S(1)}, s32[72,256]{1,0:T(8,128)S(1)}, u32[]{:S(2)}, u32[]{:S(2)}) collective-permute-start(s32[72,256]{1,0:T(8,128)S(1)} %shard_map.110.refs_0_), channel_id=1, source_target_pairs={{0,8},{2,10},{4,12},{6,14},{8,0},{10,2},{12,4},{14,6},{16,24},{18,... | collective-permute-start | bytes 221192 | tf_op jit(solution)/shard_map/ppermute | solution.py:31
  87.3 2.0 %collective-permute-done.36.refs_3_ = s32[72,256]{1,0:T(8,128)S(1)} collective-permute-done((s32[72,256]{1,0:T(8,128)S(1)}, s32[72,256]{1,0:T(8,128)S(1)}, u32[]{:S(2)}, u32[]{:S(2)}) %collective-permute-start.36) | collective-permute-done | bytes 73760 | tf_op jit(solution)/shard_map/ppermute | solution.py:31
  89.3 1.8 %collective-permute-done.35.refs_2_ = s32[72,256]{1,0:T(8,128)S(1)} collective-permute-done((s32[72,256]{1,0:T(8,128)S(1)}, s32[72,256]{1,0:T(8,128)S(1)}, u32[]{:S(2)}, u32[]{:S(2)}) %collective-permute-start.35) | collective-permute-done | bytes 73760 | tf_op jit(solution)/shard_map/ppermute | solution.py:31
  91.6 1.6 %collective-permute-done.37.other1 = s32[288,256]{1,0:T(8,128)S(1)} collective-permute-done((s32[288,256]{1,0:T(8,128)S(1)}, s32[288,256]{1,0:T(8,128)S(1)}, u32[]{:S(2)}, u32[]{:S(2)}) %collective-permute-start.37) | collective-permute-done | bytes 294944 | tf_op jit(solution)/shard_map/ppermute | solution.py:31
  93.2 2.8 %shard_map.112 = (f32[1024,512]{1,0:T(8,128)}, f32[1024,512]{1,0:T(8,128)}) custom-call(s32[2]{0:T(128)S(1)} %copy-done.5, f32[1024,512]{1,0:T(8,128)S(1)} %copy-done, f32[1024,512]{1,0:T(8,128)S(1)} %get-tuple-element.57.inner_ref, s32[288,256]{1,0:T(8,128)S(1)} %shard_map.107.own0, s32[288,256]{1,0:T(8,128)S(1)} %collective-permute-done.28.other0, ...), custom_call_target="tpu_custom_call" | custom-call | flops 1000 | bytes 1000 | tf_op jit(solution)/shard_map/pallas_call | solution.py:202
  (68 shorter events, 7.3 us)
Async XLA Ops:
  0.6 1.7 %copy-start.2 = (bf16[64,512]{1,0:T(8,128)(2,1)S(1)}, bf16[64,512]{1,0:T(8,128)(2,1)}, u32[]{:S(2)}) copy-start(bf16[64,512]{1,0:T(8,128)(2,1)} %refs_0_.3) | copy-start | bytes 196612
  2.8 8.3 %collective-permute-start = (bf16[96,1024]{1,0:T(8,128)(2,1)S(1)}, bf16[96,1024]{1,0:T(8,128)(2,1)S(1)}, u32[]{:S(2)}, u32[]{:S(2)}) collective-permute-start(bf16[96,1024]{1,0:T(8,128)(2,1)S(1)} %get-tuple-element.34.refs_1_), channel_id=1, source_target_pairs={{0,1},{1,0},{2,3},{3,2},{4,5},{5,4},{6,7},{7,6},{8,9},{9,8},{10,11... | collective-permute-start | bytes 589832 | tf_op jit(solution)/shard_map/ppermute | solution.py:31
  6.2 6.9 %collective-permute-start.5 = (bf16[64,512]{1,0:T(8,128)(2,1)S(1)}, bf16[64,512]{1,0:T(8,128)(2,1)S(1)}, u32[]{:S(2)}, u32[]{:S(2)}) collective-permute-start(bf16[64,512]{1,0:T(8,128)(2,1)S(1)} %get-tuple-element.41.refs_0_), channel_id=1, source_target_pairs={{0,24},{2,26},{4,28},{6,30},{8,16},{10,18},{12,20},{14,22},{16,8},... | collective-permute-start | bytes 196616 | tf_op jit(solution)/shard_map/ppermute | solution.py:31
  9.9 6.9 %collective-permute-start.4 = (bf16[64,512]{1,0:T(8,128)(2,1)S(1)}, bf16[64,512]{1,0:T(8,128)(2,1)S(1)}, u32[]{:S(2)}, u32[]{:S(2)}) collective-permute-start(bf16[64,512]{1,0:T(8,128)(2,1)S(1)} %get-tuple-element.41.refs_0_), channel_id=1, source_target_pairs={{0,16},{2,18},{4,20},{6,22},{8,24},{10,26},{12,28},{14,30},{16,0},... | collective-permute-start | bytes 196616 | tf_op jit(solution)/shard_map/ppermute | solution.py:31
  9.9 6.9 %collective-permute-start.3 = (bf16[64,512]{1,0:T(8,128)(2,1)S(1)}, bf16[64,512]{1,0:T(8,128)(2,1)S(1)}, u32[]{:S(2)}, u32[]{:S(2)}) collective-permute-start(bf16[64,512]{1,0:T(8,128)(2,1)S(1)} %get-tuple-element.41.refs_0_), channel_id=1, source_target_pairs={{0,8},{2,10},{4,12},{6,14},{8,0},{10,2},{12,4},{14,6},{16,24},{18,... | collective-permute-start | bytes 196616 | tf_op jit(solution)/shard_map/ppermute | solution.py:31
  10.7 13.5 %collective-permute-start.1 = (bf16[192,1024]{1,0:T(8,128)(2,1)S(1)}, bf16[192,1024]{1,0:T(8,128)(2,1)S(1)}, u32[]{:S(2)}, u32[]{:S(2)}) collective-permute-start(bf16[192,1024]{1,0:T(8,128)(2,1)S(1)} %get-tuple-element.35.refs_2_), channel_id=1, source_target_pairs={{0,1},{1,0},{2,3},{3,2},{4,5},{5,4},{6,7},{7,6},{8,9},{9,8},{10,11... | collective-permute-start | bytes 1179656 | tf_op jit(solution)/shard_map/ppermute | solution.py:31
  11.1 15.8 %collective-permute-start.15 = (bf16[144,1024]{1,0:T(8,128)(2,1)S(1)}, bf16[144,1024]{1,0:T(8,128)(2,1)S(1)}, u32[]{:S(2)}, u32[]{:S(2)}) collective-permute-start(bf16[144,1024]{1,0:T(8,128)(2,1)S(1)} %get-tuple-element.42), channel_id=1, source_target_pairs={{0,1},{1,0},{2,3},{3,2},{4,5},{5,4},{6,7},{7,6},{8,9},{9,8},{10,11... | collective-permute-start | bytes 884744 | tf_op jit(solution)/shard_map/ppermute | solution.py:31
  13.1 6.2 %collective-permute-start.11 = (bf16[64,512]{1,0:T(8,128)(2,1)S(1)}, bf16[64,512]{1,0:T(8,128)(2,1)S(1)}, u32[]{:S(2)}, u32[]{:S(2)}) collective-permute-start(bf16[64,512]{1,0:T(8,128)(2,1)S(1)} %shard_map.92.refs_0_), channel_id=1, source_target_pairs={{0,24},{2,26},{4,28},{6,30},{8,16},{10,18},{12,20},{14,22},{16,8},... | collective-permute-start | bytes 196616 | tf_op jit(solution)/shard_map/ppermute | solution.py:31
  16.8 5.2 %collective-permute-start.10 = (bf16[64,512]{1,0:T(8,128)(2,1)S(1)}, bf16[64,512]{1,0:T(8,128)(2,1)S(1)}, u32[]{:S(2)}, u32[]{:S(2)}) collective-permute-start(bf16[64,512]{1,0:T(8,128)(2,1)S(1)} %shard_map.92.refs_0_), channel_id=1, source_target_pairs={{0,16},{2,18},{4,20},{6,22},{8,24},{10,26},{12,28},{14,30},{16,0},... | collective-permute-start | bytes 196616 | tf_op jit(solution)/shard_map/ppermute | solution.py:31
  16.8 5.2 %collective-permute-start.9 = (bf16[64,512]{1,0:T(8,128)(2,1)S(1)}, bf16[64,512]{1,0:T(8,128)(2,1)S(1)}, u32[]{:S(2)}, u32[]{:S(2)}) collective-permute-start(bf16[64,512]{1,0:T(8,128)(2,1)S(1)} %shard_map.92.refs_0_), channel_id=1, source_target_pairs={{0,8},{2,10},{4,12},{6,14},{8,0},{10,2},{12,4},{14,6},{16,24},{18,... | collective-permute-start | bytes 196616 | tf_op jit(solution)/shard_map/ppermute | solution.py:31
  19.3 4.6 %copy-start = (f32[1024,512]{1,0:T(8,128)S(1)}, f32[1024,512]{1,0:T(8,128)}, u32[]{:S(2)}) copy-start(f32[1024,512]{1,0:T(8,128)} %outer_ref.7) | copy-start | bytes 6291460
  19.3 4.6 %copy-start.1 = (bf16[1,1024,512]{2,1,0:T(8,128)(2,1)S(1)}, bf16[1,1024,512]{2,1,0:T(8,128)(2,1)}, u32[]{:S(2)}) copy-start(bf16[1,1024,512]{2,1,0:T(8,128)(2,1)} %drift_ref.1) | copy-start | bytes 3145732
  19.3 9.0 %collective-permute-start.6 = (bf16[256,512]{1,0:T(8,128)(2,1)S(1)}, bf16[256,512]{1,0:T(8,128)(2,1)S(1)}, u32[]{:S(2)}, u32[]{:S(2)}) collective-permute-start(bf16[256,512]{1,0:T(8,128)(2,1)S(1)} %shard_map.91.refs_0_), channel_id=1, source_target_pairs={{0,4},{2,6},{4,0},{6,2},{8,12},{10,14},{12,8},{14,10},{16,20},{18,... | collective-permute-start | bytes 786440 | tf_op jit(solution)/shard_map/ppermute | solution.py:31
  22.3 8.8 %collective-permute-start.12 = (bf16[256,512]{1,0:T(8,128)(2,1)S(1)}, bf16[256,512]{1,0:T(8,128)(2,1)S(1)}, u32[]{:S(2)}, u32[]{:S(2)}) collective-permute-start(bf16[256,512]{1,0:T(8,128)(2,1)S(1)} %shard_map.93.refs_4_), channel_id=1, source_target_pairs={{0,4},{2,6},{4,0},{6,2},{8,12},{10,14},{12,8},{14,10},{16,20},{18,... | collective-permute-start | bytes 786440 | tf_op jit(solution)/shard_map/ppermute | solution.py:31
  23.9 7.2 %collective-permute-start.7 = (bf16[256,512]{1,0:T(8,128)(2,1)S(1)}, bf16[256,512]{1,0:T(8,128)(2,1)S(1)}, u32[]{:S(2)}, u32[]{:S(2)}) collective-permute-start(bf16[256,512]{1,0:T(8,128)(2,1)S(1)} %shard_map.91.refs_0_), channel_id=1, source_target_pairs={{0,2},{2,0},{4,6},{6,4},{8,10},{10,8},{12,14},{14,12},{16,18},{18,... | collective-permute-start | bytes 786440 | tf_op jit(solution)/shard_map/ppermute | solution.py:31
  24.7 9.0 %collective-permute-start.2 = (s32[264,256]{1,0:T(8,128)S(1)}, s32[264,256]{1,0:T(8,128)S(1)}, u32[]{:S(2)}, u32[]{:S(2)}) collective-permute-start(s32[264,256]{1,0:T(8,128)S(1)} %get-tuple-element.40.refs_0_.refs_1_), channel_id=1, source_target_pairs={{0,1},{1,0},{2,3},{3,2},{4,5},{5,4},{6,7},{7,6},{8,9},{9,8},{10,11... | collective-permute-start | bytes 811016 | tf_op jit(solution)/shard_map/ppermute | solution.py:31
  26.8 5.4 %collective-permute-start.13 = (bf16[256,512]{1,0:T(8,128)(2,1)S(1)}, bf16[256,512]{1,0:T(8,128)(2,1)S(1)}, u32[]{:S(2)}, u32[]{:S(2)}) collective-permute-start(bf16[256,512]{1,0:T(8,128)(2,1)S(1)} %shard_map.93.refs_4_), channel_id=1, source_target_pairs={{0,2},{2,0},{4,6},{6,4},{8,10},{10,8},{12,14},{14,12},{16,18},{18,... | collective-permute-start | bytes 786440 | tf_op jit(solution)/shard_map/ppermute | solution.py:31
  28.3 3.9 %collective-permute-start.8 = (bf16[256,512]{1,0:T(8,128)(2,1)S(1)}, bf16[256,512]{1,0:T(8,128)(2,1)S(1)}, u32[]{:S(2)}, u32[]{:S(2)}) collective-permute-start(bf16[256,512]{1,0:T(8,128)(2,1)S(1)} %collective-permute-done.6.refs_1_), channel_id=1, source_target_pairs={{0,2},{2,0},{4,6},{6,4},{8,10},{10,8},{12,14},{14,12},{16,18},{18,... | collective-permute-start | bytes 786440 | tf_op jit(solution)/shard_map/ppermute | solution.py:31
  31.1 1.5 %collective-permute-start.14 = (bf16[256,512]{1,0:T(8,128)(2,1)S(1)}, bf16[256,512]{1,0:T(8,128)(2,1)S(1)}, u32[]{:S(2)}, u32[]{:S(2)}) collective-permute-start(bf16[256,512]{1,0:T(8,128)(2,1)S(1)} %collective-permute-done.12.refs_5_), channel_id=1, source_target_pairs={{0,2},{2,0},{4,6},{6,4},{8,10},{10,8},{12,14},{14,12},{16,18},{18,... | collective-permute-start | bytes 786440 | tf_op jit(solution)/shard_map/ppermute | solution.py:31
  31.1 8.5 %collective-permute-start.16 = (bf16[112,1024]{1,0:T(8,128)(2,1)S(1)}, bf16[112,1024]{1,0:T(8,128)(2,1)S(1)}, u32[]{:S(2)}, u32[]{:S(2)}) collective-permute-start(bf16[112,1024]{1,0:T(8,128)(2,1)S(1)} %shard_map.96), channel_id=1, source_target_pairs={{0,1},{1,0},{2,3},{3,2},{4,5},{5,4},{6,7},{7,6},{8,9},{9,8},{10,11... | collective-permute-start | bytes 688136 | tf_op jit(solution)/shard_map/ppermute | solution.py:31
  32.2 1.5 %copy-start.3 = (s32[2,256]{1,0:T(2,128)S(1)}, s32[2,256]{1,0:T(2,128)}, u32[]{:S(2)}) copy-start(s32[2,256]{1,0:T(2,128)} %targets_ref.3) | copy-start | bytes 6148
  32.2 1.5 %copy-start.4 = (s32[2,256]{1,0:T(2,128)S(1)}, s32[2,256]{1,0:T(2,128)}, u32[]{:S(2)}) copy-start(s32[2,256]{1,0:T(2,128)} %valid_ref.3) | copy-start | bytes 6148
  34.4 10.4 %collective-permute-start.17 = (bf16[256,512]{1,0:T(8,128)(2,1)S(1)}, bf16[256,512]{1,0:T(8,128)(2,1)S(1)}, u32[]{:S(2)}, u32[]{:S(2)}) collective-permute-start(bf16[256,512]{1,0:T(8,128)(2,1)S(1)} %shard_map.95.grads_ref), channel_id=1, source_target_pairs={{0,1},{1,0},{2,3},{3,2},{4,5},{5,4},{6,7},{7,6},{8,9},{9,8},{10,11... | collective-permute-start | bytes 786440 | tf_op jit(solution)/shard_map/ppermute | solution.py:31
  40.1 4.7 %copy-start.5 = (s32[2]{0:T(128)S(1)}, s32[2]{0:T(128)}, u32[]{:S(2)}) copy-start(s32[2]{0:T(128)} %plan_ref.5) | copy-start | bytes 28
  46.4 2.0 %collective-permute-start.19 = (f32[512,256]{1,0:T(8,128)S(1)}, f32[512,256]{1,0:T(8,128)S(1)}, u32[]{:S(2)}, u32[]{:S(2)}) collective-permute-start(f32[512,256]{1,0:T(8,128)S(1)} %get-tuple-element.51), channel_id=1, source_target_pairs={{0,2},{2,0},{4,6},{6,4},{8,10},{10,8},{12,14},{14,12},{16,18},{18,... | collective-permute-start | bytes 1572872 | tf_op jit(solution)/shard_map/ppermute | solution.py:31
  46.5 8.9 %collective-permute-start.18 = (s32[264,256]{1,0:T(8,128)S(1)}, s32[264,256]{1,0:T(8,128)S(1)}, u32[]{:S(2)}, u32[]{:S(2)}) collective-permute-start(s32[264,256]{1,0:T(8,128)S(1)} %get-tuple-element.49), channel_id=1, source_target_pairs={{0,1},{1,0},{2,3},{3,2},{4,5},{5,4},{6,7},{7,6},{8,9},{9,8},{10,11... | collective-permute-start | bytes 811016 | tf_op jit(solution)/shard_map/ppermute | solution.py:31
  48.5 7.0 %collective-permute-start.20 = (s32[72,256]{1,0:T(8,128)S(1)}, s32[72,256]{1,0:T(8,128)S(1)}, u32[]{:S(2)}, u32[]{:S(2)}) collective-permute-start(s32[72,256]{1,0:T(8,128)S(1)} %get-tuple-element.52), channel_id=1, source_target_pairs={{0,24},{2,26},{4,28},{6,30},{8,16},{10,18},{12,20},{14,22},{16,8},... | collective-permute-start | bytes 221192 | tf_op jit(solution)/shard_map/ppermute | solution.py:31
  51.5 6.5 %collective-permute-start.22 = (s32[72,256]{1,0:T(8,128)S(1)}, s32[72,256]{1,0:T(8,128)S(1)}, u32[]{:S(2)}, u32[]{:S(2)}) collective-permute-start(s32[72,256]{1,0:T(8,128)S(1)} %get-tuple-element.55), channel_id=1, source_target_pairs={{0,16},{2,18},{4,20},{6,22},{8,24},{10,26},{12,28},{14,30},{16,0},... | collective-permute-start | bytes 221192 | tf_op jit(solution)/shard_map/ppermute | solution.py:31
  51.6 6.4 %collective-permute-start.23 = (s32[72,256]{1,0:T(8,128)S(1)}, s32[72,256]{1,0:T(8,128)S(1)}, u32[]{:S(2)}, u32[]{:S(2)}) collective-permute-start(s32[72,256]{1,0:T(8,128)S(1)} %get-tuple-element.56), channel_id=1, source_target_pairs={{0,8},{2,10},{4,12},{6,14},{8,0},{10,2},{12,4},{14,6},{16,24},{18,... | collective-permute-start | bytes 221192 | tf_op jit(solution)/shard_map/ppermute | solution.py:31
  56.2 7.8 %collective-permute-start.21 = (bf16[256,512]{1,0:T(8,128)(2,1)S(1)}, bf16[256,512]{1,0:T(8,128)(2,1)S(1)}, u32[]{:S(2)}, u32[]{:S(2)}) collective-permute-start(bf16[256,512]{1,0:T(8,128)(2,1)S(1)} %shard_map.102.grads_ref), channel_id=1, source_target_pairs={{0,1},{1,0},{2,3},{3,2},{4,5},{5,4},{6,7},{7,6},{8,9},{9,8},{10,11... | collective-permute-start | bytes 786440 | tf_op jit(solution)/shard_map/ppermute | solution.py:31
  65.3 2.0 %collective-permute-start.29 = (f32[512,256]{1,0:T(8,128)S(1)}, f32[512,256]{1,0:T(8,128)S(1)}, u32[]{:S(2)}, u32[]{:S(2)}) collective-permute-start(f32[512,256]{1,0:T(8,128)S(1)} %get-tuple-element.59), channel_id=1, source_target_pairs={{0,2},{2,0},{4,6},{6,4},{8,10},{10,8},{12,14},{14,12},{16,18},{18,... | collective-permute-start | bytes 1572872 | tf_op jit(solution)/shard_map/ppermute | solution.py:31
  65.3 6.5 %collective-permute-start.24 = (s32[72,256]{1,0:T(8,128)S(1)}, s32[72,256]{1,0:T(8,128)S(1)}, u32[]{:S(2)}, u32[]{:S(2)}) collective-permute-start(s32[72,256]{1,0:T(8,128)S(1)} %shard_map.104.refs_0_.one_ref), channel_id=1, source_target_pairs={{0,4},{2,6},{4,0},{6,2},{8,12},{10,14},{12,8},{14,10},{16,20},{18,... | collective-permute-start | bytes 221192 | tf_op jit(solution)/shard_map/ppermute | solution.py:31
  67.4 7.7 %collective-permute-start.30 = (s32[72,256]{1,0:T(8,128)S(1)}, s32[72,256]{1,0:T(8,128)S(1)}, u32[]{:S(2)}, u32[]{:S(2)}) collective-permute-start(s32[72,256]{1,0:T(8,128)S(1)} %get-tuple-element.61), channel_id=1, source_target_pairs={{0,24},{2,26},{4,28},{6,30},{8,16},{10,18},{12,20},{14,22},{16,8},... | collective-permute-start | bytes 221192 | tf_op jit(solution)/shard_map/ppermute | solution.py:31
  69.9 7.8 %collective-permute-start.31 = (s32[72,256]{1,0:T(8,128)S(1)}, s32[72,256]{1,0:T(8,128)S(1)}, u32[]{:S(2)}, u32[]{:S(2)}) collective-permute-start(s32[72,256]{1,0:T(8,128)S(1)} %get-tuple-element.62), channel_id=1, source_target_pairs={{0,16},{2,18},{4,20},{6,22},{8,24},{10,26},{12,28},{14,30},{16,0},... | collective-permute-start | bytes 221192 | tf_op jit(solution)/shard_map/ppermute | solution.py:31
  69.9 7.8 %collective-permute-start.32 = (s32[72,256]{1,0:T(8,128)S(1)}, s32[72,256]{1,0:T(8,128)S(1)}, u32[]{:S(2)}, u32[]{:S(2)}) collective-permute-start(s32[72,256]{1,0:T(8,128)S(1)} %get-tuple-element.63), channel_id=1, source_target_pairs={{0,8},{2,10},{4,12},{6,14},{8,0},{10,2},{12,4},{14,6},{16,24},{18,... | collective-permute-start | bytes 221192 | tf_op jit(solution)/shard_map/ppermute | solution.py:31
  71.9 9.9 %collective-permute-start.26 = (s32[72,256]{1,0:T(8,128)S(1)}, s32[72,256]{1,0:T(8,128)S(1)}, u32[]{:S(2)}, u32[]{:S(2)}) collective-permute-start(s32[72,256]{1,0:T(8,128)S(1)} %shard_map.106.refs_0_), channel_id=1, source_target_pairs={{0,16},{2,18},{4,20},{6,22},{8,24},{10,26},{12,28},{14,30},{16,0},... | collective-permute-start | bytes 221192 | tf_op jit(solution)/shard_map/ppermute | solution.py:31
  73.0 8.8 %collective-permute-start.25 = (s32[72,256]{1,0:T(8,128)S(1)}, s32[72,256]{1,0:T(8,128)S(1)}, u32[]{:S(2)}, u32[]{:S(2)}) collective-permute-start(s32[72,256]{1,0:T(8,128)S(1)} %shard_map.106.refs_0_), channel_id=1, source_target_pairs={{0,8},{2,10},{4,12},{6,14},{8,0},{10,2},{12,4},{14,6},{16,24},{18,... | collective-permute-start | bytes 221192 | tf_op jit(solution)/shard_map/ppermute | solution.py:31
  77.8 4.4 %collective-permute-start.33 = (s32[72,256]{1,0:T(8,128)S(1)}, s32[72,256]{1,0:T(8,128)S(1)}, u32[]{:S(2)}, u32[]{:S(2)}) collective-permute-start(s32[72,256]{1,0:T(8,128)S(1)} %shard_map.109.one_ref), channel_id=1, source_target_pairs={{0,4},{2,6},{4,0},{6,2},{8,12},{10,14},{12,8},{14,10},{16,20},{18,... | collective-permute-start | bytes 221192 | tf_op jit(solution)/shard_map/ppermute | solution.py:31
  79.4 7.4 %collective-permute-start.27 = (s32[72,256]{1,0:T(8,128)S(1)}, s32[72,256]{1,0:T(8,128)S(1)}, u32[]{:S(2)}, u32[]{:S(2)}) collective-permute-start(s32[72,256]{1,0:T(8,128)S(1)} %shard_map.106.refs_0_), channel_id=1, source_target_pairs={{0,24},{2,26},{4,28},{6,30},{8,16},{10,18},{12,20},{14,22},{16,8},... | collective-permute-start | bytes 221192 | tf_op jit(solution)/shard_map/ppermute | solution.py:31
  82.3 6.9 %collective-permute-start.36 = (s32[72,256]{1,0:T(8,128)S(1)}, s32[72,256]{1,0:T(8,128)S(1)}, u32[]{:S(2)}, u32[]{:S(2)}) collective-permute-start(s32[72,256]{1,0:T(8,128)S(1)} %shard_map.110.refs_0_), channel_id=1, source_target_pairs={{0,24},{2,26},{4,28},{6,30},{8,16},{10,18},{12,20},{14,22},{16,8},... | collective-permute-start | bytes 221192 | tf_op jit(solution)/shard_map/ppermute | solution.py:31
  84.8 6.3 %collective-permute-start.35 = (s32[72,256]{1,0:T(8,128)S(1)}, s32[72,256]{1,0:T(8,128)S(1)}, u32[]{:S(2)}, u32[]{:S(2)}) collective-permute-start(s32[72,256]{1,0:T(8,128)S(1)} %shard_map.110.refs_0_), channel_id=1, source_target_pairs={{0,16},{2,18},{4,20},{6,22},{8,24},{10,26},{12,28},{14,30},{16,0},... | collective-permute-start | bytes 221192 | tf_op jit(solution)/shard_map/ppermute | solution.py:31
  84.8 6.3 %collective-permute-start.34 = (s32[72,256]{1,0:T(8,128)S(1)}, s32[72,256]{1,0:T(8,128)S(1)}, u32[]{:S(2)}, u32[]{:S(2)}) collective-permute-start(s32[72,256]{1,0:T(8,128)S(1)} %shard_map.110.refs_0_), channel_id=1, source_target_pairs={{0,8},{2,10},{4,12},{6,14},{8,0},{10,2},{12,4},{14,6},{16,24},{18,... | collective-permute-start | bytes 221192 | tf_op jit(solution)/shard_map/ppermute | solution.py:31
  87.2 4.4 %collective-permute-start.28 = (s32[288,256]{1,0:T(8,128)S(1)}, s32[288,256]{1,0:T(8,128)S(1)}, u32[]{:S(2)}, u32[]{:S(2)}) collective-permute-start(s32[288,256]{1,0:T(8,128)S(1)} %shard_map.107.own0), channel_id=1, source_target_pairs={{0,2},{2,0},{4,6},{6,4},{8,10},{10,8},{12,14},{14,12},{16,18},{18,... | collective-permute-start | bytes 884744 | tf_op jit(solution)/shard_map/ppermute | solution.py:31
  91.6 1.6 %collective-permute-start.37 = (s32[288,256]{1,0:T(8,128)S(1)}, s32[288,256]{1,0:T(8,128)S(1)}, u32[]{:S(2)}, u32[]{:S(2)}) collective-permute-start(s32[288,256]{1,0:T(8,128)S(1)} %shard_map.111.own1), channel_id=1, source_target_pairs={{0,2},{2,0},{4,6},{6,4},{8,10},{10,8},{12,14},{14,12},{16,18},{18,... | collective-permute-start | bytes 884744 | tf_op jit(solution)/shard_map/ppermute | solution.py:31

commit v8 on v7

--- a/solution.py
+++ b/solution.py
@@ -186,6 +186,7 @@
 
 MASKS = (3, 2, 1)
 COST = {
+    "after": 100000000,
     "stacked": 5000000000,
     "more_reference_logs": 100000000,
     "own_logits": 100000000,
@@ -728,7 +729,7 @@
     halfway = own_update(inner, normed0, grads, features1b)
     refer_log = more_reference_logs(normed1, whole, halfway)
     inner, sent, kept, features1, weights, partial = update(
-        halfway, features0, partner_grads, outer_head, plan, 0, replicas, (features1a, features1b), (refer_log,)
+        halfway, features0, partner_grads, outer_head, plan, 0, replicas, (features1a, features1b), ()
     )
 
     received = swap(partial, "fsdp", 1)

time: 96.1 us -> 96.1 us (level)
  transfers between devices with their start and end apart: 38 -> 38, of which waited for: 19 -> 18; matrix products, arithmetic and copies ran while one was open for 0% -> 0% of each run, Pallas kernels for 9% -> 9%
where the time goes in v8:
time: 96.1 us; the launch traced here: 96 us
  starting transfers between devices  44.4 us (46%)
  waiting for transfers between devices  34.3 us (36%)
  Pallas kernels  14.6 us (15%)
  local copies, waits for them, and re-layouts  1.74 us (2%)
  between operations  0.99 us (1%)
    ppermute x38, starting transfers between devices, swap(): return lax.ppermute(value, axis, [(i, i ^ mask) for i in range(size)])  44.4 us
    ppermute x38, waiting for transfers between devices, swap(): return lax.ppermute(value, axis, [(i, i ^ mask) for i in range(size)])  34.3 us
    pallas_call x27, Pallas kernels, call(): pl.pallas_call(kernel, out_shape=out_shape, in_specs=in_specs, out_specs=...  14.6 us
  transfers between devices with their start and end apart: 38, of which 18 were waited for; matrix products, arithmetic and copies ran while one was open for 0% of the time, Pallas kernels for 9%

profile of v8, /device:TPU:0, one launch (start us, length us, event | category | flops | bytes accessed | tf_op | source)
XLA Modules:
  0.0 96.0 jit_solution(454458392553934402)
XLA Ops:
  0.6 1.7 %slice_bitcast_fusion = (bf16[256,2048]{1,0:T(8,128)(2,1)S(1)}, bf16[256,2048]{1,0:T(8,128)(2,1)S(1)}) fusion(bf16[2,256,2048]{2,1,0:T(8,128)(2,1)} %param.7), kind=kLoop, calls=%fused_computation | loop fusion | bytes 4194304 | tf_op jit(solution)/shard_map/squeeze | solution.py:715
  2.8 3.0 %collective-permute-start = (bf16[96,1024]{1,0:T(8,128)(2,1)S(1)}, bf16[96,1024]{1,0:T(8,128)(2,1)S(1)}, u32[]{:S(2)}, u32[]{:S(2)}) collective-permute-start(bf16[96,1024]{1,0:T(8,128)(2,1)S(1)} %get-tuple-element.34.refs_1_), channel_id=1, source_target_pairs={{0,1},{1,0},{2,3},{3,2},{4,5},{5,4},{6,7},{7,6},{8,9},{9,8},{10,11... | collective-permute-start | bytes 589832 | tf_op jit(solution)/shard_map/ppermute | solution.py:31
  6.2 3.7 %collective-permute-start.5 = (bf16[64,512]{1,0:T(8,128)(2,1)S(1)}, bf16[64,512]{1,0:T(8,128)(2,1)S(1)}, u32[]{:S(2)}, u32[]{:S(2)}) collective-permute-start(bf16[64,512]{1,0:T(8,128)(2,1)S(1)} %get-tuple-element.41.refs_0_), channel_id=1, source_target_pairs={{0,24},{2,26},{4,28},{6,30},{8,16},{10,18},{12,20},{14,22},{16,8},... | collective-permute-start | bytes 196616 | tf_op jit(solution)/shard_map/ppermute | solution.py:31
  9.9 0.8 collective-permute-start.3
  11.1 1.6 %collective-permute-start.15 = (bf16[144,1024]{1,0:T(8,128)(2,1)S(1)}, bf16[144,1024]{1,0:T(8,128)(2,1)S(1)}, u32[]{:S(2)}, u32[]{:S(2)}) collective-permute-start(bf16[144,1024]{1,0:T(8,128)(2,1)S(1)} %get-tuple-element.42), channel_id=1, source_target_pairs={{0,1},{1,0},{2,3},{3,2},{4,5},{5,4},{6,7},{7,6},{8,9},{9,8},{10,11... | collective-permute-start | bytes 884744 | tf_op jit(solution)/shard_map/ppermute | solution.py:31
  13.1 3.6 %collective-permute-start.11 = (bf16[64,512]{1,0:T(8,128)(2,1)S(1)}, bf16[64,512]{1,0:T(8,128)(2,1)S(1)}, u32[]{:S(2)}, u32[]{:S(2)}) collective-permute-start(bf16[64,512]{1,0:T(8,128)(2,1)S(1)} %shard_map.92.refs_0_), channel_id=1, source_target_pairs={{0,24},{2,26},{4,28},{6,30},{8,16},{10,18},{12,20},{14,22},{16,8},... | collective-permute-start | bytes 196616 | tf_op jit(solution)/shard_map/ppermute | solution.py:31
  16.8 2.2 %collective-permute-start.9 = (bf16[64,512]{1,0:T(8,128)(2,1)S(1)}, bf16[64,512]{1,0:T(8,128)(2,1)S(1)}, u32[]{:S(2)}, u32[]{:S(2)}) collective-permute-start(bf16[64,512]{1,0:T(8,128)(2,1)S(1)} %shard_map.92.refs_0_), channel_id=1, source_target_pairs={{0,8},{2,10},{4,12},{6,14},{8,0},{10,2},{12,4},{14,6},{16,24},{18,... | collective-permute-start | bytes 196616 | tf_op jit(solution)/shard_map/ppermute | solution.py:31
  19.3 1.6 %collective-permute-start.6 = (bf16[256,512]{1,0:T(8,128)(2,1)S(1)}, bf16[256,512]{1,0:T(8,128)(2,1)S(1)}, u32[]{:S(2)}, u32[]{:S(2)}) collective-permute-start(bf16[256,512]{1,0:T(8,128)(2,1)S(1)} %shard_map.91.refs_0_), channel_id=1, source_target_pairs={{0,4},{2,6},{4,0},{6,2},{8,12},{10,14},{12,8},{14,10},{16,20},{18,... | collective-permute-start | bytes 786440 | tf_op jit(solution)/shard_map/ppermute | solution.py:31
  20.9 1.0 %collective-permute-done.10.refs_2_ = bf16[64,512]{1,0:T(8,128)(2,1)S(1)} collective-permute-done((bf16[64,512]{1,0:T(8,128)(2,1)S(1)}, bf16[64,512]{1,0:T(8,128)(2,1)S(1)}, u32[]{:S(2)}, u32[]{:S(2)}) %collective-permute-start.10) | collective-permute-done | bytes 65568 | tf_op jit(solution)/shard_map/ppermute | solution.py:31
  22.3 1.6 %collective-permute-start.12 = (bf16[256,512]{1,0:T(8,128)(2,1)S(1)}, bf16[256,512]{1,0:T(8,128)(2,1)S(1)}, u32[]{:S(2)}, u32[]{:S(2)}) collective-permute-start(bf16[256,512]{1,0:T(8,128)(2,1)S(1)} %shard_map.93.refs_4_), channel_id=1, source_target_pairs={{0,4},{2,6},{4,0},{6,2},{8,12},{10,14},{12,8},{14,10},{16,20},{18,... | collective-permute-start | bytes 786440 | tf_op jit(solution)/shard_map/ppermute | solution.py:31
  24.2 0.5 shard_map.89
  24.7 0.6 collective-permute-start.2
  25.3 1.5 %collective-permute-done.15.refs_8_.refs_0_ = bf16[144,1024]{1,0:T(8,128)(2,1)S(1)} collective-permute-done((bf16[144,1024]{1,0:T(8,128)(2,1)S(1)}, bf16[144,1024]{1,0:T(8,128)(2,1)S(1)}, u32[]{:S(2)}, u32[]{:S(2)}) %collective-permute-start.15) | collective-permute-done | bytes 294944 | tf_op jit(solution)/shard_map/ppermute | solution.py:31
  26.9 1.5 %collective-permute-done.6.refs_1_ = bf16[256,512]{1,0:T(8,128)(2,1)S(1)} collective-permute-done((bf16[256,512]{1,0:T(8,128)(2,1)S(1)}, bf16[256,512]{1,0:T(8,128)(2,1)S(1)}, u32[]{:S(2)}, u32[]{:S(2)}) %collective-permute-start.6) | collective-permute-done | bytes 262176 | tf_op jit(solution)/shard_map/ppermute | solution.py:31
  28.3 2.8 %collective-permute-done.12.refs_5_ = bf16[256,512]{1,0:T(8,128)(2,1)S(1)} collective-permute-done((bf16[256,512]{1,0:T(8,128)(2,1)S(1)}, bf16[256,512]{1,0:T(8,128)(2,1)S(1)}, u32[]{:S(2)}, u32[]{:S(2)}) %collective-permute-start.12) | collective-permute-done | bytes 262176 | tf_op jit(solution)/shard_map/ppermute | solution.py:31
  31.1 0.6 collective-permute-start.16
  32.7 1.0 %shard_map.94 = (f32[256,512]{1,0:T(8,128)S(1)}, bf16[2048,512]{1,0:T(8,128)(2,1)S(1)}) custom-call(bf16[256,2048]{1,0:T(8,128)(2,1)S(1)} %get-tuple-element.38.normed_ref, bf16[256,512]{1,0:T(8,128)(2,1)S(1)} %shard_map.91.refs_0_, bf16[256,512]{1,0:T(8,128)(2,1)S(1)} %collective-permute-done.6.refs_1_, ...), custom_call_target="tpu_custom_call" | custom-call | flops 1000 | bytes 1000 | tf_op jit(solution)/shard_map/pallas_call | solution.py:203
  33.7 0.6 shard_map.95.grads_ref
  34.4 1.1 %collective-permute-start.17 = (bf16[256,512]{1,0:T(8,128)(2,1)S(1)}, bf16[256,512]{1,0:T(8,128)(2,1)S(1)}, u32[]{:S(2)}, u32[]{:S(2)}) collective-permute-start(bf16[256,512]{1,0:T(8,128)(2,1)S(1)} %shard_map.95.grads_ref), channel_id=1, source_target_pairs={{0,1},{1,0},{2,3},{3,2},{4,5},{5,4},{6,7},{7,6},{8,9},{9,8},{10,11... | collective-permute-start | bytes 786440 | tf_op jit(solution)/shard_map/ppermute | solution.py:31
  35.5 4.1 %collective-permute-done.16.refs_0_.refs_1_ = bf16[112,1024]{1,0:T(8,128)(2,1)S(1)} collective-permute-done((bf16[112,1024]{1,0:T(8,128)(2,1)S(1)}, bf16[112,1024]{1,0:T(8,128)(2,1)S(1)}, u32[]{:S(2)}, u32[]{:S(2)}) %collective-permute-start.16) | collective-permute-done | bytes 229408 | tf_op jit(solution)/shard_map/ppermute | solution.py:31
  40.1 4.7 %collective-permute-done.17.grads_ref = bf16[256,512]{1,0:T(8,128)(2,1)S(1)} collective-permute-done((bf16[256,512]{1,0:T(8,128)(2,1)S(1)}, bf16[256,512]{1,0:T(8,128)(2,1)S(1)}, u32[]{:S(2)}, u32[]{:S(2)}) %collective-permute-start.17) | collective-permute-done | bytes 262176 | tf_op jit(solution)/shard_map/ppermute | solution.py:31
  44.8 1.6 %shard_map.98 = (f32[1024,512]{1,0:T(8,128)S(1)}, f32[512,256]{1,0:T(8,128)S(1)}, f32[512,256]{1,0:T(8,128)S(1)}, bf16[256,1024]{1,0:T(8,128)(2,1)S(1)}, bf16[10...) custom-call(s32[2]{0:T(128)S(1)} %copy-done.5, f32[1024,512]{1,0:T(8,128)S(1)} %shard_map.97.inner_ref.refs_0_, ...), custom_call_target="tpu_custom_call" | custom-call | flops 1000000000 | bytes 1000 | tf_op jit(solution)/shard_map/pallas_call | solution.py:203
  46.5 0.6 collective-permute-start.18
  47.1 1.3 %collective-permute-done.19.received_ref = f32[512,256]{1,0:T(8,128)S(1)} collective-permute-done((f32[512,256]{1,0:T(8,128)S(1)}, f32[512,256]{1,0:T(8,128)S(1)}, u32[]{:S(2)}, u32[]{:S(2)}) %collective-permute-start.19) | collective-permute-done | bytes 524320 | tf_op jit(solution)/shard_map/ppermute | solution.py:31
  48.6 2.5 %collective-permute-start.20 = (s32[72,256]{1,0:T(8,128)S(1)}, s32[72,256]{1,0:T(8,128)S(1)}, u32[]{:S(2)}, u32[]{:S(2)}) collective-permute-start(s32[72,256]{1,0:T(8,128)S(1)} %get-tuple-element.52), channel_id=1, source_target_pairs={{0,24},{2,26},{4,28},{6,30},{8,16},{10,18},{12,20},{14,22},{16,8},... | collective-permute-start | bytes 221192 | tf_op jit(solution)/shard_map/ppermute | solution.py:31
  51.1 0.9 shard_map.100.refer_ref
  52.5 1.9 %collective-permute-start.23 = (s32[72,256]{1,0:T(8,128)S(1)}, s32[72,256]{1,0:T(8,128)S(1)}, u32[]{:S(2)}, u32[]{:S(2)}) collective-permute-start(s32[72,256]{1,0:T(8,128)S(1)} %get-tuple-element.56), channel_id=1, source_target_pairs={{0,8},{2,10},{4,12},{6,14},{8,0},{10,2},{12,4},{14,6},{16,24},{18,... | collective-permute-start | bytes 221192 | tf_op jit(solution)/shard_map/ppermute | solution.py:31
  54.4 1.0 %collective-permute-done.18.received_ref = s32[264,256]{1,0:T(8,128)S(1)} collective-permute-done((s32[264,256]{1,0:T(8,128)S(1)}, s32[264,256]{1,0:T(8,128)S(1)}, u32[]{:S(2)}, u32[]{:S(2)}) %collective-permute-start.18) | collective-permute-done | bytes 270368 | tf_op jit(solution)/shard_map/ppermute | solution.py:31
  55.4 0.6 shard_map.102.grads_ref
  56.1 0.6 collective-permute-start.21
  56.7 0.5 shard_map.103.refs_3_.inner_ref
  57.2 1.1 %collective-permute-done.22.refs_1_ = s32[72,256]{1,0:T(8,128)S(1)} collective-permute-done((s32[72,256]{1,0:T(8,128)S(1)}, s32[72,256]{1,0:T(8,128)S(1)}, u32[]{:S(2)}, u32[]{:S(2)}) %collective-permute-start.22) | collective-permute-done | bytes 73760 | tf_op jit(solution)/shard_map/ppermute | solution.py:31
  58.4 5.6 %collective-permute-done.21.grads_ref = bf16[256,512]{1,0:T(8,128)(2,1)S(1)} collective-permute-done((bf16[256,512]{1,0:T(8,128)(2,1)S(1)}, bf16[256,512]{1,0:T(8,128)(2,1)S(1)}, u32[]{:S(2)}, u32[]{:S(2)}) %collective-permute-start.21) | collective-permute-done | bytes 262176 | tf_op jit(solution)/shard_map/ppermute | solution.py:31
  64.0 1.3 %shard_map.105 = (f32[1024,512]{1,0:T(8,128)S(1)}, f32[512,256]{1,0:T(8,128)S(1)}, f32[512,256]{1,0:T(8,128)S(1)}) custom-call(s32[2]{0:T(128)S(1)} %copy-done.5, f32[1024,512]{1,0:T(8,128)S(1)} %shard_map.103.refs_3_.inner_ref, bf16[256,1024]{1,0:T(8,128)(2,1)S(1)} %get-tuple-element.53.features_ref, ...), custom_call_target="tpu_custom_call" | custom-call | flops 1000000000 | bytes 1000 | tf_op jit(solution)/shard_map/pallas_call | solution.py:203
  65.3 1.6 %collective-permute-start.24 = (s32[72,256]{1,0:T(8,128)S(1)}, s32[72,256]{1,0:T(8,128)S(1)}, u32[]{:S(2)}, u32[]{:S(2)}) collective-permute-start(s32[72,256]{1,0:T(8,128)S(1)} %shard_map.104.refs_0_.one_ref), channel_id=1, source_target_pairs={{0,4},{2,6},{4,0},{6,2},{8,12},{10,14},{12,8},{14,10},{16,20},{18,... | collective-permute-start | bytes 221192 | tf_op jit(solution)/shard_map/ppermute | solution.py:31
  67.4 2.5 %collective-permute-start.30 = (s32[72,256]{1,0:T(8,128)S(1)}, s32[72,256]{1,0:T(8,128)S(1)}, u32[]{:S(2)}, u32[]{:S(2)}) collective-permute-start(s32[72,256]{1,0:T(8,128)S(1)} %get-tuple-element.61), channel_id=1, source_target_pairs={{0,24},{2,26},{4,28},{6,30},{8,16},{10,18},{12,20},{14,22},{16,8},... | collective-permute-start | bytes 221192 | tf_op jit(solution)/shard_map/ppermute | solution.py:31
  69.9 1.9 %collective-permute-start.32 = (s32[72,256]{1,0:T(8,128)S(1)}, s32[72,256]{1,0:T(8,128)S(1)}, u32[]{:S(2)}, u32[]{:S(2)}) collective-permute-start(s32[72,256]{1,0:T(8,128)S(1)} %get-tuple-element.63), channel_id=1, source_target_pairs={{0,8},{2,10},{4,12},{6,14},{8,0},{10,2},{12,4},{14,6},{16,24},{18,... | collective-permute-start | bytes 221192 | tf_op jit(solution)/shard_map/ppermute | solution.py:31
  71.9 1.1 %collective-permute-start.26 = (s32[72,256]{1,0:T(8,128)S(1)}, s32[72,256]{1,0:T(8,128)S(1)}, u32[]{:S(2)}, u32[]{:S(2)}) collective-permute-start(s32[72,256]{1,0:T(8,128)S(1)} %shard_map.106.refs_0_), channel_id=1, source_target_pairs={{0,16},{2,18},{4,20},{6,22},{8,24},{10,26},{12,28},{14,30},{16,0},... | collective-permute-start | bytes 221192 | tf_op jit(solution)/shard_map/ppermute | solution.py:31
  73.0 2.0 %collective-permute-start.25 = (s32[72,256]{1,0:T(8,128)S(1)}, s32[72,256]{1,0:T(8,128)S(1)}, u32[]{:S(2)}, u32[]{:S(2)}) collective-permute-start(s32[72,256]{1,0:T(8,128)S(1)} %shard_map.106.refs_0_), channel_id=1, source_target_pairs={{0,8},{2,10},{4,12},{6,14},{8,0},{10,2},{12,4},{14,6},{16,24},{18,... | collective-permute-start | bytes 221192 | tf_op jit(solution)/shard_map/ppermute | solution.py:31
  75.1 2.7 %collective-permute-done.31.refs_1_ = s32[72,256]{1,0:T(8,128)S(1)} collective-permute-done((s32[72,256]{1,0:T(8,128)S(1)}, s32[72,256]{1,0:T(8,128)S(1)}, u32[]{:S(2)}, u32[]{:S(2)}) %collective-permute-start.31) | collective-permute-done | bytes 73760 | tf_op jit(solution)/shard_map/ppermute | solution.py:31
  77.8 1.6 %collective-permute-start.33 = (s32[72,256]{1,0:T(8,128)S(1)}, s32[72,256]{1,0:T(8,128)S(1)}, u32[]{:S(2)}, u32[]{:S(2)}) collective-permute-start(s32[72,256]{1,0:T(8,128)S(1)} %shard_map.109.one_ref), channel_id=1, source_target_pairs={{0,4},{2,6},{4,0},{6,2},{8,12},{10,14},{12,8},{14,10},{16,20},{18,... | collective-permute-start | bytes 221192 | tf_op jit(solution)/shard_map/ppermute | solution.py:31
  79.4 2.4 %collective-permute-start.27 = (s32[72,256]{1,0:T(8,128)S(1)}, s32[72,256]{1,0:T(8,128)S(1)}, u32[]{:S(2)}, u32[]{:S(2)}) collective-permute-start(s32[72,256]{1,0:T(8,128)S(1)} %shard_map.106.refs_0_), channel_id=1, source_target_pairs={{0,24},{2,26},{4,28},{6,30},{8,16},{10,18},{12,20},{14,22},{16,8},... | collective-permute-start | bytes 221192 | tf_op jit(solution)/shard_map/ppermute | solution.py:31
  82.4 2.5 %collective-permute-start.36 = (s32[72,256]{1,0:T(8,128)S(1)}, s32[72,256]{1,0:T(8,128)S(1)}, u32[]{:S(2)}, u32[]{:S(2)}) collective-permute-start(s32[72,256]{1,0:T(8,128)S(1)} %shard_map.110.refs_0_), channel_id=1, source_target_pairs={{0,24},{2,26},{4,28},{6,30},{8,16},{10,18},{12,20},{14,22},{16,8},... | collective-permute-start | bytes 221192 | tf_op jit(solution)/shard_map/ppermute | solution.py:31
  84.8 2.0 %collective-permute-start.34 = (s32[72,256]{1,0:T(8,128)S(1)}, s32[72,256]{1,0:T(8,128)S(1)}, u32[]{:S(2)}, u32[]{:S(2)}) collective-permute-start(s32[72,256]{1,0:T(8,128)S(1)} %shard_map.110.refs_0_), channel_id=1, source_target_pairs={{0,8},{2,10},{4,12},{6,14},{8,0},{10,2},{12,4},{14,6},{16,24},{18,... | collective-permute-start | bytes 221192 | tf_op jit(solution)/shard_map/ppermute | solution.py:31
  87.3 2.0 %collective-permute-done.36.refs_3_ = s32[72,256]{1,0:T(8,128)S(1)} collective-permute-done((s32[72,256]{1,0:T(8,128)S(1)}, s32[72,256]{1,0:T(8,128)S(1)}, u32[]{:S(2)}, u32[]{:S(2)}) %collective-permute-start.36) | collective-permute-done | bytes 73760 | tf_op jit(solution)/shard_map/ppermute | solution.py:31
  89.3 1.8 %collective-permute-done.35.refs_2_ = s32[72,256]{1,0:T(8,128)S(1)} collective-permute-done((s32[72,256]{1,0:T(8,128)S(1)}, s32[72,256]{1,0:T(8,128)S(1)}, u32[]{:S(2)}, u32[]{:S(2)}) %collective-permute-start.35) | collective-permute-done | bytes 73760 | tf_op jit(solution)/shard_map/ppermute | solution.py:31
  91.7 1.6 %collective-permute-done.37.other1 = s32[288,256]{1,0:T(8,128)S(1)} collective-permute-done((s32[288,256]{1,0:T(8,128)S(1)}, s32[288,256]{1,0:T(8,128)S(1)}, u32[]{:S(2)}, u32[]{:S(2)}) %collective-permute-start.37) | collective-permute-done | bytes 294944 | tf_op jit(solution)/shard_map/ppermute | solution.py:31
  93.2 2.8 %shard_map.112 = (f32[1024,512]{1,0:T(8,128)}, f32[1024,512]{1,0:T(8,128)}) custom-call(s32[2]{0:T(128)S(1)} %copy-done.5, f32[1024,512]{1,0:T(8,128)S(1)} %copy-done, f32[1024,512]{1,0:T(8,128)S(1)} %get-tuple-element.57.inner_ref, s32[288,256]{1,0:T(8,128)S(1)} %shard_map.107.own0, s32[288,256]{1,0:T(8,128)S(1)} %collective-permute-done.28.other0, ...), custom_call_target="tpu_custom_call" | custom-call | flops 1000 | bytes 1000 | tf_op jit(solution)/shard_map/pallas_call | solution.py:203
  (68 shorter events, 7.1 us)
Async XLA Ops:
  0.6 1.7 %copy-start.2 = (bf16[64,512]{1,0:T(8,128)(2,1)S(1)}, bf16[64,512]{1,0:T(8,128)(2,1)}, u32[]{:S(2)}) copy-start(bf16[64,512]{1,0:T(8,128)(2,1)} %refs_0_.3) | copy-start | bytes 196612
  2.8 8.3 %collective-permute-start = (bf16[96,1024]{1,0:T(8,128)(2,1)S(1)}, bf16[96,1024]{1,0:T(8,128)(2,1)S(1)}, u32[]{:S(2)}, u32[]{:S(2)}) collective-permute-start(bf16[96,1024]{1,0:T(8,128)(2,1)S(1)} %get-tuple-element.34.refs_1_), channel_id=1, source_target_pairs={{0,1},{1,0},{2,3},{3,2},{4,5},{5,4},{6,7},{7,6},{8,9},{9,8},{10,11... | collective-permute-start | bytes 589832 | tf_op jit(solution)/shard_map/ppermute | solution.py:31
  6.2 6.9 %collective-permute-start.5 = (bf16[64,512]{1,0:T(8,128)(2,1)S(1)}, bf16[64,512]{1,0:T(8,128)(2,1)S(1)}, u32[]{:S(2)}, u32[]{:S(2)}) collective-permute-start(bf16[64,512]{1,0:T(8,128)(2,1)S(1)} %get-tuple-element.41.refs_0_), channel_id=1, source_target_pairs={{0,24},{2,26},{4,28},{6,30},{8,16},{10,18},{12,20},{14,22},{16,8},... | collective-permute-start | bytes 196616 | tf_op jit(solution)/shard_map/ppermute | solution.py:31
  9.9 6.9 %collective-permute-start.4 = (bf16[64,512]{1,0:T(8,128)(2,1)S(1)}, bf16[64,512]{1,0:T(8,128)(2,1)S(1)}, u32[]{:S(2)}, u32[]{:S(2)}) collective-permute-start(bf16[64,512]{1,0:T(8,128)(2,1)S(1)} %get-tuple-element.41.refs_0_), channel_id=1, source_target_pairs={{0,16},{2,18},{4,20},{6,22},{8,24},{10,26},{12,28},{14,30},{16,0},... | collective-permute-start | bytes 196616 | tf_op jit(solution)/shard_map/ppermute | solution.py:31
  9.9 6.9 %collective-permute-start.3 = (bf16[64,512]{1,0:T(8,128)(2,1)S(1)}, bf16[64,512]{1,0:T(8,128)(2,1)S(1)}, u32[]{:S(2)}, u32[]{:S(2)}) collective-permute-start(bf16[64,512]{1,0:T(8,128)(2,1)S(1)} %get-tuple-element.41.refs_0_), channel_id=1, source_target_pairs={{0,8},{2,10},{4,12},{6,14},{8,0},{10,2},{12,4},{14,6},{16,24},{18,... | collective-permute-start | bytes 196616 | tf_op jit(solution)/shard_map/ppermute | solution.py:31
  10.7 13.5 %collective-permute-start.1 = (bf16[192,1024]{1,0:T(8,128)(2,1)S(1)}, bf16[192,1024]{1,0:T(8,128)(2,1)S(1)}, u32[]{:S(2)}, u32[]{:S(2)}) collective-permute-start(bf16[192,1024]{1,0:T(8,128)(2,1)S(1)} %get-tuple-element.35.refs_2_), channel_id=1, source_target_pairs={{0,1},{1,0},{2,3},{3,2},{4,5},{5,4},{6,7},{7,6},{8,9},{9,8},{10,11... | collective-permute-start | bytes 1179656 | tf_op jit(solution)/shard_map/ppermute | solution.py:31
  11.1 15.8 %collective-permute-start.15 = (bf16[144,1024]{1,0:T(8,128)(2,1)S(1)}, bf16[144,1024]{1,0:T(8,128)(2,1)S(1)}, u32[]{:S(2)}, u32[]{:S(2)}) collective-permute-start(bf16[144,1024]{1,0:T(8,128)(2,1)S(1)} %get-tuple-element.42), channel_id=1, source_target_pairs={{0,1},{1,0},{2,3},{3,2},{4,5},{5,4},{6,7},{7,6},{8,9},{9,8},{10,11... | collective-permute-start | bytes 884744 | tf_op jit(solution)/shard_map/ppermute | solution.py:31
  13.1 6.2 %collective-permute-start.11 = (bf16[64,512]{1,0:T(8,128)(2,1)S(1)}, bf16[64,512]{1,0:T(8,128)(2,1)S(1)}, u32[]{:S(2)}, u32[]{:S(2)}) collective-permute-start(bf16[64,512]{1,0:T(8,128)(2,1)S(1)} %shard_map.92.refs_0_), channel_id=1, source_target_pairs={{0,24},{2,26},{4,28},{6,30},{8,16},{10,18},{12,20},{14,22},{16,8},... | collective-permute-start | bytes 196616 | tf_op jit(solution)/shard_map/ppermute | solution.py:31
  16.8 5.2 %collective-permute-start.10 = (bf16[64,512]{1,0:T(8,128)(2,1)S(1)}, bf16[64,512]{1,0:T(8,128)(2,1)S(1)}, u32[]{:S(2)}, u32[]{:S(2)}) collective-permute-start(bf16[64,512]{1,0:T(8,128)(2,1)S(1)} %shard_map.92.refs_0_), channel_id=1, source_target_pairs={{0,16},{2,18},{4,20},{6,22},{8,24},{10,26},{12,28},{14,30},{16,0},... | collective-permute-start | bytes 196616 | tf_op jit(solution)/shard_map/ppermute | solution.py:31
  16.8 5.2 %collective-permute-start.9 = (bf16[64,512]{1,0:T(8,128)(2,1)S(1)}, bf16[64,512]{1,0:T(8,128)(2,1)S(1)}, u32[]{:S(2)}, u32[]{:S(2)}) collective-permute-start(bf16[64,512]{1,0:T(8,128)(2,1)S(1)} %shard_map.92.refs_0_), channel_id=1, source_target_pairs={{0,8},{2,10},{4,12},{6,14},{8,0},{10,2},{12,4},{14,6},{16,24},{18,... | collective-permute-start | bytes 196616 | tf_op jit(solution)/shard_map/ppermute | solution.py:31
  19.3 4.6 %copy-start = (f32[1024,512]{1,0:T(8,128)S(1)}, f32[1024,512]{1,0:T(8,128)}, u32[]{:S(2)}) copy-start(f32[1024,512]{1,0:T(8,128)} %outer_ref.7) | copy-start | bytes 6291460
  19.3 4.6 %copy-start.1 = (bf16[1,1024,512]{2,1,0:T(8,128)(2,1)S(1)}, bf16[1,1024,512]{2,1,0:T(8,128)(2,1)}, u32[]{:S(2)}) copy-start(bf16[1,1024,512]{2,1,0:T(8,128)(2,1)} %drift_ref.1) | copy-start | bytes 3145732
  19.3 9.0 %collective-permute-start.6 = (bf16[256,512]{1,0:T(8,128)(2,1)S(1)}, bf16[256,512]{1,0:T(8,128)(2,1)S(1)}, u32[]{:S(2)}, u32[]{:S(2)}) collective-permute-start(bf16[256,512]{1,0:T(8,128)(2,1)S(1)} %shard_map.91.refs_0_), channel_id=1, source_target_pairs={{0,4},{2,6},{4,0},{6,2},{8,12},{10,14},{12,8},{14,10},{16,20},{18,... | collective-permute-start | bytes 786440 | tf_op jit(solution)/shard_map/ppermute | solution.py:31
  22.3 8.8 %collective-permute-start.12 = (bf16[256,512]{1,0:T(8,128)(2,1)S(1)}, bf16[256,512]{1,0:T(8,128)(2,1)S(1)}, u32[]{:S(2)}, u32[]{:S(2)}) collective-permute-start(bf16[256,512]{1,0:T(8,128)(2,1)S(1)} %shard_map.93.refs_4_), channel_id=1, source_target_pairs={{0,4},{2,6},{4,0},{6,2},{8,12},{10,14},{12,8},{14,10},{16,20},{18,... | collective-permute-start | bytes 786440 | tf_op jit(solution)/shard_map/ppermute | solution.py:31
  23.9 7.2 %collective-permute-start.7 = (bf16[256,512]{1,0:T(8,128)(2,1)S(1)}, bf16[256,512]{1,0:T(8,128)(2,1)S(1)}, u32[]{:S(2)}, u32[]{:S(2)}) collective-permute-start(bf16[256,512]{1,0:T(8,128)(2,1)S(1)} %shard_map.91.refs_0_), channel_id=1, source_target_pairs={{0,2},{2,0},{4,6},{6,4},{8,10},{10,8},{12,14},{14,12},{16,18},{18,... | collective-permute-start | bytes 786440 | tf_op jit(solution)/shard_map/ppermute | solution.py:31
  24.7 9.0 %collective-permute-start.2 = (s32[264,256]{1,0:T(8,128)S(1)}, s32[264,256]{1,0:T(8,128)S(1)}, u32[]{:S(2)}, u32[]{:S(2)}) collective-permute-start(s32[264,256]{1,0:T(8,128)S(1)} %get-tuple-element.40.refs_0_.refs_1_), channel_id=1, source_target_pairs={{0,1},{1,0},{2,3},{3,2},{4,5},{5,4},{6,7},{7,6},{8,9},{9,8},{10,11... | collective-permute-start | bytes 811016 | tf_op jit(solution)/shard_map/ppermute | solution.py:31
  26.8 5.4 %collective-permute-start.13 = (bf16[256,512]{1,0:T(8,128)(2,1)S(1)}, bf16[256,512]{1,0:T(8,128)(2,1)S(1)}, u32[]{:S(2)}, u32[]{:S(2)}) collective-permute-start(bf16[256,512]{1,0:T(8,128)(2,1)S(1)} %shard_map.93.refs_4_), channel_id=1, source_target_pairs={{0,2},{2,0},{4,6},{6,4},{8,10},{10,8},{12,14},{14,12},{16,18},{18,... | collective-permute-start | bytes 786440 | tf_op jit(solution)/shard_map/ppermute | solution.py:31
  28.3 3.9 %collective-permute-start.8 = (bf16[256,512]{1,0:T(8,128)(2,1)S(1)}, bf16[256,512]{1,0:T(8,128)(2,1)S(1)}, u32[]{:S(2)}, u32[]{:S(2)}) collective-permute-start(bf16[256,512]{1,0:T(8,128)(2,1)S(1)} %collective-permute-done.6.refs_1_), channel_id=1, source_target_pairs={{0,2},{2,0},{4,6},{6,4},{8,10},{10,8},{12,14},{14,12},{16,18},{18,... | collective-permute-start | bytes 786440 | tf_op jit(solution)/shard_map/ppermute | solution.py:31
  31.1 1.5 %collective-permute-start.14 = (bf16[256,512]{1,0:T(8,128)(2,1)S(1)}, bf16[256,512]{1,0:T(8,128)(2,1)S(1)}, u32[]{:S(2)}, u32[]{:S(2)}) collective-permute-start(bf16[256,512]{1,0:T(8,128)(2,1)S(1)} %collective-permute-done.12.refs_5_), channel_id=1, source_target_pairs={{0,2},{2,0},{4,6},{6,4},{8,10},{10,8},{12,14},{14,12},{16,18},{18,... | collective-permute-start | bytes 786440 | tf_op jit(solution)/shard_map/ppermute | solution.py:31
  31.1 8.5 %collective-permute-start.16 = (bf16[112,1024]{1,0:T(8,128)(2,1)S(1)}, bf16[112,1024]{1,0:T(8,128)(2,1)S(1)}, u32[]{:S(2)}, u32[]{:S(2)}) collective-permute-start(bf16[112,1024]{1,0:T(8,128)(2,1)S(1)} %shard_map.96), channel_id=1, source_target_pairs={{0,1},{1,0},{2,3},{3,2},{4,5},{5,4},{6,7},{7,6},{8,9},{9,8},{10,11... | collective-permute-start | bytes 688136 | tf_op jit(solution)/shard_map/ppermute | solution.py:31
  32.2 1.5 %copy-start.3 = (s32[2,256]{1,0:T(2,128)S(1)}, s32[2,256]{1,0:T(2,128)}, u32[]{:S(2)}) copy-start(s32[2,256]{1,0:T(2,128)} %targets_ref.3) | copy-start | bytes 6148
  32.2 1.5 %copy-start.4 = (s32[2,256]{1,0:T(2,128)S(1)}, s32[2,256]{1,0:T(2,128)}, u32[]{:S(2)}) copy-start(s32[2,256]{1,0:T(2,128)} %valid_ref.3) | copy-start | bytes 6148
  34.4 10.4 %collective-permute-start.17 = (bf16[256,512]{1,0:T(8,128)(2,1)S(1)}, bf16[256,512]{1,0:T(8,128)(2,1)S(1)}, u32[]{:S(2)}, u32[]{:S(2)}) collective-permute-start(bf16[256,512]{1,0:T(8,128)(2,1)S(1)} %shard_map.95.grads_ref), channel_id=1, source_target_pairs={{0,1},{1,0},{2,3},{3,2},{4,5},{5,4},{6,7},{7,6},{8,9},{9,8},{10,11... | collective-permute-start | bytes 786440 | tf_op jit(solution)/shard_map/ppermute | solution.py:31
  39.6 5.2 %copy-start.5 = (s32[2]{0:T(128)S(1)}, s32[2]{0:T(128)}, u32[]{:S(2)}) copy-start(s32[2]{0:T(128)} %plan_ref.5) | copy-start | bytes 28
  46.4 2.0 %collective-permute-start.19 = (f32[512,256]{1,0:T(8,128)S(1)}, f32[512,256]{1,0:T(8,128)S(1)}, u32[]{:S(2)}, u32[]{:S(2)}) collective-permute-start(f32[512,256]{1,0:T(8,128)S(1)} %get-tuple-element.51), channel_id=1, source_target_pairs={{0,2},{2,0},{4,6},{6,4},{8,10},{10,8},{12,14},{14,12},{16,18},{18,... | collective-permute-start | bytes 1572872 | tf_op jit(solution)/shard_map/ppermute | solution.py:31
  46.5 8.9 %collective-permute-start.18 = (s32[264,256]{1,0:T(8,128)S(1)}, s32[264,256]{1,0:T(8,128)S(1)}, u32[]{:S(2)}, u32[]{:S(2)}) collective-permute-start(s32[264,256]{1,0:T(8,128)S(1)} %get-tuple-element.48), channel_id=1, source_target_pairs={{0,1},{1,0},{2,3},{3,2},{4,5},{5,4},{6,7},{7,6},{8,9},{9,8},{10,11... | collective-permute-start | bytes 811016 | tf_op jit(solution)/shard_map/ppermute | solution.py:31
  48.6 6.9 %collective-permute-start.20 = (s32[72,256]{1,0:T(8,128)S(1)}, s32[72,256]{1,0:T(8,128)S(1)}, u32[]{:S(2)}, u32[]{:S(2)}) collective-permute-start(s32[72,256]{1,0:T(8,128)S(1)} %get-tuple-element.52), channel_id=1, source_target_pairs={{0,24},{2,26},{4,28},{6,30},{8,16},{10,18},{12,20},{14,22},{16,8},... | collective-permute-start | bytes 221192 | tf_op jit(solution)/shard_map/ppermute | solution.py:31
  52.4 5.9 %collective-permute-start.22 = (s32[72,256]{1,0:T(8,128)S(1)}, s32[72,256]{1,0:T(8,128)S(1)}, u32[]{:S(2)}, u32[]{:S(2)}) collective-permute-start(s32[72,256]{1,0:T(8,128)S(1)} %get-tuple-element.55), channel_id=1, source_target_pairs={{0,16},{2,18},{4,20},{6,22},{8,24},{10,26},{12,28},{14,30},{16,0},... | collective-permute-start | bytes 221192 | tf_op jit(solution)/shard_map/ppermute | solution.py:31
  52.5 5.8 %collective-permute-start.23 = (s32[72,256]{1,0:T(8,128)S(1)}, s32[72,256]{1,0:T(8,128)S(1)}, u32[]{:S(2)}, u32[]{:S(2)}) collective-permute-start(s32[72,256]{1,0:T(8,128)S(1)} %get-tuple-element.56), channel_id=1, source_target_pairs={{0,8},{2,10},{4,12},{6,14},{8,0},{10,2},{12,4},{14,6},{16,24},{18,... | collective-permute-start | bytes 221192 | tf_op jit(solution)/shard_map/ppermute | solution.py:31
  56.1 7.9 %collective-permute-start.21 = (bf16[256,512]{1,0:T(8,128)(2,1)S(1)}, bf16[256,512]{1,0:T(8,128)(2,1)S(1)}, u32[]{:S(2)}, u32[]{:S(2)}) collective-permute-start(bf16[256,512]{1,0:T(8,128)(2,1)S(1)} %shard_map.102.grads_ref), channel_id=1, source_target_pairs={{0,1},{1,0},{2,3},{3,2},{4,5},{5,4},{6,7},{7,6},{8,9},{9,8},{10,11... | collective-permute-start | bytes 786440 | tf_op jit(solution)/shard_map/ppermute | solution.py:31
  65.3 2.0 %collective-permute-start.29 = (f32[512,256]{1,0:T(8,128)S(1)}, f32[512,256]{1,0:T(8,128)S(1)}, u32[]{:S(2)}, u32[]{:S(2)}) collective-permute-start(f32[512,256]{1,0:T(8,128)S(1)} %get-tuple-element.59), channel_id=1, source_target_pairs={{0,2},{2,0},{4,6},{6,4},{8,10},{10,8},{12,14},{14,12},{16,18},{18,... | collective-permute-start | bytes 1572872 | tf_op jit(solution)/shard_map/ppermute | solution.py:31
  65.3 6.5 %collective-permute-start.24 = (s32[72,256]{1,0:T(8,128)S(1)}, s32[72,256]{1,0:T(8,128)S(1)}, u32[]{:S(2)}, u32[]{:S(2)}) collective-permute-start(s32[72,256]{1,0:T(8,128)S(1)} %shard_map.104.refs_0_.one_ref), channel_id=1, source_target_pairs={{0,4},{2,6},{4,0},{6,2},{8,12},{10,14},{12,8},{14,10},{16,20},{18,... | collective-permute-start | bytes 221192 | tf_op jit(solution)/shard_map/ppermute | solution.py:31
  67.4 7.7 %collective-permute-start.30 = (s32[72,256]{1,0:T(8,128)S(1)}, s32[72,256]{1,0:T(8,128)S(1)}, u32[]{:S(2)}, u32[]{:S(2)}) collective-permute-start(s32[72,256]{1,0:T(8,128)S(1)} %get-tuple-element.61), channel_id=1, source_target_pairs={{0,24},{2,26},{4,28},{6,30},{8,16},{10,18},{12,20},{14,22},{16,8},... | collective-permute-start | bytes 221192 | tf_op jit(solution)/shard_map/ppermute | solution.py:31
  69.9 7.8 %collective-permute-start.31 = (s32[72,256]{1,0:T(8,128)S(1)}, s32[72,256]{1,0:T(8,128)S(1)}, u32[]{:S(2)}, u32[]{:S(2)}) collective-permute-start(s32[72,256]{1,0:T(8,128)S(1)} %get-tuple-element.62), channel_id=1, source_target_pairs={{0,16},{2,18},{4,20},{6,22},{8,24},{10,26},{12,28},{14,30},{16,0},... | collective-permute-start | bytes 221192 | tf_op jit(solution)/shard_map/ppermute | solution.py:31
  69.9 7.8 %collective-permute-start.32 = (s32[72,256]{1,0:T(8,128)S(1)}, s32[72,256]{1,0:T(8,128)S(1)}, u32[]{:S(2)}, u32[]{:S(2)}) collective-permute-start(s32[72,256]{1,0:T(8,128)S(1)} %get-tuple-element.63), channel_id=1, source_target_pairs={{0,8},{2,10},{4,12},{6,14},{8,0},{10,2},{12,4},{14,6},{16,24},{18,... | collective-permute-start | bytes 221192 | tf_op jit(solution)/shard_map/ppermute | solution.py:31
  71.9 9.9 %collective-permute-start.26 = (s32[72,256]{1,0:T(8,128)S(1)}, s32[72,256]{1,0:T(8,128)S(1)}, u32[]{:S(2)}, u32[]{:S(2)}) collective-permute-start(s32[72,256]{1,0:T(8,128)S(1)} %shard_map.106.refs_0_), channel_id=1, source_target_pairs={{0,16},{2,18},{4,20},{6,22},{8,24},{10,26},{12,28},{14,30},{16,0},... | collective-permute-start | bytes 221192 | tf_op jit(solution)/shard_map/ppermute | solution.py:31
  73.0 8.8 %collective-permute-start.25 = (s32[72,256]{1,0:T(8,128)S(1)}, s32[72,256]{1,0:T(8,128)S(1)}, u32[]{:S(2)}, u32[]{:S(2)}) collective-permute-start(s32[72,256]{1,0:T(8,128)S(1)} %shard_map.106.refs_0_), channel_id=1, source_target_pairs={{0,8},{2,10},{4,12},{6,14},{8,0},{10,2},{12,4},{14,6},{16,24},{18,... | collective-permute-start | bytes 221192 | tf_op jit(solution)/shard_map/ppermute | solution.py:31
  77.8 4.4 %collective-permute-start.33 = (s32[72,256]{1,0:T(8,128)S(1)}, s32[72,256]{1,0:T(8,128)S(1)}, u32[]{:S(2)}, u32[]{:S(2)}) collective-permute-start(s32[72,256]{1,0:T(8,128)S(1)} %shard_map.109.one_ref), channel_id=1, source_target_pairs={{0,4},{2,6},{4,0},{6,2},{8,12},{10,14},{12,8},{14,10},{16,20},{18,... | collective-permute-start | bytes 221192 | tf_op jit(solution)/shard_map/ppermute | solution.py:31
  79.4 7.4 %collective-permute-start.27 = (s32[72,256]{1,0:T(8,128)S(1)}, s32[72,256]{1,0:T(8,128)S(1)}, u32[]{:S(2)}, u32[]{:S(2)}) collective-permute-start(s32[72,256]{1,0:T(8,128)S(1)} %shard_map.106.refs_0_), channel_id=1, source_target_pairs={{0,24},{2,26},{4,28},{6,30},{8,16},{10,18},{12,20},{14,22},{16,8},... | collective-permute-start | bytes 221192 | tf_op jit(solution)/shard_map/ppermute | solution.py:31
  82.4 6.9 %collective-permute-start.36 = (s32[72,256]{1,0:T(8,128)S(1)}, s32[72,256]{1,0:T(8,128)S(1)}, u32[]{:S(2)}, u32[]{:S(2)}) collective-permute-start(s32[72,256]{1,0:T(8,128)S(1)} %shard_map.110.refs_0_), channel_id=1, source_target_pairs={{0,24},{2,26},{4,28},{6,30},{8,16},{10,18},{12,20},{14,22},{16,8},... | collective-permute-start | bytes 221192 | tf_op jit(solution)/shard_map/ppermute | solution.py:31
  84.8 6.3 %collective-permute-start.35 = (s32[72,256]{1,0:T(8,128)S(1)}, s32[72,256]{1,0:T(8,128)S(1)}, u32[]{:S(2)}, u32[]{:S(2)}) collective-permute-start(s32[72,256]{1,0:T(8,128)S(1)} %shard_map.110.refs_0_), channel_id=1, source_target_pairs={{0,16},{2,18},{4,20},{6,22},{8,24},{10,26},{12,28},{14,30},{16,0},... | collective-permute-start | bytes 221192 | tf_op jit(solution)/shard_map/ppermute | solution.py:31
  84.8 6.3 %collective-permute-start.34 = (s32[72,256]{1,0:T(8,128)S(1)}, s32[72,256]{1,0:T(8,128)S(1)}, u32[]{:S(2)}, u32[]{:S(2)}) collective-permute-start(s32[72,256]{1,0:T(8,128)S(1)} %shard_map.110.refs_0_), channel_id=1, source_target_pairs={{0,8},{2,10},{4,12},{6,14},{8,0},{10,2},{12,4},{14,6},{16,24},{18,... | collective-permute-start | bytes 221192 | tf_op jit(solution)/shard_map/ppermute | solution.py:31
  87.2 4.4 %collective-permute-start.28 = (s32[288,256]{1,0:T(8,128)S(1)}, s32[288,256]{1,0:T(8,128)S(1)}, u32[]{:S(2)}, u32[]{:S(2)}) collective-permute-start(s32[288,256]{1,0:T(8,128)S(1)} %shard_map.107.own0), channel_id=1, source_target_pairs={{0,2},{2,0},{4,6},{6,4},{8,10},{10,8},{12,14},{14,12},{16,18},{18,... | collective-permute-start | bytes 884744 | tf_op jit(solution)/shard_map/ppermute | solution.py:31
  91.6 1.6 %collective-permute-start.37 = (s32[288,256]{1,0:T(8,128)S(1)}, s32[288,256]{1,0:T(8,128)S(1)}, u32[]{:S(2)}, u32[]{:S(2)}) collective-permute-start(s32[288,256]{1,0:T(8,128)S(1)} %shard_map.111.own1), channel_id=1, source_target_pairs={{0,2},{2,0},{4,6},{6,4},{8,10},{10,8},{12,14},{14,12},{16,18},{18,... | collective-permute-start | bytes 884744 | tf_op jit(solution)/shard_map/ppermute | solution.py:31

commit v9 on v8

--- a/solution.py
+++ b/solution.py
@@ -645,9 +645,11 @@
                 fresh = outer_ref[at, columns] - outer_rate * mean
                 outer_held[at, columns] = fresh
                 inner_held[at, columns] = mix_weight * inner_ref[at, columns] + (1.0 - mix_weight) * fresh
-            for k, (held, out) in enumerate(((outer_held, new_outer_ref), (inner_held, new_inner_ref))):
-                copies.append(pltpu.make_async_copy(held.at[at], out.at[at], sems.at[2 * i + k]))
-                copies[-1].start()
+            if i % 2 == 1:
+                at = pl.ds((i - 1) * tile, 2 * tile)
+                for k, (held, out) in enumerate(((outer_held, new_outer_ref), (inner_held, new_inner_ref))):
+                    copies.append(pltpu.make_async_copy(held.at[at], out.at[at], sems.at[2 * i + k]))
+                    copies[-1].start()
         for copy in copies:
             copy.wait()
 

time: 96.1 us -> 96.3 us (level)
  no operation moved by 1% of the time
where the time goes in v9:
time: 96.3 us; the launch traced here: 96.1 us
  starting transfers between devices  44.4 us (46%)
  waiting for transfers between devices  34.3 us (36%)
  Pallas kernels  14.7 us (15%)
  local copies, waits for them, and re-layouts  1.74 us (2%)
  between operations  0.99 us (1%)
    ppermute x38, starting transfers between devices, swap(): return lax.ppermute(value, axis, [(i, i ^ mask) for i in range(size)])  44.4 us
    ppermute x38, waiting for transfers between devices, swap(): return lax.ppermute(value, axis, [(i, i ^ mask) for i in range(size)])  34.3 us
    pallas_call x27, Pallas kernels, call(): pl.pallas_call(kernel, out_shape=out_shape, in_specs=in_specs, out_specs=...  14.7 us
  transfers between devices with their start and end apart: 38, of which 18 were waited for; matrix products, arithmetic and copies ran while one was open for 0% of the time, Pallas kernels for 9%

profile of v9, /device:TPU:0, one launch (start us, length us, event | category | flops | bytes accessed | tf_op | source)
XLA Modules:
  0.0 96.1 jit_solution(4371215679171340818)
XLA Ops:
  0.6 1.7 %slice_bitcast_fusion = (bf16[256,2048]{1,0:T(8,128)(2,1)S(1)}, bf16[256,2048]{1,0:T(8,128)(2,1)S(1)}) fusion(bf16[2,256,2048]{2,1,0:T(8,128)(2,1)} %param.7), kind=kLoop, calls=%fused_computation | loop fusion | bytes 4194304 | tf_op jit(solution)/shard_map/squeeze | solution.py:717
  2.8 3.0 %collective-permute-start = (bf16[96,1024]{1,0:T(8,128)(2,1)S(1)}, bf16[96,1024]{1,0:T(8,128)(2,1)S(1)}, u32[]{:S(2)}, u32[]{:S(2)}) collective-permute-start(bf16[96,1024]{1,0:T(8,128)(2,1)S(1)} %get-tuple-element.34.refs_1_), channel_id=1, source_target_pairs={{0,1},{1,0},{2,3},{3,2},{4,5},{5,4},{6,7},{7,6},{8,9},{9,8},{10,11... | collective-permute-start | bytes 589832 | tf_op jit(solution)/shard_map/ppermute | solution.py:31
  6.2 3.7 %collective-permute-start.5 = (bf16[64,512]{1,0:T(8,128)(2,1)S(1)}, bf16[64,512]{1,0:T(8,128)(2,1)S(1)}, u32[]{:S(2)}, u32[]{:S(2)}) collective-permute-start(bf16[64,512]{1,0:T(8,128)(2,1)S(1)} %get-tuple-element.41.refs_0_), channel_id=1, source_target_pairs={{0,24},{2,26},{4,28},{6,30},{8,16},{10,18},{12,20},{14,22},{16,8},... | collective-permute-start | bytes 196616 | tf_op jit(solution)/shard_map/ppermute | solution.py:31
  9.9 0.8 collective-permute-start.3
  11.1 1.6 %collective-permute-start.15 = (bf16[144,1024]{1,0:T(8,128)(2,1)S(1)}, bf16[144,1024]{1,0:T(8,128)(2,1)S(1)}, u32[]{:S(2)}, u32[]{:S(2)}) collective-permute-start(bf16[144,1024]{1,0:T(8,128)(2,1)S(1)} %get-tuple-element.42), channel_id=1, source_target_pairs={{0,1},{1,0},{2,3},{3,2},{4,5},{5,4},{6,7},{7,6},{8,9},{9,8},{10,11... | collective-permute-start | bytes 884744 | tf_op jit(solution)/shard_map/ppermute | solution.py:31
  13.1 3.6 %collective-permute-start.11 = (bf16[64,512]{1,0:T(8,128)(2,1)S(1)}, bf16[64,512]{1,0:T(8,128)(2,1)S(1)}, u32[]{:S(2)}, u32[]{:S(2)}) collective-permute-start(bf16[64,512]{1,0:T(8,128)(2,1)S(1)} %shard_map.92.refs_0_), channel_id=1, source_target_pairs={{0,24},{2,26},{4,28},{6,30},{8,16},{10,18},{12,20},{14,22},{16,8},... | collective-permute-start | bytes 196616 | tf_op jit(solution)/shard_map/ppermute | solution.py:31
  16.8 2.2 %collective-permute-start.9 = (bf16[64,512]{1,0:T(8,128)(2,1)S(1)}, bf16[64,512]{1,0:T(8,128)(2,1)S(1)}, u32[]{:S(2)}, u32[]{:S(2)}) collective-permute-start(bf16[64,512]{1,0:T(8,128)(2,1)S(1)} %shard_map.92.refs_0_), channel_id=1, source_target_pairs={{0,8},{2,10},{4,12},{6,14},{8,0},{10,2},{12,4},{14,6},{16,24},{18,... | collective-permute-start | bytes 196616 | tf_op jit(solution)/shard_map/ppermute | solution.py:31
  19.3 1.6 %collective-permute-start.6 = (bf16[256,512]{1,0:T(8,128)(2,1)S(1)}, bf16[256,512]{1,0:T(8,128)(2,1)S(1)}, u32[]{:S(2)}, u32[]{:S(2)}) collective-permute-start(bf16[256,512]{1,0:T(8,128)(2,1)S(1)} %shard_map.91.refs_0_), channel_id=1, source_target_pairs={{0,4},{2,6},{4,0},{6,2},{8,12},{10,14},{12,8},{14,10},{16,20},{18,... | collective-permute-start | bytes 786440 | tf_op jit(solution)/shard_map/ppermute | solution.py:31
  20.9 1.0 %collective-permute-done.10.refs_2_ = bf16[64,512]{1,0:T(8,128)(2,1)S(1)} collective-permute-done((bf16[64,512]{1,0:T(8,128)(2,1)S(1)}, bf16[64,512]{1,0:T(8,128)(2,1)S(1)}, u32[]{:S(2)}, u32[]{:S(2)}) %collective-permute-start.10) | collective-permute-done | bytes 65568 | tf_op jit(solution)/shard_map/ppermute | solution.py:31
  22.3 1.6 %collective-permute-start.12 = (bf16[256,512]{1,0:T(8,128)(2,1)S(1)}, bf16[256,512]{1,0:T(8,128)(2,1)S(1)}, u32[]{:S(2)}, u32[]{:S(2)}) collective-permute-start(bf16[256,512]{1,0:T(8,128)(2,1)S(1)} %shard_map.93.refs_4_), channel_id=1, source_target_pairs={{0,4},{2,6},{4,0},{6,2},{8,12},{10,14},{12,8},{14,10},{16,20},{18,... | collective-permute-start | bytes 786440 | tf_op jit(solution)/shard_map/ppermute | solution.py:31
  24.2 0.5 shard_map.89
  24.7 0.6 collective-permute-start.2
  25.3 1.5 %collective-permute-done.15.refs_8_.refs_0_ = bf16[144,1024]{1,0:T(8,128)(2,1)S(1)} collective-permute-done((bf16[144,1024]{1,0:T(8,128)(2,1)S(1)}, bf16[144,1024]{1,0:T(8,128)(2,1)S(1)}, u32[]{:S(2)}, u32[]{:S(2)}) %collective-permute-start.15) | collective-permute-done | bytes 294944 | tf_op jit(solution)/shard_map/ppermute | solution.py:31
  26.9 1.5 %collective-permute-done.6.refs_1_ = bf16[256,512]{1,0:T(8,128)(2,1)S(1)} collective-permute-done((bf16[256,512]{1,0:T(8,128)(2,1)S(1)}, bf16[256,512]{1,0:T(8,128)(2,1)S(1)}, u32[]{:S(2)}, u32[]{:S(2)}) %collective-permute-start.6) | collective-permute-done | bytes 262176 | tf_op jit(solution)/shard_map/ppermute | solution.py:31
  28.3 2.8 %collective-permute-done.12.refs_5_ = bf16[256,512]{1,0:T(8,128)(2,1)S(1)} collective-permute-done((bf16[256,512]{1,0:T(8,128)(2,1)S(1)}, bf16[256,512]{1,0:T(8,128)(2,1)S(1)}, u32[]{:S(2)}, u32[]{:S(2)}) %collective-permute-start.12) | collective-permute-done | bytes 262176 | tf_op jit(solution)/shard_map/ppermute | solution.py:31
  31.1 0.6 collective-permute-start.16
  32.7 1.0 %shard_map.94 = (f32[256,512]{1,0:T(8,128)S(1)}, bf16[2048,512]{1,0:T(8,128)(2,1)S(1)}) custom-call(bf16[256,2048]{1,0:T(8,128)(2,1)S(1)} %get-tuple-element.38.normed_ref, bf16[256,512]{1,0:T(8,128)(2,1)S(1)} %shard_map.91.refs_0_, bf16[256,512]{1,0:T(8,128)(2,1)S(1)} %collective-permute-done.6.refs_1_, ...), custom_call_target="tpu_custom_call" | custom-call | flops 1000 | bytes 1000 | tf_op jit(solution)/shard_map/pallas_call | solution.py:203
  33.7 0.6 shard_map.95.grads_ref
  34.4 1.1 %collective-permute-start.17 = (bf16[256,512]{1,0:T(8,128)(2,1)S(1)}, bf16[256,512]{1,0:T(8,128)(2,1)S(1)}, u32[]{:S(2)}, u32[]{:S(2)}) collective-permute-start(bf16[256,512]{1,0:T(8,128)(2,1)S(1)} %shard_map.95.grads_ref), channel_id=1, source_target_pairs={{0,1},{1,0},{2,3},{3,2},{4,5},{5,4},{6,7},{7,6},{8,9},{9,8},{10,11... | collective-permute-start | bytes 786440 | tf_op jit(solution)/shard_map/ppermute | solution.py:31
  35.5 4.1 %collective-permute-done.16.refs_0_.refs_1_ = bf16[112,1024]{1,0:T(8,128)(2,1)S(1)} collective-permute-done((bf16[112,1024]{1,0:T(8,128)(2,1)S(1)}, bf16[112,1024]{1,0:T(8,128)(2,1)S(1)}, u32[]{:S(2)}, u32[]{:S(2)}) %collective-permute-start.16) | collective-permute-done | bytes 229408 | tf_op jit(solution)/shard_map/ppermute | solution.py:31
  40.1 4.7 %collective-permute-done.17.grads_ref = bf16[256,512]{1,0:T(8,128)(2,1)S(1)} collective-permute-done((bf16[256,512]{1,0:T(8,128)(2,1)S(1)}, bf16[256,512]{1,0:T(8,128)(2,1)S(1)}, u32[]{:S(2)}, u32[]{:S(2)}) %collective-permute-start.17) | collective-permute-done | bytes 262176 | tf_op jit(solution)/shard_map/ppermute | solution.py:31
  44.8 1.6 %shard_map.98 = (f32[1024,512]{1,0:T(8,128)S(1)}, f32[512,256]{1,0:T(8,128)S(1)}, f32[512,256]{1,0:T(8,128)S(1)}, bf16[256,1024]{1,0:T(8,128)(2,1)S(1)}, bf16[10...) custom-call(s32[2]{0:T(128)S(1)} %copy-done.5, f32[1024,512]{1,0:T(8,128)S(1)} %shard_map.97.inner_ref.refs_0_, ...), custom_call_target="tpu_custom_call" | custom-call | flops 1000000000 | bytes 1000 | tf_op jit(solution)/shard_map/pallas_call | solution.py:203
  46.5 0.6 collective-permute-start.18
  47.1 1.3 %collective-permute-done.19.received_ref = f32[512,256]{1,0:T(8,128)S(1)} collective-permute-done((f32[512,256]{1,0:T(8,128)S(1)}, f32[512,256]{1,0:T(8,128)S(1)}, u32[]{:S(2)}, u32[]{:S(2)}) %collective-permute-start.19) | collective-permute-done | bytes 524320 | tf_op jit(solution)/shard_map/ppermute | solution.py:31
  48.6 2.5 %collective-permute-start.20 = (s32[72,256]{1,0:T(8,128)S(1)}, s32[72,256]{1,0:T(8,128)S(1)}, u32[]{:S(2)}, u32[]{:S(2)}) collective-permute-start(s32[72,256]{1,0:T(8,128)S(1)} %get-tuple-element.52), channel_id=1, source_target_pairs={{0,24},{2,26},{4,28},{6,30},{8,16},{10,18},{12,20},{14,22},{16,8},... | collective-permute-start | bytes 221192 | tf_op jit(solution)/shard_map/ppermute | solution.py:31
  51.1 0.9 shard_map.100.refer_ref
  52.5 1.9 %collective-permute-start.23 = (s32[72,256]{1,0:T(8,128)S(1)}, s32[72,256]{1,0:T(8,128)S(1)}, u32[]{:S(2)}, u32[]{:S(2)}) collective-permute-start(s32[72,256]{1,0:T(8,128)S(1)} %get-tuple-element.56), channel_id=1, source_target_pairs={{0,8},{2,10},{4,12},{6,14},{8,0},{10,2},{12,4},{14,6},{16,24},{18,... | collective-permute-start | bytes 221192 | tf_op jit(solution)/shard_map/ppermute | solution.py:31
  54.4 1.0 %collective-permute-done.18.received_ref = s32[264,256]{1,0:T(8,128)S(1)} collective-permute-done((s32[264,256]{1,0:T(8,128)S(1)}, s32[264,256]{1,0:T(8,128)S(1)}, u32[]{:S(2)}, u32[]{:S(2)}) %collective-permute-start.18) | collective-permute-done | bytes 270368 | tf_op jit(solution)/shard_map/ppermute | solution.py:31
  55.4 0.6 shard_map.102.grads_ref
  56.1 0.6 collective-permute-start.21
  56.7 0.5 shard_map.103.refs_3_.inner_ref
  57.2 1.1 %collective-permute-done.22.refs_1_ = s32[72,256]{1,0:T(8,128)S(1)} collective-permute-done((s32[72,256]{1,0:T(8,128)S(1)}, s32[72,256]{1,0:T(8,128)S(1)}, u32[]{:S(2)}, u32[]{:S(2)}) %collective-permute-start.22) | collective-permute-done | bytes 73760 | tf_op jit(solution)/shard_map/ppermute | solution.py:31
  58.4 5.6 %collective-permute-done.21.grads_ref = bf16[256,512]{1,0:T(8,128)(2,1)S(1)} collective-permute-done((bf16[256,512]{1,0:T(8,128)(2,1)S(1)}, bf16[256,512]{1,0:T(8,128)(2,1)S(1)}, u32[]{:S(2)}, u32[]{:S(2)}) %collective-permute-start.21) | collective-permute-done | bytes 262176 | tf_op jit(solution)/shard_map/ppermute | solution.py:31
  64.0 1.3 %shard_map.105 = (f32[1024,512]{1,0:T(8,128)S(1)}, f32[512,256]{1,0:T(8,128)S(1)}, f32[512,256]{1,0:T(8,128)S(1)}) custom-call(s32[2]{0:T(128)S(1)} %copy-done.5, f32[1024,512]{1,0:T(8,128)S(1)} %shard_map.103.refs_3_.inner_ref, bf16[256,1024]{1,0:T(8,128)(2,1)S(1)} %get-tuple-element.53.features_ref, ...), custom_call_target="tpu_custom_call" | custom-call | flops 1000000000 | bytes 1000 | tf_op jit(solution)/shard_map/pallas_call | solution.py:203
  65.3 1.6 %collective-permute-start.24 = (s32[72,256]{1,0:T(8,128)S(1)}, s32[72,256]{1,0:T(8,128)S(1)}, u32[]{:S(2)}, u32[]{:S(2)}) collective-permute-start(s32[72,256]{1,0:T(8,128)S(1)} %shard_map.104.refs_0_.one_ref), channel_id=1, source_target_pairs={{0,4},{2,6},{4,0},{6,2},{8,12},{10,14},{12,8},{14,10},{16,20},{18,... | collective-permute-start | bytes 221192 | tf_op jit(solution)/shard_map/ppermute | solution.py:31
  67.4 2.5 %collective-permute-start.30 = (s32[72,256]{1,0:T(8,128)S(1)}, s32[72,256]{1,0:T(8,128)S(1)}, u32[]{:S(2)}, u32[]{:S(2)}) collective-permute-start(s32[72,256]{1,0:T(8,128)S(1)} %get-tuple-element.61), channel_id=1, source_target_pairs={{0,24},{2,26},{4,28},{6,30},{8,16},{10,18},{12,20},{14,22},{16,8},... | collective-permute-start | bytes 221192 | tf_op jit(solution)/shard_map/ppermute | solution.py:31
  69.9 1.9 %collective-permute-start.32 = (s32[72,256]{1,0:T(8,128)S(1)}, s32[72,256]{1,0:T(8,128)S(1)}, u32[]{:S(2)}, u32[]{:S(2)}) collective-permute-start(s32[72,256]{1,0:T(8,128)S(1)} %get-tuple-element.63), channel_id=1, source_target_pairs={{0,8},{2,10},{4,12},{6,14},{8,0},{10,2},{12,4},{14,6},{16,24},{18,... | collective-permute-start | bytes 221192 | tf_op jit(solution)/shard_map/ppermute | solution.py:31
  71.9 1.1 %collective-permute-start.26 = (s32[72,256]{1,0:T(8,128)S(1)}, s32[72,256]{1,0:T(8,128)S(1)}, u32[]{:S(2)}, u32[]{:S(2)}) collective-permute-start(s32[72,256]{1,0:T(8,128)S(1)} %shard_map.106.refs_0_), channel_id=1, source_target_pairs={{0,16},{2,18},{4,20},{6,22},{8,24},{10,26},{12,28},{14,30},{16,0},... | collective-permute-start | bytes 221192 | tf_op jit(solution)/shard_map/ppermute | solution.py:31
  73.0 2.0 %collective-permute-start.25 = (s32[72,256]{1,0:T(8,128)S(1)}, s32[72,256]{1,0:T(8,128)S(1)}, u32[]{:S(2)}, u32[]{:S(2)}) collective-permute-start(s32[72,256]{1,0:T(8,128)S(1)} %shard_map.106.refs_0_), channel_id=1, source_target_pairs={{0,8},{2,10},{4,12},{6,14},{8,0},{10,2},{12,4},{14,6},{16,24},{18,... | collective-permute-start | bytes 221192 | tf_op jit(solution)/shard_map/ppermute | solution.py:31
  75.1 2.7 %collective-permute-done.31.refs_1_ = s32[72,256]{1,0:T(8,128)S(1)} collective-permute-done((s32[72,256]{1,0:T(8,128)S(1)}, s32[72,256]{1,0:T(8,128)S(1)}, u32[]{:S(2)}, u32[]{:S(2)}) %collective-permute-start.31) | collective-permute-done | bytes 73760 | tf_op jit(solution)/shard_map/ppermute | solution.py:31
  77.8 1.6 %collective-permute-start.33 = (s32[72,256]{1,0:T(8,128)S(1)}, s32[72,256]{1,0:T(8,128)S(1)}, u32[]{:S(2)}, u32[]{:S(2)}) collective-permute-start(s32[72,256]{1,0:T(8,128)S(1)} %shard_map.109.one_ref), channel_id=1, source_target_pairs={{0,4},{2,6},{4,0},{6,2},{8,12},{10,14},{12,8},{14,10},{16,20},{18,... | collective-permute-start | bytes 221192 | tf_op jit(solution)/shard_map/ppermute | solution.py:31
  79.4 2.4 %collective-permute-start.27 = (s32[72,256]{1,0:T(8,128)S(1)}, s32[72,256]{1,0:T(8,128)S(1)}, u32[]{:S(2)}, u32[]{:S(2)}) collective-permute-start(s32[72,256]{1,0:T(8,128)S(1)} %shard_map.106.refs_0_), channel_id=1, source_target_pairs={{0,24},{2,26},{4,28},{6,30},{8,16},{10,18},{12,20},{14,22},{16,8},... | collective-permute-start | bytes 221192 | tf_op jit(solution)/shard_map/ppermute | solution.py:31
  82.4 2.5 %collective-permute-start.36 = (s32[72,256]{1,0:T(8,128)S(1)}, s32[72,256]{1,0:T(8,128)S(1)}, u32[]{:S(2)}, u32[]{:S(2)}) collective-permute-start(s32[72,256]{1,0:T(8,128)S(1)} %shard_map.110.refs_0_), channel_id=1, source_target_pairs={{0,24},{2,26},{4,28},{6,30},{8,16},{10,18},{12,20},{14,22},{16,8},... | collective-permute-start | bytes 221192 | tf_op jit(solution)/shard_map/ppermute | solution.py:31
  84.8 2.0 %collective-permute-start.34 = (s32[72,256]{1,0:T(8,128)S(1)}, s32[72,256]{1,0:T(8,128)S(1)}, u32[]{:S(2)}, u32[]{:S(2)}) collective-permute-start(s32[72,256]{1,0:T(8,128)S(1)} %shard_map.110.refs_0_), channel_id=1, source_target_pairs={{0,8},{2,10},{4,12},{6,14},{8,0},{10,2},{12,4},{14,6},{16,24},{18,... | collective-permute-start | bytes 221192 | tf_op jit(solution)/shard_map/ppermute | solution.py:31
  87.3 2.0 %collective-permute-done.36.refs_3_ = s32[72,256]{1,0:T(8,128)S(1)} collective-permute-done((s32[72,256]{1,0:T(8,128)S(1)}, s32[72,256]{1,0:T(8,128)S(1)}, u32[]{:S(2)}, u32[]{:S(2)}) %collective-permute-start.36) | collective-permute-done | bytes 73760 | tf_op jit(solution)/shard_map/ppermute | solution.py:31
  89.3 1.8 %collective-permute-done.35.refs_2_ = s32[72,256]{1,0:T(8,128)S(1)} collective-permute-done((s32[72,256]{1,0:T(8,128)S(1)}, s32[72,256]{1,0:T(8,128)S(1)}, u32[]{:S(2)}, u32[]{:S(2)}) %collective-permute-start.35) | collective-permute-done | bytes 73760 | tf_op jit(solution)/shard_map/ppermute | solution.py:31
  91.7 1.6 %collective-permute-done.37.other1 = s32[288,256]{1,0:T(8,128)S(1)} collective-permute-done((s32[288,256]{1,0:T(8,128)S(1)}, s32[288,256]{1,0:T(8,128)S(1)}, u32[]{:S(2)}, u32[]{:S(2)}) %collective-permute-start.37) | collective-permute-done | bytes 294944 | tf_op jit(solution)/shard_map/ppermute | solution.py:31
  93.2 2.9 %shard_map.112 = (f32[1024,512]{1,0:T(8,128)}, f32[1024,512]{1,0:T(8,128)}) custom-call(s32[2]{0:T(128)S(1)} %copy-done.5, f32[1024,512]{1,0:T(8,128)S(1)} %copy-done, f32[1024,512]{1,0:T(8,128)S(1)} %get-tuple-element.57.inner_ref, s32[288,256]{1,0:T(8,128)S(1)} %shard_map.107.own0, s32[288,256]{1,0:T(8,128)S(1)} %collective-permute-done.28.other0, ...), custom_call_target="tpu_custom_call" | custom-call | flops 1000 | bytes 1000 | tf_op jit(solution)/shard_map/pallas_call | solution.py:203
  (68 shorter events, 7.1 us)
Async XLA Ops:
  0.6 1.7 %copy-start.2 = (bf16[64,512]{1,0:T(8,128)(2,1)S(1)}, bf16[64,512]{1,0:T(8,128)(2,1)}, u32[]{:S(2)}) copy-start(bf16[64,512]{1,0:T(8,128)(2,1)} %refs_0_.3) | copy-start | bytes 196612
  2.8 8.3 %collective-permute-start = (bf16[96,1024]{1,0:T(8,128)(2,1)S(1)}, bf16[96,1024]{1,0:T(8,128)(2,1)S(1)}, u32[]{:S(2)}, u32[]{:S(2)}) collective-permute-start(bf16[96,1024]{1,0:T(8,128)(2,1)S(1)} %get-tuple-element.34.refs_1_), channel_id=1, source_target_pairs={{0,1},{1,0},{2,3},{3,2},{4,5},{5,4},{6,7},{7,6},{8,9},{9,8},{10,11... | collective-permute-start | bytes 589832 | tf_op jit(solution)/shard_map/ppermute | solution.py:31
  6.2 6.9 %collective-permute-start.5 = (bf16[64,512]{1,0:T(8,128)(2,1)S(1)}, bf16[64,512]{1,0:T(8,128)(2,1)S(1)}, u32[]{:S(2)}, u32[]{:S(2)}) collective-permute-start(bf16[64,512]{1,0:T(8,128)(2,1)S(1)} %get-tuple-element.41.refs_0_), channel_id=1, source_target_pairs={{0,24},{2,26},{4,28},{6,30},{8,16},{10,18},{12,20},{14,22},{16,8},... | collective-permute-start | bytes 196616 | tf_op jit(solution)/shard_map/ppermute | solution.py:31
  9.9 6.9 %collective-permute-start.4 = (bf16[64,512]{1,0:T(8,128)(2,1)S(1)}, bf16[64,512]{1,0:T(8,128)(2,1)S(1)}, u32[]{:S(2)}, u32[]{:S(2)}) collective-permute-start(bf16[64,512]{1,0:T(8,128)(2,1)S(1)} %get-tuple-element.41.refs_0_), channel_id=1, source_target_pairs={{0,16},{2,18},{4,20},{6,22},{8,24},{10,26},{12,28},{14,30},{16,0},... | collective-permute-start | bytes 196616 | tf_op jit(solution)/shard_map/ppermute | solution.py:31
  9.9 6.9 %collective-permute-start.3 = (bf16[64,512]{1,0:T(8,128)(2,1)S(1)}, bf16[64,512]{1,0:T(8,128)(2,1)S(1)}, u32[]{:S(2)}, u32[]{:S(2)}) collective-permute-start(bf16[64,512]{1,0:T(8,128)(2,1)S(1)} %get-tuple-element.41.refs_0_), channel_id=1, source_target_pairs={{0,8},{2,10},{4,12},{6,14},{8,0},{10,2},{12,4},{14,6},{16,24},{18,... | collective-permute-start | bytes 196616 | tf_op jit(solution)/shard_map/ppermute | solution.py:31
  10.7 13.5 %collective-permute-start.1 = (bf16[192,1024]{1,0:T(8,128)(2,1)S(1)}, bf16[192,1024]{1,0:T(8,128)(2,1)S(1)}, u32[]{:S(2)}, u32[]{:S(2)}) collective-permute-start(bf16[192,1024]{1,0:T(8,128)(2,1)S(1)} %get-tuple-element.35.refs_2_), channel_id=1, source_target_pairs={{0,1},{1,0},{2,3},{3,2},{4,5},{5,4},{6,7},{7,6},{8,9},{9,8},{10,11... | collective-permute-start | bytes 1179656 | tf_op jit(solution)/shard_map/ppermute | solution.py:31
  11.1 15.8 %collective-permute-start.15 = (bf16[144,1024]{1,0:T(8,128)(2,1)S(1)}, bf16[144,1024]{1,0:T(8,128)(2,1)S(1)}, u32[]{:S(2)}, u32[]{:S(2)}) collective-permute-start(bf16[144,1024]{1,0:T(8,128)(2,1)S(1)} %get-tuple-element.42), channel_id=1, source_target_pairs={{0,1},{1,0},{2,3},{3,2},{4,5},{5,4},{6,7},{7,6},{8,9},{9,8},{10,11... | collective-permute-start | bytes 884744 | tf_op jit(solution)/shard_map/ppermute | solution.py:31
  13.1 6.2 %collective-permute-start.11 = (bf16[64,512]{1,0:T(8,128)(2,1)S(1)}, bf16[64,512]{1,0:T(8,128)(2,1)S(1)}, u32[]{:S(2)}, u32[]{:S(2)}) collective-permute-start(bf16[64,512]{1,0:T(8,128)(2,1)S(1)} %shard_map.92.refs_0_), channel_id=1, source_target_pairs={{0,24},{2,26},{4,28},{6,30},{8,16},{10,18},{12,20},{14,22},{16,8},... | collective-permute-start | bytes 196616 | tf_op jit(solution)/shard_map/ppermute | solution.py:31
  16.8 5.2 %collective-permute-start.10 = (bf16[64,512]{1,0:T(8,128)(2,1)S(1)}, bf16[64,512]{1,0:T(8,128)(2,1)S(1)}, u32[]{:S(2)}, u32[]{:S(2)}) collective-permute-start(bf16[64,512]{1,0:T(8,128)(2,1)S(1)} %shard_map.92.refs_0_), channel_id=1, source_target_pairs={{0,16},{2,18},{4,20},{6,22},{8,24},{10,26},{12,28},{14,30},{16,0},... | collective-permute-start | bytes 196616 | tf_op jit(solution)/shard_map/ppermute | solution.py:31
  16.8 5.2 %collective-permute-start.9 = (bf16[64,512]{1,0:T(8,128)(2,1)S(1)}, bf16[64,512]{1,0:T(8,128)(2,1)S(1)}, u32[]{:S(2)}, u32[]{:S(2)}) collective-permute-start(bf16[64,512]{1,0:T(8,128)(2,1)S(1)} %shard_map.92.refs_0_), channel_id=1, source_target_pairs={{0,8},{2,10},{4,12},{6,14},{8,0},{10,2},{12,4},{14,6},{16,24},{18,... | collective-permute-start | bytes 196616 | tf_op jit(solution)/shard_map/ppermute | solution.py:31
  19.3 4.6 %copy-start = (f32[1024,512]{1,0:T(8,128)S(1)}, f32[1024,512]{1,0:T(8,128)}, u32[]{:S(2)}) copy-start(f32[1024,512]{1,0:T(8,128)} %outer_ref.7) | copy-start | bytes 6291460
  19.3 4.6 %copy-start.1 = (bf16[1,1024,512]{2,1,0:T(8,128)(2,1)S(1)}, bf16[1,1024,512]{2,1,0:T(8,128)(2,1)}, u32[]{:S(2)}) copy-start(bf16[1,1024,512]{2,1,0:T(8,128)(2,1)} %drift_ref.1) | copy-start | bytes 3145732
  19.3 9.0 %collective-permute-start.6 = (bf16[256,512]{1,0:T(8,128)(2,1)S(1)}, bf16[256,512]{1,0:T(8,128)(2,1)S(1)}, u32[]{:S(2)}, u32[]{:S(2)}) collective-permute-start(bf16[256,512]{1,0:T(8,128)(2,1)S(1)} %shard_map.91.refs_0_), channel_id=1, source_target_pairs={{0,4},{2,6},{4,0},{6,2},{8,12},{10,14},{12,8},{14,10},{16,20},{18,... | collective-permute-start | bytes 786440 | tf_op jit(solution)/shard_map/ppermute | solution.py:31
  22.3 8.8 %collective-permute-start.12 = (bf16[256,512]{1,0:T(8,128)(2,1)S(1)}, bf16[256,512]{1,0:T(8,128)(2,1)S(1)}, u32[]{:S(2)}, u32[]{:S(2)}) collective-permute-start(bf16[256,512]{1,0:T(8,128)(2,1)S(1)} %shard_map.93.refs_4_), channel_id=1, source_target_pairs={{0,4},{2,6},{4,0},{6,2},{8,12},{10,14},{12,8},{14,10},{16,20},{18,... | collective-permute-start | bytes 786440 | tf_op jit(solution)/shard_map/ppermute | solution.py:31
  23.9 7.2 %collective-permute-start.7 = (bf16[256,512]{1,0:T(8,128)(2,1)S(1)}, bf16[256,512]{1,0:T(8,128)(2,1)S(1)}, u32[]{:S(2)}, u32[]{:S(2)}) collective-permute-start(bf16[256,512]{1,0:T(8,128)(2,1)S(1)} %shard_map.91.refs_0_), channel_id=1, source_target_pairs={{0,2},{2,0},{4,6},{6,4},{8,10},{10,8},{12,14},{14,12},{16,18},{18,... | collective-permute-start | bytes 786440 | tf_op jit(solution)/shard_map/ppermute | solution.py:31
  24.7 9.0 %collective-permute-start.2 = (s32[264,256]{1,0:T(8,128)S(1)}, s32[264,256]{1,0:T(8,128)S(1)}, u32[]{:S(2)}, u32[]{:S(2)}) collective-permute-start(s32[264,256]{1,0:T(8,128)S(1)} %get-tuple-element.40.refs_0_.refs_1_), channel_id=1, source_target_pairs={{0,1},{1,0},{2,3},{3,2},{4,5},{5,4},{6,7},{7,6},{8,9},{9,8},{10,11... | collective-permute-start | bytes 811016 | tf_op jit(solution)/shard_map/ppermute | solution.py:31
  26.8 5.4 %collective-permute-start.13 = (bf16[256,512]{1,0:T(8,128)(2,1)S(1)}, bf16[256,512]{1,0:T(8,128)(2,1)S(1)}, u32[]{:S(2)}, u32[]{:S(2)}) collective-permute-start(bf16[256,512]{1,0:T(8,128)(2,1)S(1)} %shard_map.93.refs_4_), channel_id=1, source_target_pairs={{0,2},{2,0},{4,6},{6,4},{8,10},{10,8},{12,14},{14,12},{16,18},{18,... | collective-permute-start | bytes 786440 | tf_op jit(solution)/shard_map/ppermute | solution.py:31
  28.3 3.9 %collective-permute-start.8 = (bf16[256,512]{1,0:T(8,128)(2,1)S(1)}, bf16[256,512]{1,0:T(8,128)(2,1)S(1)}, u32[]{:S(2)}, u32[]{:S(2)}) collective-permute-start(bf16[256,512]{1,0:T(8,128)(2,1)S(1)} %collective-permute-done.6.refs_1_), channel_id=1, source_target_pairs={{0,2},{2,0},{4,6},{6,4},{8,10},{10,8},{12,14},{14,12},{16,18},{18,... | collective-permute-start | bytes 786440 | tf_op jit(solution)/shard_map/ppermute | solution.py:31
  31.1 1.5 %collective-permute-start.14 = (bf16[256,512]{1,0:T(8,128)(2,1)S(1)}, bf16[256,512]{1,0:T(8,128)(2,1)S(1)}, u32[]{:S(2)}, u32[]{:S(2)}) collective-permute-start(bf16[256,512]{1,0:T(8,128)(2,1)S(1)} %collective-permute-done.12.refs_5_), channel_id=1, source_target_pairs={{0,2},{2,0},{4,6},{6,4},{8,10},{10,8},{12,14},{14,12},{16,18},{18,... | collective-permute-start | bytes 786440 | tf_op jit(solution)/shard_map/ppermute | solution.py:31
  31.1 8.5 %collective-permute-start.16 = (bf16[112,1024]{1,0:T(8,128)(2,1)S(1)}, bf16[112,1024]{1,0:T(8,128)(2,1)S(1)}, u32[]{:S(2)}, u32[]{:S(2)}) collective-permute-start(bf16[112,1024]{1,0:T(8,128)(2,1)S(1)} %shard_map.96), channel_id=1, source_target_pairs={{0,1},{1,0},{2,3},{3,2},{4,5},{5,4},{6,7},{7,6},{8,9},{9,8},{10,11... | collective-permute-start | bytes 688136 | tf_op jit(solution)/shard_map/ppermute | solution.py:31
  32.2 1.5 %copy-start.3 = (s32[2,256]{1,0:T(2,128)S(1)}, s32[2,256]{1,0:T(2,128)}, u32[]{:S(2)}) copy-start(s32[2,256]{1,0:T(2,128)} %targets_ref.3) | copy-start | bytes 6148
  32.2 1.5 %copy-start.4 = (s32[2,256]{1,0:T(2,128)S(1)}, s32[2,256]{1,0:T(2,128)}, u32[]{:S(2)}) copy-start(s32[2,256]{1,0:T(2,128)} %valid_ref.3) | copy-start | bytes 6148
  34.4 10.4 %collective-permute-start.17 = (bf16[256,512]{1,0:T(8,128)(2,1)S(1)}, bf16[256,512]{1,0:T(8,128)(2,1)S(1)}, u32[]{:S(2)}, u32[]{:S(2)}) collective-permute-start(bf16[256,512]{1,0:T(8,128)(2,1)S(1)} %shard_map.95.grads_ref), channel_id=1, source_target_pairs={{0,1},{1,0},{2,3},{3,2},{4,5},{5,4},{6,7},{7,6},{8,9},{9,8},{10,11... | collective-permute-start | bytes 786440 | tf_op jit(solution)/shard_map/ppermute | solution.py:31
  39.6 5.2 %copy-start.5 = (s32[2]{0:T(128)S(1)}, s32[2]{0:T(128)}, u32[]{:S(2)}) copy-start(s32[2]{0:T(128)} %plan_ref.5) | copy-start | bytes 28
  46.4 2.0 %collective-permute-start.19 = (f32[512,256]{1,0:T(8,128)S(1)}, f32[512,256]{1,0:T(8,128)S(1)}, u32[]{:S(2)}, u32[]{:S(2)}) collective-permute-start(f32[512,256]{1,0:T(8,128)S(1)} %get-tuple-element.51), channel_id=1, source_target_pairs={{0,2},{2,0},{4,6},{6,4},{8,10},{10,8},{12,14},{14,12},{16,18},{18,... | collective-permute-start | bytes 1572872 | tf_op jit(solution)/shard_map/ppermute | solution.py:31
  46.5 8.9 %collective-permute-start.18 = (s32[264,256]{1,0:T(8,128)S(1)}, s32[264,256]{1,0:T(8,128)S(1)}, u32[]{:S(2)}, u32[]{:S(2)}) collective-permute-start(s32[264,256]{1,0:T(8,128)S(1)} %get-tuple-element.48), channel_id=1, source_target_pairs={{0,1},{1,0},{2,3},{3,2},{4,5},{5,4},{6,7},{7,6},{8,9},{9,8},{10,11... | collective-permute-start | bytes 811016 | tf_op jit(solution)/shard_map/ppermute | solution.py:31
  48.6 6.9 %collective-permute-start.20 = (s32[72,256]{1,0:T(8,128)S(1)}, s32[72,256]{1,0:T(8,128)S(1)}, u32[]{:S(2)}, u32[]{:S(2)}) collective-permute-start(s32[72,256]{1,0:T(8,128)S(1)} %get-tuple-element.52), channel_id=1, source_target_pairs={{0,24},{2,26},{4,28},{6,30},{8,16},{10,18},{12,20},{14,22},{16,8},... | collective-permute-start | bytes 221192 | tf_op jit(solution)/shard_map/ppermute | solution.py:31
  52.4 5.9 %collective-permute-start.22 = (s32[72,256]{1,0:T(8,128)S(1)}, s32[72,256]{1,0:T(8,128)S(1)}, u32[]{:S(2)}, u32[]{:S(2)}) collective-permute-start(s32[72,256]{1,0:T(8,128)S(1)} %get-tuple-element.55), channel_id=1, source_target_pairs={{0,16},{2,18},{4,20},{6,22},{8,24},{10,26},{12,28},{14,30},{16,0},... | collective-permute-start | bytes 221192 | tf_op jit(solution)/shard_map/ppermute | solution.py:31
  52.5 5.8 %collective-permute-start.23 = (s32[72,256]{1,0:T(8,128)S(1)}, s32[72,256]{1,0:T(8,128)S(1)}, u32[]{:S(2)}, u32[]{:S(2)}) collective-permute-start(s32[72,256]{1,0:T(8,128)S(1)} %get-tuple-element.56), channel_id=1, source_target_pairs={{0,8},{2,10},{4,12},{6,14},{8,0},{10,2},{12,4},{14,6},{16,24},{18,... | collective-permute-start | bytes 221192 | tf_op jit(solution)/shard_map/ppermute | solution.py:31
  56.1 7.9 %collective-permute-start.21 = (bf16[256,512]{1,0:T(8,128)(2,1)S(1)}, bf16[256,512]{1,0:T(8,128)(2,1)S(1)}, u32[]{:S(2)}, u32[]{:S(2)}) collective-permute-start(bf16[256,512]{1,0:T(8,128)(2,1)S(1)} %shard_map.102.grads_ref), channel_id=1, source_target_pairs={{0,1},{1,0},{2,3},{3,2},{4,5},{5,4},{6,7},{7,6},{8,9},{9,8},{10,11... | collective-permute-start | bytes 786440 | tf_op jit(solution)/shard_map/ppermute | solution.py:31
  65.3 2.0 %collective-permute-start.29 = (f32[512,256]{1,0:T(8,128)S(1)}, f32[512,256]{1,0:T(8,128)S(1)}, u32[]{:S(2)}, u32[]{:S(2)}) collective-permute-start(f32[512,256]{1,0:T(8,128)S(1)} %get-tuple-element.59), channel_id=1, source_target_pairs={{0,2},{2,0},{4,6},{6,4},{8,10},{10,8},{12,14},{14,12},{16,18},{18,... | collective-permute-start | bytes 1572872 | tf_op jit(solution)/shard_map/ppermute | solution.py:31
  65.3 6.5 %collective-permute-start.24 = (s32[72,256]{1,0:T(8,128)S(1)}, s32[72,256]{1,0:T(8,128)S(1)}, u32[]{:S(2)}, u32[]{:S(2)}) collective-permute-start(s32[72,256]{1,0:T(8,128)S(1)} %shard_map.104.refs_0_.one_ref), channel_id=1, source_target_pairs={{0,4},{2,6},{4,0},{6,2},{8,12},{10,14},{12,8},{14,10},{16,20},{18,... | collective-permute-start | bytes 221192 | tf_op jit(solution)/shard_map/ppermute | solution.py:31
  67.4 7.7 %collective-permute-start.30 = (s32[72,256]{1,0:T(8,128)S(1)}, s32[72,256]{1,0:T(8,128)S(1)}, u32[]{:S(2)}, u32[]{:S(2)}) collective-permute-start(s32[72,256]{1,0:T(8,128)S(1)} %get-tuple-element.61), channel_id=1, source_target_pairs={{0,24},{2,26},{4,28},{6,30},{8,16},{10,18},{12,20},{14,22},{16,8},... | collective-permute-start | bytes 221192 | tf_op jit(solution)/shard_map/ppermute | solution.py:31
  69.9 7.8 %collective-permute-start.31 = (s32[72,256]{1,0:T(8,128)S(1)}, s32[72,256]{1,0:T(8,128)S(1)}, u32[]{:S(2)}, u32[]{:S(2)}) collective-permute-start(s32[72,256]{1,0:T(8,128)S(1)} %get-tuple-element.62), channel_id=1, source_target_pairs={{0,16},{2,18},{4,20},{6,22},{8,24},{10,26},{12,28},{14,30},{16,0},... | collective-permute-start | bytes 221192 | tf_op jit(solution)/shard_map/ppermute | solution.py:31
  69.9 7.8 %collective-permute-start.32 = (s32[72,256]{1,0:T(8,128)S(1)}, s32[72,256]{1,0:T(8,128)S(1)}, u32[]{:S(2)}, u32[]{:S(2)}) collective-permute-start(s32[72,256]{1,0:T(8,128)S(1)} %get-tuple-element.63), channel_id=1, source_target_pairs={{0,8},{2,10},{4,12},{6,14},{8,0},{10,2},{12,4},{14,6},{16,24},{18,... | collective-permute-start | bytes 221192 | tf_op jit(solution)/shard_map/ppermute | solution.py:31
  71.9 9.9 %collective-permute-start.26 = (s32[72,256]{1,0:T(8,128)S(1)}, s32[72,256]{1,0:T(8,128)S(1)}, u32[]{:S(2)}, u32[]{:S(2)}) collective-permute-start(s32[72,256]{1,0:T(8,128)S(1)} %shard_map.106.refs_0_), channel_id=1, source_target_pairs={{0,16},{2,18},{4,20},{6,22},{8,24},{10,26},{12,28},{14,30},{16,0},... | collective-permute-start | bytes 221192 | tf_op jit(solution)/shard_map/ppermute | solution.py:31
  73.0 8.8 %collective-permute-start.25 = (s32[72,256]{1,0:T(8,128)S(1)}, s32[72,256]{1,0:T(8,128)S(1)}, u32[]{:S(2)}, u32[]{:S(2)}) collective-permute-start(s32[72,256]{1,0:T(8,128)S(1)} %shard_map.106.refs_0_), channel_id=1, source_target_pairs={{0,8},{2,10},{4,12},{6,14},{8,0},{10,2},{12,4},{14,6},{16,24},{18,... | collective-permute-start | bytes 221192 | tf_op jit(solution)/shard_map/ppermute | solution.py:31
  77.8 4.4 %collective-permute-start.33 = (s32[72,256]{1,0:T(8,128)S(1)}, s32[72,256]{1,0:T(8,128)S(1)}, u32[]{:S(2)}, u32[]{:S(2)}) collective-permute-start(s32[72,256]{1,0:T(8,128)S(1)} %shard_map.109.one_ref), channel_id=1, source_target_pairs={{0,4},{2,6},{4,0},{6,2},{8,12},{10,14},{12,8},{14,10},{16,20},{18,... | collective-permute-start | bytes 221192 | tf_op jit(solution)/shard_map/ppermute | solution.py:31
  79.4 7.4 %collective-permute-start.27 = (s32[72,256]{1,0:T(8,128)S(1)}, s32[72,256]{1,0:T(8,128)S(1)}, u32[]{:S(2)}, u32[]{:S(2)}) collective-permute-start(s32[72,256]{1,0:T(8,128)S(1)} %shard_map.106.refs_0_), channel_id=1, source_target_pairs={{0,24},{2,26},{4,28},{6,30},{8,16},{10,18},{12,20},{14,22},{16,8},... | collective-permute-start | bytes 221192 | tf_op jit(solution)/shard_map/ppermute | solution.py:31
  82.4 6.9 %collective-permute-start.36 = (s32[72,256]{1,0:T(8,128)S(1)}, s32[72,256]{1,0:T(8,128)S(1)}, u32[]{:S(2)}, u32[]{:S(2)}) collective-permute-start(s32[72,256]{1,0:T(8,128)S(1)} %shard_map.110.refs_0_), channel_id=1, source_target_pairs={{0,24},{2,26},{4,28},{6,30},{8,16},{10,18},{12,20},{14,22},{16,8},... | collective-permute-start | bytes 221192 | tf_op jit(solution)/shard_map/ppermute | solution.py:31
  84.8 6.3 %collective-permute-start.35 = (s32[72,256]{1,0:T(8,128)S(1)}, s32[72,256]{1,0:T(8,128)S(1)}, u32[]{:S(2)}, u32[]{:S(2)}) collective-permute-start(s32[72,256]{1,0:T(8,128)S(1)} %shard_map.110.refs_0_), channel_id=1, source_target_pairs={{0,16},{2,18},{4,20},{6,22},{8,24},{10,26},{12,28},{14,30},{16,0},... | collective-permute-start | bytes 221192 | tf_op jit(solution)/shard_map/ppermute | solution.py:31
  84.8 6.3 %collective-permute-start.34 = (s32[72,256]{1,0:T(8,128)S(1)}, s32[72,256]{1,0:T(8,128)S(1)}, u32[]{:S(2)}, u32[]{:S(2)}) collective-permute-start(s32[72,256]{1,0:T(8,128)S(1)} %shard_map.110.refs_0_), channel_id=1, source_target_pairs={{0,8},{2,10},{4,12},{6,14},{8,0},{10,2},{12,4},{14,6},{16,24},{18,... | collective-permute-start | bytes 221192 | tf_op jit(solution)/shard_map/ppermute | solution.py:31
  87.2 4.4 %collective-permute-start.28 = (s32[288,256]{1,0:T(8,128)S(1)}, s32[288,256]{1,0:T(8,128)S(1)}, u32[]{:S(2)}, u32[]{:S(2)}) collective-permute-start(s32[288,256]{1,0:T(8,128)S(1)} %shard_map.107.own0), channel_id=1, source_target_pairs={{0,2},{2,0},{4,6},{6,4},{8,10},{10,8},{12,14},{14,12},{16,18},{18,... | collective-permute-start | bytes 884744 | tf_op jit(solution)/shard_map/ppermute | solution.py:31
  91.6 1.6 %collective-permute-start.37 = (s32[288,256]{1,0:T(8,128)S(1)}, s32[288,256]{1,0:T(8,128)S(1)}, u32[]{:S(2)}, u32[]{:S(2)}) collective-permute-start(s32[288,256]{1,0:T(8,128)S(1)} %shard_map.111.own1), channel_id=1, source_target_pairs={{0,2},{2,0},{4,6},{6,4},{8,10},{10,8},{12,14},{14,12},{16,18},{18,... | collective-permute-start | bytes 884744 | tf_op jit(solution)/shard_map/ppermute | solution.py:31
